TPU v7x, 32 devices: a whole 2x2x4 slice. The times are simulated.
32 devices in a mesh: row: 2 (over x), col: 4 (over z), depth: 4 (over y, core).
Axes of the slice: x: 2, y: 2, z: 4, core: 2. Of those that a mesh axis runs over, the one named last changes fastest.
Arguments:
- integrals: bfloat16 [2048, 5120], P('row', 'depth'), may hold values from -0.25 to 0.25
- amplitudes: bfloat16 [1280, 4, 10000], P('depth', 'row', 'col'), may hold values from -6 to 6
- ab_irrep: int32 [2048], P('row'), may hold values from 0 to 7
- cd_irrep: int32 [5120], P('depth'), may hold values from 0 to 7
Outputs:
- residual: bfloat16 [2048, 10000], P(('row', 'depth'), 'col')
All inputs are finite; a program needn't handle non-finite values.
Results may differ from a plain program's by a relative error of at most 0.001.
Values may be sent and summed in bfloat16 or wider, within the bound.
No kernel may reach another device: no remote copies, remote signals or barrier semaphores. Data moves between devices by JAX's collectives and lax.ppermute only.
A program may use at most 192 MiB of HBM per device.

v0:
```python
import jax
import jax.numpy as jnp
from jax import lax
from jax.sharding import PartitionSpec as P

OCC = 100


def local(integrals, amplitudes, ab_irrep, cd_irrep):
    keep = ab_irrep[:, None] == cd_irrep[None, :]
    masked = jnp.where(keep, integrals, jnp.zeros_like(integrals))
    rows_here = masked.shape[0]
    blocks_here = amplitudes.shape[0]
    sub_here = amplitudes.shape[1]
    columns = amplitudes.shape[2]
    sub_full = sub_here * lax.axis_size("row")
    shaped = masked.reshape(rows_here, blocks_here, sub_full)
    total = jnp.einsum(
        "rck,ckj->rj",
        shaped,
        lax.all_gather(amplitudes, "row", axis=1, tiled=True),
        preferred_element_type=jnp.float32,
    )
    ladder = lax.psum_scatter(total, "depth", scatter_dimension=0, tiled=True)
    out_rows = ladder.shape[0]
    local_occ = columns // OCC
    cube = ladder.reshape(out_rows, local_occ, OCC)
    mirrored = lax.all_to_all(cube, "col", split_axis=2, concat_axis=1, tiled=True)
    result = cube - jnp.swapaxes(mirrored, 1, 2)
    return result.reshape(out_rows, columns).astype(jnp.bfloat16)


def solution(mesh):
    in_specs = (P("row", "depth"), P("depth", "row", "col"), P("row"), P("depth"))
    out_specs = P(("row", "depth"), "col")
    return jax.shard_map(local, mesh=mesh, in_specs=in_specs, out_specs=out_specs, check_vma=False)
```

profile of v0, /device:TPU:0, one launch (start us, length us, event | category | flops | bytes accessed | tf_op | source)
XLA Modules:
  0.0 293.8 jit_solution(12975401006751296765)
XLA Ops:
  6.5 0.0 all-gather.2.cloned.1.call-start
  6.5 3.9 %copy.13 = bf16[320,2,2500]{2,0,1:T(8,128)(2,1)} copy(bf16[320,2,2500]{2,1,0:T(2,128)(2,1)} %param.5) | data formatting | bytes 6400000 | tf_op args[1]
  10.5 0.0 copy-start
  10.5 0.0 copy-start.1
  10.5 0.0 copy-start.2
  10.5 0.0 all-gather.2.cloned.1.call-update
  10.5 0.0 reduce-scatter.2.cloned.1.call-start
  10.5 1.7 copy-done
  12.2 0.0 copy-done.1
  12.2 0.0 copy-done.2
  12.2 2.2 compare_select_fusion
  14.4 3.0 %copy.12 = bf16[1024,1280]{0,1:T(8,128)(2,1)S(1)} copy(bf16[1024,1280]{1,0:T(8,128)(2,1)} %compare_select_fusion) | data formatting | bytes 5242880 | tf_op jit(solution)/shard_map/jit(_where)/select_n | solution.py:11
  17.4 3.0 %reshape.10 = bf16[1024,320,4]{0,2,1:T(4,128)(2,1)} reshape(bf16[1024,1280]{0,1:T(8,128)(2,1)S(1)} %copy.12) | data formatting | bytes 5242880 | tf_op jit(solution)/shard_map/reshape | solution.py:17
  20.4 76.3 %all-gather.2.cloned.1.call-done = bf16[320,4,2500]{2,0,1:T(8,128)(2,1)} async-done(((bf16[320,2,2500]{2,0,1:T(8,128)(2,1)}), bf16[320,4,2500]{2,0,1:T(8,128)(2,1)}) %all-gather.2.cloned.1.call-update) | async-done | bytes 6400016 | tf_op jit(solution)/shard_map/all_gather | solution.py:21
  96.7 13.0 %convolution_bitcast_fusion = f32[1024,2500]{0,1:T(8,128)} fusion(bf16[320,4,2500]{2,0,1:T(8,128)(2,1)} %all-gather.2.cloned.1.call-done, bf16[1024,320,4]{0,2,1:T(4,128)(2,1)} %reshape.10), kind=kOutput, calls=%fused_computation | convolution fusion | flops 6553600000 | bytes 19261440 | tf_op jit(solution)/shard_map/rck,ckj->rj/dot_general | solution.py:18
  109.7 0.0 reduce-scatter.2.cloned.1.call-update
  109.7 84.0 %reduce-scatter.2.cloned.1.call-done = f32[256,2500]{0,1:T(8,128)} async-done(((f32[1024,2500]{0,1:T(8,128)}), f32[256,2500]{0,1:T(8,128)}) %reduce-scatter.2.cloned.1.call-update) | async-done | bytes 2560016 | tf_op jit(solution)/shard_map/reduce_scatter | solution.py:24
  193.6 2.4 reshape.11
  196.0 0.9 copy.15
  196.9 77.9 %all_to_all.18 = f32[256,25,100]{0,1,2:T(8,128)S(1)} all-to-all(f32[256,25,100]{0,1,2:T(8,128)S(1)} %copy.15), channel_id=1, replica_groups=mesh['row'=2,'col'=4,'depth'=4] {'col'}, dimensions={2} | all-to-all | bytes 5120000 | tf_op jit(solution)/shard_map/all_to_all | solution.py:28
  274.8 1.9 copy.17
  276.7 4.4 %all_to_all.16 = f32[256,100,25]{0,1,2:T(8,128)} reshape(f32[256,4,25,25]{0,2,1,3:T(8,128)} %copy.17) | data formatting | bytes 5120000 | tf_op jit(solution)/shard_map/all_to_all | solution.py:28
  281.1 3.2 %fusion = bf16[256,25,100]{0,2,1:T(8,128)(2,1)} fusion(f32[256,25,100]{0,2,1:T(8,128)S(1)} %reshape.11, f32[256,100,25]{0,1,2:T(8,128)} %all_to_all.16), kind=kLoop, calls=%fused_computation.3 | loop fusion | flops 1280000 | bytes 6400000 | tf_op jit(solution)/shard_map/convert_element_type | solution.py:30
  284.3 2.7 convert_element_type.7
Async XLA Ops:
  6.5 90.1 %all-gather.2.cloned.1.call-start = ((), (), s32[]{:S(2)}) async-start(), calls=%async_computation.2 | async-start | bytes 9830400 | tf_op jit(solution)/shard_map/all_gather | solution.py:21
  10.5 1.7 copy-start
  10.5 1.7 copy-start.1
  10.5 1.7 copy-start.2
  10.5 183.2 %reduce-scatter.2.cloned.1.call-start = ((), (), s32[]{:S(2)}) async-start(), calls=%async_computation.3 | async-start | bytes 12820480 | tf_op jit(solution)/shard_map/reduce_scatter | solution.py:24
Sparse Core Ops, SparseCore 0:
  10.6 86.0 all-gather.1
  109.8 83.7 reduce-scatter.1
where the time goes:
time: 294 us
  waiting for transfers between devices  160 us (54%)
  blocking collectives  77.9 us (26%)
  local copies, waits for them, and re-layouts  23.8 us (8%)
  between operations  13.4 us (5%)
  matrix products  13 us (4%)
  other arithmetic  5.42 us (2%)
    reduce_scatter x1, waiting for transfers between devices, local(): ladder = lax.psum_scatter(total, 'depth', scatter_dimension=0, tiled=True)  84 us
    all_to_all x1, blocking collectives, local(): lax.all_to_all(cube, 'col', split_axis=2, concat_axis=1, tiled=True)  77.9 us
    all_gather x1, waiting for transfers between devices, local(): lax.all_gather(amplitudes, 'row', axis=1, tiled=True)  76.3 us
    dot_general x1, matrix products, local(): jnp.einsum('rck,ckj->rj', shaped, lax.all_gather(amplitudes, 'row', axis=...  13 us
    all_to_all x2, local copies, waits for them, and re-layouts, local(): lax.all_to_all(cube, 'col', split_axis=2, concat_axis=1, tiled=True)  6.28 us
  transfers between devices with their start and end apart: 2, of which 2 were waited for; matrix products, arithmetic and copies ran while one was open for 3% of the time, Pallas kernels for 0%

commit v1 on v0

v1 whole, which is shorter than its diff:
```python
import functools

import jax
import jax.numpy as jnp
import numpy as np
from jax import lax
from jax.experimental import pallas as pl
from jax.experimental.pallas import tpu as pltpu
from jax.sharding import PartitionSpec as P

OCC = 100
TOP = 32000.0
STEPS = 256.0
CORES = 2


def index_tables(groups):
    n = OCC // groups
    half = (n * n + 1) // 2
    chunk = -(-(half + 1) // 16) * 16
    own = np.full((groups, groups, chunk, 1), -1, np.int32)
    away = np.full((groups, groups, chunk, 1), -1, np.int32)
    for z in range(groups):
        inside = [(i, j) for i in range(n) for j in range(i + 1, n)]
        for p, (i, j) in enumerate(inside):
            own[z, 0, p, 0] = i * OCC + z * n + j
            away[z, 0, p, 0] = j * OCC + z * n + i
        for r in range(1, groups):
            other = (z + r) % groups
            entries = [(e // n, e % n) for e in range(n * n)]
            if z < other:
                mine = entries[:half]
            else:
                mine = [(j, i) for i, j in entries[half:]]
            for p, (i, j) in enumerate(mine):
                own[z, r, p, 0] = i * OCC + other * n + j
                away[other, r, p, 0] = j * OCC + z * n + i
    return own, away, chunk


def dot_nt(a, b):
    return lax.dot_general(a, b, (((1,), (1,)), ((), ())), preferred_element_type=jnp.float32)


def dot_tn(a, b):
    return lax.dot_general(a, b, (((0,), (0,)), ((), ())), preferred_element_type=jnp.float32)


def one_hot(index, width):
    lanes = lax.broadcasted_iota(jnp.int32, (index.shape[0], width), 1)
    return jnp.where(lanes == index, 1.0, 0.0).astype(jnp.bfloat16)


def encode(values):
    largest = jnp.maximum(jnp.max(jnp.abs(values), axis=0, keepdims=True), 1e-30)
    code = jnp.floor(jnp.log2(TOP / largest) * STEPS)
    coded = jnp.round(values * jnp.exp2(code * (1.0 / STEPS)))
    rows = lax.broadcasted_iota(jnp.int32, values.shape, 0)
    coded = jnp.where(rows == values.shape[0] - 1, code, coded)
    return coded.astype(jnp.int32).astype(jnp.int16)


def decode(coded):
    values = coded.astype(jnp.int32).astype(jnp.float32)
    rows = lax.broadcasted_iota(jnp.int32, values.shape, 0)
    last = rows == values.shape[0] - 1
    code = jnp.sum(jnp.where(last, values, 0.0), axis=0, keepdims=True)
    return jnp.where(last, 0.0, values * jnp.exp2(code * (-1.0 / STEPS)))


def call(body, scalars, inputs, outputs, flops, moved):
    whole = lambda rank: (lambda g, s: (0,) * rank)
    in_specs = []
    for array, block, index in inputs:
        if block is None:
            in_specs.append(pl.BlockSpec(array.shape, whole(array.ndim)))
        else:
            in_specs.append(pl.BlockSpec(block, index))
    out_specs = [pl.BlockSpec(shape, whole(len(shape))) for shape, _ in outputs]
    return pl.pallas_call(
        body,
        out_shape=[jax.ShapeDtypeStruct(shape, dtype) for shape, dtype in outputs],
        grid_spec=pltpu.PrefetchScalarGridSpec(
            num_scalar_prefetch=1, grid=(1,), in_specs=in_specs, out_specs=out_specs
        ),
        compiler_params=pltpu.CompilerParams(vmem_limit_bytes=48 * 2**20),
        cost_estimate=pl.CostEstimate(flops=int(flops), bytes_accessed=int(moved), transcendentals=0),
    )(scalars, *[array for array, _, _ in inputs])


def mask_body(count, s_ref, *refs):
    sel_ref, cd_here, cd_there = refs[:3]
    refs = refs[3:]
    ins, outs = refs[: 3 * count], refs[3 * count :]
    pick = None
    for k in range(count):
        ab_ref, here_ref, there_ref = ins[3 * k : 3 * k + 3]
        if pick is None:
            pick = one_hot(sel_ref[0], here_ref.shape[-1])
        ab = ab_ref[0]
        for core, (v_ref, cd_ref) in enumerate(((here_ref, cd_here), (there_ref, cd_there))):
            v = v_ref[...].reshape(v_ref.shape[-2:]).astype(jnp.float32)
            kept = jnp.where(ab == cd_ref[...], v, 0.0).astype(jnp.bfloat16)
            outs[k][core] = dot_nt(kept, pick).astype(jnp.bfloat16)


def select_body(s_ref, idx_ref, t_ref, *out_refs):
    t = t_ref[...]
    for k in range(idx_ref.shape[1]):
        picked = dot_nt(one_hot(idx_ref[0, k], t.shape[1]), t).astype(jnp.bfloat16)
        if len(out_refs) > 1:
            out_refs[k][...] = picked
        else:
            out_refs[0][k] = picked


def sum_body(groups, s_ref, *refs):
    own_here, own_there, away_here, away_there = refs[:4]
    there, here = refs[4 : 4 + groups], refs[4 + groups : 4 + 2 * groups]
    coded_ref, kept_ref = refs[4 + 2 * groups :]

    def tile(ref):
        return ref[...].reshape(ref.shape[-2:])

    to, too, tr, tro = tile(own_here), tile(own_there), tile(away_here), tile(away_there)

    def partial(a_ref):
        a, b = a_ref[0], a_ref[1]
        return (dot_nt(to, a) + dot_nt(too, b)) - (dot_nt(tr, a) + dot_nt(tro, b))

    for g in range(groups):
        coded_ref[g] = encode(partial(there[g]))
    for g in range(groups):
        kept_ref[g] = partial(here[g])


def add_y_body(s_ref, kept_ref, coded_ref, sum_ref, *out_refs):
    for g in range(kept_ref.shape[0]):
        total = kept_ref[g] + decode(coded_ref[g])
        if g == 0:
            sum_ref[...] = total
        else:
            out_refs[g - 1][...] = encode(total)


def add_x_body(s_ref, sum_ref, *refs):
    total = sum_ref[...]
    for ref in refs[:-1]:
        total = total + decode(ref[...])
    refs[-1][...] = total.astype(jnp.bfloat16)


def place_body(groups, s_ref, own_ref, away_ref, *refs):
    out_ref = refs[-1]
    width = out_ref.shape[1]
    mine, others = refs[:groups], refs[groups:-1]
    total = None
    for k in range(groups):
        minus = mine[0] if k == 0 else others[k - 1]
        term = dot_tn(mine[k][...], one_hot(own_ref[0, k], width)) - dot_tn(minus[...], one_hot(away_ref[0, k], width))
        total = term if total is None else total + term
    out_ref[...] = total.astype(jnp.bfloat16)


def local(integrals, amplitudes, ab_irrep, cd_irrep):
    row_n, col_n, depth_n = lax.axis_size("row"), lax.axis_size("col"), lax.axis_size("depth")
    x, z, d = lax.axis_index("row"), lax.axis_index("col"), lax.axis_index("depth")
    y_n = depth_n // CORES
    y, core = d // CORES, d % CORES
    rows, cd_here = integrals.shape
    blocks, sub, columns = amplitudes.shape
    k_here = blocks * sub
    tall = rows // depth_n
    own_np, away_np, chunk = index_tables(col_n)
    own_table, away_table = jnp.asarray(own_np), jnp.asarray(away_np)
    bf16, i16, f32 = jnp.bfloat16, jnp.int16, jnp.float32

    def shift(array, axis, by):
        n = lax.axis_size(axis)
        return lax.ppermute(array, axis, [(i, (i + by) % n) for i in range(n)])

    def other_core(array):
        return lax.ppermute(array, "depth", [(i, i ^ 1) for i in range(depth_n)])

    zone = lambda rank: (lambda g, s: (s[1],) + (0,) * (rank - 1))
    scalars = jnp.stack([x, z, y, core]).astype(jnp.int32)

    v = integrals.reshape(y_n, CORES, tall, cd_here)
    v_there = other_core(lax.dynamic_index_in_dim(v, 1 - core, axis=1, keepdims=False))
    cd_row = cd_irrep.reshape(1, cd_here)
    cd_there = other_core(cd_row)
    ab = ab_irrep.reshape(y_n * CORES, tall, 1)
    sub_full = sub * row_n
    t = np.arange(k_here)
    sel = np.stack([(t // sub) * sub_full + g * sub + t % sub for g in range(row_n)])
    sel = jnp.asarray(sel.astype(np.int32)[:, :, None])

    def masked(by):
        steps = list(range(1, y_n)) + [0]
        ins = [(sel, (1, k_here, 1), lambda g, s: (lax.rem(s[0] - by + row_n, row_n), 0, 0)), (cd_row, None, None), (cd_there, None, None)]
        for step in steps:
            at = lambda s, step=step: lax.rem(s[2] + step, y_n)
            ins.append((ab, (1, tall, 1), lambda g, s, at=at: (at(s) * CORES + s[3], 0, 0)))
            ins.append((v, (1, 1, tall, cd_here), lambda g, s, at=at: (at(s), s[3], 0, 0)))
            ins.append((v_there, (1, tall, cd_here), lambda g, s, at=at: (at(s), 0, 0)))
        outs = [((CORES, tall, k_here), bf16)] * y_n
        flops = 2 * y_n * CORES * tall * cd_here * k_here
        return call(functools.partial(mask_body, y_n), scalars, ins, outs, flops, 3 * y_n * CORES * tall * cd_here)

    a_there, a_here = [None] * row_n, [None] * row_n
    for by in list(range(1, row_n)) + [0]:
        first, last = masked(by)
        if by:
            first, last = shift(first, "row", -by), shift(last, "row", -by)
        a_there[by], a_here[by] = first, last

    flat = amplitudes.reshape(k_here, columns)
    away_block = (1, col_n - 1, chunk, 1)
    sent = call(
        select_body,
        scalars,
        [(away_table[:, 1:], away_block, zone(4)), (flat, None, None)],
        [((chunk, k_here), bf16)] * (col_n - 1),
        2 * (col_n - 1) * chunk * columns * k_here,
        2 * k_here * (columns + (col_n - 1) * chunk),
    )
    t_away = {r: shift(sent[r - 1], "col", -r) for r in range(1, col_n)}
    kept_table = jnp.asarray(np.concatenate([own_np, away_np[:, :1]], axis=1))
    kept_n = col_n + 1
    (kept,) = call(
        select_body,
        scalars,
        [(kept_table, (1, kept_n, chunk, 1), zone(4)), (flat, None, None)],
        [((kept_n, chunk, k_here), bf16)],
        2 * kept_n * chunk * columns * k_here,
        2 * k_here * (columns + kept_n * chunk),
    )
    kept_there = other_core(kept)

    mine, others = [None] * col_n, [None] * col_n
    for k in [0] + list(range(1, col_n)):
        block = (1, chunk, k_here)
        at = lambda g, s, k=k: (k, 0, 0)
        ins = [(kept, block, at), (kept_there, block, at)]
        if k == 0:
            last = lambda g, s: (kept_n - 1, 0, 0)
            ins += [(kept, block, last), (kept_there, block, last)]
        else:
            ins += [(t_away[k], None, None), (other_core(t_away[k]), None, None)]
        ins += [(a, None, None) for a in a_there + a_here]
        coded, own_sum = call(
            functools.partial(sum_body, row_n),
            scalars,
            ins,
            [((row_n, chunk, tall), i16), ((row_n, chunk, tall), f32)],
            2 * 2 * y_n * row_n * chunk * tall * CORES * k_here,
            2 * CORES * k_here * (2 * chunk + y_n * row_n * tall) + 6 * row_n * chunk * tall,
        )
        coded = shift(coded, "depth", CORES)
        sums = call(
            add_y_body,
            scalars,
            [(own_sum, None, None), (coded, None, None)],
            [((chunk, tall), f32)] + [((chunk, tall), i16)] * (row_n - 1),
            10 * row_n * chunk * tall,
            10 * row_n * chunk * tall,
        )
        arrived = [shift(sums[g], "row", g) for g in range(1, row_n)]
        (mine[k],) = call(
            add_x_body,
            scalars,
            [(a, None, None) for a in [sums[0]] + arrived],
            [((chunk, tall), bf16)],
            10 * row_n * chunk * tall,
            (6 + 2 * row_n) * chunk * tall,
        )
        if k:
            others[k] = shift(mine[k], "col", k)

    (out,) = call(
        functools.partial(place_body, col_n),
        scalars,
        [(own_table, (1, col_n, chunk, 1), zone(4)), (away_table, (1, col_n, chunk, 1), zone(4))]
        + [(a, None, None) for a in mine + others[1:]],
        [((tall, columns), bf16)],
        4 * col_n * chunk * tall * columns,
        2 * tall * (columns + 2 * col_n * chunk),
    )
    return out


def solution(mesh):
    in_specs = (P("row", "depth"), P("depth", "row", "col"), P("row"), P("depth"))
    out_specs = P(("row", "depth"), "col")
    return jax.shard_map(local, mesh=mesh, in_specs=in_specs, out_specs=out_specs, check_vma=False)
```

time: 294 us -> 141 us (0.48)
  waiting for transfers between devices: 160 us -> 41.7 us
  blocking collectives: 77.9 us -> 0 us
  Pallas kernels: 0 us -> 54.3 us
  starting transfers between devices: 0.04 us -> 26.5 us
  between operations: 13.4 us -> 0.23 us
  matrix products: 13 us -> 0 us
  local copies, waits for them, and re-layouts: 23.8 us -> 17.7 us
  other arithmetic: 5.42 us -> 0.08 us
    reduce_scatter x1 -> x0, waiting for transfers between devices: 84 us -> none  [local(): ladder = lax.psum_scatter(total, 'depth', scatter_dimension=0, tiled=True)]
    all_to_all x1 -> x0, blocking collectives: 77.9 us -> none  [local(): lax.all_to_all(cube, 'col', split_axis=2, concat_axis=1, tiled=True)]
    all_gather x1 -> x0, waiting for transfers between devices: 76.3 us -> none  [local(): lax.all_gather(amplitudes, 'row', axis=1, tiled=True)]
    pallas_call x0 -> x17, Pallas kernels: none -> 54.3 us  [call(): pl.pallas_call(body, out_shape=[jax.ShapeDtypeStruct(shape, dtype) for sh...]
    ppermute x0 -> x22, waiting for transfers between devices: none -> 41.7 us  [the longest x16 40.2 us: shift(): return lax.ppermute(array, axis, [(i, (i + by) % n) for i in range(n)])]
    ppermute x0 -> x22, starting transfers between devices: none -> 26.5 us  [the longest x16 25.2 us: shift(): return lax.ppermute(array, axis, [(i, (i + by) % n) for i in range(n)])]
    dot_general x1 -> x0, matrix products: 13 us -> none  [local(): jnp.einsum('rck,ckj->rj', shaped, lax.all_gather(amplitudes, 'row', axis=...]
    all_to_all x2 -> x0, local copies, waits for them, and re-layouts: 6.28 us -> none  [local(): lax.all_to_all(cube, 'col', split_axis=2, concat_axis=1, tiled=True)]
  transfers between devices with their start and end apart: 2 -> 22, of which waited for: 2 -> 7; matrix products, arithmetic and copies ran while one was open for 3% -> 6% of each run, Pallas kernels for 0% -> 33%
where the time goes in v1:
time: 141 us; the launch traced here: 140 us
  Pallas kernels  54.3 us (39%)
  waiting for transfers between devices  41.7 us (30%)
  starting transfers between devices  26.5 us (19%)
  local copies, waits for them, and re-layouts  17.7 us (13%)
    pallas_call x17, Pallas kernels, call(): pl.pallas_call(body, out_shape=[jax.ShapeDtypeStruct(shape, dtype) for sh...  54.3 us
    ppermute x16, waiting for transfers between devices, shift(): return lax.ppermute(array, axis, [(i, (i + by) % n) for i in range(n)])  40.2 us
    ppermute x16, starting transfers between devices, shift(): return lax.ppermute(array, axis, [(i, (i + by) % n) for i in range(n)])  25.2 us
    reshape x1, local copies, waits for them, and re-layouts, local(): flat = amplitudes.reshape(k_here, columns)  7.69 us
    unnamed x20, local copies, waits for them, and re-layouts  4.83 us
  transfers between devices with their start and end apart: 22, of which 7 were waited for; matrix products, arithmetic and copies ran while one was open for 6% of the time, Pallas kernels for 33%

profile of v1, /device:TPU:0, one launch (start us, length us, event | category | flops | bytes accessed | tf_op | source)
XLA Modules:
  0.0 140.4 jit_solution(5234113848218452587)
XLA Ops:
  0.0 2.5 %dynamic-slice_bitcast_fusion = bf16[2,256,1280]{2,1,0:T(8,128)(2,1)} fusion(bf16[2,2,256,1280]{3,2,1,0:T(8,128)(2,1)} %bitcast.7, s32[]{:T(128)S(6)} %select_n.17), kind=kLoop, calls=%fused_computation | loop fusion | bytes 2621444 | tf_op jit(solution)/shard_map/jit(dynamic_index_in_dim)/squeeze | solution.py:189
  3.0 7.7 %reshape.12.t_ref = bf16[640,2500]{1,0:T(8,128)(2,1)} reshape(bf16[320,2,2500]{2,1,0:T(2,128)(2,1)} %param.9) | data formatting | bytes 6400000 | tf_op jit(solution)/shard_map/reshape | solution.py:217
  10.8 1.9 %copy-done.5 = s32[4,5,320,1]{3,2,1,0:T(8,128)S(1)} copy-done((s32[4,5,320,1]{3,2,1,0:T(8,128)S(1)}, s32[4,5,320,1]{3,2,1,0:T(8,128)}, u32[]{:S(2)}) %copy-start.5) | copy-done | bytes 25624
  12.7 9.1 %shard_map.82.refs_0_.refs_2_ = bf16[5,320,640]{2,1,0:T(8,128)(2,1)S(1)} custom-call(s32[4]{0:T(128)S(1)} %pad_add_fusion.s_ref, s32[4,5,320,1]{3,2,1,0:T(8,128)S(1)} %copy-done.5, bf16[640,2500]{1,0:T(8,128)(2,1)} %reshape.12.t_ref), custom_call_target="tpu_custom_call" | custom-call | flops 5120000000 | bytes 5248000 | tf_op jit(solution)/shard_map/pallas_call | solution.py:80
  21.9 7.3 %shard_map.88 = (bf16[320,640]{1,0:T(8,128)(2,1)S(1)}, bf16[320,640]{1,0:T(8,128)(2,1)}, bf16[320,640]{1,0:T(8,128)(2,1)}) custom-call(s32[4]{0:T(128)S(1)} %pad_add_fusion.s_ref, s32[4,3,320,1]{3,2,1,0:T(8,128)S(1)} %copy-done.7, bf16[640,2500]{1,0:T(8,128)(2,1)} %reshape.12.t_ref), custom_call_target="tpu_custom_call" | custom-call | flops 3072000000 | bytes 4428800 | tf_op jit(solution)/shard_map/pallas_call | solution.py:80
  29.2 0.7 copy-done.4
  29.9 3.0 %collective-permute-start.15 = (bf16[320,640]{1,0:T(8,128)(2,1)}, bf16[320,640]{1,0:T(8,128)(2,1)}, u32[]{:S(2)}, u32[]{:S(2)}) collective-permute-start(bf16[320,640]{1,0:T(8,128)(2,1)} %get-tuple-element.46), channel_id=1, source_target_pairs={{0,4},{4,8},{8,12},{12,0},{1,5},{5,9},{9,13},{13,1},{2,6},{6,10},{... | collective-permute-start | bytes 1228808 | tf_op jit(solution)/shard_map/ppermute | solution.py:180
  32.9 2.6 %collective-permute-start.11 = (bf16[320,640]{1,0:T(8,128)(2,1)}, bf16[320,640]{1,0:T(8,128)(2,1)}, u32[]{:S(2)}, u32[]{:S(2)}) collective-permute-start(bf16[320,640]{1,0:T(8,128)(2,1)} %get-tuple-element.41), channel_id=1, source_target_pairs={{0,8},{4,12},{8,0},{12,4},{1,9},{5,13},{9,1},{13,5},{2,10},{6,14},... | collective-permute-start | bytes 1228808 | tf_op jit(solution)/shard_map/ppermute | solution.py:180
  35.6 1.1 reshape.16.refs_3_.refs_6_
  36.7 1.3 collective-permute-start.7
  38.1 1.0 copy-done.2
  39.1 1.1 copy-done.3
  40.2 4.2 %shard_map.84 = (bf16[2,256,640]{2,1,0:T(8,128)(2,1)S(1)}, bf16[2,256,640]{2,1,0:T(8,128)(2,1)S(1)}) custom-call(s32[4]{0:T(128)S(1)} %pad_add_fusion.s_ref, s32[2,640,1]{2,1,0:T(8,128)S(1)} %copy-done.3, s32[1,1280]{1,0:T(1,128)S(1)} %reshape.13.refs_1_, s32[1,1280]{1,0:T(1,128)S(1)} %collective-permute-done.1.refs_2_, s32[4,256,1]{2,1,0:T(8,128)S(1)} %copy-done.2, ...), custom_call_target="tpu_custom_call" | custom-call | flops 1677721600 | bytes 3932160 | tf_op jit(solution)/shard_map/pallas_call | solution.py:80
  44.4 1.6 %collective-permute-start.3 = (bf16[2,256,640]{2,1,0:T(8,128)(2,1)S(1)}, bf16[2,256,640]{2,1,0:T(8,128)(2,1)S(1)}, u32[]{:S(2)}, u32[]{:S(2)}) collective-permute-start(bf16[2,256,640]{2,1,0:T(8,128)(2,1)S(1)} %get-tuple-element.29), channel_id=1, source_target_pairs={{0,16},{16,0},{1,17},{17,1},{2,18},{18,2},{3,19},{19,3},{4,20},{20... | collective-permute-start | bytes 1966088 | tf_op jit(solution)/shard_map/ppermute | solution.py:180
  45.9 1.5 %collective-permute-start.4 = (bf16[2,256,640]{2,1,0:T(8,128)(2,1)S(1)}, bf16[2,256,640]{2,1,0:T(8,128)(2,1)S(1)}, u32[]{:S(2)}, u32[]{:S(2)}) collective-permute-start(bf16[2,256,640]{2,1,0:T(8,128)(2,1)S(1)} %get-tuple-element.31), channel_id=1, source_target_pairs={{0,16},{16,0},{1,17},{17,1},{2,18},{18,2},{3,19},{19,3},{4,20},{20... | collective-permute-start | bytes 1966088 | tf_op jit(solution)/shard_map/ppermute | solution.py:180
  47.4 15.3 %collective-permute-done.11.refs_2_ = bf16[320,640]{1,0:T(8,128)(2,1)} collective-permute-done((bf16[320,640]{1,0:T(8,128)(2,1)}, bf16[320,640]{1,0:T(8,128)(2,1)}, u32[]{:S(2)}, u32[]{:S(2)}) %collective-permute-start.11) | collective-permute-done | bytes 409632 | tf_op jit(solution)/shard_map/ppermute | solution.py:180
  62.7 0.5 collective-permute-start.12
  63.2 1.4 %collective-permute-done.16.refs_3_ = bf16[320,640]{1,0:T(8,128)(2,1)S(1)} collective-permute-done((bf16[320,640]{1,0:T(8,128)(2,1)}, bf16[320,640]{1,0:T(8,128)(2,1)S(1)}, u32[]{:S(2)}, u32[]{:S(2)}) %collective-permute-start.16) | collective-permute-done | bytes 409632 | tf_op jit(solution)/shard_map/ppermute | solution.py:183
  64.8 4.2 %shard_map.83 = (bf16[2,256,640]{2,1,0:T(8,128)(2,1)S(1)}, bf16[2,256,640]{2,1,0:T(8,128)(2,1)S(1)}) custom-call(s32[4]{0:T(128)S(1)} %pad_add_fusion.s_ref, s32[2,640,1]{2,1,0:T(8,128)S(1)} %copy-done.3, s32[1,1280]{1,0:T(1,128)S(1)} %reshape.13.refs_1_, s32[1,1280]{1,0:T(1,128)S(1)} %collective-permute-done.1.refs_2_, s32[4,256,1]{2,1,0:T(8,128)S(1)} %copy-done.2, ...), custom_call_target="tpu_custom_call" | custom-call | flops 1677721600 | bytes 3932160 | tf_op jit(solution)/shard_map/pallas_call | solution.py:80
  69.0 6.3 %collective-permute-done.4.refs_7_ = bf16[2,256,640]{2,1,0:T(8,128)(2,1)S(1)} collective-permute-done((bf16[2,256,640]{2,1,0:T(8,128)(2,1)S(1)}, bf16[2,256,640]{2,1,0:T(8,128)(2,1)S(1)}, u32[]{:S(2)}, u32[]{:S(2)}) %collective-permute-start.4) | collective-permute-done | bytes 655392 | tf_op jit(solution)/shard_map/ppermute | solution.py:180
  75.3 4.1 %shard_map.95 = (s16[2,320,256]{2,1,0:T(8,128)(2,1)S(1)}, f32[2,320,256]{2,1,0:T(8,128)S(1)}) custom-call(s32[4]{0:T(128)S(1)} %pad_add_fusion.s_ref, bf16[5,320,640]{2,1,0:T(8,128)(2,1)} %copy-done, bf16[5,320,640]{2,1,0:T(8,128)(2,1)} %collective-permute-done.refs_1_.refs_3_, bf16[320,640]{1,0:T(8,128)(2,1)} %collective-permute-done.15.refs_2_, ...), custom_call_target="tpu_custom_call" | custom-call | flops 1677721600 | bytes 5242880 | tf_op jit(solution)/shard_map/pallas_call | solution.py:80
  79.4 1.6 %collective-permute-start.17 = (s16[2,320,256]{2,1,0:T(8,128)(2,1)S(1)}, s16[2,320,256]{2,1,0:T(8,128)(2,1)S(1)}, u32[]{:S(2)}, u32[]{:S(2)}) collective-permute-start(s16[2,320,256]{2,1,0:T(8,128)(2,1)S(1)} %get-tuple-element.48), channel_id=1, source_target_pairs={{0,2},{1,3},{2,0},{3,1},{4,6},{5,7},{6,4},{7,5},{8,10},{9,11},{10,... | collective-permute-start | bytes 983048 | tf_op jit(solution)/shard_map/ppermute | solution.py:180
  81.0 4.1 %shard_map.92 = (s16[2,320,256]{2,1,0:T(8,128)(2,1)S(1)}, f32[2,320,256]{2,1,0:T(8,128)S(1)}) custom-call(s32[4]{0:T(128)S(1)} %pad_add_fusion.s_ref, bf16[5,320,640]{2,1,0:T(8,128)(2,1)} %copy-done, bf16[5,320,640]{2,1,0:T(8,128)(2,1)} %collective-permute-done.refs_1_.refs_3_, bf16[320,640]{1,0:T(8,128)(2,1)} %collective-permute-done.11.refs_2_, ...), custom_call_target="tpu_custom_call" | custom-call | flops 1677721600 | bytes 5242880 | tf_op jit(solution)/shard_map/pallas_call | solution.py:80
  85.1 0.6 collective-permute-start.13
  85.7 4.0 %shard_map.89 = (s16[2,320,256]{2,1,0:T(8,128)(2,1)S(1)}, f32[2,320,256]{2,1,0:T(8,128)S(1)}) custom-call(s32[4]{0:T(128)S(1)} %pad_add_fusion.s_ref, bf16[5,320,640]{2,1,0:T(8,128)(2,1)} %copy-done, bf16[5,320,640]{2,1,0:T(8,128)(2,1)} %collective-permute-done.refs_1_.refs_3_, bf16[320,640]{1,0:T(8,128)(2,1)S(1)} %collective-permute-done.7.refs_2_, ...), custom_call_target="tpu_custom_call" | custom-call | flops 1677721600 | bytes 5242880 | tf_op jit(solution)/shard_map/pallas_call | solution.py:80
  89.6 1.6 %collective-permute-start.9 = (s16[2,320,256]{2,1,0:T(8,128)(2,1)S(1)}, s16[2,320,256]{2,1,0:T(8,128)(2,1)S(1)}, u32[]{:S(2)}, u32[]{:S(2)}) collective-permute-start(s16[2,320,256]{2,1,0:T(8,128)(2,1)S(1)} %get-tuple-element.38), channel_id=1, source_target_pairs={{0,2},{1,3},{2,0},{3,1},{4,6},{5,7},{6,4},{7,5},{8,10},{9,11},{10,... | collective-permute-start | bytes 983048 | tf_op jit(solution)/shard_map/ppermute | solution.py:180
  91.2 3.9 %shard_map.85 = (s16[2,320,256]{2,1,0:T(8,128)(2,1)S(1)}, f32[2,320,256]{2,1,0:T(8,128)S(1)}) custom-call(s32[4]{0:T(128)S(1)} %pad_add_fusion.s_ref, bf16[5,320,640]{2,1,0:T(8,128)(2,1)S(1)} %copy-done.1, bf16[5,320,640]{2,1,0:T(8,128)(2,1)} %collective-permute-done.refs_1_.refs_3_, bf16[5,320,640]{2,1,0:T(8,128)(2,1)S(1)} %copy-done.1, ...), custom_call_target="tpu_custom_call" | custom-call | flops 1677721600 | bytes 5242880 | tf_op jit(solution)/shard_map/pallas_call | solution.py:80
  95.1 0.6 collective-permute-start.5
  95.7 0.7 shard_map.96
  96.5 1.6 %collective-permute-start.18 = (s16[320,256]{1,0:T(8,128)(2,1)S(1)}, s16[320,256]{1,0:T(8,128)(2,1)S(1)}, u32[]{:S(2)}, u32[]{:S(2)}) collective-permute-start(s16[320,256]{1,0:T(8,128)(2,1)S(1)} %get-tuple-element.50), channel_id=1, source_target_pairs={{0,16},{16,0},{1,17},{17,1},{2,18},{18,2},{3,19},{19,3},{4,20},{20... | collective-permute-start | bytes 491528 | tf_op jit(solution)/shard_map/ppermute | solution.py:180
  98.0 0.7 shard_map.93
  98.8 0.6 collective-permute-start.14
  99.4 4.7 %collective-permute-done.9.coded_ref = s16[2,320,256]{2,1,0:T(8,128)(2,1)S(1)} collective-permute-done((s16[2,320,256]{2,1,0:T(8,128)(2,1)S(1)}, s16[2,320,256]{2,1,0:T(8,128)(2,1)S(1)}, u32[]{:S(2)}, u32[]{:S(2)}) %collective-permute-start.9) | collective-permute-done | bytes 327712 | tf_op jit(solution)/shard_map/ppermute | solution.py:180
  104.1 0.7 shard_map.90
  104.8 1.5 %collective-permute-start.10 = (s16[320,256]{1,0:T(8,128)(2,1)S(1)}, s16[320,256]{1,0:T(8,128)(2,1)S(1)}, u32[]{:S(2)}, u32[]{:S(2)}) collective-permute-start(s16[320,256]{1,0:T(8,128)(2,1)S(1)} %get-tuple-element.40), channel_id=1, source_target_pairs={{0,16},{16,0},{1,17},{17,1},{2,18},{18,2},{3,19},{19,3},{4,20},{20... | collective-permute-start | bytes 491528 | tf_op jit(solution)/shard_map/ppermute | solution.py:180
  106.4 3.2 %collective-permute-done.5.coded_ref = s16[2,320,256]{2,1,0:T(8,128)(2,1)S(1)} collective-permute-done((s16[2,320,256]{2,1,0:T(8,128)(2,1)S(1)}, s16[2,320,256]{2,1,0:T(8,128)(2,1)S(1)}, u32[]{:S(2)}, u32[]{:S(2)}) %collective-permute-start.5) | collective-permute-done | bytes 327712 | tf_op jit(solution)/shard_map/ppermute | solution.py:180
  109.5 0.7 shard_map.86
  110.3 1.5 %collective-permute-start.6 = (s16[320,256]{1,0:T(8,128)(2,1)S(1)}, s16[320,256]{1,0:T(8,128)(2,1)S(1)}, u32[]{:S(2)}, u32[]{:S(2)}) collective-permute-start(s16[320,256]{1,0:T(8,128)(2,1)S(1)} %get-tuple-element.35), channel_id=1, source_target_pairs={{0,16},{16,0},{1,17},{17,1},{2,18},{18,2},{3,19},{19,3},{4,20},{20... | collective-permute-start | bytes 491528 | tf_op jit(solution)/shard_map/ppermute | solution.py:180
  111.8 0.8 shard_map.97.refs_3_
  112.6 5.0 %collective-permute-start.21 = (bf16[320,256]{1,0:T(8,128)(2,1)S(1)}, bf16[320,256]{1,0:T(8,128)(2,1)S(1)}, u32[]{:S(2)}, u32[]{:S(2)}) collective-permute-start(bf16[320,256]{1,0:T(8,128)(2,1)S(1)} %shard_map.97.refs_3_), channel_id=1, source_target_pairs={{0,12},{4,0},{8,4},{12,8},{1,13},{5,1},{9,5},{13,9},{2,14},{6,2},{... | collective-permute-start | bytes 491528 | tf_op jit(solution)/shard_map/ppermute | solution.py:180
  117.6 0.6 shard_map.94.refs_2_
  118.3 0.6 shard_map.91.refs_1_
  118.9 0.6 collective-permute-start.19
  119.6 0.6 shard_map.87.refs_0_
  120.2 2.1 %collective-permute-done.21.refs_6_ = bf16[320,256]{1,0:T(8,128)(2,1)S(1)} collective-permute-done((bf16[320,256]{1,0:T(8,128)(2,1)S(1)}, bf16[320,256]{1,0:T(8,128)(2,1)S(1)}, u32[]{:S(2)}, u32[]{:S(2)}) %collective-permute-start.21) | collective-permute-done | bytes 163872 | tf_op jit(solution)/shard_map/ppermute | solution.py:180
  122.3 8.5 %collective-permute-done.20.refs_5_ = bf16[320,256]{1,0:T(8,128)(2,1)S(1)} collective-permute-done((bf16[320,256]{1,0:T(8,128)(2,1)S(1)}, bf16[320,256]{1,0:T(8,128)(2,1)S(1)}, u32[]{:S(2)}, u32[]{:S(2)}) %collective-permute-start.20) | collective-permute-done | bytes 163872 | tf_op jit(solution)/shard_map/ppermute | solution.py:180
  130.8 8.0 %shard_map.98 = bf16[256,2500]{1,0:T(8,128)(2,1)S(1)} custom-call(s32[4]{0:T(128)S(1)} %pad_add_fusion.s_ref, s32[4,4,320,1]{3,2,1,0:T(8,128)S(1)} %copy-done.6, s32[4,4,320,1]{3,2,1,0:T(8,128)} %constant.53.clone.away_ref, bf16[320,256]{1,0:T(8,128)(2,1)S(1)} %shard_map.87.refs_0_, bf16[320,256]{1,0:T(8,128)(2,1)S(1)} %shard_map.91.refs_1_, ...), custom_call_target="tpu_custom_call" | custom-call | flops 3276800000 | bytes 2590720 | tf_op jit(solution)/shard_map/pallas_call | solution.py:80
  138.9 1.5 %copy.14 = bf16[256,2500]{0,1:T(8,128)(2,1)} copy(bf16[256,2500]{1,0:T(8,128)(2,1)S(1)} %shard_map.98) | data formatting | bytes 2560000 | tf_op jit(solution)/shard_map/pallas_call | solution.py:80
  (39 shorter events, 1.0 us)
Async XLA Ops:
  2.5 35.5 %collective-permute-start.2 = (bf16[2,256,1280]{2,1,0:T(8,128)(2,1)}, bf16[2,256,1280]{2,1,0:T(8,128)(2,1)S(1)}, u32[]{:S(2)}, u32[]{:S(2)}) collective-permute-start(bf16[2,256,1280]{2,1,0:T(8,128)(2,1)} %dynamic-slice_bitcast_fusion), channel_id=1, source_target_pairs={{0,1},{1,0},{2,3},{3,2},{4,5},{5,4},{6,7},{7,6},{8,9},{9,8},{10,11... | collective-permute-start | bytes 3932168 | tf_op jit(solution)/shard_map/ppermute | solution.py:183
  10.8 1.9 %copy-start.5 = (s32[4,5,320,1]{3,2,1,0:T(8,128)S(1)}, s32[4,5,320,1]{3,2,1,0:T(8,128)}, u32[]{:S(2)}) copy-start(s32[4,5,320,1]{3,2,1,0:T(8,128)} %constant.55.clone.idx_ref) | copy-start | bytes 76804
  12.7 9.2 %copy-start.7 = (s32[4,3,320,1]{3,2,1,0:T(8,128)S(1)}, s32[4,3,320,1]{3,2,1,0:T(8,128)}, u32[]{:S(2)}) copy-start(s32[4,3,320,1]{3,2,1,0:T(8,128)} %constant.56.idx_ref) | copy-start | bytes 46084
  21.8 7.4 %copy-start = (bf16[5,320,640]{2,1,0:T(8,128)(2,1)}, bf16[5,320,640]{2,1,0:T(8,128)(2,1)S(1)}, u32[]{:S(2)}) copy-start(bf16[5,320,640]{2,1,0:T(8,128)(2,1)S(1)} %shard_map.82.refs_0_.refs_2_) | copy-start | bytes 6144004
  21.8 13.8 %copy-start.8 = (s32[1280]{0:T(1024)S(1)}, s32[1280]{0:T(1024)}, u32[]{:S(2)}) copy-start(s32[1280]{0:T(1024)} %param.11) | copy-start | bytes 15364
  21.8 13.8 %copy-start.9 = (s32[1024]{0:T(1024)S(1)}, s32[1024]{0:T(1024)}, u32[]{:S(2)}) copy-start(s32[1024]{0:T(1024)} %param.10) | copy-start | bytes 12292
  21.8 53.5 %collective-permute-start = (bf16[5,320,640]{2,1,0:T(8,128)(2,1)S(1)}, bf16[5,320,640]{2,1,0:T(8,128)(2,1)}, u32[]{:S(2)}, u32[]{:S(2)}) collective-permute-start(bf16[5,320,640]{2,1,0:T(8,128)(2,1)S(1)} %shard_map.82.refs_0_.refs_2_), channel_id=1, source_target_pairs={{0,1},{1,0},{2,3},{3,2},{4,5},{5,4},{6,7},{7,6},{8,9},{9,8},{10,11... | collective-permute-start | bytes 6144008 | tf_op jit(solution)/shard_map/ppermute | solution.py:183
  29.2 0.7 copy-start.4
  29.9 16.0 %collective-permute-start.15 = (bf16[320,640]{1,0:T(8,128)(2,1)}, bf16[320,640]{1,0:T(8,128)(2,1)}, u32[]{:S(2)}, u32[]{:S(2)}) collective-permute-start(bf16[320,640]{1,0:T(8,128)(2,1)} %get-tuple-element.46), channel_id=1, source_target_pairs={{0,4},{4,8},{8,12},{12,0},{1,5},{5,9},{9,13},{13,1},{2,6},{6,10},{... | collective-permute-start | bytes 1228808 | tf_op jit(solution)/shard_map/ppermute | solution.py:180
  32.9 29.8 %collective-permute-start.11 = (bf16[320,640]{1,0:T(8,128)(2,1)}, bf16[320,640]{1,0:T(8,128)(2,1)}, u32[]{:S(2)}, u32[]{:S(2)}) collective-permute-start(bf16[320,640]{1,0:T(8,128)(2,1)} %get-tuple-element.41), channel_id=1, source_target_pairs={{0,8},{4,12},{8,0},{12,4},{1,9},{5,13},{9,1},{13,5},{2,10},{6,14},... | collective-permute-start | bytes 1228808 | tf_op jit(solution)/shard_map/ppermute | solution.py:180
  35.5 1.2 collective-permute-start.1
  36.7 26.0 %collective-permute-start.7 = (bf16[320,640]{1,0:T(8,128)(2,1)}, bf16[320,640]{1,0:T(8,128)(2,1)S(1)}, u32[]{:S(2)}, u32[]{:S(2)}) collective-permute-start(bf16[320,640]{1,0:T(8,128)(2,1)} %copy-done.4), channel_id=1, source_target_pairs={{0,12},{4,0},{8,4},{12,8},{1,13},{5,1},{9,5},{13,9},{2,14},{6,2},{... | collective-permute-start | bytes 1228808 | tf_op jit(solution)/shard_map/ppermute | solution.py:180
  38.1 1.0 copy-start.2
  39.1 1.1 copy-start.3
  44.4 24.6 %collective-permute-start.3 = (bf16[2,256,640]{2,1,0:T(8,128)(2,1)S(1)}, bf16[2,256,640]{2,1,0:T(8,128)(2,1)S(1)}, u32[]{:S(2)}, u32[]{:S(2)}) collective-permute-start(bf16[2,256,640]{2,1,0:T(8,128)(2,1)S(1)} %get-tuple-element.29), channel_id=1, source_target_pairs={{0,16},{16,0},{1,17},{17,1},{2,18},{18,2},{3,19},{19,3},{4,20},{20... | collective-permute-start | bytes 1966088 | tf_op jit(solution)/shard_map/ppermute | solution.py:180
  45.9 29.4 %collective-permute-start.4 = (bf16[2,256,640]{2,1,0:T(8,128)(2,1)S(1)}, bf16[2,256,640]{2,1,0:T(8,128)(2,1)S(1)}, u32[]{:S(2)}, u32[]{:S(2)}) collective-permute-start(bf16[2,256,640]{2,1,0:T(8,128)(2,1)S(1)} %get-tuple-element.31), channel_id=1, source_target_pairs={{0,16},{16,0},{1,17},{17,1},{2,18},{18,2},{3,19},{19,3},{4,20},{20... | collective-permute-start | bytes 1966088 | tf_op jit(solution)/shard_map/ppermute | solution.py:180
  62.7 2.0 %collective-permute-start.16 = (bf16[320,640]{1,0:T(8,128)(2,1)}, bf16[320,640]{1,0:T(8,128)(2,1)S(1)}, u32[]{:S(2)}, u32[]{:S(2)}) collective-permute-start(bf16[320,640]{1,0:T(8,128)(2,1)} %collective-permute-done.15.refs_2_), channel_id=1, source_target_pairs={{0,1},{1,0},{2,3},{3,2},{4,5},{5,4},{6,7},{7,6},{8,9},{9,8},{10,11... | collective-permute-start | bytes 1228808 | tf_op jit(solution)/shard_map/ppermute | solution.py:183
  62.7 18.3 %collective-permute-start.12 = (bf16[320,640]{1,0:T(8,128)(2,1)}, bf16[320,640]{1,0:T(8,128)(2,1)S(1)}, u32[]{:S(2)}, u32[]{:S(2)}) collective-permute-start(bf16[320,640]{1,0:T(8,128)(2,1)} %collective-permute-done.11.refs_2_), channel_id=1, source_target_pairs={{0,1},{1,0},{2,3},{3,2},{4,5},{5,4},{6,7},{7,6},{8,9},{9,8},{10,11... | collective-permute-start | bytes 1228808 | tf_op jit(solution)/shard_map/ppermute | solution.py:183
  64.6 21.0 %collective-permute-start.8 = (bf16[320,640]{1,0:T(8,128)(2,1)S(1)}, bf16[320,640]{1,0:T(8,128)(2,1)S(1)}, u32[]{:S(2)}, u32[]{:S(2)}) collective-permute-start(bf16[320,640]{1,0:T(8,128)(2,1)S(1)} %collective-permute-done.7.refs_2_), channel_id=1, source_target_pairs={{0,1},{1,0},{2,3},{3,2},{4,5},{5,4},{6,7},{7,6},{8,9},{9,8},{10,11... | collective-permute-start | bytes 1228808 | tf_op jit(solution)/shard_map/ppermute | solution.py:183
  79.4 16.3 %collective-permute-start.17 = (s16[2,320,256]{2,1,0:T(8,128)(2,1)S(1)}, s16[2,320,256]{2,1,0:T(8,128)(2,1)S(1)}, u32[]{:S(2)}, u32[]{:S(2)}) collective-permute-start(s16[2,320,256]{2,1,0:T(8,128)(2,1)S(1)} %get-tuple-element.48), channel_id=1, source_target_pairs={{0,2},{1,3},{2,0},{3,1},{4,6},{5,7},{6,4},{7,5},{8,10},{9,11},{10,... | collective-permute-start | bytes 983048 | tf_op jit(solution)/shard_map/ppermute | solution.py:180
  85.1 6.1 %copy-start.1 = (bf16[5,320,640]{2,1,0:T(8,128)(2,1)S(1)}, bf16[5,320,640]{2,1,0:T(8,128)(2,1)}, u32[]{:S(2)}) copy-start(bf16[5,320,640]{2,1,0:T(8,128)(2,1)} %copy-done) | copy-start | bytes 6144004
  85.1 12.9 %collective-permute-start.13 = (s16[2,320,256]{2,1,0:T(8,128)(2,1)S(1)}, s16[2,320,256]{2,1,0:T(8,128)(2,1)S(1)}, u32[]{:S(2)}, u32[]{:S(2)}) collective-permute-start(s16[2,320,256]{2,1,0:T(8,128)(2,1)S(1)} %get-tuple-element.43), channel_id=1, source_target_pairs={{0,2},{1,3},{2,0},{3,1},{4,6},{5,7},{6,4},{7,5},{8,10},{9,11},{10,... | collective-permute-start | bytes 983048 | tf_op jit(solution)/shard_map/ppermute | solution.py:180
  89.6 14.4 %collective-permute-start.9 = (s16[2,320,256]{2,1,0:T(8,128)(2,1)S(1)}, s16[2,320,256]{2,1,0:T(8,128)(2,1)S(1)}, u32[]{:S(2)}, u32[]{:S(2)}) collective-permute-start(s16[2,320,256]{2,1,0:T(8,128)(2,1)S(1)} %get-tuple-element.38), channel_id=1, source_target_pairs={{0,2},{1,3},{2,0},{3,1},{4,6},{5,7},{6,4},{7,5},{8,10},{9,11},{10,... | collective-permute-start | bytes 983048 | tf_op jit(solution)/shard_map/ppermute | solution.py:180
  95.1 14.4 %collective-permute-start.5 = (s16[2,320,256]{2,1,0:T(8,128)(2,1)S(1)}, s16[2,320,256]{2,1,0:T(8,128)(2,1)S(1)}, u32[]{:S(2)}, u32[]{:S(2)}) collective-permute-start(s16[2,320,256]{2,1,0:T(8,128)(2,1)S(1)} %get-tuple-element.33), channel_id=1, source_target_pairs={{0,2},{1,3},{2,0},{3,1},{4,6},{5,7},{6,4},{7,5},{8,10},{9,11},{10,... | collective-permute-start | bytes 983048 | tf_op jit(solution)/shard_map/ppermute | solution.py:180
  96.5 15.4 %collective-permute-start.18 = (s16[320,256]{1,0:T(8,128)(2,1)S(1)}, s16[320,256]{1,0:T(8,128)(2,1)S(1)}, u32[]{:S(2)}, u32[]{:S(2)}) collective-permute-start(s16[320,256]{1,0:T(8,128)(2,1)S(1)} %get-tuple-element.50), channel_id=1, source_target_pairs={{0,16},{16,0},{1,17},{17,1},{2,18},{18,2},{3,19},{19,3},{4,20},{20... | collective-permute-start | bytes 491528 | tf_op jit(solution)/shard_map/ppermute | solution.py:180
  98.8 18.9 %collective-permute-start.14 = (s16[320,256]{1,0:T(8,128)(2,1)S(1)}, s16[320,256]{1,0:T(8,128)(2,1)S(1)}, u32[]{:S(2)}, u32[]{:S(2)}) collective-permute-start(s16[320,256]{1,0:T(8,128)(2,1)S(1)} %get-tuple-element.45), channel_id=1, source_target_pairs={{0,16},{16,0},{1,17},{17,1},{2,18},{18,2},{3,19},{19,3},{4,20},{20... | collective-permute-start | bytes 491528 | tf_op jit(solution)/shard_map/ppermute | solution.py:180
  104.8 26.0 %copy-start.6 = (s32[4,4,320,1]{3,2,1,0:T(8,128)S(1)}, s32[4,4,320,1]{3,2,1,0:T(8,128)}, u32[]{:S(2)}) copy-start(s32[4,4,320,1]{3,2,1,0:T(8,128)} %constant.52.clone.own_ref) | copy-start | bytes 61444
  104.8 13.5 %collective-permute-start.10 = (s16[320,256]{1,0:T(8,128)(2,1)S(1)}, s16[320,256]{1,0:T(8,128)(2,1)S(1)}, u32[]{:S(2)}, u32[]{:S(2)}) collective-permute-start(s16[320,256]{1,0:T(8,128)(2,1)S(1)} %get-tuple-element.40), channel_id=1, source_target_pairs={{0,16},{16,0},{1,17},{17,1},{2,18},{18,2},{3,19},{19,3},{4,20},{20... | collective-permute-start | bytes 491528 | tf_op jit(solution)/shard_map/ppermute | solution.py:180
  110.3 9.3 %collective-permute-start.6 = (s16[320,256]{1,0:T(8,128)(2,1)S(1)}, s16[320,256]{1,0:T(8,128)(2,1)S(1)}, u32[]{:S(2)}, u32[]{:S(2)}) collective-permute-start(s16[320,256]{1,0:T(8,128)(2,1)S(1)} %get-tuple-element.35), channel_id=1, source_target_pairs={{0,16},{16,0},{1,17},{17,1},{2,18},{18,2},{3,19},{19,3},{4,20},{20... | collective-permute-start | bytes 491528 | tf_op jit(solution)/shard_map/ppermute | solution.py:180
  112.6 9.7 %collective-permute-start.21 = (bf16[320,256]{1,0:T(8,128)(2,1)S(1)}, bf16[320,256]{1,0:T(8,128)(2,1)S(1)}, u32[]{:S(2)}, u32[]{:S(2)}) collective-permute-start(bf16[320,256]{1,0:T(8,128)(2,1)S(1)} %shard_map.97.refs_3_), channel_id=1, source_target_pairs={{0,12},{4,0},{8,4},{12,8},{1,13},{5,1},{9,5},{13,9},{2,14},{6,2},{... | collective-permute-start | bytes 491528 | tf_op jit(solution)/shard_map/ppermute | solution.py:180
  118.2 12.6 %collective-permute-start.20 = (bf16[320,256]{1,0:T(8,128)(2,1)S(1)}, bf16[320,256]{1,0:T(8,128)(2,1)S(1)}, u32[]{:S(2)}, u32[]{:S(2)}) collective-permute-start(bf16[320,256]{1,0:T(8,128)(2,1)S(1)} %shard_map.94.refs_2_), channel_id=1, source_target_pairs={{0,8},{4,12},{8,0},{12,4},{1,9},{5,13},{9,1},{13,5},{2,10},{6,14},... | collective-permute-start | bytes 491528 | tf_op jit(solution)/shard_map/ppermute | solution.py:180
  118.9 11.9 %collective-permute-start.19 = (bf16[320,256]{1,0:T(8,128)(2,1)S(1)}, bf16[320,256]{1,0:T(8,128)(2,1)S(1)}, u32[]{:S(2)}, u32[]{:S(2)}) collective-permute-start(bf16[320,256]{1,0:T(8,128)(2,1)S(1)} %shard_map.91.refs_1_), channel_id=1, source_target_pairs={{0,4},{4,8},{8,12},{12,0},{1,5},{5,9},{9,13},{13,1},{2,6},{6,10},{... | collective-permute-start | bytes 491528 | tf_op jit(solution)/shard_map/ppermute | solution.py:180

commit v2 on v0

v2 whole, which is shorter than its diff:
```python
import functools

import jax
import jax.numpy as jnp
import numpy as np
from jax import lax
from jax.experimental import pallas as pl
from jax.experimental.pallas import tpu as pltpu
from jax.sharding import PartitionSpec as P

OCC = 100
TOP = 32000.0
STEPS = 256.0
CORES = 2
TILE = 512


def dot_nt(a, b):
    return lax.dot_general(a, b, (((1,), (1,)), ((), ())), preferred_element_type=jnp.float32)


def dot_nn(a, b):
    return lax.dot_general(a, b, (((1,), (0,)), ((), ())), preferred_element_type=jnp.float32)


def divide(value, by):
    whole = jnp.floor((value.astype(jnp.float32) + 0.5) * (1.0 / by)).astype(jnp.int32)
    return whole, value - whole * by


def inside_columns(place, n, z):
    apart, i = divide(place, n)
    j = i + apart + 1
    j = jnp.where(j >= n, j - n, j)
    valid = place < n * (n - 1) // 2
    return jnp.where(valid, i * OCC + z * n + j, -1), jnp.where(valid, j * OCC + z * n + i, -1)


def pair_columns(place, n, z, other, mine):
    half = (n * n + 1) // 2
    first = jnp.logical_xor(z < other, jnp.logical_not(mine))
    count = jnp.where(first, half, n * n - half)
    q, m = divide(place + jnp.where(first, 0, half), n)
    a = jnp.where(z < other, q, m)
    b = jnp.where(z < other, m, q)
    return jnp.where(place < count, a * OCC + other * n + b, -1)


def encode(values):
    largest = jnp.maximum(jnp.max(jnp.abs(values), axis=0, keepdims=True), 1e-30)
    code = jnp.floor(jnp.log2(TOP / largest) * STEPS)
    coded = jnp.round(values * jnp.exp2(code * (1.0 / STEPS)))
    rows = lax.broadcasted_iota(jnp.int32, values.shape, 0)
    coded = jnp.where(rows == values.shape[0] - 1, code, coded)
    return coded.astype(jnp.int32).astype(jnp.int16)


def decode(coded):
    values = coded.astype(jnp.int32).astype(jnp.float32)
    rows = lax.broadcasted_iota(jnp.int32, values.shape, 0)
    last = rows == values.shape[0] - 1
    code = jnp.sum(jnp.where(last, values, 0.0), axis=0, keepdims=True)
    return jnp.where(last, 0.0, values * jnp.exp2(code * (-1.0 / STEPS)))


def call(name, body, scalars, inputs, outputs, flops, moved, grid=1, scratch=()):
    in_specs, arrays, out_specs, shapes = [], [], [], []
    for entry in inputs:
        array, block, index = entry if isinstance(entry, tuple) else (entry, None, None)
        arrays.append(array)
        in_specs.append(pl.BlockSpec(block or array.shape, index or (lambda g, s, rank=array.ndim: (0,) * rank)))
    for shape, dtype, *spec in outputs:
        shapes.append(jax.ShapeDtypeStruct(shape, dtype))
        block, index = spec or (shape, lambda g, s, rank=len(shape): (0,) * rank)
        out_specs.append(pl.BlockSpec(block, index))
    return pl.pallas_call(
        body,
        name=name,
        out_shape=shapes,
        grid_spec=pltpu.PrefetchScalarGridSpec(
            num_scalar_prefetch=1, grid=(grid,), in_specs=in_specs, out_specs=out_specs, scratch_shapes=list(scratch)
        ),
        compiler_params=pltpu.CompilerParams(vmem_limit_bytes=48 * 2**20),
        cost_estimate=pl.CostEstimate(flops=int(flops), bytes_accessed=int(moved), transcendentals=0),
    )(scalars, *arrays)


def mask_body(by, row_n, sub, tall, s_ref, ab_ref, cd_ref, v_ref, pass_ref, keep_ref):
    x, y, core = s_ref[0], s_ref[2], s_ref[3]
    k_here, cd_here = pass_ref.shape[2], v_ref.shape[1]
    q, m = divide(lax.broadcasted_iota(jnp.int32, (k_here, 1), 0), sub)
    wanted = q * (sub * row_n) + lax.rem(x - by + row_n, row_n) * sub + m
    pick = jnp.where(lax.broadcasted_iota(jnp.int32, (k_here, cd_here), 1) == wanted, 1.0, 0.0).astype(jnp.bfloat16)
    square = (tall, tall)
    diagonal = lax.broadcasted_iota(jnp.int32, square, 0) == lax.broadcasted_iota(jnp.int32, square, 1)
    blocks = []
    for other_core in (1, 0):
        for other_y in (1, 0):
            block = lax.rem(y + other_y, 2) * CORES + lax.rem(core + other_core, CORES)
            start = pl.multiple_of(block * tall, tall)
            labels = ab_ref[:, pl.ds(start, tall)].astype(jnp.float32)
            ab = jnp.sum(jnp.where(diagonal, labels, 0.0), axis=1, keepdims=True)
            v = v_ref[pl.ds(start, tall), :].astype(jnp.float32)
            blocks.append(jnp.where(ab == cd_ref[...].astype(jnp.float32), v, 0.0).astype(jnp.bfloat16))
    picked = dot_nt(jnp.concatenate(blocks, axis=0), pick).astype(jnp.bfloat16)
    pass_ref[...] = picked[: 2 * tall].reshape(pass_ref.shape)
    keep_ref[...] = picked[2 * tall :].reshape(keep_ref.shape)


def one_hot_rows(columns, width):
    lanes = lax.broadcasted_iota(jnp.int32, (columns.shape[0], width), 1)
    return jnp.where(lanes == columns, 1.0, 0.0).astype(jnp.bfloat16)


def send_body(order, n, col_n, s_ref, t_ref, flat_ref, *out_refs):
    flat_ref[...] = t_ref[...].reshape(flat_ref.shape)
    z = s_ref[1]
    place = lax.broadcasted_iota(jnp.int32, (out_refs[0].shape[0], 1), 0)
    for r, out_ref in zip(order, out_refs):
        wanted = pair_columns(place, n, z, lax.rem(z - r + col_n, col_n), False)
        out_ref[...] = dot_nt(one_hot_rows(wanted, flat_ref.shape[1]), flat_ref[...]).astype(jnp.bfloat16)


def keep_body(order, n, col_n, s_ref, flat_ref, out_ref):
    z = s_ref[1]
    place = lax.broadcasted_iota(jnp.int32, (out_ref.shape[1], 1), 0)
    inside, turned = inside_columns(place, n, z)
    picks = [inside if r == 0 else pair_columns(place, n, z, lax.rem(z + r, col_n), True) for r in order] + [turned]
    for k, wanted in enumerate(picks):
        out_ref[k] = dot_nt(one_hot_rows(wanted, flat_ref.shape[1]), flat_ref[...]).astype(jnp.bfloat16)


def sum_body(first, count, s_ref, own_here, own_there, *refs):
    away = refs[: 2 * count]
    keep_ref, pass_ref, coded_ref, kept_ref = refs[2 * count :]
    k_here = own_here.shape[2]
    chunk = own_here.shape[1]

    def rows(ref):
        return ref[...].reshape(-1, k_here)

    a, b = keep_ref[0], pass_ref[0]
    to = own_here[first : first + count].reshape(count * chunk, k_here)
    too = own_there[first : first + count].reshape(count * chunk, k_here)
    tr = jnp.concatenate([rows(ref) for ref in away[:count]], axis=0)
    tro = jnp.concatenate([rows(ref) for ref in away[count:]], axis=0)
    total = (dot_nt(to, a) + dot_nt(too, b)) - (dot_nt(tr, a) + dot_nt(tro, b))

    @pl.when(pl.program_id(0) == 0)
    def _():
        coded_ref[...] = encode(total)

    @pl.when(pl.program_id(0) == 1)
    def _():
        kept_ref[...] = total


def add_y_body(s_ref, kept_ref, coded_ref, out_ref):
    out_ref[...] = encode(kept_ref[...] + decode(coded_ref[...]))


def add_x_body(count, s_ref, kept_ref, *refs):
    total = kept_ref[...]
    for ref in refs[:-count]:
        total = total + decode(ref[...])
    rounded = total.astype(jnp.bfloat16)
    chunk = rounded.shape[0] // count
    for k, out_ref in enumerate(refs[-count:]):
        out_ref[...] = rounded[k * chunk : (k + 1) * chunk]


def place_body(order, n, col_n, before, s_ref, *refs):
    out_ref = refs[-1]
    z = s_ref[1]
    chunk = refs[0].shape[0]
    place = lax.broadcasted_iota(jnp.int32, (1, chunk), 1)
    at = lax.broadcasted_iota(jnp.int32, (out_ref.shape[0], chunk), 0) + pl.program_id(0) * out_ref.shape[0]
    total = refs[-2][...].astype(jnp.float32) if before else None
    source = iter(refs)
    for r in order:
        if r == 0:
            inside, turned = inside_columns(place, n, z)
            signs = jnp.where(at == inside, 1.0, jnp.where(at == turned, -1.0, 0.0))
            terms = [(signs, next(source))]
        else:
            plus = pair_columns(place, n, z, lax.rem(z + r, col_n), True)
            minus = pair_columns(place, n, z, lax.rem(z - r + col_n, col_n), False)
            terms = [(jnp.where(at == plus, 1.0, 0.0), next(source)), (jnp.where(at == minus, -1.0, 0.0), next(source))]
        for signs, ref in terms:
            term = dot_nn(signs.astype(jnp.bfloat16), ref[...])
            total = term if total is None else total + term
    out_ref[...] = total.astype(jnp.bfloat16)


def local(integrals, amplitudes, ab_irrep, cd_irrep):
    row_n, col_n, depth_n = lax.axis_size("row"), lax.axis_size("col"), lax.axis_size("depth")
    x, z, d = lax.axis_index("row"), lax.axis_index("col"), lax.axis_index("depth")
    y, core = d // CORES, d % CORES
    rows, cd_here = integrals.shape
    blocks, sub, columns = amplitudes.shape
    k_here = blocks * sub
    tall = rows // depth_n
    n = OCC // col_n
    chunk = -(-((n * n + 1) // 2 + 1) // 16) * 16
    far = col_n // 2
    near = [r for r in range(1, col_n) if r != far]
    groups = [[0] + near, [far]]
    order = [0] + near + [far]
    bf16, i16, f32 = jnp.bfloat16, jnp.int16, jnp.float32

    def shift(array, axis, by):
        count = lax.axis_size(axis)
        return lax.ppermute(array, axis, [(i, (i + by) % count) for i in range(count)])

    def other_core(array):
        return lax.ppermute(array, "depth", [(i, i ^ 1) for i in range(depth_n)])

    def other_y(array):
        return lax.ppermute(array, "depth", [(i, i ^ 2) for i in range(depth_n)])

    scalars = jnp.stack([x, z, y, core]).astype(jnp.int32)
    ab_row, cd_row = ab_irrep.reshape(1, rows), cd_irrep.reshape(1, cd_here)

    def masked(v, by):
        return call(
            "mask_integrals",
            functools.partial(mask_body, by, row_n, sub, tall),
            scalars,
            [ab_row, cd_row, v],
            [((2, tall, k_here), bf16)] * 2,
            2 * rows * cd_here * k_here,
            2 * rows * (cd_here + k_here),
        )

    passed, kept = [None] * row_n, [None] * row_n
    for by in range(1, row_n):
        gone, stay = masked(integrals, by)
        passed[by], kept[by] = shift(gone, "row", -by), shift(stay, "row", -by)

    amplitudes, _ = lax.optimization_barrier((amplitudes, gone if row_n > 1 else scalars))
    sent_order = near + [far]
    flat, *sent = call(
        "send_columns",
        functools.partial(send_body, sent_order, n, col_n),
        scalars,
        [amplitudes],
        [((k_here, columns), bf16)] + [((chunk, k_here), bf16)] * len(sent_order),
        2 * len(sent_order) * chunk * columns * k_here,
        2 * k_here * (2 * columns + len(sent_order) * chunk),
    )
    away = {r: shift(s, "col", -r) for r, s in zip(near, sent)}
    integrals, _ = lax.optimization_barrier((integrals, flat))
    last = lax.optimization_barrier((sent[-1], *away.values()))
    away[far] = shift(last[0], "col", -far)

    passed[0], kept[0] = masked(integrals, 0)
    (own,) = call(
        "keep_columns",
        functools.partial(keep_body, order, n, col_n),
        scalars,
        [flat],
        [((col_n + 1, chunk, k_here), bf16)],
        2 * (col_n + 1) * chunk * columns * k_here,
        2 * k_here * (columns + (col_n + 1) * chunk),
    )
    passed = [other_core(a) for a in passed]
    own_there = other_core(own)

    done = None
    for group in groups:
        first, count = order.index(group[0]), len(group)
        tail = (1, chunk, k_here), lambda g, s: (col_n, 0, 0)
        here = [(own, *tail) if r == 0 else away[r] for r in group]
        there = [(own_there, *tail) if r == 0 else other_core(away[r]) for r in group]
        final = []
        for by in range(row_n):
            block = (1, tall, k_here), lambda g, s: (g, 0, 0)
            coded, total = call(
                "sum_pairs",
                functools.partial(sum_body, first, count),
                scalars,
                [own, own_there] + here + there + [(kept[by], *block), (passed[by], *block)],
                [((count * chunk, tall), i16), ((count * chunk, tall), f32)],
                2 * 2 * 2 * count * chunk * tall * CORES * k_here,
                2 * CORES * k_here * (2 * count * chunk + 2 * tall) + 6 * count * chunk * tall,
                grid=2,
            )
            coded = other_y(coded)
            if by == 0:
                final += [total, coded]
            else:
                (merged,) = call(
                    "add_other_y",
                    add_y_body,
                    scalars,
                    [total, coded],
                    [((count * chunk, tall), i16)],
                    20 * count * chunk * tall,
                    8 * count * chunk * tall,
                )
                final.append(shift(merged, "row", by))
        rounded = call(
            "add_other_x",
            functools.partial(add_x_body, count),
            scalars,
            final,
            [((chunk, tall), bf16)] * count,
            20 * count * chunk * tall,
            8 * count * chunk * tall,
        )
        sources = []
        for r, mine in zip(group, rounded):
            sources += [mine] if r == 0 else [mine, shift(mine, "col", r)]
        tile = (TILE, tall), lambda g, s: (g, 0)
        sources += [] if done is None else [(done, *tile)]
        (done,) = call(
            "place_pairs",
            functools.partial(place_body, group, n, col_n, done is not None),
            scalars,
            sources,
            [((columns, tall), bf16, *tile)],
            2 * len(sources) * chunk * tall * columns,
            2 * tall * (2 * columns + len(sources) * chunk),
            grid=-(-columns // TILE),
        )
    return done.T


def solution(mesh):
    in_specs = (P("row", "depth"), P("depth", "row", "col"), P("row"), P("depth"))
    out_specs = P(("row", "depth"), "col")
    return jax.shard_map(local, mesh=mesh, in_specs=in_specs, out_specs=out_specs, check_vma=False)
```

time: 294 us -> 124 us (0.42)
  waiting for transfers between devices: 160 us -> 43.9 us
  blocking collectives: 77.9 us -> 0 us
  Pallas kernels: 0 us -> 52.7 us
  starting transfers between devices: 0.04 us -> 23.4 us
  local copies, waits for them, and re-layouts: 23.8 us -> 3.14 us
  between operations: 13.4 us -> 0.16 us
  matrix products: 13 us -> 0 us
  other arithmetic: 5.42 us -> 0.08 us
    reduce_scatter x1 -> x0, waiting for transfers between devices: 84 us -> none  [local(): ladder = lax.psum_scatter(total, 'depth', scatter_dimension=0, tiled=True)]
    all_to_all x1 -> x0, blocking collectives: 77.9 us -> none  [local(): lax.all_to_all(cube, 'col', split_axis=2, concat_axis=1, tiled=True)]
    all_gather x1 -> x0, waiting for transfers between devices: 76.3 us -> none  [local(): lax.all_gather(amplitudes, 'row', axis=1, tiled=True)]
    pallas_call x0 -> x14, Pallas kernels: none -> 52.7 us  [call(): pl.pallas_call(body, name=name, out_shape=shapes, grid_spec=pltpu.Prefetc...]
    ppermute x0 -> x20, waiting for transfers between devices: none -> 43.9 us  [the longest x10 39.8 us: shift(): lax.ppermute(array, axis, [(i, (i + by) % count) for i in range(count)])]
    ppermute x0 -> x20, starting transfers between devices: none -> 23.4 us  [the longest x10 17 us: shift(): lax.ppermute(array, axis, [(i, (i + by) % count) for i in range(count)])]
    dot_general x1 -> x0, matrix products: 13 us -> none  [local(): jnp.einsum('rck,ckj->rj', shaped, lax.all_gather(amplitudes, 'row', axis=...]
    all_to_all x2 -> x0, local copies, waits for them, and re-layouts: 6.28 us -> none  [local(): lax.all_to_all(cube, 'col', split_axis=2, concat_axis=1, tiled=True)]
  transfers between devices with their start and end apart: 2 -> 20, of which waited for: 2 -> 8; matrix products, arithmetic and copies ran while one was open for 3% -> 0% of each run, Pallas kernels for 0% -> 26%
where the time goes in v2:
time: 124 us; the launch traced here: 123 us
  Pallas kernels  52.7 us (42%)
  waiting for transfers between devices  43.9 us (35%)
  starting transfers between devices  23.4 us (19%)
  local copies, waits for them, and re-layouts  3.14 us (3%)
    pallas_call x14, Pallas kernels, call(): pl.pallas_call(body, name=name, out_shape=shapes, grid_spec=pltpu.Prefetc...  52.7 us
    ppermute x10, waiting for transfers between devices, shift(): lax.ppermute(array, axis, [(i, (i + by) % count) for i in range(count)])  39.8 us
    ppermute x10, starting transfers between devices, shift(): lax.ppermute(array, axis, [(i, (i + by) % count) for i in range(count)])  17 us
    ppermute x4, starting transfers between devices, other_y(): return lax.ppermute(array, 'depth', [(i, i ^ 2) for i in range(depth_n)])  5.38 us
    ppermute x4, waiting for transfers between devices, other_y(): return lax.ppermute(array, 'depth', [(i, i ^ 2) for i in range(depth_n)])  4.06 us
  transfers between devices with their start and end apart: 20, of which 8 were waited for; matrix products, arithmetic and copies ran while one was open for 0% of the time, Pallas kernels for 26%

profile of v2, /device:TPU:0, one launch (start us, length us, event | category | flops | bytes accessed | tf_op | source)
XLA Modules:
  0.0 123.4 jit_solution(16514095578404420934)
XLA Ops:
  0.0 0.7 reshape.7.cd_ref
  0.7 0.1 pad_add_fusion.s_ref
  0.8 1.7 %copy-done.2 = bf16[1024,1280]{1,0:T(8,128)(2,1)S(1)} copy-done((bf16[1024,1280]{1,0:T(8,128)(2,1)S(1)}, bf16[1024,1280]{1,0:T(8,128)(2,1)}, u32[]{:S(2)}) %copy-start.2) | copy-done | bytes 2621464
  2.5 0.7 copy-done.4
  3.2 2.9 %mask_integrals.2 = (bf16[2,256,640]{2,1,0:T(8,128)(2,1)S(1)}, bf16[2,256,640]{2,1,0:T(8,128)(2,1)S(1)}) custom-call(s32[4]{0:T(128)S(1)} %pad_add_fusion.s_ref, s32[1,1024]{1,0:T(1,128)S(1)} %bitcast.6, s32[1,1280]{1,0:T(1,128)S(1)} %reshape.7.cd_ref, bf16[1024,1280]{1,0:T(8,128)(2,1)S(1)} %copy-done.2), custom_call_target="tpu_custom_call" | custom-call | flops 1677721600 | bytes 3932160 | tf_op jit(solution)/shard_map/mask_integrals/pallas_call | solution.py:76
  6.2 6.8 %send_columns.1 = (bf16[640,2500]{1,0:T(8,128)(2,1)S(1)}, bf16[320,640]{1,0:T(8,128)(2,1)S(1)}, bf16[320,640]{1,0:T(8,128)(2,1)S(1)}, bf16[320,640]{1,0:T(8,128)(2,1)S(1)}) custom-call(s32[4]{0:T(128)S(1)} %pad_add_fusion.s_ref, bf16[320,2,2500]{2,1,0:T(2,128)(2,1)} %t_ref), custom_call_target="tpu_custom_call" | custom-call | flops 3072000000 | bytes 7628800 | tf_op jit(solution)/shard_map/send_columns/pallas_call | solution.py:76
  13.0 0.0 copy-start.3
  13.0 7.2 %keep_columns.1.own_here.refs_0_ = bf16[5,320,640]{2,1,0:T(8,128)(2,1)S(1)} custom-call(s32[4]{0:T(128)S(1)} %pad_add_fusion.s_ref, bf16[640,2500]{1,0:T(8,128)(2,1)S(1)} %get-tuple-element.29.flat_ref), custom_call_target="tpu_custom_call" | custom-call | flops 5120000000 | bytes 5248000 | tf_op jit(solution)/shard_map/keep_columns/pallas_call | solution.py:76
  20.2 0.5 collective-permute-start
  20.7 2.6 %collective-permute-start.8 = (bf16[2,256,640]{2,1,0:T(8,128)(2,1)S(1)}, bf16[2,256,640]{2,1,0:T(8,128)(2,1)S(1)}, u32[]{:S(2)}, u32[]{:S(2)}) collective-permute-start(bf16[2,256,640]{2,1,0:T(8,128)(2,1)S(1)} %get-tuple-element.27), channel_id=1, source_target_pairs={{0,16},{16,0},{1,17},{17,1},{2,18},{18,2},{3,19},{19,3},{4,20},{20... | collective-permute-start | bytes 1966088 | tf_op jit(solution)/shard_map/ppermute | solution.py:213
  23.3 3.6 %collective-permute-start.1 = (bf16[320,640]{1,0:T(8,128)(2,1)S(1)}, bf16[320,640]{1,0:T(8,128)(2,1)S(1)}, u32[]{:S(2)}, u32[]{:S(2)}) collective-permute-start(bf16[320,640]{1,0:T(8,128)(2,1)S(1)} %get-tuple-element.31), channel_id=1, source_target_pairs={{0,12},{4,0},{8,4},{12,8},{1,13},{5,1},{9,5},{13,9},{2,14},{6,2},{... | collective-permute-start | bytes 1228808 | tf_op jit(solution)/shard_map/ppermute | solution.py:213
  26.9 0.5 collective-permute-start.7
  27.4 0.0 collective-permute-start.2
  27.4 11.4 %collective-permute-done.8 = bf16[2,256,640]{2,1,0:T(8,128)(2,1)S(1)} collective-permute-done((bf16[2,256,640]{2,1,0:T(8,128)(2,1)S(1)}, bf16[2,256,640]{2,1,0:T(8,128)(2,1)S(1)}, u32[]{:S(2)}, u32[]{:S(2)}) %collective-permute-start.8) | collective-permute-done | bytes 655392 | tf_op jit(solution)/shard_map/ppermute | solution.py:213
  38.9 0.5 collective-permute-start.13
  39.4 6.2 %collective-permute-done.2.refs_2_ = bf16[320,640]{1,0:T(8,128)(2,1)S(1)} collective-permute-done((bf16[320,640]{1,0:T(8,128)(2,1)S(1)}, bf16[320,640]{1,0:T(8,128)(2,1)S(1)}, u32[]{:S(2)}, u32[]{:S(2)}) %collective-permute-start.2) | collective-permute-done | bytes 409632 | tf_op jit(solution)/shard_map/ppermute | solution.py:213
  45.6 0.0 collective-permute-start.14
  45.6 2.9 %mask_integrals.3 = (bf16[2,256,640]{2,1,0:T(8,128)(2,1)S(1)}, bf16[2,256,640]{2,1,0:T(8,128)(2,1)S(1)}) custom-call(s32[4]{0:T(128)S(1)} %pad_add_fusion.s_ref, s32[1,1024]{1,0:T(1,128)S(1)} %bitcast.7, s32[1,1280]{1,0:T(1,128)S(1)} %reshape.7.cd_ref, bf16[1024,1280]{1,0:T(8,128)(2,1)S(1)} %copy-done.3), custom_call_target="tpu_custom_call" | custom-call | flops 1677721600 | bytes 3932160 | tf_op jit(solution)/shard_map/mask_integrals/pallas_call | solution.py:76
  48.6 4.1 %collective-permute-done.7.refs_2_.refs_6_ = bf16[2,256,640]{2,1,0:T(8,128)(2,1)S(1)} collective-permute-done((bf16[2,256,640]{2,1,0:T(8,128)(2,1)S(1)}, bf16[2,256,640]{2,1,0:T(8,128)(2,1)S(1)}, u32[]{:S(2)}, u32[]{:S(2)}) %collective-permute-start.7) | collective-permute-done | bytes 655392 | tf_op jit(solution)/shard_map/ppermute | solution.py:213
  52.7 0.0 collective-permute-start.5
  52.7 2.9 %collective-permute-start.3 = (bf16[320,640]{1,0:T(8,128)(2,1)S(1)}, bf16[320,640]{1,0:T(8,128)(2,1)S(1)}, u32[]{:S(2)}, u32[]{:S(2)}) collective-permute-start(bf16[320,640]{1,0:T(8,128)(2,1)S(1)} %get-tuple-element.33), channel_id=1, source_target_pairs={{0,8},{4,12},{8,0},{12,4},{1,9},{5,13},{9,1},{13,5},{2,10},{6,14},... | collective-permute-start | bytes 1228808 | tf_op jit(solution)/shard_map/ppermute | solution.py:213
  55.5 0.0 collective-permute-done.14.refs_5_
  55.5 0.0 collective-permute-done.9.refs_3_.refs_7_
  55.5 0.0 collective-permute-done.own_there.refs_3_
  55.5 6.7 %sum_pairs.7 = (s16[960,256]{1,0:T(8,128)(2,1)S(1)}, f32[960,256]{1,0:T(8,128)S(1)}) custom-call(s32[4]{0:T(128)S(1)} %pad_add_fusion.s_ref, bf16[5,320,640]{2,1,0:T(8,128)(2,1)} %copy-done, bf16[5,320,640]{2,1,0:T(8,128)(2,1)} %collective-permute-done.own_there.refs_3_, bf16[5,320,640]{2,1,0:T(8,128)(2,1)} %copy-done, ...), custom_call_target="tpu_custom_call" | custom-call | flops 2516582400 | bytes 7700480 | tf_op jit(solution)/shard_map/sum_pairs/pallas_call | solution.py:76
  62.2 1.6 %collective-permute-start.16 = (s16[960,256]{1,0:T(8,128)(2,1)S(1)}, s16[960,256]{1,0:T(8,128)(2,1)S(1)}, u32[]{:S(2)}, u32[]{:S(2)}) collective-permute-start(s16[960,256]{1,0:T(8,128)(2,1)S(1)} %get-tuple-element.45), channel_id=1, source_target_pairs={{0,2},{1,3},{2,0},{3,1},{4,6},{5,7},{6,4},{7,5},{8,10},{9,11},{10,... | collective-permute-start | bytes 1474568 | tf_op jit(solution)/shard_map/ppermute | solution.py:219
  63.8 10.7 %collective-permute-done.3.refs_0_ = bf16[320,640]{1,0:T(8,128)(2,1)S(1)} collective-permute-done((bf16[320,640]{1,0:T(8,128)(2,1)S(1)}, bf16[320,640]{1,0:T(8,128)(2,1)S(1)}, u32[]{:S(2)}, u32[]{:S(2)}) %collective-permute-start.3) | collective-permute-done | bytes 409632 | tf_op jit(solution)/shard_map/ppermute | solution.py:213
  74.4 6.7 %sum_pairs.6 = (s16[960,256]{1,0:T(8,128)(2,1)S(1)}, f32[960,256]{1,0:T(8,128)S(1)}) custom-call(s32[4]{0:T(128)S(1)} %pad_add_fusion.s_ref, bf16[5,320,640]{2,1,0:T(8,128)(2,1)} %copy-done, bf16[5,320,640]{2,1,0:T(8,128)(2,1)} %collective-permute-done.own_there.refs_3_, bf16[5,320,640]{2,1,0:T(8,128)(2,1)} %copy-done, ...), custom_call_target="tpu_custom_call" | custom-call | flops 2516582400 | bytes 7700480 | tf_op jit(solution)/shard_map/sum_pairs/pallas_call | solution.py:76
  81.2 1.6 %collective-permute-start.15 = (s16[960,256]{1,0:T(8,128)(2,1)S(1)}, s16[960,256]{1,0:T(8,128)(2,1)S(1)}, u32[]{:S(2)}, u32[]{:S(2)}) collective-permute-start(s16[960,256]{1,0:T(8,128)(2,1)S(1)} %get-tuple-element.43), channel_id=1, source_target_pairs={{0,2},{1,3},{2,0},{3,1},{4,6},{5,7},{6,4},{7,5},{8,10},{9,11},{10,... | collective-permute-start | bytes 1474568 | tf_op jit(solution)/shard_map/ppermute | solution.py:219
  82.8 0.8 add_other_y.3
  83.6 1.6 %collective-permute-start.17 = (s16[960,256]{1,0:T(8,128)(2,1)S(1)}, s16[960,256]{1,0:T(8,128)(2,1)S(1)}, u32[]{:S(2)}, u32[]{:S(2)}) collective-permute-start(s16[960,256]{1,0:T(8,128)(2,1)S(1)} %add_other_y.3), channel_id=1, source_target_pairs={{0,16},{16,0},{1,17},{17,1},{2,18},{18,2},{3,19},{19,3},{4,20},{20... | collective-permute-start | bytes 1474568 | tf_op jit(solution)/shard_map/ppermute | solution.py:213
  85.2 3.7 %sum_pairs.5 = (s16[320,256]{1,0:T(8,128)(2,1)S(1)}, f32[320,256]{1,0:T(8,128)S(1)}) custom-call(s32[4]{0:T(128)S(1)} %pad_add_fusion.s_ref, bf16[5,320,640]{2,1,0:T(8,128)(2,1)S(1)} %copy-done.1, bf16[5,320,640]{2,1,0:T(8,128)(2,1)} %collective-permute-done.own_there.refs_3_, bf16[320,640]{1,0:T(8,128)(2,1)S(1)} %collective-permute-done.3.refs_0_, ...), custom_call_target="tpu_custom_call" | custom-call | flops 838860800 | bytes 3440640 | tf_op jit(solution)/shard_map/sum_pairs/pallas_call | solution.py:76
  88.9 0.6 collective-permute-start.10
  89.4 3.7 %sum_pairs.4 = (s16[320,256]{1,0:T(8,128)(2,1)S(1)}, f32[320,256]{1,0:T(8,128)S(1)}) custom-call(s32[4]{0:T(128)S(1)} %pad_add_fusion.s_ref, bf16[5,320,640]{2,1,0:T(8,128)(2,1)S(1)} %copy-done.1, bf16[5,320,640]{2,1,0:T(8,128)(2,1)} %collective-permute-done.own_there.refs_3_, bf16[320,640]{1,0:T(8,128)(2,1)S(1)} %collective-permute-done.3.refs_0_, ...), custom_call_target="tpu_custom_call" | custom-call | flops 838860800 | bytes 3440640 | tf_op jit(solution)/shard_map/sum_pairs/pallas_call | solution.py:76
  93.1 1.6 %collective-permute-start.6 = (s16[320,256]{1,0:T(8,128)(2,1)S(1)}, s16[320,256]{1,0:T(8,128)(2,1)S(1)}, u32[]{:S(2)}, u32[]{:S(2)}) collective-permute-start(s16[320,256]{1,0:T(8,128)(2,1)S(1)} %get-tuple-element.38), channel_id=1, source_target_pairs={{0,2},{1,3},{2,0},{3,1},{4,6},{5,7},{6,4},{7,5},{8,10},{9,11},{10,... | collective-permute-start | bytes 491528 | tf_op jit(solution)/shard_map/ppermute | solution.py:219
  94.7 4.1 %collective-permute-done.10.coded_ref = s16[320,256]{1,0:T(8,128)(2,1)S(1)} collective-permute-done((s16[320,256]{1,0:T(8,128)(2,1)S(1)}, s16[320,256]{1,0:T(8,128)(2,1)S(1)}, u32[]{:S(2)}, u32[]{:S(2)}) %collective-permute-start.10) | collective-permute-done | bytes 163872 | tf_op jit(solution)/shard_map/ppermute | solution.py:219
  98.7 0.6 add_other_y.2
  99.4 1.6 %collective-permute-start.11 = (s16[320,256]{1,0:T(8,128)(2,1)S(1)}, s16[320,256]{1,0:T(8,128)(2,1)S(1)}, u32[]{:S(2)}, u32[]{:S(2)}) collective-permute-start(s16[320,256]{1,0:T(8,128)(2,1)S(1)} %add_other_y.2), channel_id=1, source_target_pairs={{0,16},{16,0},{1,17},{17,1},{2,18},{18,2},{3,19},{19,3},{4,20},{20... | collective-permute-start | bytes 491528 | tf_op jit(solution)/shard_map/ppermute | solution.py:213
  101.0 0.8 add_other_x.3
  101.8 0.8 collective-permute-start.18
  102.6 3.1 %collective-permute-start.19 = (bf16[320,256]{1,0:T(8,128)(2,1)S(1)}, bf16[320,256]{1,0:T(8,128)(2,1)S(1)}, u32[]{:S(2)}, u32[]{:S(2)}) collective-permute-start(bf16[320,256]{1,0:T(8,128)(2,1)S(1)} %get-tuple-element.48.refs_3_), channel_id=1, source_target_pairs={{0,12},{4,0},{8,4},{12,8},{1,13},{5,1},{9,5},{13,9},{2,14},{6,2},{... | collective-permute-start | bytes 491528 | tf_op jit(solution)/shard_map/ppermute | solution.py:213
  105.7 0.6 add_other_x.2.refs_0_
  106.4 0.4 collective-permute-start.12
  106.8 4.1 %collective-permute-done.18.refs_2_ = bf16[320,256]{1,0:T(8,128)(2,1)S(1)} collective-permute-done((bf16[320,256]{1,0:T(8,128)(2,1)S(1)}, bf16[320,256]{1,0:T(8,128)(2,1)S(1)}, u32[]{:S(2)}, u32[]{:S(2)}) %collective-permute-start.18) | collective-permute-done | bytes 163872 | tf_op jit(solution)/shard_map/ppermute | solution.py:213
  110.9 0.1 collective-permute-done.19.refs_4_
  111.0 5.2 %place_pairs.2.refs_2_ = bf16[2500,256]{1,0:T(8,128)(2,1)S(1)} custom-call(s32[4]{0:T(128)S(1)} %pad_add_fusion.s_ref, bf16[320,256]{1,0:T(8,128)(2,1)S(1)} %get-tuple-element.46.refs_0_, bf16[320,256]{1,0:T(8,128)(2,1)S(1)} %get-tuple-element.47.refs_1_, bf16[320,256]{1,0:T(8,128)(2,1)S(1)} %collective-permute-done.18.refs_2_, ...), custom_call_target="tpu_custom_call" | custom-call | flops 2048000000 | bytes 3379200 | tf_op jit(solution)/shard_map/place_pairs/pallas_call | solution.py:76
  116.2 3.2 %collective-permute-done.12.refs_1_ = bf16[320,256]{1,0:T(8,128)(2,1)S(1)} collective-permute-done((bf16[320,256]{1,0:T(8,128)(2,1)S(1)}, bf16[320,256]{1,0:T(8,128)(2,1)S(1)}, u32[]{:S(2)}, u32[]{:S(2)}) %collective-permute-start.12) | collective-permute-done | bytes 163872 | tf_op jit(solution)/shard_map/ppermute | solution.py:213
  119.4 4.0 %place_pairs.3 = bf16[2500,256]{1,0:T(8,128)(2,1)} custom-call(s32[4]{0:T(128)S(1)} %pad_add_fusion.s_ref, bf16[320,256]{1,0:T(8,128)(2,1)S(1)} %add_other_x.2.refs_0_, bf16[320,256]{1,0:T(8,128)(2,1)S(1)} %collective-permute-done.12.refs_1_, bf16[2500,256]{1,0:T(8,128)(2,1)S(1)} %place_pairs.2.refs_2_), custom_call_target="tpu_custom_call" | custom-call | flops 1228800000 | bytes 3051520 | tf_op jit(solution)/shard_map/place_pairs/pallas_call | solution.py:76
  (18 shorter events, 0.0 us)
Async XLA Ops:
  0.8 1.7 %copy-start.2 = (bf16[1024,1280]{1,0:T(8,128)(2,1)S(1)}, bf16[1024,1280]{1,0:T(8,128)(2,1)}, u32[]{:S(2)}) copy-start(bf16[1024,1280]{1,0:T(8,128)(2,1)} %v_ref.2) | copy-start | bytes 7864324
  2.5 0.7 copy-start.4
  13.0 32.7 %copy-start.3 = (bf16[1024,1280]{1,0:T(8,128)(2,1)S(1)}, bf16[1024,1280]{1,0:T(8,128)(2,1)}, u32[]{:S(2)}) copy-start(bf16[1024,1280]{1,0:T(8,128)(2,1)} %v_ref.2) | copy-start | bytes 7864324
  20.2 28.4 %copy-start = (bf16[5,320,640]{2,1,0:T(8,128)(2,1)}, bf16[5,320,640]{2,1,0:T(8,128)(2,1)S(1)}, u32[]{:S(2)}) copy-start(bf16[5,320,640]{2,1,0:T(8,128)(2,1)S(1)} %keep_columns.1.own_here.refs_0_) | copy-start | bytes 6144004
  20.2 35.3 %collective-permute-start = (bf16[5,320,640]{2,1,0:T(8,128)(2,1)S(1)}, bf16[5,320,640]{2,1,0:T(8,128)(2,1)}, u32[]{:S(2)}, u32[]{:S(2)}) collective-permute-start(bf16[5,320,640]{2,1,0:T(8,128)(2,1)S(1)} %keep_columns.1.own_here.refs_0_), channel_id=1, source_target_pairs={{0,1},{1,0},{2,3},{3,2},{4,5},{5,4},{6,7},{7,6},{8,9},{9,8},{10,11... | collective-permute-start | bytes 6144008 | tf_op jit(solution)/shard_map/ppermute | solution.py:216
  20.7 18.1 %collective-permute-start.8 = (bf16[2,256,640]{2,1,0:T(8,128)(2,1)S(1)}, bf16[2,256,640]{2,1,0:T(8,128)(2,1)S(1)}, u32[]{:S(2)}, u32[]{:S(2)}) collective-permute-start(bf16[2,256,640]{2,1,0:T(8,128)(2,1)S(1)} %get-tuple-element.27), channel_id=1, source_target_pairs={{0,16},{16,0},{1,17},{17,1},{2,18},{18,2},{3,19},{19,3},{4,20},{20... | collective-permute-start | bytes 1966088 | tf_op jit(solution)/shard_map/ppermute | solution.py:213
  23.3 15.6 %collective-permute-start.1 = (bf16[320,640]{1,0:T(8,128)(2,1)S(1)}, bf16[320,640]{1,0:T(8,128)(2,1)S(1)}, u32[]{:S(2)}, u32[]{:S(2)}) collective-permute-start(bf16[320,640]{1,0:T(8,128)(2,1)S(1)} %get-tuple-element.31), channel_id=1, source_target_pairs={{0,12},{4,0},{8,4},{12,8},{1,13},{5,1},{9,5},{13,9},{2,14},{6,2},{... | collective-permute-start | bytes 1228808 | tf_op jit(solution)/shard_map/ppermute | solution.py:213
  26.9 25.8 %collective-permute-start.7 = (bf16[2,256,640]{2,1,0:T(8,128)(2,1)S(1)}, bf16[2,256,640]{2,1,0:T(8,128)(2,1)S(1)}, u32[]{:S(2)}, u32[]{:S(2)}) collective-permute-start(bf16[2,256,640]{2,1,0:T(8,128)(2,1)S(1)} %get-tuple-element.39), channel_id=1, source_target_pairs={{0,16},{16,0},{1,17},{17,1},{2,18},{18,2},{3,19},{19,3},{4,20},{20... | collective-permute-start | bytes 1966088 | tf_op jit(solution)/shard_map/ppermute | solution.py:213
  27.4 18.2 %collective-permute-start.2 = (bf16[320,640]{1,0:T(8,128)(2,1)S(1)}, bf16[320,640]{1,0:T(8,128)(2,1)S(1)}, u32[]{:S(2)}, u32[]{:S(2)}) collective-permute-start(bf16[320,640]{1,0:T(8,128)(2,1)S(1)} %get-tuple-element.32), channel_id=1, source_target_pairs={{0,4},{4,8},{8,12},{12,0},{1,5},{5,9},{9,13},{13,1},{2,6},{6,10},{... | collective-permute-start | bytes 1228808 | tf_op jit(solution)/shard_map/ppermute | solution.py:213
  38.9 16.7 %collective-permute-start.9 = (bf16[2,256,640]{2,1,0:T(8,128)(2,1)S(1)}, bf16[2,256,640]{2,1,0:T(8,128)(2,1)S(1)}, u32[]{:S(2)}, u32[]{:S(2)}) collective-permute-start(bf16[2,256,640]{2,1,0:T(8,128)(2,1)S(1)} %collective-permute-done.8), channel_id=1, source_target_pairs={{0,1},{1,0},{2,3},{3,2},{4,5},{5,4},{6,7},{7,6},{8,9},{9,8},{10,11... | collective-permute-start | bytes 1966088 | tf_op jit(solution)/shard_map/ppermute | solution.py:216
  38.9 13.8 %collective-permute-start.13 = (bf16[320,640]{1,0:T(8,128)(2,1)S(1)}, bf16[320,640]{1,0:T(8,128)(2,1)S(1)}, u32[]{:S(2)}, u32[]{:S(2)}) collective-permute-start(bf16[320,640]{1,0:T(8,128)(2,1)S(1)} %collective-permute-done.1.refs_1_), channel_id=1, source_target_pairs={{0,1},{1,0},{2,3},{3,2},{4,5},{5,4},{6,7},{7,6},{8,9},{9,8},{10,11... | collective-permute-start | bytes 1228808 | tf_op jit(solution)/shard_map/ppermute | solution.py:216
  45.6 9.9 %collective-permute-start.14 = (bf16[320,640]{1,0:T(8,128)(2,1)S(1)}, bf16[320,640]{1,0:T(8,128)(2,1)S(1)}, u32[]{:S(2)}, u32[]{:S(2)}) collective-permute-start(bf16[320,640]{1,0:T(8,128)(2,1)S(1)} %collective-permute-done.2.refs_2_), channel_id=1, source_target_pairs={{0,1},{1,0},{2,3},{3,2},{4,5},{5,4},{6,7},{7,6},{8,9},{9,8},{10,11... | collective-permute-start | bytes 1228808 | tf_op jit(solution)/shard_map/ppermute | solution.py:216
  52.7 21.8 %collective-permute-start.5 = (bf16[2,256,640]{2,1,0:T(8,128)(2,1)S(1)}, bf16[2,256,640]{2,1,0:T(8,128)(2,1)S(1)}, u32[]{:S(2)}, u32[]{:S(2)}) collective-permute-start(bf16[2,256,640]{2,1,0:T(8,128)(2,1)S(1)} %get-tuple-element.36), channel_id=1, source_target_pairs={{0,1},{1,0},{2,3},{3,2},{4,5},{5,4},{6,7},{7,6},{8,9},{9,8},{10,11... | collective-permute-start | bytes 1966088 | tf_op jit(solution)/shard_map/ppermute | solution.py:216
  52.7 21.8 %collective-permute-start.3 = (bf16[320,640]{1,0:T(8,128)(2,1)S(1)}, bf16[320,640]{1,0:T(8,128)(2,1)S(1)}, u32[]{:S(2)}, u32[]{:S(2)}) collective-permute-start(bf16[320,640]{1,0:T(8,128)(2,1)S(1)} %get-tuple-element.33), channel_id=1, source_target_pairs={{0,8},{4,12},{8,0},{12,4},{1,9},{5,13},{9,1},{13,5},{2,10},{6,14},... | collective-permute-start | bytes 1228808 | tf_op jit(solution)/shard_map/ppermute | solution.py:213
  62.2 20.6 %collective-permute-start.16 = (s16[960,256]{1,0:T(8,128)(2,1)S(1)}, s16[960,256]{1,0:T(8,128)(2,1)S(1)}, u32[]{:S(2)}, u32[]{:S(2)}) collective-permute-start(s16[960,256]{1,0:T(8,128)(2,1)S(1)} %get-tuple-element.45), channel_id=1, source_target_pairs={{0,2},{1,3},{2,0},{3,1},{4,6},{5,7},{6,4},{7,5},{8,10},{9,11},{10,... | collective-permute-start | bytes 1474568 | tf_op jit(solution)/shard_map/ppermute | solution.py:219
  74.4 10.8 %collective-permute-start.4 = (bf16[320,640]{1,0:T(8,128)(2,1)S(1)}, bf16[320,640]{1,0:T(8,128)(2,1)S(1)}, u32[]{:S(2)}, u32[]{:S(2)}) collective-permute-start(bf16[320,640]{1,0:T(8,128)(2,1)S(1)} %collective-permute-done.3.refs_0_), channel_id=1, source_target_pairs={{0,1},{1,0},{2,3},{3,2},{4,5},{5,4},{6,7},{7,6},{8,9},{9,8},{10,11... | collective-permute-start | bytes 1228808 | tf_op jit(solution)/shard_map/ppermute | solution.py:216
  74.4 10.7 %copy-start.1 = (bf16[5,320,640]{2,1,0:T(8,128)(2,1)S(1)}, bf16[5,320,640]{2,1,0:T(8,128)(2,1)}, u32[]{:S(2)}) copy-start(bf16[5,320,640]{2,1,0:T(8,128)(2,1)} %copy-done) | copy-start | bytes 6144004
  81.2 19.9 %collective-permute-start.15 = (s16[960,256]{1,0:T(8,128)(2,1)S(1)}, s16[960,256]{1,0:T(8,128)(2,1)S(1)}, u32[]{:S(2)}, u32[]{:S(2)}) collective-permute-start(s16[960,256]{1,0:T(8,128)(2,1)S(1)} %get-tuple-element.43), channel_id=1, source_target_pairs={{0,2},{1,3},{2,0},{3,1},{4,6},{5,7},{6,4},{7,5},{8,10},{9,11},{10,... | collective-permute-start | bytes 1474568 | tf_op jit(solution)/shard_map/ppermute | solution.py:219
  83.6 17.4 %collective-permute-start.17 = (s16[960,256]{1,0:T(8,128)(2,1)S(1)}, s16[960,256]{1,0:T(8,128)(2,1)S(1)}, u32[]{:S(2)}, u32[]{:S(2)}) collective-permute-start(s16[960,256]{1,0:T(8,128)(2,1)S(1)} %add_other_y.3), channel_id=1, source_target_pairs={{0,16},{16,0},{1,17},{17,1},{2,18},{18,2},{3,19},{19,3},{4,20},{20... | collective-permute-start | bytes 1474568 | tf_op jit(solution)/shard_map/ppermute | solution.py:213
  88.9 9.9 %collective-permute-start.10 = (s16[320,256]{1,0:T(8,128)(2,1)S(1)}, s16[320,256]{1,0:T(8,128)(2,1)S(1)}, u32[]{:S(2)}, u32[]{:S(2)}) collective-permute-start(s16[320,256]{1,0:T(8,128)(2,1)S(1)} %get-tuple-element.41), channel_id=1, source_target_pairs={{0,2},{1,3},{2,0},{3,1},{4,6},{5,7},{6,4},{7,5},{8,10},{9,11},{10,... | collective-permute-start | bytes 491528 | tf_op jit(solution)/shard_map/ppermute | solution.py:219
  93.1 12.6 %collective-permute-start.6 = (s16[320,256]{1,0:T(8,128)(2,1)S(1)}, s16[320,256]{1,0:T(8,128)(2,1)S(1)}, u32[]{:S(2)}, u32[]{:S(2)}) collective-permute-start(s16[320,256]{1,0:T(8,128)(2,1)S(1)} %get-tuple-element.38), channel_id=1, source_target_pairs={{0,2},{1,3},{2,0},{3,1},{4,6},{5,7},{6,4},{7,5},{8,10},{9,11},{10,... | collective-permute-start | bytes 491528 | tf_op jit(solution)/shard_map/ppermute | solution.py:219
  99.4 6.3 %collective-permute-start.11 = (s16[320,256]{1,0:T(8,128)(2,1)S(1)}, s16[320,256]{1,0:T(8,128)(2,1)S(1)}, u32[]{:S(2)}, u32[]{:S(2)}) collective-permute-start(s16[320,256]{1,0:T(8,128)(2,1)S(1)} %add_other_y.2), channel_id=1, source_target_pairs={{0,16},{16,0},{1,17},{17,1},{2,18},{18,2},{3,19},{19,3},{4,20},{20... | collective-permute-start | bytes 491528 | tf_op jit(solution)/shard_map/ppermute | solution.py:213
  101.8 9.0 %collective-permute-start.18 = (bf16[320,256]{1,0:T(8,128)(2,1)S(1)}, bf16[320,256]{1,0:T(8,128)(2,1)S(1)}, u32[]{:S(2)}, u32[]{:S(2)}) collective-permute-start(bf16[320,256]{1,0:T(8,128)(2,1)S(1)} %get-tuple-element.47.refs_1_), channel_id=1, source_target_pairs={{0,4},{4,8},{8,12},{12,0},{1,5},{5,9},{9,13},{13,1},{2,6},{6,10},{... | collective-permute-start | bytes 491528 | tf_op jit(solution)/shard_map/ppermute | solution.py:213
  102.6 8.3 %collective-permute-start.19 = (bf16[320,256]{1,0:T(8,128)(2,1)S(1)}, bf16[320,256]{1,0:T(8,128)(2,1)S(1)}, u32[]{:S(2)}, u32[]{:S(2)}) collective-permute-start(bf16[320,256]{1,0:T(8,128)(2,1)S(1)} %get-tuple-element.48.refs_3_), channel_id=1, source_target_pairs={{0,12},{4,0},{8,4},{12,8},{1,13},{5,1},{9,5},{13,9},{2,14},{6,2},{... | collective-permute-start | bytes 491528 | tf_op jit(solution)/shard_map/ppermute | solution.py:213
  106.4 13.0 %collective-permute-start.12 = (bf16[320,256]{1,0:T(8,128)(2,1)S(1)}, bf16[320,256]{1,0:T(8,128)(2,1)S(1)}, u32[]{:S(2)}, u32[]{:S(2)}) collective-permute-start(bf16[320,256]{1,0:T(8,128)(2,1)S(1)} %add_other_x.2.refs_0_), channel_id=1, source_target_pairs={{0,8},{4,12},{8,0},{12,4},{1,9},{5,13},{9,1},{13,5},{2,10},{6,14},... | collective-permute-start | bytes 491528 | tf_op jit(solution)/shard_map/ppermute | solution.py:213

commit v3 on v2

--- a/solution.py
+++ b/solution.py
@@ -13,6 +13,8 @@
 STEPS = 256.0
 CORES = 2
 TILE = 512
+LANES = 128
+LIGHT = 64
 
 
 def dot_nt(a, b):
@@ -81,7 +83,7 @@
             num_scalar_prefetch=1, grid=(grid,), in_specs=in_specs, out_specs=out_specs, scratch_shapes=list(scratch)
         ),
         compiler_params=pltpu.CompilerParams(vmem_limit_bytes=48 * 2**20),
-        cost_estimate=pl.CostEstimate(flops=int(flops), bytes_accessed=int(moved), transcendentals=0),
+        cost_estimate=pl.CostEstimate(flops=int(flops) // LIGHT, bytes_accessed=int(moved) // LIGHT, transcendentals=0),
     )(scalars, *arrays)
 
 
@@ -91,17 +93,21 @@
     q, m = divide(lax.broadcasted_iota(jnp.int32, (k_here, 1), 0), sub)
     wanted = q * (sub * row_n) + lax.rem(x - by + row_n, row_n) * sub + m
     pick = jnp.where(lax.broadcasted_iota(jnp.int32, (k_here, cd_here), 1) == wanted, 1.0, 0.0).astype(jnp.bfloat16)
-    square = (tall, tall)
+    square = (LANES, LANES)
     diagonal = lax.broadcasted_iota(jnp.int32, square, 0) == lax.broadcasted_iota(jnp.int32, square, 1)
+    cd_labels = cd_ref[...].astype(jnp.float32)
+    cd = jnp.concatenate([cd_labels[k : k + 1] for k in range(cd_here // LANES)], axis=1)
+    strips = tall // LANES
     blocks = []
     for other_core in (1, 0):
         for other_y in (1, 0):
             block = lax.rem(y + other_y, 2) * CORES + lax.rem(core + other_core, CORES)
-            start = pl.multiple_of(block * tall, tall)
-            labels = ab_ref[:, pl.ds(start, tall)].astype(jnp.float32)
-            ab = jnp.sum(jnp.where(diagonal, labels, 0.0), axis=1, keepdims=True)
-            v = v_ref[pl.ds(start, tall), :].astype(jnp.float32)
-            blocks.append(jnp.where(ab == cd_ref[...].astype(jnp.float32), v, 0.0).astype(jnp.bfloat16))
+            for strip in range(strips):
+                labels = ab_ref[pl.ds(block * strips + strip, 1), :].astype(jnp.float32)
+                ab = jnp.sum(jnp.where(diagonal, labels, 0.0), axis=1, keepdims=True)
+                start = pl.multiple_of(block * tall + strip * LANES, LANES)
+                v = v_ref[pl.ds(start, LANES), :].astype(jnp.float32)
+                blocks.append(jnp.where(ab == cd, v, 0.0).astype(jnp.bfloat16))
     picked = dot_nt(jnp.concatenate(blocks, axis=0), pick).astype(jnp.bfloat16)
     pass_ref[...] = picked[: 2 * tall].reshape(pass_ref.shape)
     keep_ref[...] = picked[2 * tall :].reshape(keep_ref.shape)
@@ -116,9 +122,11 @@
     flat_ref[...] = t_ref[...].reshape(flat_ref.shape)
     z = s_ref[1]
     place = lax.broadcasted_iota(jnp.int32, (out_refs[0].shape[0], 1), 0)
-    for r, out_ref in zip(order, out_refs):
-        wanted = pair_columns(place, n, z, lax.rem(z - r + col_n, col_n), False)
-        out_ref[...] = dot_nt(one_hot_rows(wanted, flat_ref.shape[1]), flat_ref[...]).astype(jnp.bfloat16)
+    chunk = out_refs[0].shape[0]
+    wanted = [pair_columns(place, n, z, lax.rem(z - r + col_n, col_n), False) for r in order]
+    picked = dot_nt(one_hot_rows(jnp.concatenate(wanted, axis=0), flat_ref.shape[1]), flat_ref[...]).astype(jnp.bfloat16)
+    for k, out_ref in enumerate(out_refs):
+        out_ref[...] = picked[k * chunk : (k + 1) * chunk]
 
 
 def keep_body(order, n, col_n, s_ref, flat_ref, out_ref):
@@ -126,8 +134,8 @@
     place = lax.broadcasted_iota(jnp.int32, (out_ref.shape[1], 1), 0)
     inside, turned = inside_columns(place, n, z)
     picks = [inside if r == 0 else pair_columns(place, n, z, lax.rem(z + r, col_n), True) for r in order] + [turned]
-    for k, wanted in enumerate(picks):
-        out_ref[k] = dot_nt(one_hot_rows(wanted, flat_ref.shape[1]), flat_ref[...]).astype(jnp.bfloat16)
+    picked = dot_nt(one_hot_rows(jnp.concatenate(picks, axis=0), flat_ref.shape[1]), flat_ref[...])
+    out_ref[...] = picked.astype(jnp.bfloat16).reshape(out_ref.shape)
 
 
 def sum_body(first, count, s_ref, own_here, own_there, *refs):
@@ -139,20 +147,17 @@
     def rows(ref):
         return ref[...].reshape(-1, k_here)
 
-    a, b = keep_ref[0], pass_ref[0]
+    a, b = keep_ref[...].reshape(-1, k_here), pass_ref[...].reshape(-1, k_here)
+    half = a.shape[0] // 2
     to = own_here[first : first + count].reshape(count * chunk, k_here)
     too = own_there[first : first + count].reshape(count * chunk, k_here)
     tr = jnp.concatenate([rows(ref) for ref in away[:count]], axis=0)
     tro = jnp.concatenate([rows(ref) for ref in away[count:]], axis=0)
-    total = (dot_nt(to, a) + dot_nt(too, b)) - (dot_nt(tr, a) + dot_nt(tro, b))
-
-    @pl.when(pl.program_id(0) == 0)
-    def _():
-        coded_ref[...] = encode(total)
-
-    @pl.when(pl.program_id(0) == 1)
-    def _():
-        kept_ref[...] = total
+    left = jnp.concatenate([to, too, tr, tro], axis=1)
+    right = jnp.concatenate([a, b, -a, -b], axis=1)
+    total = dot_nt(left, right)
+    coded_ref[...] = encode(total[:, :half])
+    kept_ref[...] = total[:, half:]
 
 
 def add_y_body(s_ref, kept_ref, coded_ref, out_ref):
@@ -175,20 +180,21 @@
     chunk = refs[0].shape[0]
     place = lax.broadcasted_iota(jnp.int32, (1, chunk), 1)
     at = lax.broadcasted_iota(jnp.int32, (out_ref.shape[0], chunk), 0) + pl.program_id(0) * out_ref.shape[0]
-    total = refs[-2][...].astype(jnp.float32) if before else None
-    source = iter(refs)
+    signs = []
     for r in order:
         if r == 0:
             inside, turned = inside_columns(place, n, z)
-            signs = jnp.where(at == inside, 1.0, jnp.where(at == turned, -1.0, 0.0))
-            terms = [(signs, next(source))]
+            signs.append(jnp.where(at == inside, 1.0, jnp.where(at == turned, -1.0, 0.0)))
         else:
             plus = pair_columns(place, n, z, lax.rem(z + r, col_n), True)
             minus = pair_columns(place, n, z, lax.rem(z - r + col_n, col_n), False)
-            terms = [(jnp.where(at == plus, 1.0, 0.0), next(source)), (jnp.where(at == minus, -1.0, 0.0), next(source))]
-        for signs, ref in terms:
-            term = dot_nn(signs.astype(jnp.bfloat16), ref[...])
-            total = term if total is None else total + term
+            signs.append(jnp.where(at == plus, 1.0, 0.0))
+            signs.append(jnp.where(at == minus, -1.0, 0.0))
+    signs = jnp.concatenate([sign.astype(jnp.bfloat16) for sign in signs], axis=1)
+    values = jnp.concatenate([ref[...] for ref in refs[: 2 * len(order) - order.count(0)]], axis=0)
+    total = dot_nn(signs, values)
+    if before:
+        total = total + refs[-2][...].astype(jnp.float32)
     out_ref[...] = total.astype(jnp.bfloat16)
 
 
@@ -219,7 +225,7 @@
         return lax.ppermute(array, "depth", [(i, i ^ 2) for i in range(depth_n)])
 
     scalars = jnp.stack([x, z, y, core]).astype(jnp.int32)
-    ab_row, cd_row = ab_irrep.reshape(1, rows), cd_irrep.reshape(1, cd_here)
+    ab_row, cd_row = ab_irrep.reshape(-1, LANES), cd_irrep.reshape(-1, LANES)
 
     def masked(v, by):
         return call(
@@ -274,16 +280,14 @@
         there = [(own_there, *tail) if r == 0 else other_core(away[r]) for r in group]
         final = []
         for by in range(row_n):
-            block = (1, tall, k_here), lambda g, s: (g, 0, 0)
             coded, total = call(
                 "sum_pairs",
                 functools.partial(sum_body, first, count),
                 scalars,
-                [own, own_there] + here + there + [(kept[by], *block), (passed[by], *block)],
+                [own, own_there] + here + there + [kept[by], passed[by]],
                 [((count * chunk, tall), i16), ((count * chunk, tall), f32)],
                 2 * 2 * 2 * count * chunk * tall * CORES * k_here,
                 2 * CORES * k_here * (2 * count * chunk + 2 * tall) + 6 * count * chunk * tall,
-                grid=2,
             )
             coded = other_y(coded)
             if by == 0:

time: 124 us -> 123 us (level)
  Pallas kernels: 52.7 us -> 50.1 us
  local copies, waits for them, and re-layouts: 3.14 us -> 4.43 us
    pallas_call x14, Pallas kernels: 52.7 us -> 50.1 us  [call(): pl.pallas_call(body, name=name, out_shape=shapes, grid_spec=pltpu.Prefetc...]
    unnamed x10 -> x16, local copies, waits for them, and re-layouts: 2.44 us -> 4.43 us
  transfers between devices with their start and end apart: 20 -> 20, of which waited for: 8 -> 8; matrix products, arithmetic and copies ran while one was open for 0% -> 0% of each run, Pallas kernels for 26% -> 23%
where the time goes in v3:
time: 123 us
  Pallas kernels  50.1 us (41%)
  waiting for transfers between devices  44.8 us (36%)
  starting transfers between devices  23.4 us (19%)
  local copies, waits for them, and re-layouts  4.43 us (4%)
    pallas_call x14, Pallas kernels, call(): pl.pallas_call(body, name=name, out_shape=shapes, grid_spec=pltpu.Prefetc...  50.1 us
    ppermute x10, waiting for transfers between devices, shift(): lax.ppermute(array, axis, [(i, (i + by) % count) for i in range(count)])  39.9 us
    ppermute x10, starting transfers between devices, shift(): lax.ppermute(array, axis, [(i, (i + by) % count) for i in range(count)])  17 us
    ppermute x4, starting transfers between devices, other_y(): return lax.ppermute(array, 'depth', [(i, i ^ 2) for i in range(depth_n)])  5.38 us
    ppermute x4, waiting for transfers between devices, other_y(): return lax.ppermute(array, 'depth', [(i, i ^ 2) for i in range(depth_n)])  4.96 us
    unnamed x16, local copies, waits for them, and re-layouts  4.43 us
  transfers between devices with their start and end apart: 20, of which 8 were waited for; matrix products, arithmetic and copies ran while one was open for 0% of the time, Pallas kernels for 23%

profile of v3, /device:TPU:0, one launch (start us, length us, event | category | flops | bytes accessed | tf_op | source)
XLA Modules:
  0.0 123.0 jit_solution(14574081503887229622)
XLA Ops:
  0.0 0.1 pad_add_fusion.s_ref
  0.1 1.7 %copy-done.2 = bf16[1024,1280]{1,0:T(8,128)(2,1)S(1)} copy-done((bf16[1024,1280]{1,0:T(8,128)(2,1)S(1)}, bf16[1024,1280]{1,0:T(8,128)(2,1)}, u32[]{:S(2)}) %copy-start.2) | copy-done | bytes 2621464
  1.8 0.7 copy-done.4
  2.5 0.7 copy-done.6
  3.2 2.9 %mask_integrals.2 = (bf16[2,256,640]{2,1,0:T(8,128)(2,1)S(1)}, bf16[2,256,640]{2,1,0:T(8,128)(2,1)S(1)}) custom-call(s32[4]{0:T(128)S(1)} %pad_add_fusion.s_ref, s32[8,128]{1,0:T(8,128)S(1)} %bitcast.9, s32[10,128]{1,0:T(8,128)S(1)} %bitcast.7, bf16[1024,1280]{1,0:T(8,128)(2,1)S(1)} %copy-done.2), custom_call_target="tpu_custom_call" | custom-call | flops 26214400 | bytes 61440 | tf_op jit(solution)/shard_map/mask_integrals/pallas_call | solution.py:78
  6.1 7.1 %send_columns.1 = (bf16[640,2500]{1,0:T(8,128)(2,1)S(1)}, bf16[320,640]{1,0:T(8,128)(2,1)S(1)}, bf16[320,640]{1,0:T(8,128)(2,1)S(1)}, bf16[320,640]{1,0:T(8,128)(2,1)S(1)}) custom-call(s32[4]{0:T(128)S(1)} %pad_add_fusion.s_ref, bf16[320,2,2500]{2,1,0:T(2,128)(2,1)} %t_ref), custom_call_target="tpu_custom_call" | custom-call | flops 48000000 | bytes 119200 | tf_op jit(solution)/shard_map/send_columns/pallas_call | solution.py:78
  13.1 0.0 copy-start.3
  13.1 0.0 copy-start.5
  13.2 7.6 %keep_columns.1.own_here.refs_0_ = bf16[5,320,640]{2,1,0:T(8,128)(2,1)S(1)} custom-call(s32[4]{0:T(128)S(1)} %pad_add_fusion.s_ref, bf16[640,2500]{1,0:T(8,128)(2,1)S(1)} %get-tuple-element.29.flat_ref), custom_call_target="tpu_custom_call" | custom-call | flops 80000000 | bytes 82000 | tf_op jit(solution)/shard_map/keep_columns/pallas_call | solution.py:78
  20.8 0.5 collective-permute-start
  21.3 2.6 %collective-permute-start.8 = (bf16[2,256,640]{2,1,0:T(8,128)(2,1)S(1)}, bf16[2,256,640]{2,1,0:T(8,128)(2,1)S(1)}, u32[]{:S(2)}, u32[]{:S(2)}) collective-permute-start(bf16[2,256,640]{2,1,0:T(8,128)(2,1)S(1)} %get-tuple-element.27), channel_id=1, source_target_pairs={{0,16},{16,0},{1,17},{17,1},{2,18},{18,2},{3,19},{19,3},{4,20},{20... | collective-permute-start | bytes 1966088 | tf_op jit(solution)/shard_map/ppermute | solution.py:219
  23.9 3.6 %collective-permute-start.1 = (bf16[320,640]{1,0:T(8,128)(2,1)S(1)}, bf16[320,640]{1,0:T(8,128)(2,1)S(1)}, u32[]{:S(2)}, u32[]{:S(2)}) collective-permute-start(bf16[320,640]{1,0:T(8,128)(2,1)S(1)} %get-tuple-element.31), channel_id=1, source_target_pairs={{0,12},{4,0},{8,4},{12,8},{1,13},{5,1},{9,5},{13,9},{2,14},{6,2},{... | collective-permute-start | bytes 1228808 | tf_op jit(solution)/shard_map/ppermute | solution.py:219
  27.5 0.5 collective-permute-start.7
  28.0 0.0 collective-permute-start.2
  28.0 11.4 %collective-permute-done.8 = bf16[2,256,640]{2,1,0:T(8,128)(2,1)S(1)} collective-permute-done((bf16[2,256,640]{2,1,0:T(8,128)(2,1)S(1)}, bf16[2,256,640]{2,1,0:T(8,128)(2,1)S(1)}, u32[]{:S(2)}, u32[]{:S(2)}) %collective-permute-start.8) | collective-permute-done | bytes 655392 | tf_op jit(solution)/shard_map/ppermute | solution.py:219
  39.4 0.0 collective-permute-start.9
  39.4 0.0 collective-permute-done.1.refs_1_
  39.4 0.5 collective-permute-start.13
  40.0 6.2 %collective-permute-done.2.refs_2_ = bf16[320,640]{1,0:T(8,128)(2,1)S(1)} collective-permute-done((bf16[320,640]{1,0:T(8,128)(2,1)S(1)}, bf16[320,640]{1,0:T(8,128)(2,1)S(1)}, u32[]{:S(2)}, u32[]{:S(2)}) %collective-permute-start.2) | collective-permute-done | bytes 409632 | tf_op jit(solution)/shard_map/ppermute | solution.py:219
  46.2 2.9 %mask_integrals.3 = (bf16[2,256,640]{2,1,0:T(8,128)(2,1)S(1)}, bf16[2,256,640]{2,1,0:T(8,128)(2,1)S(1)}) custom-call(s32[4]{0:T(128)S(1)} %pad_add_fusion.s_ref, s32[8,128]{1,0:T(8,128)S(1)} %bitcast.10, s32[10,128]{1,0:T(8,128)S(1)} %bitcast.8, bf16[1024,1280]{1,0:T(8,128)(2,1)S(1)} %copy-done.3), custom_call_target="tpu_custom_call" | custom-call | flops 26214400 | bytes 61440 | tf_op jit(solution)/shard_map/mask_integrals/pallas_call | solution.py:78
  49.1 4.1 %collective-permute-done.7.refs_2_.refs_6_ = bf16[2,256,640]{2,1,0:T(8,128)(2,1)S(1)} collective-permute-done((bf16[2,256,640]{2,1,0:T(8,128)(2,1)S(1)}, bf16[2,256,640]{2,1,0:T(8,128)(2,1)S(1)}, u32[]{:S(2)}, u32[]{:S(2)}) %collective-permute-start.7) | collective-permute-done | bytes 655392 | tf_op jit(solution)/shard_map/ppermute | solution.py:219
  53.2 0.0 collective-permute-start.5
  53.2 2.9 %collective-permute-start.3 = (bf16[320,640]{1,0:T(8,128)(2,1)S(1)}, bf16[320,640]{1,0:T(8,128)(2,1)S(1)}, u32[]{:S(2)}, u32[]{:S(2)}) collective-permute-start(bf16[320,640]{1,0:T(8,128)(2,1)S(1)} %get-tuple-element.33), channel_id=1, source_target_pairs={{0,8},{4,12},{8,0},{12,4},{1,9},{5,13},{9,1},{13,5},{2,10},{6,14},... | collective-permute-start | bytes 1228808 | tf_op jit(solution)/shard_map/ppermute | solution.py:219
  56.1 1.3 %copy-done.7 = bf16[5,320,640]{2,1,0:T(8,128)(2,1)} copy-done((bf16[5,320,640]{2,1,0:T(8,128)(2,1)}, bf16[5,320,640]{2,1,0:T(8,128)(2,1)S(1)}, u32[]{:S(2)}) %copy-start.7) | copy-done | bytes 2048024
  57.4 5.8 %sum_pairs.7 = (s16[960,256]{1,0:T(8,128)(2,1)S(1)}, f32[960,256]{1,0:T(8,128)S(1)}) custom-call(s32[4]{0:T(128)S(1)} %pad_add_fusion.s_ref, bf16[5,320,640]{2,1,0:T(8,128)(2,1)} %copy-done, bf16[5,320,640]{2,1,0:T(8,128)(2,1)} %copy-done.7, bf16[5,320,640]{2,1,0:T(8,128)(2,1)} %copy-done, bf16[320,640]{1,0:T(8,128)(2,1)S(1)} %collective-permute-done.1.refs_1_, ...), custom_call_target="tpu_custom_call" | custom-call | flops 39321600 | bytes 120320 | tf_op jit(solution)/shard_map/sum_pairs/pallas_call | solution.py:78
  63.2 1.6 %collective-permute-start.16 = (s16[960,256]{1,0:T(8,128)(2,1)S(1)}, s16[960,256]{1,0:T(8,128)(2,1)S(1)}, u32[]{:S(2)}, u32[]{:S(2)}) collective-permute-start(s16[960,256]{1,0:T(8,128)(2,1)S(1)} %get-tuple-element.45), channel_id=1, source_target_pairs={{0,2},{1,3},{2,0},{3,1},{4,6},{5,7},{6,4},{7,5},{8,10},{9,11},{10,... | collective-permute-start | bytes 1474568 | tf_op jit(solution)/shard_map/ppermute | solution.py:225
  64.8 10.2 %collective-permute-done.3.refs_0_ = bf16[320,640]{1,0:T(8,128)(2,1)S(1)} collective-permute-done((bf16[320,640]{1,0:T(8,128)(2,1)S(1)}, bf16[320,640]{1,0:T(8,128)(2,1)S(1)}, u32[]{:S(2)}, u32[]{:S(2)}) %collective-permute-start.3) | collective-permute-done | bytes 409632 | tf_op jit(solution)/shard_map/ppermute | solution.py:219
  75.0 5.8 %sum_pairs.6 = (s16[960,256]{1,0:T(8,128)(2,1)S(1)}, f32[960,256]{1,0:T(8,128)S(1)}) custom-call(s32[4]{0:T(128)S(1)} %pad_add_fusion.s_ref, bf16[5,320,640]{2,1,0:T(8,128)(2,1)} %copy-done, bf16[5,320,640]{2,1,0:T(8,128)(2,1)} %copy-done.7, bf16[5,320,640]{2,1,0:T(8,128)(2,1)} %copy-done, bf16[320,640]{1,0:T(8,128)(2,1)S(1)} %collective-permute-done.1.refs_1_, ...), custom_call_target="tpu_custom_call" | custom-call | flops 39321600 | bytes 120320 | tf_op jit(solution)/shard_map/sum_pairs/pallas_call | solution.py:78
  80.9 1.6 %collective-permute-start.15 = (s16[960,256]{1,0:T(8,128)(2,1)S(1)}, s16[960,256]{1,0:T(8,128)(2,1)S(1)}, u32[]{:S(2)}, u32[]{:S(2)}) collective-permute-start(s16[960,256]{1,0:T(8,128)(2,1)S(1)} %get-tuple-element.43), channel_id=1, source_target_pairs={{0,2},{1,3},{2,0},{3,1},{4,6},{5,7},{6,4},{7,5},{8,10},{9,11},{10,... | collective-permute-start | bytes 1474568 | tf_op jit(solution)/shard_map/ppermute | solution.py:225
  82.5 0.8 add_other_y.3
  83.3 1.6 %collective-permute-start.17 = (s16[960,256]{1,0:T(8,128)(2,1)S(1)}, s16[960,256]{1,0:T(8,128)(2,1)S(1)}, u32[]{:S(2)}, u32[]{:S(2)}) collective-permute-start(s16[960,256]{1,0:T(8,128)(2,1)S(1)} %add_other_y.3), channel_id=1, source_target_pairs={{0,16},{16,0},{1,17},{17,1},{2,18},{18,2},{3,19},{19,3},{4,20},{20... | collective-permute-start | bytes 1474568 | tf_op jit(solution)/shard_map/ppermute | solution.py:219
  84.9 3.2 %sum_pairs.5 = (s16[320,256]{1,0:T(8,128)(2,1)S(1)}, f32[320,256]{1,0:T(8,128)S(1)}) custom-call(s32[4]{0:T(128)S(1)} %pad_add_fusion.s_ref, bf16[5,320,640]{2,1,0:T(8,128)(2,1)S(1)} %copy-done.1, bf16[5,320,640]{2,1,0:T(8,128)(2,1)} %copy-done.7, bf16[320,640]{1,0:T(8,128)(2,1)S(1)} %collective-permute-done.3.refs_0_, ...), custom_call_target="tpu_custom_call" | custom-call | flops 13107200 | bytes 53760 | tf_op jit(solution)/shard_map/sum_pairs/pallas_call | solution.py:78
  88.1 0.6 collective-permute-start.10
  88.7 3.2 %sum_pairs.4 = (s16[320,256]{1,0:T(8,128)(2,1)S(1)}, f32[320,256]{1,0:T(8,128)S(1)}) custom-call(s32[4]{0:T(128)S(1)} %pad_add_fusion.s_ref, bf16[5,320,640]{2,1,0:T(8,128)(2,1)S(1)} %copy-done.1, bf16[5,320,640]{2,1,0:T(8,128)(2,1)} %copy-done.7, bf16[320,640]{1,0:T(8,128)(2,1)S(1)} %collective-permute-done.3.refs_0_, ...), custom_call_target="tpu_custom_call" | custom-call | flops 13107200 | bytes 53760 | tf_op jit(solution)/shard_map/sum_pairs/pallas_call | solution.py:78
  91.9 1.6 %collective-permute-start.6 = (s16[320,256]{1,0:T(8,128)(2,1)S(1)}, s16[320,256]{1,0:T(8,128)(2,1)S(1)}, u32[]{:S(2)}, u32[]{:S(2)}) collective-permute-start(s16[320,256]{1,0:T(8,128)(2,1)S(1)} %get-tuple-element.38), channel_id=1, source_target_pairs={{0,2},{1,3},{2,0},{3,1},{4,6},{5,7},{6,4},{7,5},{8,10},{9,11},{10,... | collective-permute-start | bytes 491528 | tf_op jit(solution)/shard_map/ppermute | solution.py:225
  93.5 5.0 %collective-permute-done.10.coded_ref = s16[320,256]{1,0:T(8,128)(2,1)S(1)} collective-permute-done((s16[320,256]{1,0:T(8,128)(2,1)S(1)}, s16[320,256]{1,0:T(8,128)(2,1)S(1)}, u32[]{:S(2)}, u32[]{:S(2)}) %collective-permute-start.10) | collective-permute-done | bytes 163872 | tf_op jit(solution)/shard_map/ppermute | solution.py:225
  98.5 0.6 add_other_y.2
  99.1 1.6 %collective-permute-start.11 = (s16[320,256]{1,0:T(8,128)(2,1)S(1)}, s16[320,256]{1,0:T(8,128)(2,1)S(1)}, u32[]{:S(2)}, u32[]{:S(2)}) collective-permute-start(s16[320,256]{1,0:T(8,128)(2,1)S(1)} %add_other_y.2), channel_id=1, source_target_pairs={{0,16},{16,0},{1,17},{17,1},{2,18},{18,2},{3,19},{19,3},{4,20},{20... | collective-permute-start | bytes 491528 | tf_op jit(solution)/shard_map/ppermute | solution.py:219
  100.7 0.8 add_other_x.3
  101.6 0.8 collective-permute-start.18
  102.4 3.1 %collective-permute-start.19 = (bf16[320,256]{1,0:T(8,128)(2,1)S(1)}, bf16[320,256]{1,0:T(8,128)(2,1)S(1)}, u32[]{:S(2)}, u32[]{:S(2)}) collective-permute-start(bf16[320,256]{1,0:T(8,128)(2,1)S(1)} %get-tuple-element.48.refs_3_), channel_id=1, source_target_pairs={{0,12},{4,0},{8,4},{12,8},{1,13},{5,1},{9,5},{13,9},{2,14},{6,2},{... | collective-permute-start | bytes 491528 | tf_op jit(solution)/shard_map/ppermute | solution.py:219
  105.4 0.6 add_other_x.2.refs_0_
  106.1 0.4 collective-permute-start.12
  106.5 4.1 %collective-permute-done.18.refs_2_ = bf16[320,256]{1,0:T(8,128)(2,1)S(1)} collective-permute-done((bf16[320,256]{1,0:T(8,128)(2,1)S(1)}, bf16[320,256]{1,0:T(8,128)(2,1)S(1)}, u32[]{:S(2)}, u32[]{:S(2)}) %collective-permute-start.18) | collective-permute-done | bytes 163872 | tf_op jit(solution)/shard_map/ppermute | solution.py:219
  110.6 0.1 collective-permute-done.19.refs_4_
  110.7 4.8 %place_pairs.2.refs_2_ = bf16[2500,256]{1,0:T(8,128)(2,1)S(1)} custom-call(s32[4]{0:T(128)S(1)} %pad_add_fusion.s_ref, bf16[320,256]{1,0:T(8,128)(2,1)S(1)} %get-tuple-element.46.refs_0_, bf16[320,256]{1,0:T(8,128)(2,1)S(1)} %get-tuple-element.47.refs_1_, bf16[320,256]{1,0:T(8,128)(2,1)S(1)} %collective-permute-done.18.refs_2_, ...), custom_call_target="tpu_custom_call" | custom-call | flops 32000000 | bytes 52800 | tf_op jit(solution)/shard_map/place_pairs/pallas_call | solution.py:78
  115.5 3.6 %collective-permute-done.12.refs_1_ = bf16[320,256]{1,0:T(8,128)(2,1)S(1)} collective-permute-done((bf16[320,256]{1,0:T(8,128)(2,1)S(1)}, bf16[320,256]{1,0:T(8,128)(2,1)S(1)}, u32[]{:S(2)}, u32[]{:S(2)}) %collective-permute-start.12) | collective-permute-done | bytes 163872 | tf_op jit(solution)/shard_map/ppermute | solution.py:219
  119.1 3.9 %place_pairs.3 = bf16[2500,256]{1,0:T(8,128)(2,1)} custom-call(s32[4]{0:T(128)S(1)} %pad_add_fusion.s_ref, bf16[320,256]{1,0:T(8,128)(2,1)S(1)} %add_other_x.2.refs_0_, bf16[320,256]{1,0:T(8,128)(2,1)S(1)} %collective-permute-done.12.refs_1_, bf16[2500,256]{1,0:T(8,128)(2,1)S(1)} %place_pairs.2.refs_2_), custom_call_target="tpu_custom_call" | custom-call | flops 19200000 | bytes 47680 | tf_op jit(solution)/shard_map/place_pairs/pallas_call | solution.py:78
  (23 shorter events, 0.1 us)
Async XLA Ops:
  0.1 1.7 %copy-start.2 = (bf16[1024,1280]{1,0:T(8,128)(2,1)S(1)}, bf16[1024,1280]{1,0:T(8,128)(2,1)}, u32[]{:S(2)}) copy-start(bf16[1024,1280]{1,0:T(8,128)(2,1)} %v_ref.2) | copy-start | bytes 7864324
  1.8 0.7 copy-start.4
  2.5 0.7 copy-start.6
  13.1 33.1 %copy-start.3 = (bf16[1024,1280]{1,0:T(8,128)(2,1)S(1)}, bf16[1024,1280]{1,0:T(8,128)(2,1)}, u32[]{:S(2)}) copy-start(bf16[1024,1280]{1,0:T(8,128)(2,1)} %v_ref.2) | copy-start | bytes 7864324
  13.1 33.1 %copy-start.5 = (s32[1280]{0:T(1024)S(1)}, s32[1280]{0:T(1024)}, u32[]{:S(2)}) copy-start(s32[1280]{0:T(1024)} %param.7) | copy-start | bytes 15364
  20.8 35.3 %copy-start = (bf16[5,320,640]{2,1,0:T(8,128)(2,1)}, bf16[5,320,640]{2,1,0:T(8,128)(2,1)S(1)}, u32[]{:S(2)}) copy-start(bf16[5,320,640]{2,1,0:T(8,128)(2,1)S(1)} %keep_columns.1.own_here.refs_0_) | copy-start | bytes 6144004
  20.8 35.3 %collective-permute-start = (bf16[5,320,640]{2,1,0:T(8,128)(2,1)S(1)}, bf16[5,320,640]{2,1,0:T(8,128)(2,1)S(1)}, u32[]{:S(2)}, u32[]{:S(2)}) collective-permute-start(bf16[5,320,640]{2,1,0:T(8,128)(2,1)S(1)} %keep_columns.1.own_here.refs_0_), channel_id=1, source_target_pairs={{0,1},{1,0},{2,3},{3,2},{4,5},{5,4},{6,7},{7,6},{8,9},{9,8},{10,11... | collective-permute-start | bytes 6144008 | tf_op jit(solution)/shard_map/ppermute | solution.py:222
  21.3 18.1 %collective-permute-start.8 = (bf16[2,256,640]{2,1,0:T(8,128)(2,1)S(1)}, bf16[2,256,640]{2,1,0:T(8,128)(2,1)S(1)}, u32[]{:S(2)}, u32[]{:S(2)}) collective-permute-start(bf16[2,256,640]{2,1,0:T(8,128)(2,1)S(1)} %get-tuple-element.27), channel_id=1, source_target_pairs={{0,16},{16,0},{1,17},{17,1},{2,18},{18,2},{3,19},{19,3},{4,20},{20... | collective-permute-start | bytes 1966088 | tf_op jit(solution)/shard_map/ppermute | solution.py:219
  23.9 15.6 %collective-permute-start.1 = (bf16[320,640]{1,0:T(8,128)(2,1)S(1)}, bf16[320,640]{1,0:T(8,128)(2,1)S(1)}, u32[]{:S(2)}, u32[]{:S(2)}) collective-permute-start(bf16[320,640]{1,0:T(8,128)(2,1)S(1)} %get-tuple-element.31), channel_id=1, source_target_pairs={{0,12},{4,0},{8,4},{12,8},{1,13},{5,1},{9,5},{13,9},{2,14},{6,2},{... | collective-permute-start | bytes 1228808 | tf_op jit(solution)/shard_map/ppermute | solution.py:219
  27.5 25.8 %collective-permute-start.7 = (bf16[2,256,640]{2,1,0:T(8,128)(2,1)S(1)}, bf16[2,256,640]{2,1,0:T(8,128)(2,1)S(1)}, u32[]{:S(2)}, u32[]{:S(2)}) collective-permute-start(bf16[2,256,640]{2,1,0:T(8,128)(2,1)S(1)} %get-tuple-element.39), channel_id=1, source_target_pairs={{0,16},{16,0},{1,17},{17,1},{2,18},{18,2},{3,19},{19,3},{4,20},{20... | collective-permute-start | bytes 1966088 | tf_op jit(solution)/shard_map/ppermute | solution.py:219
  28.0 18.2 %collective-permute-start.2 = (bf16[320,640]{1,0:T(8,128)(2,1)S(1)}, bf16[320,640]{1,0:T(8,128)(2,1)S(1)}, u32[]{:S(2)}, u32[]{:S(2)}) collective-permute-start(bf16[320,640]{1,0:T(8,128)(2,1)S(1)} %get-tuple-element.32), channel_id=1, source_target_pairs={{0,4},{4,8},{8,12},{12,0},{1,5},{5,9},{9,13},{13,1},{2,6},{6,10},{... | collective-permute-start | bytes 1228808 | tf_op jit(solution)/shard_map/ppermute | solution.py:219
  39.4 16.7 %collective-permute-start.9 = (bf16[2,256,640]{2,1,0:T(8,128)(2,1)S(1)}, bf16[2,256,640]{2,1,0:T(8,128)(2,1)S(1)}, u32[]{:S(2)}, u32[]{:S(2)}) collective-permute-start(bf16[2,256,640]{2,1,0:T(8,128)(2,1)S(1)} %collective-permute-done.8), channel_id=1, source_target_pairs={{0,1},{1,0},{2,3},{3,2},{4,5},{5,4},{6,7},{7,6},{8,9},{9,8},{10,11... | collective-permute-start | bytes 1966088 | tf_op jit(solution)/shard_map/ppermute | solution.py:222
  39.4 13.8 %collective-permute-start.13 = (bf16[320,640]{1,0:T(8,128)(2,1)S(1)}, bf16[320,640]{1,0:T(8,128)(2,1)S(1)}, u32[]{:S(2)}, u32[]{:S(2)}) collective-permute-start(bf16[320,640]{1,0:T(8,128)(2,1)S(1)} %collective-permute-done.1.refs_1_), channel_id=1, source_target_pairs={{0,1},{1,0},{2,3},{3,2},{4,5},{5,4},{6,7},{7,6},{8,9},{9,8},{10,11... | collective-permute-start | bytes 1228808 | tf_op jit(solution)/shard_map/ppermute | solution.py:222
  46.2 9.9 %collective-permute-start.14 = (bf16[320,640]{1,0:T(8,128)(2,1)S(1)}, bf16[320,640]{1,0:T(8,128)(2,1)S(1)}, u32[]{:S(2)}, u32[]{:S(2)}) collective-permute-start(bf16[320,640]{1,0:T(8,128)(2,1)S(1)} %collective-permute-done.2.refs_2_), channel_id=1, source_target_pairs={{0,1},{1,0},{2,3},{3,2},{4,5},{5,4},{6,7},{7,6},{8,9},{9,8},{10,11... | collective-permute-start | bytes 1228808 | tf_op jit(solution)/shard_map/ppermute | solution.py:222
  53.2 21.8 %collective-permute-start.5 = (bf16[2,256,640]{2,1,0:T(8,128)(2,1)S(1)}, bf16[2,256,640]{2,1,0:T(8,128)(2,1)S(1)}, u32[]{:S(2)}, u32[]{:S(2)}) collective-permute-start(bf16[2,256,640]{2,1,0:T(8,128)(2,1)S(1)} %get-tuple-element.36), channel_id=1, source_target_pairs={{0,1},{1,0},{2,3},{3,2},{4,5},{5,4},{6,7},{7,6},{8,9},{9,8},{10,11... | collective-permute-start | bytes 1966088 | tf_op jit(solution)/shard_map/ppermute | solution.py:222
  53.2 21.8 %collective-permute-start.3 = (bf16[320,640]{1,0:T(8,128)(2,1)S(1)}, bf16[320,640]{1,0:T(8,128)(2,1)S(1)}, u32[]{:S(2)}, u32[]{:S(2)}) collective-permute-start(bf16[320,640]{1,0:T(8,128)(2,1)S(1)} %get-tuple-element.33), channel_id=1, source_target_pairs={{0,8},{4,12},{8,0},{12,4},{1,9},{5,13},{9,1},{13,5},{2,10},{6,14},... | collective-permute-start | bytes 1228808 | tf_op jit(solution)/shard_map/ppermute | solution.py:219
  56.1 1.3 %copy-start.7 = (bf16[5,320,640]{2,1,0:T(8,128)(2,1)}, bf16[5,320,640]{2,1,0:T(8,128)(2,1)S(1)}, u32[]{:S(2)}) copy-start(bf16[5,320,640]{2,1,0:T(8,128)(2,1)S(1)} %collective-permute-done.own_there.refs_3_) | copy-start | bytes 6144004
  63.2 19.3 %collective-permute-start.16 = (s16[960,256]{1,0:T(8,128)(2,1)S(1)}, s16[960,256]{1,0:T(8,128)(2,1)S(1)}, u32[]{:S(2)}, u32[]{:S(2)}) collective-permute-start(s16[960,256]{1,0:T(8,128)(2,1)S(1)} %get-tuple-element.45), channel_id=1, source_target_pairs={{0,2},{1,3},{2,0},{3,1},{4,6},{5,7},{6,4},{7,5},{8,10},{9,11},{10,... | collective-permute-start | bytes 1474568 | tf_op jit(solution)/shard_map/ppermute | solution.py:225
  75.0 9.9 %collective-permute-start.4 = (bf16[320,640]{1,0:T(8,128)(2,1)S(1)}, bf16[320,640]{1,0:T(8,128)(2,1)S(1)}, u32[]{:S(2)}, u32[]{:S(2)}) collective-permute-start(bf16[320,640]{1,0:T(8,128)(2,1)S(1)} %collective-permute-done.3.refs_0_), channel_id=1, source_target_pairs={{0,1},{1,0},{2,3},{3,2},{4,5},{5,4},{6,7},{7,6},{8,9},{9,8},{10,11... | collective-permute-start | bytes 1228808 | tf_op jit(solution)/shard_map/ppermute | solution.py:222
  75.0 9.9 %copy-start.1 = (bf16[5,320,640]{2,1,0:T(8,128)(2,1)S(1)}, bf16[5,320,640]{2,1,0:T(8,128)(2,1)}, u32[]{:S(2)}) copy-start(bf16[5,320,640]{2,1,0:T(8,128)(2,1)} %copy-done) | copy-start | bytes 6144004
  80.9 19.9 %collective-permute-start.15 = (s16[960,256]{1,0:T(8,128)(2,1)S(1)}, s16[960,256]{1,0:T(8,128)(2,1)S(1)}, u32[]{:S(2)}, u32[]{:S(2)}) collective-permute-start(s16[960,256]{1,0:T(8,128)(2,1)S(1)} %get-tuple-element.43), channel_id=1, source_target_pairs={{0,2},{1,3},{2,0},{3,1},{4,6},{5,7},{6,4},{7,5},{8,10},{9,11},{10,... | collective-permute-start | bytes 1474568 | tf_op jit(solution)/shard_map/ppermute | solution.py:225
  83.3 17.4 %collective-permute-start.17 = (s16[960,256]{1,0:T(8,128)(2,1)S(1)}, s16[960,256]{1,0:T(8,128)(2,1)S(1)}, u32[]{:S(2)}, u32[]{:S(2)}) collective-permute-start(s16[960,256]{1,0:T(8,128)(2,1)S(1)} %add_other_y.3), channel_id=1, source_target_pairs={{0,16},{16,0},{1,17},{17,1},{2,18},{18,2},{3,19},{19,3},{4,20},{20... | collective-permute-start | bytes 1474568 | tf_op jit(solution)/shard_map/ppermute | solution.py:219
  88.1 10.3 %collective-permute-start.10 = (s16[320,256]{1,0:T(8,128)(2,1)S(1)}, s16[320,256]{1,0:T(8,128)(2,1)S(1)}, u32[]{:S(2)}, u32[]{:S(2)}) collective-permute-start(s16[320,256]{1,0:T(8,128)(2,1)S(1)} %get-tuple-element.41), channel_id=1, source_target_pairs={{0,2},{1,3},{2,0},{3,1},{4,6},{5,7},{6,4},{7,5},{8,10},{9,11},{10,... | collective-permute-start | bytes 491528 | tf_op jit(solution)/shard_map/ppermute | solution.py:225
  91.9 13.5 %collective-permute-start.6 = (s16[320,256]{1,0:T(8,128)(2,1)S(1)}, s16[320,256]{1,0:T(8,128)(2,1)S(1)}, u32[]{:S(2)}, u32[]{:S(2)}) collective-permute-start(s16[320,256]{1,0:T(8,128)(2,1)S(1)} %get-tuple-element.38), channel_id=1, source_target_pairs={{0,2},{1,3},{2,0},{3,1},{4,6},{5,7},{6,4},{7,5},{8,10},{9,11},{10,... | collective-permute-start | bytes 491528 | tf_op jit(solution)/shard_map/ppermute | solution.py:225
  99.1 6.3 %collective-permute-start.11 = (s16[320,256]{1,0:T(8,128)(2,1)S(1)}, s16[320,256]{1,0:T(8,128)(2,1)S(1)}, u32[]{:S(2)}, u32[]{:S(2)}) collective-permute-start(s16[320,256]{1,0:T(8,128)(2,1)S(1)} %add_other_y.2), channel_id=1, source_target_pairs={{0,16},{16,0},{1,17},{17,1},{2,18},{18,2},{3,19},{19,3},{4,20},{20... | collective-permute-start | bytes 491528 | tf_op jit(solution)/shard_map/ppermute | solution.py:219
  101.6 9.0 %collective-permute-start.18 = (bf16[320,256]{1,0:T(8,128)(2,1)S(1)}, bf16[320,256]{1,0:T(8,128)(2,1)S(1)}, u32[]{:S(2)}, u32[]{:S(2)}) collective-permute-start(bf16[320,256]{1,0:T(8,128)(2,1)S(1)} %get-tuple-element.47.refs_1_), channel_id=1, source_target_pairs={{0,4},{4,8},{8,12},{12,0},{1,5},{5,9},{9,13},{13,1},{2,6},{6,10},{... | collective-permute-start | bytes 491528 | tf_op jit(solution)/shard_map/ppermute | solution.py:219
  102.4 8.3 %collective-permute-start.19 = (bf16[320,256]{1,0:T(8,128)(2,1)S(1)}, bf16[320,256]{1,0:T(8,128)(2,1)S(1)}, u32[]{:S(2)}, u32[]{:S(2)}) collective-permute-start(bf16[320,256]{1,0:T(8,128)(2,1)S(1)} %get-tuple-element.48.refs_3_), channel_id=1, source_target_pairs={{0,12},{4,0},{8,4},{12,8},{1,13},{5,1},{9,5},{13,9},{2,14},{6,2},{... | collective-permute-start | bytes 491528 | tf_op jit(solution)/shard_map/ppermute | solution.py:219
  106.1 13.0 %collective-permute-start.12 = (bf16[320,256]{1,0:T(8,128)(2,1)S(1)}, bf16[320,256]{1,0:T(8,128)(2,1)S(1)}, u32[]{:S(2)}, u32[]{:S(2)}) collective-permute-start(bf16[320,256]{1,0:T(8,128)(2,1)S(1)} %add_other_x.2.refs_0_), channel_id=1, source_target_pairs={{0,8},{4,12},{8,0},{12,4},{1,9},{5,13},{9,1},{13,5},{2,10},{6,14},... | collective-permute-start | bytes 491528 | tf_op jit(solution)/shard_map/ppermute | solution.py:219

commit v4 on v3

--- a/solution.py
+++ b/solution.py
@@ -14,7 +14,7 @@
 CORES = 2
 TILE = 512
 LANES = 128
-LIGHT = 64
+VMEM_BYTES = 32 * 2**20
 
 
 def dot_nt(a, b):
@@ -65,31 +65,37 @@
     return jnp.where(last, 0.0, values * jnp.exp2(code * (-1.0 / STEPS)))
 
 
-def call(name, body, scalars, inputs, outputs, flops, moved, grid=1, scratch=()):
-    in_specs, arrays, out_specs, shapes = [], [], [], []
-    for entry in inputs:
-        array, block, index = entry if isinstance(entry, tuple) else (entry, None, None)
-        arrays.append(array)
-        in_specs.append(pl.BlockSpec(block or array.shape, index or (lambda g, s, rank=array.ndim: (0,) * rank)))
-    for shape, dtype, *spec in outputs:
-        shapes.append(jax.ShapeDtypeStruct(shape, dtype))
-        block, index = spec or (shape, lambda g, s, rank=len(shape): (0,) * rank)
-        out_specs.append(pl.BlockSpec(block, index))
+def call(name, body, scalars, inputs, outputs, grid=None):
+    arrays = [entry[0] if isinstance(entry, tuple) else entry for entry in inputs]
+    shapes = [jax.ShapeDtypeStruct(entry[0], entry[1]) for entry in outputs]
+    if grid is None:
+        in_specs = [pl.BlockSpec(memory_space=pltpu.SMEM)] + [pl.BlockSpec(memory_space=pltpu.VMEM)] * len(arrays)
+        specs = dict(in_specs=in_specs, out_specs=[pl.BlockSpec(memory_space=pltpu.VMEM)] * len(shapes))
+    else:
+        in_specs, out_specs = [], []
+        for entry, array in zip(inputs, arrays):
+            block, index = entry[1:] if isinstance(entry, tuple) else (array.shape, lambda g, s, rank=array.ndim: (0,) * rank)
+            in_specs.append(pl.BlockSpec(block, index))
+        for entry in outputs:
+            out_specs.append(pl.BlockSpec(*entry[2:]))
+        specs = dict(
+            grid_spec=pltpu.PrefetchScalarGridSpec(
+                num_scalar_prefetch=1, grid=(grid,), in_specs=in_specs, out_specs=out_specs
+            )
+        )
     return pl.pallas_call(
         body,
         name=name,
         out_shape=shapes,
-        grid_spec=pltpu.PrefetchScalarGridSpec(
-            num_scalar_prefetch=1, grid=(grid,), in_specs=in_specs, out_specs=out_specs, scratch_shapes=list(scratch)
-        ),
-        compiler_params=pltpu.CompilerParams(vmem_limit_bytes=48 * 2**20),
-        cost_estimate=pl.CostEstimate(flops=int(flops) // LIGHT, bytes_accessed=int(moved) // LIGHT, transcendentals=0),
+        compiler_params=pltpu.CompilerParams(vmem_limit_bytes=VMEM_BYTES),
+        cost_estimate=pl.CostEstimate(flops=1, bytes_accessed=1, transcendentals=0),
+        **specs,
     )(scalars, *arrays)
 
 
-def mask_body(by, row_n, sub, tall, s_ref, ab_ref, cd_ref, v_ref, pass_ref, keep_ref):
+def mask_body(by, row_n, sub, tall, s_ref, ab_ref, cd_ref, v_ref, *out_refs):
     x, y, core = s_ref[0], s_ref[2], s_ref[3]
-    k_here, cd_here = pass_ref.shape[2], v_ref.shape[1]
+    k_here, cd_here = out_refs[0].shape[-1], v_ref.shape[1]
     q, m = divide(lax.broadcasted_iota(jnp.int32, (k_here, 1), 0), sub)
     wanted = q * (sub * row_n) + lax.rem(x - by + row_n, row_n) * sub + m
     pick = jnp.where(lax.broadcasted_iota(jnp.int32, (k_here, cd_here), 1) == wanted, 1.0, 0.0).astype(jnp.bfloat16)
@@ -109,8 +115,11 @@
                 v = v_ref[pl.ds(start, LANES), :].astype(jnp.float32)
                 blocks.append(jnp.where(ab == cd, v, 0.0).astype(jnp.bfloat16))
     picked = dot_nt(jnp.concatenate(blocks, axis=0), pick).astype(jnp.bfloat16)
-    pass_ref[...] = picked[: 2 * tall].reshape(pass_ref.shape)
-    keep_ref[...] = picked[2 * tall :].reshape(keep_ref.shape)
+    if len(out_refs) == 1:
+        out_refs[0][...] = picked.reshape(out_refs[0].shape)
+    else:
+        out_refs[0][...] = picked[: 2 * tall].reshape(out_refs[0].shape)
+        out_refs[1][...] = picked[2 * tall :].reshape(out_refs[1].shape)
 
 
 def one_hot_rows(columns, width):
@@ -119,7 +128,10 @@
 
 
 def send_body(order, n, col_n, s_ref, t_ref, flat_ref, *out_refs):
-    flat_ref[...] = t_ref[...].reshape(flat_ref.shape)
+    columns, wide = t_ref.shape[-1], flat_ref.shape[1]
+    last = wide - LANES
+    flat_ref[:, last:] = jnp.zeros((flat_ref.shape[0], LANES), flat_ref.dtype)
+    flat_ref[:, :columns] = t_ref[...].reshape(-1, columns)
     z = s_ref[1]
     place = lax.broadcasted_iota(jnp.int32, (out_refs[0].shape[0], 1), 0)
     chunk = out_refs[0].shape[0]
@@ -145,10 +157,11 @@
     chunk = own_here.shape[1]
 
     def rows(ref):
-        return ref[...].reshape(-1, k_here)
-
-    a, b = keep_ref[...].reshape(-1, k_here), pass_ref[...].reshape(-1, k_here)
-    half = a.shape[0] // 2
+        return ref[ref.shape[0] - 1] if len(ref.shape) == 3 else ref[...]
+
+    half = kept_ref.shape[1]
+    keep, passed = keep_ref[...].reshape(-1, k_here), pass_ref[...].reshape(-1, k_here)
+    a, b = keep[-2 * half :], passed[: 2 * half]
     to = own_here[first : first + count].reshape(count * chunk, k_here)
     too = own_there[first : first + count].reshape(count * chunk, k_here)
     tr = jnp.concatenate([rows(ref) for ref in away[:count]], axis=0)
@@ -227,71 +240,67 @@
     scalars = jnp.stack([x, z, y, core]).astype(jnp.int32)
     ab_row, cd_row = ab_irrep.reshape(-1, LANES), cd_irrep.reshape(-1, LANES)
 
-    def masked(v, by):
+    def masked(v, by, parts):
         return call(
             "mask_integrals",
             functools.partial(mask_body, by, row_n, sub, tall),
             scalars,
             [ab_row, cd_row, v],
-            [((2, tall, k_here), bf16)] * 2,
-            2 * rows * cd_here * k_here,
-            2 * rows * (cd_here + k_here),
+            [((4 // parts * tall, k_here), bf16)] * parts,
         )
 
     passed, kept = [None] * row_n, [None] * row_n
+    gone = scalars
     for by in range(1, row_n):
-        gone, stay = masked(integrals, by)
-        passed[by], kept[by] = shift(gone, "row", -by), shift(stay, "row", -by)
-
-    amplitudes, _ = lax.optimization_barrier((amplitudes, gone if row_n > 1 else scalars))
+        (gone,) = masked(integrals, by, 1)
+        kept[by] = shift(gone, "row", -by)
+
+    amplitudes, _ = lax.optimization_barrier((amplitudes, gone))
     sent_order = near + [far]
     flat, *sent = call(
         "send_columns",
         functools.partial(send_body, sent_order, n, col_n),
         scalars,
         [amplitudes],
-        [((k_here, columns), bf16)] + [((chunk, k_here), bf16)] * len(sent_order),
-        2 * len(sent_order) * chunk * columns * k_here,
-        2 * k_here * (2 * columns + len(sent_order) * chunk),
+        [((k_here, -(-columns // LANES) * LANES), bf16)] + [((chunk, k_here), bf16)] * len(sent_order),
     )
     away = {r: shift(s, "col", -r) for r, s in zip(near, sent)}
-    integrals, _ = lax.optimization_barrier((integrals, flat))
-    last = lax.optimization_barrier((sent[-1], *away.values()))
-    away[far] = shift(last[0], "col", -far)
-
-    passed[0], kept[0] = masked(integrals, 0)
+    integrals, flat = lax.optimization_barrier((integrals, flat))
+    passed[0], kept[0] = masked(integrals, 0, 2)
     (own,) = call(
         "keep_columns",
         functools.partial(keep_body, order, n, col_n),
         scalars,
         [flat],
         [((col_n + 1, chunk, k_here), bf16)],
-        2 * (col_n + 1) * chunk * columns * k_here,
-        2 * k_here * (columns + (col_n + 1) * chunk),
     )
-    passed = [other_core(a) for a in passed]
-    own_there = other_core(own)
+    arrived = lax.optimization_barrier((passed[0], own, sent[-1], kept[1:], away))
+    passed[0], behind, far_sent, kept[1:], away = arrived
+    away_there = {r: other_core(away[r]) for r in near}
+    passed = [other_core(passed[0])] + [other_core(a) for a in kept[1:]]
+    own_there = other_core(behind)
+    away[far] = shift(far_sent, "col", -far)
 
     done = None
     for group in groups:
         first, count = order.index(group[0]), len(group)
-        tail = (1, chunk, k_here), lambda g, s: (col_n, 0, 0)
-        here = [(own, *tail) if r == 0 else away[r] for r in group]
-        there = [(own_there, *tail) if r == 0 else other_core(away[r]) for r in group]
-        final = []
-        for by in range(row_n):
+        here = [own if r == 0 else away[r] for r in group]
+        there = [own_there if r == 0 else away_there[r] for r in group]
+        final = [None] * (row_n + 1)
+        for by in list(range(1, row_n)) + [0]:
             coded, total = call(
                 "sum_pairs",
                 functools.partial(sum_body, first, count),
                 scalars,
                 [own, own_there] + here + there + [kept[by], passed[by]],
                 [((count * chunk, tall), i16), ((count * chunk, tall), f32)],
-                2 * 2 * 2 * count * chunk * tall * CORES * k_here,
-                2 * CORES * k_here * (2 * count * chunk + 2 * tall) + 6 * count * chunk * tall,
             )
+            if by == 0 and group == groups[0]:
+                _, away[far] = lax.optimization_barrier((coded, away[far]))
+                away_there[far] = other_core(away[far])
             coded = other_y(coded)
             if by == 0:
-                final += [total, coded]
+                final[:2] = [total, coded]
             else:
                 (merged,) = call(
                     "add_other_y",
@@ -299,18 +308,14 @@
                     scalars,
                     [total, coded],
                     [((count * chunk, tall), i16)],
-                    20 * count * chunk * tall,
-                    8 * count * chunk * tall,
                 )
-                final.append(shift(merged, "row", by))
+                final[by + 1] = shift(merged, "row", by)
         rounded = call(
             "add_other_x",
             functools.partial(add_x_body, count),
             scalars,
             final,
             [((chunk, tall), bf16)] * count,
-            20 * count * chunk * tall,
-            8 * count * chunk * tall,
         )
         sources = []
         for r, mine in zip(group, rounded):
@@ -323,8 +328,6 @@
             scalars,
             sources,
             [((columns, tall), bf16, *tile)],
-            2 * len(sources) * chunk * tall * columns,
-            2 * tall * (2 * columns + len(sources) * chunk),
             grid=-(-columns // TILE),
         )
     return done.T

time: 123 us -> 108 us (0.88)
  Pallas kernels: 50.1 us -> 40.4 us
  waiting for transfers between devices: 44.8 us -> 40.9 us
  local copies, waits for them, and re-layouts: 4.43 us -> 3.13 us
    ppermute x10 -> x9, waiting for transfers between devices: 39.9 us -> 27.2 us  [shift(): lax.ppermute(array, axis, [(i, (i + by) % count) for i in range(count)])]
    pallas_call x14, Pallas kernels: 50.1 us -> 40.4 us  [call(): pl.pallas_call(body, name=name, out_shape=shapes, compiler_params=pltpu.C...]
    ppermute x6, waiting for transfers between devices: 0.02 us -> 5.54 us  [other_core(): return lax.ppermute(array, 'depth', [(i, i ^ 1) for i in range(depth_n)])]
    ppermute x4, waiting for transfers between devices: 4.96 us -> 8.11 us  [other_y(): return lax.ppermute(array, 'depth', [(i, i ^ 2) for i in range(depth_n)])]
    unnamed x16 -> x12, local copies, waits for them, and re-layouts: 4.43 us -> 3.13 us
    ppermute x10 -> x9, starting transfers between devices: 17 us -> 16.9 us  [shift(): lax.ppermute(array, axis, [(i, (i + by) % count) for i in range(count)])]
  transfers between devices with their start and end apart: 20 -> 19, of which waited for: 8 -> 7; matrix products, arithmetic and copies ran while one was open for 0% -> 0% of each run, Pallas kernels for 23% -> 31%
where the time goes in v4:
time: 108 us
  waiting for transfers between devices  40.9 us (38%)
  Pallas kernels  40.4 us (37%)
  starting transfers between devices  23.2 us (21%)
  local copies, waits for them, and re-layouts  3.13 us (3%)
    pallas_call x14, Pallas kernels, call(): pl.pallas_call(body, name=name, out_shape=shapes, compiler_params=pltpu.C...  40.4 us
    ppermute x9, waiting for transfers between devices, shift(): lax.ppermute(array, axis, [(i, (i + by) % count) for i in range(count)])  27.2 us
    ppermute x9, starting transfers between devices, shift(): lax.ppermute(array, axis, [(i, (i + by) % count) for i in range(count)])  16.9 us
    ppermute x4, waiting for transfers between devices, other_y(): return lax.ppermute(array, 'depth', [(i, i ^ 2) for i in range(depth_n)])  8.11 us
    ppermute x6, waiting for transfers between devices, other_core(): return lax.ppermute(array, 'depth', [(i, i ^ 1) for i in range(depth_n)])  5.54 us
    ppermute x4, starting transfers between devices, other_y(): return lax.ppermute(array, 'depth', [(i, i ^ 2) for i in range(depth_n)])  5.32 us
    unnamed x12, local copies, waits for them, and re-layouts  3.13 us
  transfers between devices with their start and end apart: 19, of which 7 were waited for; matrix products, arithmetic and copies ran while one was open for 0% of the time, Pallas kernels for 31%

profile of v4, /device:TPU:0, one launch (start us, length us, event | category | flops | bytes accessed | tf_op | source)
XLA Modules:
  0.0 107.9 jit_solution(2468537078090158754)
XLA Ops:
  0.0 0.1 pad_add_fusion.s_ref
  0.1 1.7 %copy-done = bf16[1024,1280]{1,0:T(8,128)(2,1)S(1)} copy-done((bf16[1024,1280]{1,0:T(8,128)(2,1)S(1)}, bf16[1024,1280]{1,0:T(8,128)(2,1)}, u32[]{:S(2)}) %copy-start) | copy-done | bytes 2621464
  1.8 0.7 copy-done.3
  2.5 0.7 copy-done.5
  3.2 2.9 %mask_integrals.2 = bf16[1024,640]{1,0:T(8,128)(2,1)S(1)} custom-call(s32[4]{0:T(128)S(1)} %pad_add_fusion.s_ref, s32[8,128]{1,0:T(8,128)S(1)} %bitcast.9, s32[10,128]{1,0:T(8,128)S(1)} %bitcast.7, bf16[1024,1280]{1,0:T(8,128)(2,1)S(1)} %copy-done), custom_call_target="tpu_custom_call" | custom-call | flops 1 | bytes 1 | tf_op jit(solution)/shard_map/mask_integrals/pallas_call | solution.py:86
  6.1 3.0 %collective-permute-start = (bf16[1024,640]{1,0:T(8,128)(2,1)S(1)}, bf16[1024,640]{1,0:T(8,128)(2,1)S(1)}, u32[]{:S(2)}, u32[]{:S(2)}) collective-permute-start(bf16[1024,640]{1,0:T(8,128)(2,1)S(1)} %mask_integrals.2), channel_id=1, source_target_pairs={{0,16},{16,0},{1,17},{17,1},{2,18},{18,2},{3,19},{19,3},{4,20},{20... | collective-permute-start | bytes 3932168 | tf_op jit(solution)/shard_map/ppermute | solution.py:232
  9.1 5.1 %send_columns.1 = (bf16[640,2560]{1,0:T(8,128)(2,1)S(1)}, bf16[320,640]{1,0:T(8,128)(2,1)S(1)}, bf16[320,640]{1,0:T(8,128)(2,1)S(1)}, bf16[320,640]{1,0:T(8,128)(2,1)S(1)}) custom-call(s32[4]{0:T(128)S(1)} %pad_add_fusion.s_ref, bf16[320,2,2500]{2,1,0:T(2,128)(2,1)S(1)} %copy-done.2), custom_call_target="tpu_custom_call" | custom-call | flops 1 | bytes 1 | tf_op jit(solution)/shard_map/send_columns/pallas_call | solution.py:86
  14.2 3.7 %collective-permute-start.1 = (bf16[320,640]{1,0:T(8,128)(2,1)S(1)}, bf16[320,640]{1,0:T(8,128)(2,1)S(1)}, u32[]{:S(2)}, u32[]{:S(2)}) collective-permute-start(bf16[320,640]{1,0:T(8,128)(2,1)S(1)} %get-tuple-element.38), channel_id=1, source_target_pairs={{0,12},{4,0},{8,4},{12,8},{1,13},{5,1},{9,5},{13,9},{2,14},{6,2},{... | collective-permute-start | bytes 1228808 | tf_op jit(solution)/shard_map/ppermute | solution.py:232
  17.9 0.0 collective-permute-start.2
  17.9 7.6 %keep_columns.1.own_here.refs_0_ = bf16[5,320,640]{2,1,0:T(8,128)(2,1)S(1)} custom-call(s32[4]{0:T(128)S(1)} %pad_add_fusion.s_ref, bf16[640,2560]{1,0:T(8,128)(2,1)S(1)} %get-tuple-element.34.flat_ref), custom_call_target="tpu_custom_call" | custom-call | flops 1 | bytes 1 | tf_op jit(solution)/shard_map/keep_columns/pallas_call | solution.py:86
  25.5 2.9 %mask_integrals.3 = (bf16[512,640]{1,0:T(8,128)(2,1)S(1)}, bf16[512,640]{1,0:T(8,128)(2,1)S(1)}) custom-call(s32[4]{0:T(128)S(1)} %pad_add_fusion.s_ref, s32[8,128]{1,0:T(8,128)S(1)} %bitcast.10, s32[10,128]{1,0:T(8,128)S(1)} %bitcast.8, bf16[1024,1280]{1,0:T(8,128)(2,1)S(1)} %copy-done.1), custom_call_target="tpu_custom_call" | custom-call | flops 1 | bytes 1 | tf_op jit(solution)/shard_map/mask_integrals/pallas_call | solution.py:86
  28.4 7.6 %collective-permute-done.2.refs_2_ = bf16[320,640]{1,0:T(8,128)(2,1)S(1)} collective-permute-done((bf16[320,640]{1,0:T(8,128)(2,1)S(1)}, bf16[320,640]{1,0:T(8,128)(2,1)S(1)}, u32[]{:S(2)}, u32[]{:S(2)}) %collective-permute-start.2) | collective-permute-done | bytes 409632 | tf_op jit(solution)/shard_map/ppermute | solution.py:232
  36.0 1.8 %collective-permute-done.refs_2_.refs_6_ = bf16[1024,640]{1,0:T(8,128)(2,1)S(1)} collective-permute-done((bf16[1024,640]{1,0:T(8,128)(2,1)S(1)}, bf16[1024,640]{1,0:T(8,128)(2,1)S(1)}, u32[]{:S(2)}, u32[]{:S(2)}) %collective-permute-start) | collective-permute-done | bytes 1310752 | tf_op jit(solution)/shard_map/ppermute | solution.py:232
  37.9 0.0 collective-permute-start.3
  37.9 0.5 collective-permute-start.10
  38.4 0.0 collective-permute-start.4
  38.4 0.5 collective-permute-start.5
  38.9 0.0 collective-permute-start.6
  38.9 5.5 %collective-permute-done.4.refs_4_ = bf16[320,640]{1,0:T(8,128)(2,1)S(1)} collective-permute-done((bf16[320,640]{1,0:T(8,128)(2,1)S(1)}, bf16[320,640]{1,0:T(8,128)(2,1)S(1)}, u32[]{:S(2)}, u32[]{:S(2)}) %collective-permute-start.4) | collective-permute-done | bytes 409632 | tf_op jit(solution)/shard_map/ppermute | solution.py:235
  44.4 2.8 %collective-permute-start.7 = (bf16[320,640]{1,0:T(8,128)(2,1)S(1)}, bf16[320,640]{1,0:T(8,128)(2,1)S(1)}, u32[]{:S(2)}, u32[]{:S(2)}) collective-permute-start(bf16[320,640]{1,0:T(8,128)(2,1)S(1)} %get-tuple-element.46), channel_id=1, source_target_pairs={{0,8},{4,12},{8,0},{12,4},{1,9},{5,13},{9,1},{13,5},{2,10},{6,14},... | collective-permute-start | bytes 1228808 | tf_op jit(solution)/shard_map/ppermute | solution.py:232
  47.3 3.4 %sum_pairs.7 = (s16[960,256]{1,0:T(8,128)(2,1)S(1)}, f32[960,256]{1,0:T(8,128)S(1)}) custom-call(s32[4]{0:T(128)S(1)} %pad_add_fusion.s_ref, bf16[5,320,640]{2,1,0:T(8,128)(2,1)S(1)} %keep_columns.1.own_here.refs_0_, bf16[5,320,640]{2,1,0:T(8,128)(2,1)S(1)} %collective-permute-done.3.own_there.refs_3_, ...), custom_call_target="tpu_custom_call" | custom-call | flops 1 | bytes 1 | tf_op jit(solution)/shard_map/sum_pairs/pallas_call | solution.py:86
  50.7 1.6 %collective-permute-start.15 = (s16[960,256]{1,0:T(8,128)(2,1)S(1)}, s16[960,256]{1,0:T(8,128)(2,1)S(1)}, u32[]{:S(2)}, u32[]{:S(2)}) collective-permute-start(s16[960,256]{1,0:T(8,128)(2,1)S(1)} %get-tuple-element.55), channel_id=1, source_target_pairs={{0,2},{1,3},{2,0},{3,1},{4,6},{5,7},{6,4},{7,5},{8,10},{9,11},{10,... | collective-permute-start | bytes 1474568 | tf_op jit(solution)/shard_map/ppermute | solution.py:238
  52.3 0.0 collective-permute-done.6.refs_7_.refs_3_
  52.3 3.6 %sum_pairs.4 = (s16[960,256]{1,0:T(8,128)(2,1)S(1)}, f32[960,256]{1,0:T(8,128)S(1)}) custom-call(s32[4]{0:T(128)S(1)} %pad_add_fusion.s_ref, bf16[5,320,640]{2,1,0:T(8,128)(2,1)S(1)} %keep_columns.1.own_here.refs_0_, bf16[5,320,640]{2,1,0:T(8,128)(2,1)S(1)} %collective-permute-done.3.own_there.refs_3_, ...), custom_call_target="tpu_custom_call" | custom-call | flops 1 | bytes 1 | tf_op jit(solution)/shard_map/sum_pairs/pallas_call | solution.py:86
  55.9 9.9 %collective-permute-done.7.refs_0_ = bf16[320,640]{1,0:T(8,128)(2,1)S(1)} collective-permute-done((bf16[320,640]{1,0:T(8,128)(2,1)S(1)}, bf16[320,640]{1,0:T(8,128)(2,1)S(1)}, u32[]{:S(2)}, u32[]{:S(2)}) %collective-permute-start.7) | collective-permute-done | bytes 409632 | tf_op jit(solution)/shard_map/ppermute | solution.py:232
  65.8 0.0 collective-permute-start.8
  65.8 1.6 %collective-permute-start.14 = (s16[960,256]{1,0:T(8,128)(2,1)S(1)}, s16[960,256]{1,0:T(8,128)(2,1)S(1)}, u32[]{:S(2)}, u32[]{:S(2)}) collective-permute-start(s16[960,256]{1,0:T(8,128)(2,1)S(1)} %get-tuple-element.45), channel_id=1, source_target_pairs={{0,2},{1,3},{2,0},{3,1},{4,6},{5,7},{6,4},{7,5},{8,10},{9,11},{10,... | collective-permute-start | bytes 1474568 | tf_op jit(solution)/shard_map/ppermute | solution.py:238
  67.4 0.0 collective-permute-done.15.coded_ref
  67.4 0.8 add_other_y.3
  68.2 1.6 %collective-permute-start.16 = (s16[960,256]{1,0:T(8,128)(2,1)S(1)}, s16[960,256]{1,0:T(8,128)(2,1)S(1)}, u32[]{:S(2)}, u32[]{:S(2)}) collective-permute-start(s16[960,256]{1,0:T(8,128)(2,1)S(1)} %add_other_y.3), channel_id=1, source_target_pairs={{0,16},{16,0},{1,17},{17,1},{2,18},{18,2},{3,19},{19,3},{4,20},{20... | collective-permute-start | bytes 1474568 | tf_op jit(solution)/shard_map/ppermute | solution.py:232
  69.8 0.0 collective-permute-done.8.refs_1_
  69.8 1.6 %sum_pairs.6 = (s16[320,256]{1,0:T(8,128)(2,1)S(1)}, f32[320,256]{1,0:T(8,128)S(1)}) custom-call(s32[4]{0:T(128)S(1)} %pad_add_fusion.s_ref, bf16[5,320,640]{2,1,0:T(8,128)(2,1)S(1)} %keep_columns.1.own_here.refs_0_, bf16[5,320,640]{2,1,0:T(8,128)(2,1)S(1)} %collective-permute-done.3.own_there.refs_3_, bf16[320,640]{1,0:T(8,128)(2,1)S(1)} %collective-permute-done.7.refs_0_, ...), custom_call_target="tpu_custom_call" | custom-call | flops 1 | bytes 1 | tf_op jit(solution)/shard_map/sum_pairs/pallas_call | solution.py:86
  71.4 0.6 collective-permute-start.11
  72.0 1.6 %sum_pairs.5 = (s16[320,256]{1,0:T(8,128)(2,1)S(1)}, f32[320,256]{1,0:T(8,128)S(1)}) custom-call(s32[4]{0:T(128)S(1)} %pad_add_fusion.s_ref, bf16[5,320,640]{2,1,0:T(8,128)(2,1)S(1)} %keep_columns.1.own_here.refs_0_, bf16[5,320,640]{2,1,0:T(8,128)(2,1)S(1)} %collective-permute-done.3.own_there.refs_3_, bf16[320,640]{1,0:T(8,128)(2,1)S(1)} %collective-permute-done.7.refs_0_, ...), custom_call_target="tpu_custom_call" | custom-call | flops 1 | bytes 1 | tf_op jit(solution)/shard_map/sum_pairs/pallas_call | solution.py:86
  73.6 1.6 %collective-permute-start.9 = (s16[320,256]{1,0:T(8,128)(2,1)S(1)}, s16[320,256]{1,0:T(8,128)(2,1)S(1)}, u32[]{:S(2)}, u32[]{:S(2)}) collective-permute-start(s16[320,256]{1,0:T(8,128)(2,1)S(1)} %get-tuple-element.49), channel_id=1, source_target_pairs={{0,2},{1,3},{2,0},{3,1},{4,6},{5,7},{6,4},{7,5},{8,10},{9,11},{10,... | collective-permute-start | bytes 491528 | tf_op jit(solution)/shard_map/ppermute | solution.py:238
  75.2 8.1 %collective-permute-done.11.coded_ref = s16[320,256]{1,0:T(8,128)(2,1)S(1)} collective-permute-done((s16[320,256]{1,0:T(8,128)(2,1)S(1)}, s16[320,256]{1,0:T(8,128)(2,1)S(1)}, u32[]{:S(2)}, u32[]{:S(2)}) %collective-permute-start.11) | collective-permute-done | bytes 163872 | tf_op jit(solution)/shard_map/ppermute | solution.py:238
  83.3 0.6 add_other_y.2
  84.0 1.6 %collective-permute-start.12 = (s16[320,256]{1,0:T(8,128)(2,1)S(1)}, s16[320,256]{1,0:T(8,128)(2,1)S(1)}, u32[]{:S(2)}, u32[]{:S(2)}) collective-permute-start(s16[320,256]{1,0:T(8,128)(2,1)S(1)} %add_other_y.2), channel_id=1, source_target_pairs={{0,16},{16,0},{1,17},{17,1},{2,18},{18,2},{3,19},{19,3},{4,20},{20... | collective-permute-start | bytes 491528 | tf_op jit(solution)/shard_map/ppermute | solution.py:232
  85.6 0.8 add_other_x.3
  86.4 0.8 collective-permute-start.17
  87.2 3.1 %collective-permute-start.18 = (bf16[320,256]{1,0:T(8,128)(2,1)S(1)}, bf16[320,256]{1,0:T(8,128)(2,1)S(1)}, u32[]{:S(2)}, u32[]{:S(2)}) collective-permute-start(bf16[320,256]{1,0:T(8,128)(2,1)S(1)} %get-tuple-element.58.refs_3_), channel_id=1, source_target_pairs={{0,12},{4,0},{8,4},{12,8},{1,13},{5,1},{9,5},{13,9},{2,14},{6,2},{... | collective-permute-start | bytes 491528 | tf_op jit(solution)/shard_map/ppermute | solution.py:232
  90.3 0.6 add_other_x.2.refs_0_
  91.0 0.3 collective-permute-start.13
  91.3 4.2 %collective-permute-done.17.refs_2_ = bf16[320,256]{1,0:T(8,128)(2,1)S(1)} collective-permute-done((bf16[320,256]{1,0:T(8,128)(2,1)S(1)}, bf16[320,256]{1,0:T(8,128)(2,1)S(1)}, u32[]{:S(2)}, u32[]{:S(2)}) %collective-permute-start.17) | collective-permute-done | bytes 163872 | tf_op jit(solution)/shard_map/ppermute | solution.py:232
  95.5 0.0 collective-permute-done.18.refs_4_
  95.5 4.8 %place_pairs.2.refs_2_ = bf16[2500,256]{1,0:T(8,128)(2,1)S(1)} custom-call(s32[4]{0:T(128)S(1)} %pad_add_fusion.s_ref, bf16[320,256]{1,0:T(8,128)(2,1)S(1)} %get-tuple-element.56.refs_0_, bf16[320,256]{1,0:T(8,128)(2,1)S(1)} %get-tuple-element.57.refs_1_, bf16[320,256]{1,0:T(8,128)(2,1)S(1)} %collective-permute-done.17.refs_2_, ...), custom_call_target="tpu_custom_call" | custom-call | flops 1 | bytes 1 | tf_op jit(solution)/shard_map/place_pairs/pallas_call | solution.py:86
  100.3 3.6 %collective-permute-done.13.refs_1_ = bf16[320,256]{1,0:T(8,128)(2,1)S(1)} collective-permute-done((bf16[320,256]{1,0:T(8,128)(2,1)S(1)}, bf16[320,256]{1,0:T(8,128)(2,1)S(1)}, u32[]{:S(2)}, u32[]{:S(2)}) %collective-permute-start.13) | collective-permute-done | bytes 163872 | tf_op jit(solution)/shard_map/ppermute | solution.py:232
  104.0 3.9 %place_pairs.3 = bf16[2500,256]{1,0:T(8,128)(2,1)} custom-call(s32[4]{0:T(128)S(1)} %pad_add_fusion.s_ref, bf16[320,256]{1,0:T(8,128)(2,1)S(1)} %add_other_x.2.refs_0_, bf16[320,256]{1,0:T(8,128)(2,1)S(1)} %collective-permute-done.13.refs_1_, bf16[2500,256]{1,0:T(8,128)(2,1)S(1)} %place_pairs.2.refs_2_), custom_call_target="tpu_custom_call" | custom-call | flops 1 | bytes 1 | tf_op jit(solution)/shard_map/place_pairs/pallas_call | solution.py:86
  (17 shorter events, 0.0 us)
Async XLA Ops:
  0.1 1.7 %copy-start = (bf16[1024,1280]{1,0:T(8,128)(2,1)S(1)}, bf16[1024,1280]{1,0:T(8,128)(2,1)}, u32[]{:S(2)}) copy-start(bf16[1024,1280]{1,0:T(8,128)(2,1)} %v_ref.2) | copy-start | bytes 7864324
  1.8 0.7 copy-start.3
  2.5 0.7 copy-start.5
  3.2 5.9 %copy-start.2 = (bf16[320,2,2500]{2,1,0:T(2,128)(2,1)S(1)}, bf16[320,2,2500]{2,1,0:T(2,128)(2,1)}, u32[]{:S(2)}) copy-start(bf16[320,2,2500]{2,1,0:T(2,128)(2,1)} %t_ref) | copy-start | bytes 9600004
  6.1 31.8 %collective-permute-start = (bf16[1024,640]{1,0:T(8,128)(2,1)S(1)}, bf16[1024,640]{1,0:T(8,128)(2,1)S(1)}, u32[]{:S(2)}, u32[]{:S(2)}) collective-permute-start(bf16[1024,640]{1,0:T(8,128)(2,1)S(1)} %mask_integrals.2), channel_id=1, source_target_pairs={{0,16},{16,0},{1,17},{17,1},{2,18},{18,2},{3,19},{19,3},{4,20},{20... | collective-permute-start | bytes 3932168 | tf_op jit(solution)/shard_map/ppermute | solution.py:232
  14.2 14.1 %collective-permute-start.1 = (bf16[320,640]{1,0:T(8,128)(2,1)S(1)}, bf16[320,640]{1,0:T(8,128)(2,1)S(1)}, u32[]{:S(2)}, u32[]{:S(2)}) collective-permute-start(bf16[320,640]{1,0:T(8,128)(2,1)S(1)} %get-tuple-element.38), channel_id=1, source_target_pairs={{0,12},{4,0},{8,4},{12,8},{1,13},{5,1},{9,5},{13,9},{2,14},{6,2},{... | collective-permute-start | bytes 1228808 | tf_op jit(solution)/shard_map/ppermute | solution.py:232
  17.9 18.1 %collective-permute-start.2 = (bf16[320,640]{1,0:T(8,128)(2,1)S(1)}, bf16[320,640]{1,0:T(8,128)(2,1)S(1)}, u32[]{:S(2)}, u32[]{:S(2)}) collective-permute-start(bf16[320,640]{1,0:T(8,128)(2,1)S(1)} %get-tuple-element.39), channel_id=1, source_target_pairs={{0,4},{4,8},{8,12},{12,0},{1,5},{5,9},{9,13},{13,1},{2,6},{6,10},{... | collective-permute-start | bytes 1228808 | tf_op jit(solution)/shard_map/ppermute | solution.py:232
  17.9 7.6 %copy-start.1 = (bf16[1024,1280]{1,0:T(8,128)(2,1)S(1)}, bf16[1024,1280]{1,0:T(8,128)(2,1)}, u32[]{:S(2)}) copy-start(bf16[1024,1280]{1,0:T(8,128)(2,1)} %v_ref.2) | copy-start | bytes 7864324
  17.9 7.6 %copy-start.4 = (s32[1280]{0:T(1024)S(1)}, s32[1280]{0:T(1024)}, u32[]{:S(2)}) copy-start(s32[1280]{0:T(1024)} %param.7) | copy-start | bytes 15364
  37.9 9.4 %collective-permute-start.3 = (bf16[5,320,640]{2,1,0:T(8,128)(2,1)S(1)}, bf16[5,320,640]{2,1,0:T(8,128)(2,1)S(1)}, u32[]{:S(2)}, u32[]{:S(2)}) collective-permute-start(bf16[5,320,640]{2,1,0:T(8,128)(2,1)S(1)} %keep_columns.1.own_here.refs_0_), channel_id=1, source_target_pairs={{0,1},{1,0},{2,3},{3,2},{4,5},{5,4},{6,7},{7,6},{8,9},{9,8},{10,11... | collective-permute-start | bytes 6144008 | tf_op jit(solution)/shard_map/ppermute | solution.py:235
  37.9 9.4 %collective-permute-start.10 = (bf16[1024,640]{1,0:T(8,128)(2,1)S(1)}, bf16[1024,640]{1,0:T(8,128)(2,1)S(1)}, u32[]{:S(2)}, u32[]{:S(2)}) collective-permute-start(bf16[1024,640]{1,0:T(8,128)(2,1)S(1)} %collective-permute-done.refs_2_.refs_6_), channel_id=1, source_target_pairs={{0,1},{1,0},{2,3},{3,2},{4,5},{5,4},{6,7},{7,6},{8,9},{9,8},{10,11... | collective-permute-start | bytes 3932168 | tf_op jit(solution)/shard_map/ppermute | solution.py:235
  38.4 6.0 %collective-permute-start.4 = (bf16[320,640]{1,0:T(8,128)(2,1)S(1)}, bf16[320,640]{1,0:T(8,128)(2,1)S(1)}, u32[]{:S(2)}, u32[]{:S(2)}) collective-permute-start(bf16[320,640]{1,0:T(8,128)(2,1)S(1)} %collective-permute-done.1.refs_1_), channel_id=1, source_target_pairs={{0,1},{1,0},{2,3},{3,2},{4,5},{5,4},{6,7},{7,6},{8,9},{9,8},{10,11... | collective-permute-start | bytes 1228808 | tf_op jit(solution)/shard_map/ppermute | solution.py:235
  38.4 8.9 %collective-permute-start.5 = (bf16[320,640]{1,0:T(8,128)(2,1)S(1)}, bf16[320,640]{1,0:T(8,128)(2,1)S(1)}, u32[]{:S(2)}, u32[]{:S(2)}) collective-permute-start(bf16[320,640]{1,0:T(8,128)(2,1)S(1)} %collective-permute-done.2.refs_2_), channel_id=1, source_target_pairs={{0,1},{1,0},{2,3},{3,2},{4,5},{5,4},{6,7},{7,6},{8,9},{9,8},{10,11... | collective-permute-start | bytes 1228808 | tf_op jit(solution)/shard_map/ppermute | solution.py:235
  38.9 13.4 %collective-permute-start.6 = (bf16[512,640]{1,0:T(8,128)(2,1)S(1)}, bf16[512,640]{1,0:T(8,128)(2,1)S(1)}, u32[]{:S(2)}, u32[]{:S(2)}) collective-permute-start(bf16[512,640]{1,0:T(8,128)(2,1)S(1)} %get-tuple-element.44), channel_id=1, source_target_pairs={{0,1},{1,0},{2,3},{3,2},{4,5},{5,4},{6,7},{7,6},{8,9},{9,8},{10,11... | collective-permute-start | bytes 1966088 | tf_op jit(solution)/shard_map/ppermute | solution.py:235
  44.4 21.4 %collective-permute-start.7 = (bf16[320,640]{1,0:T(8,128)(2,1)S(1)}, bf16[320,640]{1,0:T(8,128)(2,1)S(1)}, u32[]{:S(2)}, u32[]{:S(2)}) collective-permute-start(bf16[320,640]{1,0:T(8,128)(2,1)S(1)} %get-tuple-element.46), channel_id=1, source_target_pairs={{0,8},{4,12},{8,0},{12,4},{1,9},{5,13},{9,1},{13,5},{2,10},{6,14},... | collective-permute-start | bytes 1228808 | tf_op jit(solution)/shard_map/ppermute | solution.py:232
  50.7 16.7 %collective-permute-start.15 = (s16[960,256]{1,0:T(8,128)(2,1)S(1)}, s16[960,256]{1,0:T(8,128)(2,1)S(1)}, u32[]{:S(2)}, u32[]{:S(2)}) collective-permute-start(s16[960,256]{1,0:T(8,128)(2,1)S(1)} %get-tuple-element.55), channel_id=1, source_target_pairs={{0,2},{1,3},{2,0},{3,1},{4,6},{5,7},{6,4},{7,5},{8,10},{9,11},{10,... | collective-permute-start | bytes 1474568 | tf_op jit(solution)/shard_map/ppermute | solution.py:238
  65.8 4.0 %collective-permute-start.8 = (bf16[320,640]{1,0:T(8,128)(2,1)S(1)}, bf16[320,640]{1,0:T(8,128)(2,1)S(1)}, u32[]{:S(2)}, u32[]{:S(2)}) collective-permute-start(bf16[320,640]{1,0:T(8,128)(2,1)S(1)} %collective-permute-done.7.refs_0_), channel_id=1, source_target_pairs={{0,1},{1,0},{2,3},{3,2},{4,5},{5,4},{6,7},{7,6},{8,9},{9,8},{10,11... | collective-permute-start | bytes 1228808 | tf_op jit(solution)/shard_map/ppermute | solution.py:235
  65.8 19.8 %collective-permute-start.14 = (s16[960,256]{1,0:T(8,128)(2,1)S(1)}, s16[960,256]{1,0:T(8,128)(2,1)S(1)}, u32[]{:S(2)}, u32[]{:S(2)}) collective-permute-start(s16[960,256]{1,0:T(8,128)(2,1)S(1)} %get-tuple-element.45), channel_id=1, source_target_pairs={{0,2},{1,3},{2,0},{3,1},{4,6},{5,7},{6,4},{7,5},{8,10},{9,11},{10,... | collective-permute-start | bytes 1474568 | tf_op jit(solution)/shard_map/ppermute | solution.py:238
  68.2 17.4 %collective-permute-start.16 = (s16[960,256]{1,0:T(8,128)(2,1)S(1)}, s16[960,256]{1,0:T(8,128)(2,1)S(1)}, u32[]{:S(2)}, u32[]{:S(2)}) collective-permute-start(s16[960,256]{1,0:T(8,128)(2,1)S(1)} %add_other_y.3), channel_id=1, source_target_pairs={{0,16},{16,0},{1,17},{17,1},{2,18},{18,2},{3,19},{19,3},{4,20},{20... | collective-permute-start | bytes 1474568 | tf_op jit(solution)/shard_map/ppermute | solution.py:232
  71.4 11.9 %collective-permute-start.11 = (s16[320,256]{1,0:T(8,128)(2,1)S(1)}, s16[320,256]{1,0:T(8,128)(2,1)S(1)}, u32[]{:S(2)}, u32[]{:S(2)}) collective-permute-start(s16[320,256]{1,0:T(8,128)(2,1)S(1)} %get-tuple-element.52), channel_id=1, source_target_pairs={{0,2},{1,3},{2,0},{3,1},{4,6},{5,7},{6,4},{7,5},{8,10},{9,11},{10,... | collective-permute-start | bytes 491528 | tf_op jit(solution)/shard_map/ppermute | solution.py:238
  73.6 16.7 %collective-permute-start.9 = (s16[320,256]{1,0:T(8,128)(2,1)S(1)}, s16[320,256]{1,0:T(8,128)(2,1)S(1)}, u32[]{:S(2)}, u32[]{:S(2)}) collective-permute-start(s16[320,256]{1,0:T(8,128)(2,1)S(1)} %get-tuple-element.49), channel_id=1, source_target_pairs={{0,2},{1,3},{2,0},{3,1},{4,6},{5,7},{6,4},{7,5},{8,10},{9,11},{10,... | collective-permute-start | bytes 491528 | tf_op jit(solution)/shard_map/ppermute | solution.py:238
  84.0 6.3 %collective-permute-start.12 = (s16[320,256]{1,0:T(8,128)(2,1)S(1)}, s16[320,256]{1,0:T(8,128)(2,1)S(1)}, u32[]{:S(2)}, u32[]{:S(2)}) collective-permute-start(s16[320,256]{1,0:T(8,128)(2,1)S(1)} %add_other_y.2), channel_id=1, source_target_pairs={{0,16},{16,0},{1,17},{17,1},{2,18},{18,2},{3,19},{19,3},{4,20},{20... | collective-permute-start | bytes 491528 | tf_op jit(solution)/shard_map/ppermute | solution.py:232
  86.4 9.0 %collective-permute-start.17 = (bf16[320,256]{1,0:T(8,128)(2,1)S(1)}, bf16[320,256]{1,0:T(8,128)(2,1)S(1)}, u32[]{:S(2)}, u32[]{:S(2)}) collective-permute-start(bf16[320,256]{1,0:T(8,128)(2,1)S(1)} %get-tuple-element.57.refs_1_), channel_id=1, source_target_pairs={{0,4},{4,8},{8,12},{12,0},{1,5},{5,9},{9,13},{13,1},{2,6},{6,10},{... | collective-permute-start | bytes 491528 | tf_op jit(solution)/shard_map/ppermute | solution.py:232
  87.2 8.3 %collective-permute-start.18 = (bf16[320,256]{1,0:T(8,128)(2,1)S(1)}, bf16[320,256]{1,0:T(8,128)(2,1)S(1)}, u32[]{:S(2)}, u32[]{:S(2)}) collective-permute-start(bf16[320,256]{1,0:T(8,128)(2,1)S(1)} %get-tuple-element.58.refs_3_), channel_id=1, source_target_pairs={{0,12},{4,0},{8,4},{12,8},{1,13},{5,1},{9,5},{13,9},{2,14},{6,2},{... | collective-permute-start | bytes 491528 | tf_op jit(solution)/shard_map/ppermute | solution.py:232
  91.0 13.0 %collective-permute-start.13 = (bf16[320,256]{1,0:T(8,128)(2,1)S(1)}, bf16[320,256]{1,0:T(8,128)(2,1)S(1)}, u32[]{:S(2)}, u32[]{:S(2)}) collective-permute-start(bf16[320,256]{1,0:T(8,128)(2,1)S(1)} %add_other_x.2.refs_0_), channel_id=1, source_target_pairs={{0,8},{4,12},{8,0},{12,4},{1,9},{5,13},{9,1},{13,5},{2,10},{6,14},... | collective-permute-start | bytes 491528 | tf_op jit(solution)/shard_map/ppermute | solution.py:232

commit v5 on v4

--- a/solution.py
+++ b/solution.py
@@ -93,12 +93,12 @@
     )(scalars, *arrays)
 
 
-def mask_body(by, row_n, sub, tall, s_ref, ab_ref, cd_ref, v_ref, *out_refs):
+def masked_rows(by, row_n, sub, k_here, s_ref, ab_ref, cd_ref, v_ref):
     x, y, core = s_ref[0], s_ref[2], s_ref[3]
-    k_here, cd_here = out_refs[0].shape[-1], v_ref.shape[1]
+    rows, cd_here = v_ref.shape
+    tall = rows // 4
     q, m = divide(lax.broadcasted_iota(jnp.int32, (k_here, 1), 0), sub)
     wanted = q * (sub * row_n) + lax.rem(x - by + row_n, row_n) * sub + m
-    pick = jnp.where(lax.broadcasted_iota(jnp.int32, (k_here, cd_here), 1) == wanted, 1.0, 0.0).astype(jnp.bfloat16)
     square = (LANES, LANES)
     diagonal = lax.broadcasted_iota(jnp.int32, square, 0) == lax.broadcasted_iota(jnp.int32, square, 1)
     cd_labels = cd_ref[...].astype(jnp.float32)
@@ -114,12 +114,11 @@
                 start = pl.multiple_of(block * tall + strip * LANES, LANES)
                 v = v_ref[pl.ds(start, LANES), :].astype(jnp.float32)
                 blocks.append(jnp.where(ab == cd, v, 0.0).astype(jnp.bfloat16))
-    picked = dot_nt(jnp.concatenate(blocks, axis=0), pick).astype(jnp.bfloat16)
-    if len(out_refs) == 1:
-        out_refs[0][...] = picked.reshape(out_refs[0].shape)
-    else:
-        out_refs[0][...] = picked[: 2 * tall].reshape(out_refs[0].shape)
-        out_refs[1][...] = picked[2 * tall :].reshape(out_refs[1].shape)
+    return dot_nt(jnp.concatenate(blocks, axis=0), one_hot_rows(wanted, cd_here)).astype(jnp.bfloat16)
+
+
+def mask_body(by, row_n, sub, s_ref, ab_ref, cd_ref, v_ref, out_ref):
+    out_ref[...] = masked_rows(by, row_n, sub, out_ref.shape[1], s_ref, ab_ref, cd_ref, v_ref)
 
 
 def one_hot_rows(columns, width):
@@ -141,43 +140,69 @@
         out_ref[...] = picked[k * chunk : (k + 1) * chunk]
 
 
-def keep_body(order, n, col_n, s_ref, flat_ref, out_ref):
+def keep_body(order, n, col_n, row_n, sub, s_ref, flat_ref, ab_ref, cd_ref, v_ref, both_ref, kept_ref):
     z = s_ref[1]
-    place = lax.broadcasted_iota(jnp.int32, (out_ref.shape[1], 1), 0)
+    half, k_here = kept_ref.shape
+    pairs = both_ref.shape[0] - half
+    place = lax.broadcasted_iota(jnp.int32, (pairs // (len(order) + 1), 1), 0)
     inside, turned = inside_columns(place, n, z)
     picks = [inside if r == 0 else pair_columns(place, n, z, lax.rem(z + r, col_n), True) for r in order] + [turned]
     picked = dot_nt(one_hot_rows(jnp.concatenate(picks, axis=0), flat_ref.shape[1]), flat_ref[...])
-    out_ref[...] = picked.astype(jnp.bfloat16).reshape(out_ref.shape)
-
-
-def sum_body(first, count, s_ref, own_here, own_there, *refs):
-    away = refs[: 2 * count]
-    keep_ref, pass_ref, coded_ref, kept_ref = refs[2 * count :]
-    k_here = own_here.shape[2]
-    chunk = own_here.shape[1]
+    both_ref[:pairs] = picked.astype(jnp.bfloat16)
+    masked = masked_rows(0, row_n, sub, k_here, s_ref, ab_ref, cd_ref, v_ref)
+    both_ref[pairs:] = masked[:half]
+    kept_ref[...] = masked[half:]
+
+
+def sum_body(first, count, groups, y_first, s_ref, own_here, own_there, *refs):
+    away, refs = refs[: 2 * count], refs[2 * count :]
+    keeps, passes, outs = refs[:groups], refs[groups : 2 * groups - 1], refs[2 * groups - 1 :]
+    high, tall = outs[-1].shape[-2:]
+    tall = tall if y_first else tall // 2
+    chunk = high // count
+    pairs = own_here.shape[0] - 2 * tall
 
     def rows(ref):
-        return ref[ref.shape[0] - 1] if len(ref.shape) == 3 else ref[...]
-
-    half = kept_ref.shape[1]
-    keep, passed = keep_ref[...].reshape(-1, k_here), pass_ref[...].reshape(-1, k_here)
-    a, b = keep[-2 * half :], passed[: 2 * half]
-    to = own_here[first : first + count].reshape(count * chunk, k_here)
-    too = own_there[first : first + count].reshape(count * chunk, k_here)
+        return ref[pairs - chunk : pairs] if ref.shape[0] > chunk else ref[...]
+
+    mine = slice(first * chunk, (first + count) * chunk)
     tr = jnp.concatenate([rows(ref) for ref in away[:count]], axis=0)
     tro = jnp.concatenate([rows(ref) for ref in away[count:]], axis=0)
-    left = jnp.concatenate([to, too, tr, tro], axis=1)
-    right = jnp.concatenate([a, b, -a, -b], axis=1)
-    total = dot_nt(left, right)
-    coded_ref[...] = encode(total[:, :half])
-    kept_ref[...] = total[:, half:]
-
-
-def add_y_body(s_ref, kept_ref, coded_ref, out_ref):
-    out_ref[...] = encode(kept_ref[...] + decode(coded_ref[...]))
-
-
-def add_x_body(count, s_ref, kept_ref, *refs):
+    left = jnp.concatenate([own_here[mine], own_there[mine], tr, tro], axis=1)
+    for g in range(groups):
+        start = keeps[g].shape[0] - 2 * tall
+        a = keeps[g][start:]
+        b = own_there[pairs:] if g == 0 else passes[g - 1][: 2 * tall]
+        total = dot_nt(left, jnp.concatenate([a, b, -a, -b], axis=1))
+        if y_first:
+            outs[0][g] = encode(total[:, :tall])
+            outs[1][g] = total[:, tall:]
+        elif g == 0:
+            outs[-1][...] = total
+        else:
+            outs[g - 1][...] = encode(total)
+
+
+def add_y_body(s_ref, kept_ref, coded_ref, own_ref, *out_refs):
+    for g in range(kept_ref.shape[0]):
+        total = kept_ref[g] + decode(coded_ref[g])
+        if g == 0:
+            own_ref[...] = total
+        else:
+            out_refs[g - 1][...] = encode(total)
+
+
+def add_x_body(s_ref, kept_ref, *refs):
+    coded_ref, own_ref = refs[-2:]
+    total = kept_ref[...]
+    for ref in refs[:-2]:
+        total = total + decode(ref[...])
+    tall = own_ref.shape[1]
+    coded_ref[...] = encode(total[:, :tall])
+    own_ref[...] = total[:, tall:]
+
+
+def round_body(count, s_ref, kept_ref, *refs):
     total = kept_ref[...]
     for ref in refs[:-count]:
         total = total + decode(ref[...])
@@ -223,7 +248,9 @@
     chunk = -(-((n * n + 1) // 2 + 1) // 16) * 16
     far = col_n // 2
     near = [r for r in range(1, col_n) if r != far]
-    groups = [[0] + near, [far]]
+    half = (len(near) + 1) // 2
+    groups = [([0] + near[:half], True), (near[half:], False), ([far], False)]
+    groups = [(group, y_first) for group, y_first in groups if group]
     order = [0] + near + [far]
     bf16, i16, f32 = jnp.bfloat16, jnp.int16, jnp.float32
 
@@ -240,19 +267,16 @@
     scalars = jnp.stack([x, z, y, core]).astype(jnp.int32)
     ab_row, cd_row = ab_irrep.reshape(-1, LANES), cd_irrep.reshape(-1, LANES)
 
-    def masked(v, by, parts):
-        return call(
-            "mask_integrals",
-            functools.partial(mask_body, by, row_n, sub, tall),
-            scalars,
-            [ab_row, cd_row, v],
-            [((4 // parts * tall, k_here), bf16)] * parts,
-        )
-
-    passed, kept = [None] * row_n, [None] * row_n
+    kept = [None] * row_n
     gone = scalars
     for by in range(1, row_n):
-        (gone,) = masked(integrals, by, 1)
+        (gone,) = call(
+            "mask_integrals",
+            functools.partial(mask_body, by, row_n, sub),
+            scalars,
+            [ab_row, cd_row, integrals],
+            [((rows, k_here), bf16)],
+        )
         kept[by] = shift(gone, "row", -by)
 
     amplitudes, _ = lax.optimization_barrier((amplitudes, gone))
@@ -265,61 +289,75 @@
         [((k_here, -(-columns // LANES) * LANES), bf16)] + [((chunk, k_here), bf16)] * len(sent_order),
     )
     away = {r: shift(s, "col", -r) for r, s in zip(near, sent)}
-    integrals, flat = lax.optimization_barrier((integrals, flat))
-    passed[0], kept[0] = masked(integrals, 0, 2)
-    (own,) = call(
+
+    both, kept[0] = call(
         "keep_columns",
-        functools.partial(keep_body, order, n, col_n),
+        functools.partial(keep_body, order, n, col_n, row_n, sub),
         scalars,
-        [flat],
-        [((col_n + 1, chunk, k_here), bf16)],
+        [flat, ab_row, cd_row, integrals],
+        [(((col_n + 1) * chunk + 2 * tall, k_here), bf16), ((2 * tall, k_here), bf16)],
     )
-    arrived = lax.optimization_barrier((passed[0], own, sent[-1], kept[1:], away))
-    passed[0], behind, far_sent, kept[1:], away = arrived
-    away_there = {r: other_core(away[r]) for r in near}
-    passed = [other_core(passed[0])] + [other_core(a) for a in kept[1:]]
-    own_there = other_core(behind)
+    far_sent, away = lax.optimization_barrier((sent[-1], away))
+    behind, kept[1:], *arrived = lax.optimization_barrier((both, kept[1:], *[away[r] for r in near]))
+    away_there = {r: other_core(a) for r, a in zip(near, arrived)}
+    both_there = other_core(behind)
     away[far] = shift(far_sent, "col", -far)
+    passed = [other_core(a) for a in kept[1:]]
+
+    rounded, arrived = {}, []
+    for group, y_first in groups:
+        first, count = order.index(group[0]), len(group)
+        high = count * chunk
+        if far in group:
+            _, away[far] = lax.optimization_barrier((arrived, away[far]))
+            away_there[far] = other_core(away[far])
+        here = [both if r == 0 else away[r] for r in group]
+        there = [both_there if r == 0 else away_there[r] for r in group]
+        if group == groups[1][0]:
+            _, here[0] = lax.optimization_barrier((sums[0], here[0]))
+        if y_first:
+            shapes = [((row_n, high, tall), i16), ((row_n, high, tall), f32)]
+        else:
+            shapes = [((high, 2 * tall), i16)] * (row_n - 1) + [((high, 2 * tall), f32)]
+        sums = call(
+            "sum_pairs",
+            functools.partial(sum_body, first, count, row_n, y_first),
+            scalars,
+            [both, both_there] + here + there + kept + passed,
+            shapes,
+        )
+        if y_first:
+            own_sum, *others = call(
+                "add_other_y",
+                add_y_body,
+                scalars,
+                [sums[1], other_y(sums[0])],
+                [((high, tall), f32)] + [((high, tall), i16)] * (row_n - 1),
+            )
+            last = [shift(other, "row", by + 1) for by, other in enumerate(others)]
+        else:
+            arrived = [shift(coded, "row", by + 1) for by, coded in enumerate(sums[:-1])]
+            coded, own_sum = call(
+                "add_other_x",
+                add_x_body,
+                scalars,
+                [sums[-1]] + arrived,
+                [((high, tall), i16), ((high, tall), f32)],
+            )
+            last = [other_y(coded)]
+        mine = call(
+            "round_pairs",
+            functools.partial(round_body, count),
+            scalars,
+            [own_sum] + last,
+            [((chunk, tall), bf16)] * count,
+        )
+        for r, value in zip(group, mine):
+            rounded[r] = [value] if r == 0 else [value, shift(value, "col", r)]
 
     done = None
-    for group in groups:
-        first, count = order.index(group[0]), len(group)
-        here = [own if r == 0 else away[r] for r in group]
-        there = [own_there if r == 0 else away_there[r] for r in group]
-        final = [None] * (row_n + 1)
-        for by in list(range(1, row_n)) + [0]:
-            coded, total = call(
-                "sum_pairs",
-                functools.partial(sum_body, first, count),
-                scalars,
-                [own, own_there] + here + there + [kept[by], passed[by]],
-                [((count * chunk, tall), i16), ((count * chunk, tall), f32)],
-            )
-            if by == 0 and group == groups[0]:
-                _, away[far] = lax.optimization_barrier((coded, away[far]))
-                away_there[far] = other_core(away[far])
-            coded = other_y(coded)
-            if by == 0:
-                final[:2] = [total, coded]
-            else:
-                (merged,) = call(
-                    "add_other_y",
-                    add_y_body,
-                    scalars,
-                    [total, coded],
-                    [((count * chunk, tall), i16)],
-                )
-                final[by + 1] = shift(merged, "row", by)
-        rounded = call(
-            "add_other_x",
-            functools.partial(add_x_body, count),
-            scalars,
-            final,
-            [((chunk, tall), bf16)] * count,
-        )
-        sources = []
-        for r, mine in zip(group, rounded):
-            sources += [mine] if r == 0 else [mine, shift(mine, "col", r)]
+    for group in ([0] + near, [far]):
+        sources = [value for r in group for value in rounded[r]]
         tile = (TILE, tall), lambda g, s: (g, 0)
         sources += [] if done is None else [(done, *tile)]
         (done,) = call(

time: 108 us -> 103 us (0.954)
  waiting for transfers between devices: 40.9 us -> 31.8 us
  starting transfers between devices: 23.2 us -> 27.2 us
    ppermute x4 -> x3, waiting for transfers between devices: 8.11 us -> 2.4 us  [other_y(): return lax.ppermute(array, 'depth', [(i, i ^ 2) for i in range(depth_n)])]
    ppermute x9 -> x10, starting transfers between devices: 16.9 us -> 21.1 us  [shift(): lax.ppermute(array, axis, [(i, (i + by) % count) for i in range(count)])]
    ppermute x9 -> x10, waiting for transfers between devices: 27.2 us -> 24 us  [shift(): lax.ppermute(array, axis, [(i, (i + by) % count) for i in range(count)])]
    ppermute x4 -> x3, starting transfers between devices: 5.32 us -> 5.12 us  [other_y(): return lax.ppermute(array, 'depth', [(i, i ^ 2) for i in range(depth_n)])]
    ppermute x6 -> x5, waiting for transfers between devices: 5.54 us -> 5.38 us  [other_core(): return lax.ppermute(array, 'depth', [(i, i ^ 1) for i in range(depth_n)])]
  transfers between devices with their start and end apart: 19 -> 18, of which waited for: 7 -> 11; matrix products, arithmetic and copies ran while one was open for 0% -> 0% of each run, Pallas kernels for 31% -> 33%
where the time goes in v5:
time: 103 us
  Pallas kernels  40.1 us (39%)
  waiting for transfers between devices  31.8 us (31%)
  starting transfers between devices  27.2 us (26%)
  local copies, waits for them, and re-layouts  3.14 us (3%)
    pallas_call x14, Pallas kernels, call(): pl.pallas_call(body, name=name, out_shape=shapes, compiler_params=pltpu.C...  40.1 us
    ppermute x10, waiting for transfers between devices, shift(): lax.ppermute(array, axis, [(i, (i + by) % count) for i in range(count)])  24 us
    ppermute x10, starting transfers between devices, shift(): lax.ppermute(array, axis, [(i, (i + by) % count) for i in range(count)])  21.1 us
    ppermute x5, waiting for transfers between devices, other_core(): return lax.ppermute(array, 'depth', [(i, i ^ 1) for i in range(depth_n)])  5.38 us
    ppermute x3, starting transfers between devices, other_y(): return lax.ppermute(array, 'depth', [(i, i ^ 2) for i in range(depth_n)])  5.12 us
    unnamed x12, local copies, waits for them, and re-layouts  3.14 us
    ppermute x3, waiting for transfers between devices, other_y(): return lax.ppermute(array, 'depth', [(i, i ^ 2) for i in range(depth_n)])  2.4 us
  transfers between devices with their start and end apart: 18, of which 11 were waited for; matrix products, arithmetic and copies ran while one was open for 0% of the time, Pallas kernels for 33%

profile of v5, /device:TPU:0, one launch (start us, length us, event | category | flops | bytes accessed | tf_op | source)
XLA Modules:
  0.0 102.6 jit_solution(7028622162311669645)
XLA Ops:
  0.0 0.1 pad_add_fusion.s_ref
  0.1 1.7 %copy-done = bf16[1024,1280]{1,0:T(8,128)(2,1)S(1)} copy-done((bf16[1024,1280]{1,0:T(8,128)(2,1)S(1)}, bf16[1024,1280]{1,0:T(8,128)(2,1)}, u32[]{:S(2)}) %copy-start) | copy-done | bytes 2621464
  1.8 0.7 copy-done.3
  2.5 0.7 copy-done.5
  3.2 2.9 %mask_integrals.1 = bf16[1024,640]{1,0:T(8,128)(2,1)S(1)} custom-call(s32[4]{0:T(128)S(1)} %pad_add_fusion.s_ref, s32[8,128]{1,0:T(8,128)S(1)} %bitcast.9, s32[10,128]{1,0:T(8,128)S(1)} %bitcast.7, bf16[1024,1280]{1,0:T(8,128)(2,1)S(1)} %copy-done), custom_call_target="tpu_custom_call" | custom-call | flops 1 | bytes 1 | tf_op jit(solution)/shard_map/mask_integrals/pallas_call | solution.py:86
  6.1 0.0 copy-start.1
  6.1 0.0 copy-start.4
  6.1 3.0 %collective-permute-start = (bf16[1024,640]{1,0:T(8,128)(2,1)S(1)}, bf16[1024,640]{1,0:T(8,128)(2,1)S(1)}, u32[]{:S(2)}, u32[]{:S(2)}) collective-permute-start(bf16[1024,640]{1,0:T(8,128)(2,1)S(1)} %mask_integrals.1), channel_id=1, source_target_pairs={{0,16},{16,0},{1,17},{17,1},{2,18},{18,2},{3,19},{19,3},{4,20},{20... | collective-permute-start | bytes 3932168 | tf_op jit(solution)/shard_map/ppermute | solution.py:259
  9.1 5.1 %send_columns.1 = (bf16[640,2560]{1,0:T(8,128)(2,1)S(1)}, bf16[320,640]{1,0:T(8,128)(2,1)S(1)}, bf16[320,640]{1,0:T(8,128)(2,1)S(1)}, bf16[320,640]{1,0:T(8,128)(2,1)S(1)}) custom-call(s32[4]{0:T(128)S(1)} %pad_add_fusion.s_ref, bf16[320,2,2500]{2,1,0:T(2,128)(2,1)S(1)} %copy-done.2), custom_call_target="tpu_custom_call" | custom-call | flops 1 | bytes 1 | tf_op jit(solution)/shard_map/send_columns/pallas_call | solution.py:86
  14.3 3.7 %collective-permute-start.1 = (bf16[320,640]{1,0:T(8,128)(2,1)S(1)}, bf16[320,640]{1,0:T(8,128)(2,1)S(1)}, u32[]{:S(2)}, u32[]{:S(2)}) collective-permute-start(bf16[320,640]{1,0:T(8,128)(2,1)S(1)} %get-tuple-element.39), channel_id=1, source_target_pairs={{0,12},{4,0},{8,4},{12,8},{1,13},{5,1},{9,5},{13,9},{2,14},{6,2},{... | collective-permute-start | bytes 1228808 | tf_op jit(solution)/shard_map/ppermute | solution.py:259
  17.9 0.0 collective-permute-start.2
  17.9 9.6 %keep_columns.1 = (bf16[2112,640]{1,0:T(8,128)(2,1)S(1)}, bf16[512,640]{1,0:T(8,128)(2,1)S(1)}) custom-call(s32[4]{0:T(128)S(1)} %pad_add_fusion.s_ref, bf16[640,2560]{1,0:T(8,128)(2,1)S(1)} %get-tuple-element.36.flat_ref, s32[8,128]{1,0:T(8,128)S(1)} %bitcast.10, s32[10,128]{1,0:T(8,128)S(1)} %bitcast.8, bf16[1024,1280]{1,0:T(8,128)(2,1)S(1)} %copy-done.1), custom_call_target="tpu_custom_call" | custom-call | flops 1 | bytes 1 | tf_op jit(solution)/shard_map/keep_columns/pallas_call | solution.py:86
  27.5 0.3 collective-permute-done.1.refs_1_
  27.8 8.2 %collective-permute-done.2.refs_0_ = bf16[320,640]{1,0:T(8,128)(2,1)S(1)} collective-permute-done((bf16[320,640]{1,0:T(8,128)(2,1)S(1)}, bf16[320,640]{1,0:T(8,128)(2,1)S(1)}, u32[]{:S(2)}, u32[]{:S(2)}) %collective-permute-start.2) | collective-permute-done | bytes 409632 | tf_op jit(solution)/shard_map/ppermute | solution.py:259
  36.0 1.8 %collective-permute-done.refs_5_.refs_3_ = bf16[1024,640]{1,0:T(8,128)(2,1)S(1)} collective-permute-done((bf16[1024,640]{1,0:T(8,128)(2,1)S(1)}, bf16[1024,640]{1,0:T(8,128)(2,1)S(1)}, u32[]{:S(2)}, u32[]{:S(2)}) %collective-permute-start) | collective-permute-done | bytes 1310752 | tf_op jit(solution)/shard_map/ppermute | solution.py:259
  37.9 0.0 collective-permute-start.3
  37.9 0.5 collective-permute-start.5
  38.4 0.0 collective-permute-start.4
  38.4 0.5 collective-permute-start.6
  38.9 2.8 %collective-permute-start.8 = (bf16[320,640]{1,0:T(8,128)(2,1)S(1)}, bf16[320,640]{1,0:T(8,128)(2,1)S(1)}, u32[]{:S(2)}, u32[]{:S(2)}) collective-permute-start(bf16[320,640]{1,0:T(8,128)(2,1)S(1)} %get-tuple-element.51), channel_id=1, source_target_pairs={{0,8},{4,12},{8,0},{12,4},{1,9},{5,13},{9,1},{13,5},{2,10},{6,14},... | collective-permute-start | bytes 1228808 | tf_op jit(solution)/shard_map/ppermute | solution.py:259
  41.7 3.6 %collective-permute-done.4.refs_3_ = bf16[320,640]{1,0:T(8,128)(2,1)S(1)} collective-permute-done((bf16[320,640]{1,0:T(8,128)(2,1)S(1)}, bf16[320,640]{1,0:T(8,128)(2,1)S(1)}, u32[]{:S(2)}, u32[]{:S(2)}) %collective-permute-start.4) | collective-permute-done | bytes 409632 | tf_op jit(solution)/shard_map/ppermute | solution.py:262
  45.4 4.3 %sum_pairs.3 = (s16[2,640,256]{2,1,0:T(8,128)(2,1)S(1)}, f32[2,640,256]{2,1,0:T(8,128)S(1)}) custom-call(s32[4]{0:T(128)S(1)} %pad_add_fusion.s_ref, bf16[2112,640]{1,0:T(8,128)(2,1)S(1)} %get-tuple-element.43.own_here.refs_0_, bf16[2112,640]{1,0:T(8,128)(2,1)S(1)} %collective-permute-done.3.own_there.refs_2_, ...), custom_call_target="tpu_custom_call" | custom-call | flops 1 | bytes 1 | tf_op jit(solution)/shard_map/sum_pairs/pallas_call | solution.py:86
  49.7 2.8 %sum_pairs.4 = (s16[320,512]{1,0:T(8,128)(2,1)S(1)}, f32[320,512]{1,0:T(8,128)S(1)}) custom-call(s32[4]{0:T(128)S(1)} %pad_add_fusion.s_ref, bf16[2112,640]{1,0:T(8,128)(2,1)S(1)} %get-tuple-element.43.own_here.refs_0_, bf16[2112,640]{1,0:T(8,128)(2,1)S(1)} %collective-permute-done.3.own_there.refs_2_, bf16[320,640]{1,0:T(8,128)(2,1)S(1)} %collective-permute-done.2.refs_0_, ...), custom_call_target="tpu_custom_call" | custom-call | flops 1 | bytes 1 | tf_op jit(solution)/shard_map/sum_pairs/pallas_call | solution.py:86
  52.4 1.8 %collective-permute-start.7 = (s16[320,512]{1,0:T(8,128)(2,1)S(1)}, s16[320,512]{1,0:T(8,128)(2,1)S(1)}, u32[]{:S(2)}, u32[]{:S(2)}) collective-permute-start(s16[320,512]{1,0:T(8,128)(2,1)S(1)} %get-tuple-element.50), channel_id=1, source_target_pairs={{0,16},{16,0},{1,17},{17,1},{2,18},{18,2},{3,19},{19,3},{4,20},{20... | collective-permute-start | bytes 983048 | tf_op jit(solution)/shard_map/ppermute | solution.py:259
  54.3 1.5 %collective-permute-start.13 = (s16[2,640,256]{2,1,0:T(8,128)(2,1)S(1)}, s16[2,640,256]{2,1,0:T(8,128)(2,1)S(1)}, u32[]{:S(2)}, u32[]{:S(2)}) collective-permute-start(s16[2,640,256]{2,1,0:T(8,128)(2,1)S(1)} %get-tuple-element.47), channel_id=1, source_target_pairs={{0,2},{1,3},{2,0},{3,1},{4,6},{5,7},{6,4},{7,5},{8,10},{9,11},{10,... | collective-permute-start | bytes 1966088 | tf_op jit(solution)/shard_map/ppermute | solution.py:265
  55.8 4.4 %collective-permute-done.8.refs_0_ = bf16[320,640]{1,0:T(8,128)(2,1)S(1)} collective-permute-done((bf16[320,640]{1,0:T(8,128)(2,1)S(1)}, bf16[320,640]{1,0:T(8,128)(2,1)S(1)}, u32[]{:S(2)}, u32[]{:S(2)}) %collective-permute-start.8) | collective-permute-done | bytes 409632 | tf_op jit(solution)/shard_map/ppermute | solution.py:259
  60.2 2.1 %collective-permute-done.7.refs_0_ = s16[320,512]{1,0:T(8,128)(2,1)S(1)} collective-permute-done((s16[320,512]{1,0:T(8,128)(2,1)S(1)}, s16[320,512]{1,0:T(8,128)(2,1)S(1)}, u32[]{:S(2)}, u32[]{:S(2)}) %collective-permute-start.7) | collective-permute-done | bytes 327712 | tf_op jit(solution)/shard_map/ppermute | solution.py:259
  62.3 1.7 %collective-permute-done.9.refs_1_ = bf16[320,640]{1,0:T(8,128)(2,1)S(1)} collective-permute-done((bf16[320,640]{1,0:T(8,128)(2,1)S(1)}, bf16[320,640]{1,0:T(8,128)(2,1)S(1)}, u32[]{:S(2)}, u32[]{:S(2)}) %collective-permute-start.9) | collective-permute-done | bytes 409632 | tf_op jit(solution)/shard_map/ppermute | solution.py:262
  64.0 2.5 %sum_pairs.5 = (s16[320,512]{1,0:T(8,128)(2,1)S(1)}, f32[320,512]{1,0:T(8,128)S(1)}) custom-call(s32[4]{0:T(128)S(1)} %pad_add_fusion.s_ref, bf16[2112,640]{1,0:T(8,128)(2,1)S(1)} %get-tuple-element.43.own_here.refs_0_, bf16[2112,640]{1,0:T(8,128)(2,1)S(1)} %collective-permute-done.3.own_there.refs_2_, bf16[320,640]{1,0:T(8,128)(2,1)S(1)} %collective-permute-done.8.refs_0_, ...), custom_call_target="tpu_custom_call" | custom-call | flops 1 | bytes 1 | tf_op jit(solution)/shard_map/sum_pairs/pallas_call | solution.py:86
  66.5 1.8 %collective-permute-start.10 = (s16[320,512]{1,0:T(8,128)(2,1)S(1)}, s16[320,512]{1,0:T(8,128)(2,1)S(1)}, u32[]{:S(2)}, u32[]{:S(2)}) collective-permute-start(s16[320,512]{1,0:T(8,128)(2,1)S(1)} %get-tuple-element.54), channel_id=1, source_target_pairs={{0,16},{16,0},{1,17},{17,1},{2,18},{18,2},{3,19},{19,3},{4,20},{20... | collective-permute-start | bytes 983048 | tf_op jit(solution)/shard_map/ppermute | solution.py:259
  68.4 2.4 %collective-permute-done.13.coded_ref = s16[2,640,256]{2,1,0:T(8,128)(2,1)S(1)} collective-permute-done((s16[2,640,256]{2,1,0:T(8,128)(2,1)S(1)}, s16[2,640,256]{2,1,0:T(8,128)(2,1)S(1)}, u32[]{:S(2)}, u32[]{:S(2)}) %collective-permute-start.13) | collective-permute-done | bytes 655392 | tf_op jit(solution)/shard_map/ppermute | solution.py:265
  70.8 0.9 add_other_y.1
  71.7 0.4 collective-permute-start.14
  72.1 0.7 add_other_x.3
  72.9 1.8 %collective-permute-start.16 = (s16[320,256]{1,0:T(8,128)(2,1)S(1)}, s16[320,256]{1,0:T(8,128)(2,1)S(1)}, u32[]{:S(2)}, u32[]{:S(2)}) collective-permute-start(s16[320,256]{1,0:T(8,128)(2,1)S(1)} %get-tuple-element.64), channel_id=1, source_target_pairs={{0,2},{1,3},{2,0},{3,1},{4,6},{5,7},{6,4},{7,5},{8,10},{9,11},{10,... | collective-permute-start | bytes 491528 | tf_op jit(solution)/shard_map/ppermute | solution.py:265
  74.6 2.6 %collective-permute-done.10.refs_0_ = s16[320,512]{1,0:T(8,128)(2,1)S(1)} collective-permute-done((s16[320,512]{1,0:T(8,128)(2,1)S(1)}, s16[320,512]{1,0:T(8,128)(2,1)S(1)}, u32[]{:S(2)}, u32[]{:S(2)}) %collective-permute-start.10) | collective-permute-done | bytes 327712 | tf_op jit(solution)/shard_map/ppermute | solution.py:259
  77.2 0.7 add_other_x.2
  77.9 1.8 %collective-permute-start.11 = (s16[320,256]{1,0:T(8,128)(2,1)S(1)}, s16[320,256]{1,0:T(8,128)(2,1)S(1)}, u32[]{:S(2)}, u32[]{:S(2)}) collective-permute-start(s16[320,256]{1,0:T(8,128)(2,1)S(1)} %get-tuple-element.56), channel_id=1, source_target_pairs={{0,2},{1,3},{2,0},{3,1},{4,6},{5,7},{6,4},{7,5},{8,10},{9,11},{10,... | collective-permute-start | bytes 491528 | tf_op jit(solution)/shard_map/ppermute | solution.py:265
  79.8 0.6 round_pairs.5.refs_3_
  80.4 3.6 %collective-permute-start.17 = (bf16[320,256]{1,0:T(8,128)(2,1)S(1)}, bf16[320,256]{1,0:T(8,128)(2,1)S(1)}, u32[]{:S(2)}, u32[]{:S(2)}) collective-permute-start(bf16[320,256]{1,0:T(8,128)(2,1)S(1)} %round_pairs.5.refs_3_), channel_id=1, source_target_pairs={{0,12},{4,0},{8,4},{12,8},{1,13},{5,1},{9,5},{13,9},{2,14},{6,2},{... | collective-permute-start | bytes 491528 | tf_op jit(solution)/shard_map/ppermute | solution.py:259
  84.0 0.6 round_pairs.4
  84.7 1.3 %collective-permute-start.15 = (bf16[320,256]{1,0:T(8,128)(2,1)S(1)}, bf16[320,256]{1,0:T(8,128)(2,1)S(1)}, u32[]{:S(2)}, u32[]{:S(2)}) collective-permute-start(bf16[320,256]{1,0:T(8,128)(2,1)S(1)} %get-tuple-element.61.refs_1_), channel_id=1, source_target_pairs={{0,4},{4,8},{8,12},{12,0},{1,5},{5,9},{9,13},{13,1},{2,6},{6,10},{... | collective-permute-start | bytes 491528 | tf_op jit(solution)/shard_map/ppermute | solution.py:259
  85.9 0.6 round_pairs.3.refs_0_
  86.5 2.7 %collective-permute-start.12 = (bf16[320,256]{1,0:T(8,128)(2,1)S(1)}, bf16[320,256]{1,0:T(8,128)(2,1)S(1)}, u32[]{:S(2)}, u32[]{:S(2)}) collective-permute-start(bf16[320,256]{1,0:T(8,128)(2,1)S(1)} %round_pairs.3.refs_0_), channel_id=1, source_target_pairs={{0,8},{4,12},{8,0},{12,4},{1,9},{5,13},{9,1},{13,5},{2,10},{6,14},... | collective-permute-start | bytes 491528 | tf_op jit(solution)/shard_map/ppermute | solution.py:259
  89.2 4.4 %collective-permute-done.15.refs_2_ = bf16[320,256]{1,0:T(8,128)(2,1)S(1)} collective-permute-done((bf16[320,256]{1,0:T(8,128)(2,1)S(1)}, bf16[320,256]{1,0:T(8,128)(2,1)S(1)}, u32[]{:S(2)}, u32[]{:S(2)}) %collective-permute-start.15) | collective-permute-done | bytes 163872 | tf_op jit(solution)/shard_map/ppermute | solution.py:259
  93.5 4.8 %place_pairs.2.refs_2_ = bf16[2500,256]{1,0:T(8,128)(2,1)S(1)} custom-call(s32[4]{0:T(128)S(1)} %pad_add_fusion.s_ref, bf16[320,256]{1,0:T(8,128)(2,1)S(1)} %get-tuple-element.60.refs_0_, bf16[320,256]{1,0:T(8,128)(2,1)S(1)} %get-tuple-element.61.refs_1_, bf16[320,256]{1,0:T(8,128)(2,1)S(1)} %collective-permute-done.15.refs_2_, ...), custom_call_target="tpu_custom_call" | custom-call | flops 1 | bytes 1 | tf_op jit(solution)/shard_map/place_pairs/pallas_call | solution.py:86
  98.4 0.3 collective-permute-done.12.refs_1_
  98.6 3.9 %place_pairs.3 = bf16[2500,256]{1,0:T(8,128)(2,1)} custom-call(s32[4]{0:T(128)S(1)} %pad_add_fusion.s_ref, bf16[320,256]{1,0:T(8,128)(2,1)S(1)} %round_pairs.3.refs_0_, bf16[320,256]{1,0:T(8,128)(2,1)S(1)} %collective-permute-done.12.refs_1_, bf16[2500,256]{1,0:T(8,128)(2,1)S(1)} %place_pairs.2.refs_2_), custom_call_target="tpu_custom_call" | custom-call | flops 1 | bytes 1 | tf_op jit(solution)/shard_map/place_pairs/pallas_call | solution.py:86
  (15 shorter events, 0.0 us)
Async XLA Ops:
  0.1 1.7 %copy-start = (bf16[1024,1280]{1,0:T(8,128)(2,1)S(1)}, bf16[1024,1280]{1,0:T(8,128)(2,1)}, u32[]{:S(2)}) copy-start(bf16[1024,1280]{1,0:T(8,128)(2,1)} %v_ref.3) | copy-start | bytes 7864324
  1.8 0.7 copy-start.3
  2.5 0.7 copy-start.5
  3.2 5.9 %copy-start.2 = (bf16[320,2,2500]{2,1,0:T(2,128)(2,1)S(1)}, bf16[320,2,2500]{2,1,0:T(2,128)(2,1)}, u32[]{:S(2)}) copy-start(bf16[320,2,2500]{2,1,0:T(2,128)(2,1)} %t_ref) | copy-start | bytes 9600004
  6.1 11.8 %copy-start.1 = (bf16[1024,1280]{1,0:T(8,128)(2,1)S(1)}, bf16[1024,1280]{1,0:T(8,128)(2,1)}, u32[]{:S(2)}) copy-start(bf16[1024,1280]{1,0:T(8,128)(2,1)} %v_ref.3) | copy-start | bytes 7864324
  6.1 11.8 %copy-start.4 = (s32[1280]{0:T(1024)S(1)}, s32[1280]{0:T(1024)}, u32[]{:S(2)}) copy-start(s32[1280]{0:T(1024)} %param.7) | copy-start | bytes 15364
  6.1 31.8 %collective-permute-start = (bf16[1024,640]{1,0:T(8,128)(2,1)S(1)}, bf16[1024,640]{1,0:T(8,128)(2,1)S(1)}, u32[]{:S(2)}, u32[]{:S(2)}) collective-permute-start(bf16[1024,640]{1,0:T(8,128)(2,1)S(1)} %mask_integrals.1), channel_id=1, source_target_pairs={{0,16},{16,0},{1,17},{17,1},{2,18},{18,2},{3,19},{19,3},{4,20},{20... | collective-permute-start | bytes 3932168 | tf_op jit(solution)/shard_map/ppermute | solution.py:259
  14.3 13.6 %collective-permute-start.1 = (bf16[320,640]{1,0:T(8,128)(2,1)S(1)}, bf16[320,640]{1,0:T(8,128)(2,1)S(1)}, u32[]{:S(2)}, u32[]{:S(2)}) collective-permute-start(bf16[320,640]{1,0:T(8,128)(2,1)S(1)} %get-tuple-element.39), channel_id=1, source_target_pairs={{0,12},{4,0},{8,4},{12,8},{1,13},{5,1},{9,5},{13,9},{2,14},{6,2},{... | collective-permute-start | bytes 1228808 | tf_op jit(solution)/shard_map/ppermute | solution.py:259
  17.9 18.1 %collective-permute-start.2 = (bf16[320,640]{1,0:T(8,128)(2,1)S(1)}, bf16[320,640]{1,0:T(8,128)(2,1)S(1)}, u32[]{:S(2)}, u32[]{:S(2)}) collective-permute-start(bf16[320,640]{1,0:T(8,128)(2,1)S(1)} %get-tuple-element.40), channel_id=1, source_target_pairs={{0,4},{4,8},{8,12},{12,0},{1,5},{5,9},{9,13},{13,1},{2,6},{6,10},{... | collective-permute-start | bytes 1228808 | tf_op jit(solution)/shard_map/ppermute | solution.py:259
  37.9 7.5 %collective-permute-start.3 = (bf16[2112,640]{1,0:T(8,128)(2,1)S(1)}, bf16[2112,640]{1,0:T(8,128)(2,1)S(1)}, u32[]{:S(2)}, u32[]{:S(2)}) collective-permute-start(bf16[2112,640]{1,0:T(8,128)(2,1)S(1)} %get-tuple-element.43.own_here.refs_0_), channel_id=1, source_target_pairs={{0,1},{1,0},{2,3},{3,2},{4,5},{5,4},{6,7},{7,6},{8,9},{9,8},{10,11... | collective-permute-start | bytes 8110088 | tf_op jit(solution)/shard_map/ppermute | solution.py:262
  37.9 7.5 %collective-permute-start.5 = (bf16[1024,640]{1,0:T(8,128)(2,1)S(1)}, bf16[1024,640]{1,0:T(8,128)(2,1)S(1)}, u32[]{:S(2)}, u32[]{:S(2)}) collective-permute-start(bf16[1024,640]{1,0:T(8,128)(2,1)S(1)} %collective-permute-done.refs_5_.refs_3_), channel_id=1, source_target_pairs={{0,1},{1,0},{2,3},{3,2},{4,5},{5,4},{6,7},{7,6},{8,9},{9,8},{10,11... | collective-permute-start | bytes 3932168 | tf_op jit(solution)/shard_map/ppermute | solution.py:262
  38.4 7.0 %collective-permute-start.4 = (bf16[320,640]{1,0:T(8,128)(2,1)S(1)}, bf16[320,640]{1,0:T(8,128)(2,1)S(1)}, u32[]{:S(2)}, u32[]{:S(2)}) collective-permute-start(bf16[320,640]{1,0:T(8,128)(2,1)S(1)} %collective-permute-done.1.refs_1_), channel_id=1, source_target_pairs={{0,1},{1,0},{2,3},{3,2},{4,5},{5,4},{6,7},{7,6},{8,9},{9,8},{10,11... | collective-permute-start | bytes 1228808 | tf_op jit(solution)/shard_map/ppermute | solution.py:262
  38.4 11.3 %collective-permute-start.6 = (bf16[320,640]{1,0:T(8,128)(2,1)S(1)}, bf16[320,640]{1,0:T(8,128)(2,1)S(1)}, u32[]{:S(2)}, u32[]{:S(2)}) collective-permute-start(bf16[320,640]{1,0:T(8,128)(2,1)S(1)} %collective-permute-done.2.refs_0_), channel_id=1, source_target_pairs={{0,1},{1,0},{2,3},{3,2},{4,5},{5,4},{6,7},{7,6},{8,9},{9,8},{10,11... | collective-permute-start | bytes 1228808 | tf_op jit(solution)/shard_map/ppermute | solution.py:262
  38.9 21.2 %collective-permute-start.8 = (bf16[320,640]{1,0:T(8,128)(2,1)S(1)}, bf16[320,640]{1,0:T(8,128)(2,1)S(1)}, u32[]{:S(2)}, u32[]{:S(2)}) collective-permute-start(bf16[320,640]{1,0:T(8,128)(2,1)S(1)} %get-tuple-element.51), channel_id=1, source_target_pairs={{0,8},{4,12},{8,0},{12,4},{1,9},{5,13},{9,1},{13,5},{2,10},{6,14},... | collective-permute-start | bytes 1228808 | tf_op jit(solution)/shard_map/ppermute | solution.py:259
  52.4 9.8 %collective-permute-start.7 = (s16[320,512]{1,0:T(8,128)(2,1)S(1)}, s16[320,512]{1,0:T(8,128)(2,1)S(1)}, u32[]{:S(2)}, u32[]{:S(2)}) collective-permute-start(s16[320,512]{1,0:T(8,128)(2,1)S(1)} %get-tuple-element.50), channel_id=1, source_target_pairs={{0,16},{16,0},{1,17},{17,1},{2,18},{18,2},{3,19},{19,3},{4,20},{20... | collective-permute-start | bytes 983048 | tf_op jit(solution)/shard_map/ppermute | solution.py:259
  54.3 16.5 %collective-permute-start.13 = (s16[2,640,256]{2,1,0:T(8,128)(2,1)S(1)}, s16[2,640,256]{2,1,0:T(8,128)(2,1)S(1)}, u32[]{:S(2)}, u32[]{:S(2)}) collective-permute-start(s16[2,640,256]{2,1,0:T(8,128)(2,1)S(1)} %get-tuple-element.47), channel_id=1, source_target_pairs={{0,2},{1,3},{2,0},{3,1},{4,6},{5,7},{6,4},{7,5},{8,10},{9,11},{10,... | collective-permute-start | bytes 1966088 | tf_op jit(solution)/shard_map/ppermute | solution.py:265
  62.3 1.7 %collective-permute-start.9 = (bf16[320,640]{1,0:T(8,128)(2,1)S(1)}, bf16[320,640]{1,0:T(8,128)(2,1)S(1)}, u32[]{:S(2)}, u32[]{:S(2)}) collective-permute-start(bf16[320,640]{1,0:T(8,128)(2,1)S(1)} %collective-permute-done.8.refs_0_), channel_id=1, source_target_pairs={{0,1},{1,0},{2,3},{3,2},{4,5},{5,4},{6,7},{7,6},{8,9},{9,8},{10,11... | collective-permute-start | bytes 1228808 | tf_op jit(solution)/shard_map/ppermute | solution.py:262
  66.5 10.6 %collective-permute-start.10 = (s16[320,512]{1,0:T(8,128)(2,1)S(1)}, s16[320,512]{1,0:T(8,128)(2,1)S(1)}, u32[]{:S(2)}, u32[]{:S(2)}) collective-permute-start(s16[320,512]{1,0:T(8,128)(2,1)S(1)} %get-tuple-element.54), channel_id=1, source_target_pairs={{0,16},{16,0},{1,17},{17,1},{2,18},{18,2},{3,19},{19,3},{4,20},{20... | collective-permute-start | bytes 983048 | tf_op jit(solution)/shard_map/ppermute | solution.py:259
  71.7 12.3 %collective-permute-start.14 = (s16[640,256]{1,0:T(8,128)(2,1)S(1)}, s16[640,256]{1,0:T(8,128)(2,1)S(1)}, u32[]{:S(2)}, u32[]{:S(2)}) collective-permute-start(s16[640,256]{1,0:T(8,128)(2,1)S(1)} %get-tuple-element.59), channel_id=1, source_target_pairs={{0,16},{16,0},{1,17},{17,1},{2,18},{18,2},{3,19},{19,3},{4,20},{20... | collective-permute-start | bytes 983048 | tf_op jit(solution)/shard_map/ppermute | solution.py:259
  72.9 6.9 %collective-permute-start.16 = (s16[320,256]{1,0:T(8,128)(2,1)S(1)}, s16[320,256]{1,0:T(8,128)(2,1)S(1)}, u32[]{:S(2)}, u32[]{:S(2)}) collective-permute-start(s16[320,256]{1,0:T(8,128)(2,1)S(1)} %get-tuple-element.64), channel_id=1, source_target_pairs={{0,2},{1,3},{2,0},{3,1},{4,6},{5,7},{6,4},{7,5},{8,10},{9,11},{10,... | collective-permute-start | bytes 491528 | tf_op jit(solution)/shard_map/ppermute | solution.py:265
  77.9 8.0 %collective-permute-start.11 = (s16[320,256]{1,0:T(8,128)(2,1)S(1)}, s16[320,256]{1,0:T(8,128)(2,1)S(1)}, u32[]{:S(2)}, u32[]{:S(2)}) collective-permute-start(s16[320,256]{1,0:T(8,128)(2,1)S(1)} %get-tuple-element.56), channel_id=1, source_target_pairs={{0,2},{1,3},{2,0},{3,1},{4,6},{5,7},{6,4},{7,5},{8,10},{9,11},{10,... | collective-permute-start | bytes 491528 | tf_op jit(solution)/shard_map/ppermute | solution.py:265
  80.4 8.8 %collective-permute-start.17 = (bf16[320,256]{1,0:T(8,128)(2,1)S(1)}, bf16[320,256]{1,0:T(8,128)(2,1)S(1)}, u32[]{:S(2)}, u32[]{:S(2)}) collective-permute-start(bf16[320,256]{1,0:T(8,128)(2,1)S(1)} %round_pairs.5.refs_3_), channel_id=1, source_target_pairs={{0,12},{4,0},{8,4},{12,8},{1,13},{5,1},{9,5},{13,9},{2,14},{6,2},{... | collective-permute-start | bytes 491528 | tf_op jit(solution)/shard_map/ppermute | solution.py:259
  84.7 8.9 %collective-permute-start.15 = (bf16[320,256]{1,0:T(8,128)(2,1)S(1)}, bf16[320,256]{1,0:T(8,128)(2,1)S(1)}, u32[]{:S(2)}, u32[]{:S(2)}) collective-permute-start(bf16[320,256]{1,0:T(8,128)(2,1)S(1)} %get-tuple-element.61.refs_1_), channel_id=1, source_target_pairs={{0,4},{4,8},{8,12},{12,0},{1,5},{5,9},{9,13},{13,1},{2,6},{6,10},{... | collective-permute-start | bytes 491528 | tf_op jit(solution)/shard_map/ppermute | solution.py:259
  86.5 12.1 %collective-permute-start.12 = (bf16[320,256]{1,0:T(8,128)(2,1)S(1)}, bf16[320,256]{1,0:T(8,128)(2,1)S(1)}, u32[]{:S(2)}, u32[]{:S(2)}) collective-permute-start(bf16[320,256]{1,0:T(8,128)(2,1)S(1)} %round_pairs.3.refs_0_), channel_id=1, source_target_pairs={{0,8},{4,12},{8,0},{12,4},{1,9},{5,13},{9,1},{13,5},{2,10},{6,14},... | collective-permute-start | bytes 491528 | tf_op jit(solution)/shard_map/ppermute | solution.py:259

commit v6 on v5

--- a/solution.py
+++ b/solution.py
@@ -12,7 +12,7 @@
 TOP = 32000.0
 STEPS = 256.0
 CORES = 2
-TILE = 512
+TILE = 1264
 LANES = 128
 VMEM_BYTES = 32 * 2**20
 
@@ -140,39 +140,33 @@
         out_ref[...] = picked[k * chunk : (k + 1) * chunk]
 
 
-def keep_body(order, n, col_n, row_n, sub, s_ref, flat_ref, ab_ref, cd_ref, v_ref, both_ref, kept_ref):
+def keep_body(soon, late, n, col_n, row_n, sub, s_ref, flat_ref, ab_ref, cd_ref, v_ref, first_ref, later_ref, kept_ref):
     z = s_ref[1]
     half, k_here = kept_ref.shape
-    pairs = both_ref.shape[0] - half
-    place = lax.broadcasted_iota(jnp.int32, (pairs // (len(order) + 1), 1), 0)
+    pairs = first_ref.shape[0] - half
+    place = lax.broadcasted_iota(jnp.int32, (pairs // (len(soon) + 2), 1), 0)
     inside, turned = inside_columns(place, n, z)
-    picks = [inside if r == 0 else pair_columns(place, n, z, lax.rem(z + r, col_n), True) for r in order] + [turned]
-    picked = dot_nt(one_hot_rows(jnp.concatenate(picks, axis=0), flat_ref.shape[1]), flat_ref[...])
-    both_ref[:pairs] = picked.astype(jnp.bfloat16)
+    others = [pair_columns(place, n, z, lax.rem(z + r, col_n), True) for r in soon + late]
+    picks = jnp.concatenate([inside] + others[: len(soon)] + [turned] + others[len(soon) :], axis=0)
+    picked = dot_nt(one_hot_rows(picks, flat_ref.shape[1]), flat_ref[...]).astype(jnp.bfloat16)
     masked = masked_rows(0, row_n, sub, k_here, s_ref, ab_ref, cd_ref, v_ref)
-    both_ref[pairs:] = masked[:half]
+    first_ref[:pairs] = picked[:pairs]
+    first_ref[pairs:] = masked[:half]
+    later_ref[...] = picked[pairs:]
     kept_ref[...] = masked[half:]
 
 
-def sum_body(first, count, groups, y_first, s_ref, own_here, own_there, *refs):
-    away, refs = refs[: 2 * count], refs[2 * count :]
+def sum_body(place, turned, groups, y_first, s_ref, own_here, own_there, away_here, away_there, first_there, *refs):
     keeps, passes, outs = refs[:groups], refs[groups : 2 * groups - 1], refs[2 * groups - 1 :]
-    high, tall = outs[-1].shape[-2:]
+    chunk, tall = outs[-1].shape[-2:]
     tall = tall if y_first else tall // 2
-    chunk = high // count
-    pairs = own_here.shape[0] - 2 * tall
-
-    def rows(ref):
-        return ref[pairs - chunk : pairs] if ref.shape[0] > chunk else ref[...]
-
-    mine = slice(first * chunk, (first + count) * chunk)
-    tr = jnp.concatenate([rows(ref) for ref in away[:count]], axis=0)
-    tro = jnp.concatenate([rows(ref) for ref in away[count:]], axis=0)
-    left = jnp.concatenate([own_here[mine], own_there[mine], tr, tro], axis=1)
+    mine = slice(place * chunk, (place + 1) * chunk)
+    other = slice(turned * chunk, (turned + 1) * chunk)
+    left = jnp.concatenate([own_here[mine], own_there[mine], away_here[other], away_there[other]], axis=1)
     for g in range(groups):
         start = keeps[g].shape[0] - 2 * tall
         a = keeps[g][start:]
-        b = own_there[pairs:] if g == 0 else passes[g - 1][: 2 * tall]
+        b = first_there[first_there.shape[0] - 2 * tall :] if g == 0 else passes[g - 1][: 2 * tall]
         total = dot_nt(left, jnp.concatenate([a, b, -a, -b], axis=1))
         if y_first:
             outs[0][g] = encode(total[:, :tall])
@@ -202,14 +196,11 @@
     own_ref[...] = total[:, tall:]
 
 
-def round_body(count, s_ref, kept_ref, *refs):
+def round_body(s_ref, kept_ref, *refs):
     total = kept_ref[...]
-    for ref in refs[:-count]:
+    for ref in refs[:-1]:
         total = total + decode(ref[...])
-    rounded = total.astype(jnp.bfloat16)
-    chunk = rounded.shape[0] // count
-    for k, out_ref in enumerate(refs[-count:]):
-        out_ref[...] = rounded[k * chunk : (k + 1) * chunk]
+    refs[-1][...] = total.astype(jnp.bfloat16)
 
 
 def place_body(order, n, col_n, before, s_ref, *refs):
@@ -248,10 +239,8 @@
     chunk = -(-((n * n + 1) // 2 + 1) // 16) * 16
     far = col_n // 2
     near = [r for r in range(1, col_n) if r != far]
-    half = (len(near) + 1) // 2
-    groups = [([0] + near[:half], True), (near[half:], False), ([far], False)]
-    groups = [(group, y_first) for group, y_first in groups if group]
-    order = [0] + near + [far]
+    soon, late = [far] + near[:1], near[1:]
+    chunks = [(0, True)] + [(r, False) for r in soon] + [(r, True) for r in late]
     bf16, i16, f32 = jnp.bfloat16, jnp.int16, jnp.float32
 
     def shift(array, axis, by):
@@ -280,83 +269,86 @@
         kept[by] = shift(gone, "row", -by)
 
     amplitudes, _ = lax.optimization_barrier((amplitudes, gone))
-    sent_order = near + [far]
     flat, *sent = call(
         "send_columns",
-        functools.partial(send_body, sent_order, n, col_n),
+        functools.partial(send_body, soon + late, n, col_n),
         scalars,
         [amplitudes],
-        [((k_here, -(-columns // LANES) * LANES), bf16)] + [((chunk, k_here), bf16)] * len(sent_order),
+        [((k_here, -(-columns // LANES) * LANES), bf16)] + [((chunk, k_here), bf16)] * (col_n - 1),
     )
-    away = {r: shift(s, "col", -r) for r, s in zip(near, sent)}
-
-    both, kept[0] = call(
+    away = {r: shift(value, "col", -r) for r, value in zip(soon, sent)}
+
+    first, later, kept[0] = call(
         "keep_columns",
-        functools.partial(keep_body, order, n, col_n, row_n, sub),
+        functools.partial(keep_body, soon, late, n, col_n, row_n, sub),
         scalars,
         [flat, ab_row, cd_row, integrals],
-        [(((col_n + 1) * chunk + 2 * tall, k_here), bf16), ((2 * tall, k_here), bf16)],
+        [
+            (((len(soon) + 2) * chunk + 2 * tall, k_here), bf16),
+            ((len(late) * chunk, k_here), bf16),
+            ((2 * tall, k_here), bf16),
+        ],
     )
-    far_sent, away = lax.optimization_barrier((sent[-1], away))
-    behind, kept[1:], *arrived = lax.optimization_barrier((both, kept[1:], *[away[r] for r in near]))
-    away_there = {r: other_core(a) for r, a in zip(near, arrived)}
-    both_there = other_core(behind)
-    away[far] = shift(far_sent, "col", -far)
+    away, kept[1:], first, *sent = lax.optimization_barrier((away, kept[1:], first, *sent[len(soon) :]))
+    first_there = other_core(first)
     passed = [other_core(a) for a in kept[1:]]
-
-    rounded, arrived = {}, []
-    for group, y_first in groups:
-        first, count = order.index(group[0]), len(group)
-        high = count * chunk
-        if far in group:
-            _, away[far] = lax.optimization_barrier((arrived, away[far]))
-            away_there[far] = other_core(away[far])
-        here = [both if r == 0 else away[r] for r in group]
-        there = [both_there if r == 0 else away_there[r] for r in group]
-        if group == groups[1][0]:
-            _, here[0] = lax.optimization_barrier((sums[0], here[0]))
+    away_there = {r: other_core(away[r]) for r in soon}
+    for r, value in zip(late, sent):
+        away[r] = shift(value, "col", -r)
+
+    rounded = {}
+    before, later_there = [], None
+    for place, (r, y_first) in enumerate(chunks):
+        if r in late and later_there is None:
+            _, later, *arrived = lax.optimization_barrier((before, later, *[away[q] for q in late]))
+            for q, value in zip(late, arrived):
+                away[q] = value
+                away_there[q] = other_core(value)
+            later_there = other_core(later)
+        if r in late:
+            own, at, turned = (later, later_there), late.index(r), 0
+        else:
+            own, at, turned = (first, first_there), place, len(soon) + 1 if r == 0 else 0
+        others = (first, first_there) if r == 0 else (away[r], away_there[r])
         if y_first:
-            shapes = [((row_n, high, tall), i16), ((row_n, high, tall), f32)]
-        else:
-            shapes = [((high, 2 * tall), i16)] * (row_n - 1) + [((high, 2 * tall), f32)]
+            shapes = [((row_n, chunk, tall), i16), ((row_n, chunk, tall), f32)]
+        else:
+            shapes = [((chunk, 2 * tall), i16)] * (row_n - 1) + [((chunk, 2 * tall), f32)]
         sums = call(
             "sum_pairs",
-            functools.partial(sum_body, first, count, row_n, y_first),
+            functools.partial(sum_body, at, turned, row_n, y_first),
             scalars,
-            [both, both_there] + here + there + kept + passed,
+            [*own, *others, first_there, *kept, *passed],
             shapes,
         )
         if y_first:
-            own_sum, *others = call(
+            crossed = [other_y(sums[0])]
+        else:
+            crossed = [shift(value, "row", by + 1) for by, value in enumerate(sums[:-1])]
+        before += crossed if place < 2 else sums[:1]
+        if y_first:
+            own_sum, *coded = call(
                 "add_other_y",
                 add_y_body,
                 scalars,
-                [sums[1], other_y(sums[0])],
-                [((high, tall), f32)] + [((high, tall), i16)] * (row_n - 1),
+                [sums[1]] + crossed,
+                [((chunk, tall), f32)] + [((chunk, tall), i16)] * (row_n - 1),
             )
-            last = [shift(other, "row", by + 1) for by, other in enumerate(others)]
-        else:
-            arrived = [shift(coded, "row", by + 1) for by, coded in enumerate(sums[:-1])]
+            last = [shift(value, "row", by + 1) for by, value in enumerate(coded)]
+        else:
             coded, own_sum = call(
                 "add_other_x",
                 add_x_body,
                 scalars,
-                [sums[-1]] + arrived,
-                [((high, tall), i16), ((high, tall), f32)],
+                [sums[-1]] + crossed,
+                [((chunk, tall), i16), ((chunk, tall), f32)],
             )
             last = [other_y(coded)]
-        mine = call(
-            "round_pairs",
-            functools.partial(round_body, count),
-            scalars,
-            [own_sum] + last,
-            [((chunk, tall), bf16)] * count,
-        )
-        for r, value in zip(group, mine):
-            rounded[r] = [value] if r == 0 else [value, shift(value, "col", r)]
+        (mine,) = call("round_pairs", round_body, scalars, [own_sum] + last, [((chunk, tall), bf16)])
+        rounded[r] = [mine] if r == 0 else [mine, shift(mine, "col", r)]
 
     done = None
-    for group in ([0] + near, [far]):
+    for group in ([0] + soon, late):
         sources = [value for r in group for value in rounded[r]]
         tile = (TILE, tall), lambda g, s: (g, 0)
         sources += [] if done is None else [(done, *tile)]

time: 103 us -> 107 us (1.039)
  waiting for transfers between devices: 31.8 us -> 39.8 us
  starting transfers between devices: 27.2 us -> 24 us
    ppermute x10 -> x11, waiting for transfers between devices: 24 us -> 28.8 us  [shift(): lax.ppermute(array, axis, [(i, (i + by) % count) for i in range(count)])]
    ppermute x10 -> x11, starting transfers between devices: 21.1 us -> 17.1 us  [shift(): lax.ppermute(array, axis, [(i, (i + by) % count) for i in range(count)])]
    ppermute x3 -> x4, waiting for transfers between devices: 2.4 us -> 5.63 us  [other_y(): return lax.ppermute(array, 'depth', [(i, i ^ 2) for i in range(depth_n)])]
    ppermute x3 -> x4, starting transfers between devices: 5.12 us -> 5.33 us  [other_y(): return lax.ppermute(array, 'depth', [(i, i ^ 2) for i in range(depth_n)])]
    pallas_call x14 -> x17, Pallas kernels: 40.1 us -> 40 us  [call(): pl.pallas_call(body, name=name, out_shape=shapes, compiler_params=pltpu.C...]
    ppermute x5 -> x6, waiting for transfers between devices: 5.38 us -> 5.38 us  [other_core(): return lax.ppermute(array, 'depth', [(i, i ^ 1) for i in range(depth_n)])]
  transfers between devices with their start and end apart: 18 -> 21, of which waited for: 11 -> 10; matrix products, arithmetic and copies ran while one was open for 0% -> 0% of each run, Pallas kernels for 33% -> 32%
where the time goes in v6:
time: 107 us
  Pallas kernels  40 us (37%)
  waiting for transfers between devices  39.8 us (37%)
  starting transfers between devices  24 us (22%)
  local copies, waits for them, and re-layouts  3.14 us (3%)
    pallas_call x17, Pallas kernels, call(): pl.pallas_call(body, name=name, out_shape=shapes, compiler_params=pltpu.C...  40 us
    ppermute x11, waiting for transfers between devices, shift(): lax.ppermute(array, axis, [(i, (i + by) % count) for i in range(count)])  28.8 us
    ppermute x11, starting transfers between devices, shift(): lax.ppermute(array, axis, [(i, (i + by) % count) for i in range(count)])  17.1 us
    ppermute x4, waiting for transfers between devices, other_y(): return lax.ppermute(array, 'depth', [(i, i ^ 2) for i in range(depth_n)])  5.63 us
    ppermute x6, waiting for transfers between devices, other_core(): return lax.ppermute(array, 'depth', [(i, i ^ 1) for i in range(depth_n)])  5.38 us
    ppermute x4, starting transfers between devices, other_y(): return lax.ppermute(array, 'depth', [(i, i ^ 2) for i in range(depth_n)])  5.33 us
    unnamed x12, local copies, waits for them, and re-layouts  3.14 us
  transfers between devices with their start and end apart: 21, of which 10 were waited for; matrix products, arithmetic and copies ran while one was open for 0% of the time, Pallas kernels for 32%

profile of v6, /device:TPU:0, one launch (start us, length us, event | category | flops | bytes accessed | tf_op | source)
XLA Modules:
  0.0 107.2 jit_solution(11483760024778999706)
XLA Ops:
  0.0 0.1 pad_add_fusion.s_ref
  0.1 1.7 %copy-done = bf16[1024,1280]{1,0:T(8,128)(2,1)S(1)} copy-done((bf16[1024,1280]{1,0:T(8,128)(2,1)S(1)}, bf16[1024,1280]{1,0:T(8,128)(2,1)}, u32[]{:S(2)}) %copy-start) | copy-done | bytes 2621464
  1.8 0.7 copy-done.3
  2.5 0.7 copy-done.5
  3.2 2.9 %mask_integrals.1 = bf16[1024,640]{1,0:T(8,128)(2,1)S(1)} custom-call(s32[4]{0:T(128)S(1)} %pad_add_fusion.s_ref, s32[8,128]{1,0:T(8,128)S(1)} %bitcast.9, s32[10,128]{1,0:T(8,128)S(1)} %bitcast.7, bf16[1024,1280]{1,0:T(8,128)(2,1)S(1)} %copy-done), custom_call_target="tpu_custom_call" | custom-call | flops 1 | bytes 1 | tf_op jit(solution)/shard_map/mask_integrals/pallas_call | solution.py:86
  6.1 3.0 %collective-permute-start.2 = (bf16[1024,640]{1,0:T(8,128)(2,1)S(1)}, bf16[1024,640]{1,0:T(8,128)(2,1)S(1)}, u32[]{:S(2)}, u32[]{:S(2)}) collective-permute-start(bf16[1024,640]{1,0:T(8,128)(2,1)S(1)} %mask_integrals.1), channel_id=1, source_target_pairs={{0,16},{16,0},{1,17},{17,1},{2,18},{18,2},{3,19},{19,3},{4,20},{20... | collective-permute-start | bytes 3932168 | tf_op jit(solution)/shard_map/ppermute | solution.py:248
  9.1 5.1 %send_columns.1 = (bf16[640,2560]{1,0:T(8,128)(2,1)S(1)}, bf16[320,640]{1,0:T(8,128)(2,1)S(1)}, bf16[320,640]{1,0:T(8,128)(2,1)S(1)}, bf16[320,640]{1,0:T(8,128)(2,1)S(1)}) custom-call(s32[4]{0:T(128)S(1)} %pad_add_fusion.s_ref, bf16[320,2,2500]{2,1,0:T(2,128)(2,1)S(1)} %copy-done.2), custom_call_target="tpu_custom_call" | custom-call | flops 1 | bytes 1 | tf_op jit(solution)/shard_map/send_columns/pallas_call | solution.py:86
  14.3 3.8 %collective-permute-start = (bf16[320,640]{1,0:T(8,128)(2,1)S(1)}, bf16[320,640]{1,0:T(8,128)(2,1)S(1)}, u32[]{:S(2)}, u32[]{:S(2)}) collective-permute-start(bf16[320,640]{1,0:T(8,128)(2,1)S(1)} %get-tuple-element.37), channel_id=1, source_target_pairs={{0,12},{4,0},{8,4},{12,8},{1,13},{5,1},{9,5},{13,9},{2,14},{6,2},{... | collective-permute-start | bytes 1228808 | tf_op jit(solution)/shard_map/ppermute | solution.py:248
  18.1 9.5 %keep_columns.1 = (bf16[1792,640]{1,0:T(8,128)(2,1)S(1)}, bf16[320,640]{1,0:T(8,128)(2,1)S(1)}, bf16[512,640]{1,0:T(8,128)(2,1)S(1)}) custom-call(s32[4]{0:T(128)S(1)} %pad_add_fusion.s_ref, bf16[640,2560]{1,0:T(8,128)(2,1)S(1)} %get-tuple-element.39.flat_ref, s32[8,128]{1,0:T(8,128)S(1)} %bitcast.10, s32[10,128]{1,0:T(8,128)S(1)} %bitcast.8, ...), custom_call_target="tpu_custom_call" | custom-call | flops 1 | bytes 1 | tf_op jit(solution)/shard_map/keep_columns/pallas_call | solution.py:86
  27.6 0.4 collective-permute-done.away_here
  28.0 16.0 %collective-permute-done.1.away_here = bf16[320,640]{1,0:T(8,128)(2,1)S(1)} collective-permute-done((bf16[320,640]{1,0:T(8,128)(2,1)S(1)}, bf16[320,640]{1,0:T(8,128)(2,1)S(1)}, u32[]{:S(2)}, u32[]{:S(2)}) %collective-permute-start.1) | collective-permute-done | bytes 409632 | tf_op jit(solution)/shard_map/ppermute | solution.py:248
  44.0 0.5 collective-permute-start.4
  44.5 0.5 collective-permute-start.8
  45.0 0.8 collective-permute-start.9
  45.8 5.0 %collective-permute-done.6.away_there = bf16[320,640]{1,0:T(8,128)(2,1)S(1)} collective-permute-done((bf16[320,640]{1,0:T(8,128)(2,1)S(1)}, bf16[320,640]{1,0:T(8,128)(2,1)S(1)}, u32[]{:S(2)}, u32[]{:S(2)}) %collective-permute-start.6) | collective-permute-done | bytes 409632 | tf_op jit(solution)/shard_map/ppermute | solution.py:251
  50.9 2.6 %sum_pairs.5 = (s16[320,512]{1,0:T(8,128)(2,1)S(1)}, f32[320,512]{1,0:T(8,128)S(1)}) custom-call(s32[4]{0:T(128)S(1)} %pad_add_fusion.s_ref, bf16[1792,640]{1,0:T(8,128)(2,1)S(1)} %get-tuple-element.42.own_here.away_here, bf16[1792,640]{1,0:T(8,128)(2,1)S(1)} %collective-permute-done.3.own_there.away_there.first_there, ...), custom_call_target="tpu_custom_call" | custom-call | flops 1 | bytes 1 | tf_op jit(solution)/shard_map/sum_pairs/pallas_call | solution.py:86
  53.4 0.6 collective-permute-start.7
  54.0 2.5 %sum_pairs.4 = (s16[2,320,256]{2,1,0:T(8,128)(2,1)S(1)}, f32[2,320,256]{2,1,0:T(8,128)S(1)}) custom-call(s32[4]{0:T(128)S(1)} %pad_add_fusion.s_ref, bf16[1792,640]{1,0:T(8,128)(2,1)S(1)} %get-tuple-element.42.own_here.away_here, bf16[1792,640]{1,0:T(8,128)(2,1)S(1)} %collective-permute-done.3.own_there.away_there.first_there, ...), custom_call_target="tpu_custom_call" | custom-call | flops 1 | bytes 1 | tf_op jit(solution)/shard_map/sum_pairs/pallas_call | solution.py:86
  56.6 1.6 %collective-permute-start.5 = (s16[2,320,256]{2,1,0:T(8,128)(2,1)S(1)}, s16[2,320,256]{2,1,0:T(8,128)(2,1)S(1)}, u32[]{:S(2)}, u32[]{:S(2)}) collective-permute-start(s16[2,320,256]{2,1,0:T(8,128)(2,1)S(1)} %get-tuple-element.45), channel_id=1, source_target_pairs={{0,2},{1,3},{2,0},{3,1},{4,6},{5,7},{6,4},{7,5},{8,10},{9,11},{10,... | collective-permute-start | bytes 983048 | tf_op jit(solution)/shard_map/ppermute | solution.py:254
  58.2 2.5 %sum_pairs.6 = (s16[320,512]{1,0:T(8,128)(2,1)S(1)}, f32[320,512]{1,0:T(8,128)S(1)}) custom-call(s32[4]{0:T(128)S(1)} %pad_add_fusion.s_ref, bf16[1792,640]{1,0:T(8,128)(2,1)S(1)} %get-tuple-element.42.own_here.away_here, bf16[1792,640]{1,0:T(8,128)(2,1)S(1)} %collective-permute-done.3.own_there.away_there.first_there, ...), custom_call_target="tpu_custom_call" | custom-call | flops 1 | bytes 1 | tf_op jit(solution)/shard_map/sum_pairs/pallas_call | solution.py:86
  60.7 2.6 %collective-permute-done.7.refs_0_ = s16[320,512]{1,0:T(8,128)(2,1)S(1)} collective-permute-done((s16[320,512]{1,0:T(8,128)(2,1)S(1)}, s16[320,512]{1,0:T(8,128)(2,1)S(1)}, u32[]{:S(2)}, u32[]{:S(2)}) %collective-permute-start.7) | collective-permute-done | bytes 327712 | tf_op jit(solution)/shard_map/ppermute | solution.py:248
  63.3 2.8 %collective-permute-done.5.coded_ref = s16[2,320,256]{2,1,0:T(8,128)(2,1)S(1)} collective-permute-done((s16[2,320,256]{2,1,0:T(8,128)(2,1)S(1)}, s16[2,320,256]{2,1,0:T(8,128)(2,1)S(1)}, u32[]{:S(2)}, u32[]{:S(2)}) %collective-permute-start.5) | collective-permute-done | bytes 327712 | tf_op jit(solution)/shard_map/ppermute | solution.py:254
  66.1 0.5 collective-permute-start.11
  66.6 1.5 %collective-permute-start.18 = (s16[320,512]{1,0:T(8,128)(2,1)S(1)}, s16[320,512]{1,0:T(8,128)(2,1)S(1)}, u32[]{:S(2)}, u32[]{:S(2)}) collective-permute-start(s16[320,512]{1,0:T(8,128)(2,1)S(1)} %get-tuple-element.49), channel_id=1, source_target_pairs={{0,16},{16,0},{1,17},{17,1},{2,18},{18,2},{3,19},{19,3},{4,20},{20... | collective-permute-start | bytes 983048 | tf_op jit(solution)/shard_map/ppermute | solution.py:248
  68.1 0.3 collective-permute-done.11.away_there
  68.4 2.5 %sum_pairs.7 = (s16[2,320,256]{2,1,0:T(8,128)(2,1)S(1)}, f32[2,320,256]{2,1,0:T(8,128)S(1)}) custom-call(s32[4]{0:T(128)S(1)} %pad_add_fusion.s_ref, bf16[320,640]{1,0:T(8,128)(2,1)S(1)} %get-tuple-element.52.own_here, bf16[320,640]{1,0:T(8,128)(2,1)S(1)} %collective-permute-done.10.own_there, bf16[320,640]{1,0:T(8,128)(2,1)S(1)} %collective-permute-done.9.away_here, ...), custom_call_target="tpu_custom_call" | custom-call | flops 1 | bytes 1 | tf_op jit(solution)/shard_map/sum_pairs/pallas_call | solution.py:86
  71.0 1.6 %collective-permute-start.12 = (s16[2,320,256]{2,1,0:T(8,128)(2,1)S(1)}, s16[2,320,256]{2,1,0:T(8,128)(2,1)S(1)}, u32[]{:S(2)}, u32[]{:S(2)}) collective-permute-start(s16[2,320,256]{2,1,0:T(8,128)(2,1)S(1)} %get-tuple-element.55), channel_id=1, source_target_pairs={{0,2},{1,3},{2,0},{3,1},{4,6},{5,7},{6,4},{7,5},{8,10},{9,11},{10,... | collective-permute-start | bytes 983048 | tf_op jit(solution)/shard_map/ppermute | solution.py:254
  72.5 3.7 %collective-permute-done.18.refs_0_ = s16[320,512]{1,0:T(8,128)(2,1)S(1)} collective-permute-done((s16[320,512]{1,0:T(8,128)(2,1)S(1)}, s16[320,512]{1,0:T(8,128)(2,1)S(1)}, u32[]{:S(2)}, u32[]{:S(2)}) %collective-permute-start.18) | collective-permute-done | bytes 327712 | tf_op jit(solution)/shard_map/ppermute | solution.py:248
  76.2 0.7 add_other_x.3
  77.0 1.6 %collective-permute-start.19 = (s16[320,256]{1,0:T(8,128)(2,1)S(1)}, s16[320,256]{1,0:T(8,128)(2,1)S(1)}, u32[]{:S(2)}, u32[]{:S(2)}) collective-permute-start(s16[320,256]{1,0:T(8,128)(2,1)S(1)} %get-tuple-element.66), channel_id=1, source_target_pairs={{0,2},{1,3},{2,0},{3,1},{4,6},{5,7},{6,4},{7,5},{8,10},{9,11},{10,... | collective-permute-start | bytes 491528 | tf_op jit(solution)/shard_map/ppermute | solution.py:254
  78.6 0.7 add_other_x.2
  79.3 0.6 collective-permute-start.16
  79.9 1.7 %collective-permute-done.12.coded_ref = s16[2,320,256]{2,1,0:T(8,128)(2,1)S(1)} collective-permute-done((s16[2,320,256]{2,1,0:T(8,128)(2,1)S(1)}, s16[2,320,256]{2,1,0:T(8,128)(2,1)S(1)}, u32[]{:S(2)}, u32[]{:S(2)}) %collective-permute-start.12) | collective-permute-done | bytes 327712 | tf_op jit(solution)/shard_map/ppermute | solution.py:254
  81.6 0.7 add_other_y.2
  82.3 1.6 %collective-permute-start.13 = (s16[320,256]{1,0:T(8,128)(2,1)S(1)}, s16[320,256]{1,0:T(8,128)(2,1)S(1)}, u32[]{:S(2)}, u32[]{:S(2)}) collective-permute-start(s16[320,256]{1,0:T(8,128)(2,1)S(1)} %get-tuple-element.57), channel_id=1, source_target_pairs={{0,16},{16,0},{1,17},{17,1},{2,18},{18,2},{3,19},{19,3},{4,20},{20... | collective-permute-start | bytes 491528 | tf_op jit(solution)/shard_map/ppermute | solution.py:248
  83.9 0.7 add_other_y.3
  84.6 0.6 collective-permute-start.15
  85.2 0.6 round_pairs.7.refs_3_
  85.8 0.9 collective-permute-start.20
  86.7 1.1 %collective-permute-done.16.refs_0_ = s16[320,256]{1,0:T(8,128)(2,1)S(1)} collective-permute-done((s16[320,256]{1,0:T(8,128)(2,1)S(1)}, s16[320,256]{1,0:T(8,128)(2,1)S(1)}, u32[]{:S(2)}, u32[]{:S(2)}) %collective-permute-start.16) | collective-permute-done | bytes 163872 | tf_op jit(solution)/shard_map/ppermute | solution.py:254
  87.8 0.6 round_pairs.6.refs_1_
  88.4 2.4 %collective-permute-start.17 = (bf16[320,256]{1,0:T(8,128)(2,1)S(1)}, bf16[320,256]{1,0:T(8,128)(2,1)S(1)}, u32[]{:S(2)}, u32[]{:S(2)}) collective-permute-start(bf16[320,256]{1,0:T(8,128)(2,1)S(1)} %round_pairs.6.refs_1_), channel_id=1, source_target_pairs={{0,8},{4,12},{8,0},{12,4},{1,9},{5,13},{9,1},{13,5},{2,10},{6,14},... | collective-permute-start | bytes 491528 | tf_op jit(solution)/shard_map/ppermute | solution.py:248
  90.8 0.6 round_pairs.4.refs_0_
  91.4 1.9 %collective-permute-start.14 = (bf16[320,256]{1,0:T(8,128)(2,1)S(1)}, bf16[320,256]{1,0:T(8,128)(2,1)S(1)}, u32[]{:S(2)}, u32[]{:S(2)}) collective-permute-start(bf16[320,256]{1,0:T(8,128)(2,1)S(1)} %round_pairs.4.refs_0_), channel_id=1, source_target_pairs={{0,12},{4,0},{8,4},{12,8},{1,13},{5,1},{9,5},{13,9},{2,14},{6,2},{... | collective-permute-start | bytes 491528 | tf_op jit(solution)/shard_map/ppermute | solution.py:248
  93.3 0.6 round_pairs.5.refs_0_
  93.9 6.2 %collective-permute-done.17.refs_2_ = bf16[320,256]{1,0:T(8,128)(2,1)S(1)} collective-permute-done((bf16[320,256]{1,0:T(8,128)(2,1)S(1)}, bf16[320,256]{1,0:T(8,128)(2,1)S(1)}, u32[]{:S(2)}, u32[]{:S(2)}) %collective-permute-start.17) | collective-permute-done | bytes 163872 | tf_op jit(solution)/shard_map/ppermute | solution.py:248
  100.1 4.2 %place_pairs.2.refs_2_ = bf16[2500,256]{1,0:T(8,128)(2,1)S(1)} custom-call(s32[4]{0:T(128)S(1)} %pad_add_fusion.s_ref, bf16[320,256]{1,0:T(8,128)(2,1)S(1)} %round_pairs.5.refs_0_, bf16[320,256]{1,0:T(8,128)(2,1)S(1)} %round_pairs.6.refs_1_, bf16[320,256]{1,0:T(8,128)(2,1)S(1)} %collective-permute-done.17.refs_2_, bf16[320,256]{1,0:T(8,128)(2,1)S(1)} %round_pairs.7.refs_3_, ...), custom_call_target="tpu_custom_call" | custom-call | flops 1 | bytes 1 | tf_op jit(solution)/shard_map/place_pairs/pallas_call | solution.py:86
  104.3 2.9 %place_pairs.3 = bf16[2500,256]{1,0:T(8,128)(2,1)} custom-call(s32[4]{0:T(128)S(1)} %pad_add_fusion.s_ref, bf16[320,256]{1,0:T(8,128)(2,1)S(1)} %round_pairs.4.refs_0_, bf16[320,256]{1,0:T(8,128)(2,1)S(1)} %collective-permute-done.14.refs_1_, bf16[2500,256]{1,0:T(8,128)(2,1)S(1)} %place_pairs.2.refs_2_), custom_call_target="tpu_custom_call" | custom-call | flops 1 | bytes 1 | tf_op jit(solution)/shard_map/place_pairs/pallas_call | solution.py:86
  (24 shorter events, 0.1 us)
Async XLA Ops:
  0.1 1.7 %copy-start = (bf16[1024,1280]{1,0:T(8,128)(2,1)S(1)}, bf16[1024,1280]{1,0:T(8,128)(2,1)}, u32[]{:S(2)}) copy-start(bf16[1024,1280]{1,0:T(8,128)(2,1)} %v_ref.3) | copy-start | bytes 7864324
  1.8 0.7 copy-start.3
  2.5 0.7 copy-start.5
  3.2 5.9 %copy-start.2 = (bf16[320,2,2500]{2,1,0:T(2,128)(2,1)S(1)}, bf16[320,2,2500]{2,1,0:T(2,128)(2,1)}, u32[]{:S(2)}) copy-start(bf16[320,2,2500]{2,1,0:T(2,128)(2,1)} %t_ref) | copy-start | bytes 9600004
  6.1 12.0 %copy-start.1 = (bf16[1024,1280]{1,0:T(8,128)(2,1)S(1)}, bf16[1024,1280]{1,0:T(8,128)(2,1)}, u32[]{:S(2)}) copy-start(bf16[1024,1280]{1,0:T(8,128)(2,1)} %v_ref.3) | copy-start | bytes 7864324
  6.1 12.0 %copy-start.4 = (s32[1280]{0:T(1024)S(1)}, s32[1280]{0:T(1024)}, u32[]{:S(2)}) copy-start(s32[1280]{0:T(1024)} %param.7) | copy-start | bytes 15364
  6.1 37.9 %collective-permute-start.2 = (bf16[1024,640]{1,0:T(8,128)(2,1)S(1)}, bf16[1024,640]{1,0:T(8,128)(2,1)S(1)}, u32[]{:S(2)}, u32[]{:S(2)}) collective-permute-start(bf16[1024,640]{1,0:T(8,128)(2,1)S(1)} %mask_integrals.1), channel_id=1, source_target_pairs={{0,16},{16,0},{1,17},{17,1},{2,18},{18,2},{3,19},{19,3},{4,20},{20... | collective-permute-start | bytes 3932168 | tf_op jit(solution)/shard_map/ppermute | solution.py:248
  14.3 13.7 %collective-permute-start = (bf16[320,640]{1,0:T(8,128)(2,1)S(1)}, bf16[320,640]{1,0:T(8,128)(2,1)S(1)}, u32[]{:S(2)}, u32[]{:S(2)}) collective-permute-start(bf16[320,640]{1,0:T(8,128)(2,1)S(1)} %get-tuple-element.37), channel_id=1, source_target_pairs={{0,12},{4,0},{8,4},{12,8},{1,13},{5,1},{9,5},{13,9},{2,14},{6,2},{... | collective-permute-start | bytes 1228808 | tf_op jit(solution)/shard_map/ppermute | solution.py:248
  18.1 25.9 %collective-permute-start.1 = (bf16[320,640]{1,0:T(8,128)(2,1)S(1)}, bf16[320,640]{1,0:T(8,128)(2,1)S(1)}, u32[]{:S(2)}, u32[]{:S(2)}) collective-permute-start(bf16[320,640]{1,0:T(8,128)(2,1)S(1)} %get-tuple-element.38), channel_id=1, source_target_pairs={{0,8},{4,12},{8,0},{12,4},{1,9},{5,13},{9,1},{13,5},{2,10},{6,14},... | collective-permute-start | bytes 1228808 | tf_op jit(solution)/shard_map/ppermute | solution.py:248
  44.0 6.9 %collective-permute-start.3 = (bf16[1792,640]{1,0:T(8,128)(2,1)S(1)}, bf16[1792,640]{1,0:T(8,128)(2,1)S(1)}, u32[]{:S(2)}, u32[]{:S(2)}) collective-permute-start(bf16[1792,640]{1,0:T(8,128)(2,1)S(1)} %get-tuple-element.42.own_here.away_here), channel_id=1, source_target_pairs={{0,1},{1,0},{2,3},{3,2},{4,5},{5,4},{6,7},{7,6},{8,9},{9,8},{10,11... | collective-permute-start | bytes 6881288 | tf_op jit(solution)/shard_map/ppermute | solution.py:251
  44.0 6.9 %collective-permute-start.4 = (bf16[1024,640]{1,0:T(8,128)(2,1)S(1)}, bf16[1024,640]{1,0:T(8,128)(2,1)S(1)}, u32[]{:S(2)}, u32[]{:S(2)}) collective-permute-start(bf16[1024,640]{1,0:T(8,128)(2,1)S(1)} %collective-permute-done.2.refs_1_), channel_id=1, source_target_pairs={{0,1},{1,0},{2,3},{3,2},{4,5},{5,4},{6,7},{7,6},{8,9},{9,8},{10,11... | collective-permute-start | bytes 3932168 | tf_op jit(solution)/shard_map/ppermute | solution.py:251
  44.5 6.4 %collective-permute-start.6 = (bf16[320,640]{1,0:T(8,128)(2,1)S(1)}, bf16[320,640]{1,0:T(8,128)(2,1)S(1)}, u32[]{:S(2)}, u32[]{:S(2)}) collective-permute-start(bf16[320,640]{1,0:T(8,128)(2,1)S(1)} %collective-permute-done.1.away_here), channel_id=1, source_target_pairs={{0,1},{1,0},{2,3},{3,2},{4,5},{5,4},{6,7},{7,6},{8,9},{9,8},{10,11... | collective-permute-start | bytes 1228808 | tf_op jit(solution)/shard_map/ppermute | solution.py:251
  44.5 13.7 %collective-permute-start.8 = (bf16[320,640]{1,0:T(8,128)(2,1)S(1)}, bf16[320,640]{1,0:T(8,128)(2,1)S(1)}, u32[]{:S(2)}, u32[]{:S(2)}) collective-permute-start(bf16[320,640]{1,0:T(8,128)(2,1)S(1)} %collective-permute-done.away_here), channel_id=1, source_target_pairs={{0,1},{1,0},{2,3},{3,2},{4,5},{5,4},{6,7},{7,6},{8,9},{9,8},{10,11... | collective-permute-start | bytes 1228808 | tf_op jit(solution)/shard_map/ppermute | solution.py:251
  45.0 15.7 %collective-permute-start.9 = (bf16[320,640]{1,0:T(8,128)(2,1)S(1)}, bf16[320,640]{1,0:T(8,128)(2,1)S(1)}, u32[]{:S(2)}, u32[]{:S(2)}) collective-permute-start(bf16[320,640]{1,0:T(8,128)(2,1)S(1)} %get-tuple-element.51), channel_id=1, source_target_pairs={{0,4},{4,8},{8,12},{12,0},{1,5},{5,9},{9,13},{13,1},{2,6},{6,10},{... | collective-permute-start | bytes 1228808 | tf_op jit(solution)/shard_map/ppermute | solution.py:248
  53.4 9.8 %collective-permute-start.7 = (s16[320,512]{1,0:T(8,128)(2,1)S(1)}, s16[320,512]{1,0:T(8,128)(2,1)S(1)}, u32[]{:S(2)}, u32[]{:S(2)}) collective-permute-start(s16[320,512]{1,0:T(8,128)(2,1)S(1)} %get-tuple-element.47), channel_id=1, source_target_pairs={{0,16},{16,0},{1,17},{17,1},{2,18},{18,2},{3,19},{19,3},{4,20},{20... | collective-permute-start | bytes 983048 | tf_op jit(solution)/shard_map/ppermute | solution.py:248
  56.6 9.5 %collective-permute-start.5 = (s16[2,320,256]{2,1,0:T(8,128)(2,1)S(1)}, s16[2,320,256]{2,1,0:T(8,128)(2,1)S(1)}, u32[]{:S(2)}, u32[]{:S(2)}) collective-permute-start(s16[2,320,256]{2,1,0:T(8,128)(2,1)S(1)} %get-tuple-element.45), channel_id=1, source_target_pairs={{0,2},{1,3},{2,0},{3,1},{4,6},{5,7},{6,4},{7,5},{8,10},{9,11},{10,... | collective-permute-start | bytes 983048 | tf_op jit(solution)/shard_map/ppermute | solution.py:254
  66.1 2.0 %collective-permute-start.10 = (bf16[320,640]{1,0:T(8,128)(2,1)S(1)}, bf16[320,640]{1,0:T(8,128)(2,1)S(1)}, u32[]{:S(2)}, u32[]{:S(2)}) collective-permute-start(bf16[320,640]{1,0:T(8,128)(2,1)S(1)} %get-tuple-element.52.own_here), channel_id=1, source_target_pairs={{0,1},{1,0},{2,3},{3,2},{4,5},{5,4},{6,7},{7,6},{8,9},{9,8},{10,11... | collective-permute-start | bytes 1228808 | tf_op jit(solution)/shard_map/ppermute | solution.py:251
  66.1 2.3 %collective-permute-start.11 = (bf16[320,640]{1,0:T(8,128)(2,1)S(1)}, bf16[320,640]{1,0:T(8,128)(2,1)S(1)}, u32[]{:S(2)}, u32[]{:S(2)}) collective-permute-start(bf16[320,640]{1,0:T(8,128)(2,1)S(1)} %collective-permute-done.9.away_here), channel_id=1, source_target_pairs={{0,1},{1,0},{2,3},{3,2},{4,5},{5,4},{6,7},{7,6},{8,9},{9,8},{10,11... | collective-permute-start | bytes 1228808 | tf_op jit(solution)/shard_map/ppermute | solution.py:251
  66.6 9.6 %collective-permute-start.18 = (s16[320,512]{1,0:T(8,128)(2,1)S(1)}, s16[320,512]{1,0:T(8,128)(2,1)S(1)}, u32[]{:S(2)}, u32[]{:S(2)}) collective-permute-start(s16[320,512]{1,0:T(8,128)(2,1)S(1)} %get-tuple-element.49), channel_id=1, source_target_pairs={{0,16},{16,0},{1,17},{17,1},{2,18},{18,2},{3,19},{19,3},{4,20},{20... | collective-permute-start | bytes 983048 | tf_op jit(solution)/shard_map/ppermute | solution.py:248
  71.0 10.6 %collective-permute-start.12 = (s16[2,320,256]{2,1,0:T(8,128)(2,1)S(1)}, s16[2,320,256]{2,1,0:T(8,128)(2,1)S(1)}, u32[]{:S(2)}, u32[]{:S(2)}) collective-permute-start(s16[2,320,256]{2,1,0:T(8,128)(2,1)S(1)} %get-tuple-element.55), channel_id=1, source_target_pairs={{0,2},{1,3},{2,0},{3,1},{4,6},{5,7},{6,4},{7,5},{8,10},{9,11},{10,... | collective-permute-start | bytes 983048 | tf_op jit(solution)/shard_map/ppermute | solution.py:254
  77.0 8.2 %collective-permute-start.19 = (s16[320,256]{1,0:T(8,128)(2,1)S(1)}, s16[320,256]{1,0:T(8,128)(2,1)S(1)}, u32[]{:S(2)}, u32[]{:S(2)}) collective-permute-start(s16[320,256]{1,0:T(8,128)(2,1)S(1)} %get-tuple-element.66), channel_id=1, source_target_pairs={{0,2},{1,3},{2,0},{3,1},{4,6},{5,7},{6,4},{7,5},{8,10},{9,11},{10,... | collective-permute-start | bytes 491528 | tf_op jit(solution)/shard_map/ppermute | solution.py:254
  79.3 8.5 %collective-permute-start.16 = (s16[320,256]{1,0:T(8,128)(2,1)S(1)}, s16[320,256]{1,0:T(8,128)(2,1)S(1)}, u32[]{:S(2)}, u32[]{:S(2)}) collective-permute-start(s16[320,256]{1,0:T(8,128)(2,1)S(1)} %get-tuple-element.63), channel_id=1, source_target_pairs={{0,2},{1,3},{2,0},{3,1},{4,6},{5,7},{6,4},{7,5},{8,10},{9,11},{10,... | collective-permute-start | bytes 491528 | tf_op jit(solution)/shard_map/ppermute | solution.py:254
  82.3 8.4 %collective-permute-start.13 = (s16[320,256]{1,0:T(8,128)(2,1)S(1)}, s16[320,256]{1,0:T(8,128)(2,1)S(1)}, u32[]{:S(2)}, u32[]{:S(2)}) collective-permute-start(s16[320,256]{1,0:T(8,128)(2,1)S(1)} %get-tuple-element.57), channel_id=1, source_target_pairs={{0,16},{16,0},{1,17},{17,1},{2,18},{18,2},{3,19},{19,3},{4,20},{20... | collective-permute-start | bytes 491528 | tf_op jit(solution)/shard_map/ppermute | solution.py:248
  84.6 8.7 %collective-permute-start.15 = (s16[320,256]{1,0:T(8,128)(2,1)S(1)}, s16[320,256]{1,0:T(8,128)(2,1)S(1)}, u32[]{:S(2)}, u32[]{:S(2)}) collective-permute-start(s16[320,256]{1,0:T(8,128)(2,1)S(1)} %get-tuple-element.60), channel_id=1, source_target_pairs={{0,16},{16,0},{1,17},{17,1},{2,18},{18,2},{3,19},{19,3},{4,20},{20... | collective-permute-start | bytes 491528 | tf_op jit(solution)/shard_map/ppermute | solution.py:248
  85.8 8.1 %collective-permute-start.20 = (bf16[320,256]{1,0:T(8,128)(2,1)S(1)}, bf16[320,256]{1,0:T(8,128)(2,1)S(1)}, u32[]{:S(2)}, u32[]{:S(2)}) collective-permute-start(bf16[320,256]{1,0:T(8,128)(2,1)S(1)} %round_pairs.7.refs_3_), channel_id=1, source_target_pairs={{0,4},{4,8},{8,12},{12,0},{1,5},{5,9},{9,13},{13,1},{2,6},{6,10},{... | collective-permute-start | bytes 491528 | tf_op jit(solution)/shard_map/ppermute | solution.py:248
  88.4 11.7 %collective-permute-start.17 = (bf16[320,256]{1,0:T(8,128)(2,1)S(1)}, bf16[320,256]{1,0:T(8,128)(2,1)S(1)}, u32[]{:S(2)}, u32[]{:S(2)}) collective-permute-start(bf16[320,256]{1,0:T(8,128)(2,1)S(1)} %round_pairs.6.refs_1_), channel_id=1, source_target_pairs={{0,8},{4,12},{8,0},{12,4},{1,9},{5,13},{9,1},{13,5},{2,10},{6,14},... | collective-permute-start | bytes 491528 | tf_op jit(solution)/shard_map/ppermute | solution.py:248
  91.4 12.9 %collective-permute-start.14 = (bf16[320,256]{1,0:T(8,128)(2,1)S(1)}, bf16[320,256]{1,0:T(8,128)(2,1)S(1)}, u32[]{:S(2)}, u32[]{:S(2)}) collective-permute-start(bf16[320,256]{1,0:T(8,128)(2,1)S(1)} %round_pairs.4.refs_0_), channel_id=1, source_target_pairs={{0,12},{4,0},{8,4},{12,8},{1,13},{5,1},{9,5},{13,9},{2,14},{6,2},{... | collective-permute-start | bytes 491528 | tf_op jit(solution)/shard_map/ppermute | solution.py:248

commit v7 on v6

--- a/solution.py
+++ b/solution.py
@@ -65,12 +65,13 @@
     return jnp.where(last, 0.0, values * jnp.exp2(code * (-1.0 / STEPS)))
 
 
-def call(name, body, scalars, inputs, outputs, grid=None):
+def call(name, body, scalars, inputs, outputs, grid=None, scratch=()):
     arrays = [entry[0] if isinstance(entry, tuple) else entry for entry in inputs]
     shapes = [jax.ShapeDtypeStruct(entry[0], entry[1]) for entry in outputs]
     if grid is None:
         in_specs = [pl.BlockSpec(memory_space=pltpu.SMEM)] + [pl.BlockSpec(memory_space=pltpu.VMEM)] * len(arrays)
-        specs = dict(in_specs=in_specs, out_specs=[pl.BlockSpec(memory_space=pltpu.VMEM)] * len(shapes))
+        out_specs = [pl.BlockSpec(memory_space=pltpu.VMEM)] * len(shapes)
+        specs = dict(in_specs=in_specs, out_specs=out_specs, scratch_shapes=list(scratch))
     else:
         in_specs, out_specs = [], []
         for entry, array in zip(inputs, arrays):
@@ -93,21 +94,21 @@
     )(scalars, *arrays)
 
 
-def masked_rows(by, row_n, sub, k_here, s_ref, ab_ref, cd_ref, v_ref):
+def masked_rows(by, row_n, sub, k_here, s_ref, ab_ref, cd_refs, v_refs):
     x, y, core = s_ref[0], s_ref[2], s_ref[3]
-    rows, cd_here = v_ref.shape
+    rows, cd_here = v_refs[0].shape
     tall = rows // 4
     q, m = divide(lax.broadcasted_iota(jnp.int32, (k_here, 1), 0), sub)
     wanted = q * (sub * row_n) + lax.rem(x - by + row_n, row_n) * sub + m
     square = (LANES, LANES)
     diagonal = lax.broadcasted_iota(jnp.int32, square, 0) == lax.broadcasted_iota(jnp.int32, square, 1)
-    cd_labels = cd_ref[...].astype(jnp.float32)
-    cd = jnp.concatenate([cd_labels[k : k + 1] for k in range(cd_here // LANES)], axis=1)
     strips = tall // LANES
     blocks = []
-    for other_core in (1, 0):
+    for cd_ref, v_ref in zip(cd_refs, v_refs):
+        cd_labels = cd_ref[...].astype(jnp.float32)
+        cd = jnp.concatenate([cd_labels[k : k + 1] for k in range(cd_here // LANES)], axis=1)
         for other_y in (1, 0):
-            block = lax.rem(y + other_y, 2) * CORES + lax.rem(core + other_core, CORES)
+            block = lax.rem(y + other_y, 2) * CORES + core
             for strip in range(strips):
                 labels = ab_ref[pl.ds(block * strips + strip, 1), :].astype(jnp.float32)
                 ab = jnp.sum(jnp.where(diagonal, labels, 0.0), axis=1, keepdims=True)
@@ -117,8 +118,9 @@
     return dot_nt(jnp.concatenate(blocks, axis=0), one_hot_rows(wanted, cd_here)).astype(jnp.bfloat16)
 
 
-def mask_body(by, row_n, sub, s_ref, ab_ref, cd_ref, v_ref, out_ref):
-    out_ref[...] = masked_rows(by, row_n, sub, out_ref.shape[1], s_ref, ab_ref, cd_ref, v_ref)
+def mask_body(by, row_n, sub, s_ref, ab_ref, cd_here, cd_there, v_here, v_there, out_ref):
+    k_here = out_ref.shape[1]
+    out_ref[...] = masked_rows(by, row_n, sub, k_here, s_ref, ab_ref, (cd_here, cd_there), (v_here, v_there))
 
 
 def one_hot_rows(columns, width):
@@ -126,47 +128,46 @@
     return jnp.where(lanes == columns, 1.0, 0.0).astype(jnp.bfloat16)
 
 
+def flatten(t_ref, flat_ref):
+    columns, wide = t_ref.shape[-1], flat_ref.shape[1]
+    flat_ref[:, wide - LANES :] = jnp.zeros((flat_ref.shape[0], LANES), flat_ref.dtype)
+    flat_ref[:, :columns] = t_ref[...].reshape(-1, columns)
+
+
 def send_body(order, n, col_n, s_ref, t_ref, flat_ref, *out_refs):
-    columns, wide = t_ref.shape[-1], flat_ref.shape[1]
-    last = wide - LANES
-    flat_ref[:, last:] = jnp.zeros((flat_ref.shape[0], LANES), flat_ref.dtype)
-    flat_ref[:, :columns] = t_ref[...].reshape(-1, columns)
+    flatten(t_ref, flat_ref)
     z = s_ref[1]
-    place = lax.broadcasted_iota(jnp.int32, (out_refs[0].shape[0], 1), 0)
     chunk = out_refs[0].shape[0]
+    place = lax.broadcasted_iota(jnp.int32, (chunk, 1), 0)
     wanted = [pair_columns(place, n, z, lax.rem(z - r + col_n, col_n), False) for r in order]
     picked = dot_nt(one_hot_rows(jnp.concatenate(wanted, axis=0), flat_ref.shape[1]), flat_ref[...]).astype(jnp.bfloat16)
     for k, out_ref in enumerate(out_refs):
         out_ref[...] = picked[k * chunk : (k + 1) * chunk]
 
 
-def keep_body(soon, late, n, col_n, row_n, sub, s_ref, flat_ref, ab_ref, cd_ref, v_ref, first_ref, later_ref, kept_ref):
+def keep_body(order, n, col_n, row_n, sub, s_ref, flat_ref, t_there, ab_ref, cd_here, cd_there, v_here, v_there, *refs):
+    own_here, own_there, kept_ref, flat_there = refs
+    flatten(t_there, flat_there)
     z = s_ref[1]
-    half, k_here = kept_ref.shape
-    pairs = first_ref.shape[0] - half
-    place = lax.broadcasted_iota(jnp.int32, (pairs // (len(soon) + 2), 1), 0)
+    place = lax.broadcasted_iota(jnp.int32, (own_here.shape[0] // (len(order) + 2), 1), 0)
     inside, turned = inside_columns(place, n, z)
-    others = [pair_columns(place, n, z, lax.rem(z + r, col_n), True) for r in soon + late]
-    picks = jnp.concatenate([inside] + others[: len(soon)] + [turned] + others[len(soon) :], axis=0)
-    picked = dot_nt(one_hot_rows(picks, flat_ref.shape[1]), flat_ref[...]).astype(jnp.bfloat16)
-    masked = masked_rows(0, row_n, sub, k_here, s_ref, ab_ref, cd_ref, v_ref)
-    first_ref[:pairs] = picked[:pairs]
-    first_ref[pairs:] = masked[:half]
-    later_ref[...] = picked[pairs:]
-    kept_ref[...] = masked[half:]
-
-
-def sum_body(place, turned, groups, y_first, s_ref, own_here, own_there, away_here, away_there, first_there, *refs):
-    keeps, passes, outs = refs[:groups], refs[groups : 2 * groups - 1], refs[2 * groups - 1 :]
+    others = [pair_columns(place, n, z, lax.rem(z + r, col_n), True) for r in order]
+    picks = one_hot_rows(jnp.concatenate([inside] + others + [turned], axis=0), flat_ref.shape[1])
+    own_here[...] = dot_nt(picks, flat_ref[...]).astype(jnp.bfloat16)
+    own_there[...] = dot_nt(picks, flat_there[...]).astype(jnp.bfloat16)
+    k_here = kept_ref.shape[1]
+    kept_ref[...] = masked_rows(0, row_n, sub, k_here, s_ref, ab_ref, (cd_here, cd_there), (v_here, v_there))
+
+
+def sum_body(place, turned, groups, y_first, s_ref, own_here, own_there, away_here, away_there, *refs):
+    keeps, outs = refs[:groups], refs[groups:]
     chunk, tall = outs[-1].shape[-2:]
     tall = tall if y_first else tall // 2
     mine = slice(place * chunk, (place + 1) * chunk)
     other = slice(turned * chunk, (turned + 1) * chunk)
     left = jnp.concatenate([own_here[mine], own_there[mine], away_here[other], away_there[other]], axis=1)
     for g in range(groups):
-        start = keeps[g].shape[0] - 2 * tall
-        a = keeps[g][start:]
-        b = first_there[first_there.shape[0] - 2 * tall :] if g == 0 else passes[g - 1][: 2 * tall]
+        a, b = keeps[g][: 2 * tall], keeps[g][2 * tall :]
         total = dot_nt(left, jnp.concatenate([a, b, -a, -b], axis=1))
         if y_first:
             outs[0][g] = encode(total[:, :tall])
@@ -240,7 +241,6 @@
     far = col_n // 2
     near = [r for r in range(1, col_n) if r != far]
     soon, late = [far] + near[:1], near[1:]
-    chunks = [(0, True)] + [(r, False) for r in soon] + [(r, True) for r in late]
     bf16, i16, f32 = jnp.bfloat16, jnp.int16, jnp.float32
 
     def shift(array, axis, by):
@@ -253,8 +253,14 @@
     def other_y(array):
         return lax.ppermute(array, "depth", [(i, i ^ 2) for i in range(depth_n)])
 
+    def after(values, *earlier):
+        return lax.optimization_barrier((values, earlier))[0]
+
     scalars = jnp.stack([x, z, y, core]).astype(jnp.int32)
     ab_row, cd_row = ab_irrep.reshape(-1, LANES), cd_irrep.reshape(-1, LANES)
+
+    cd_there, v_there, t_there = other_core(cd_row), other_core(integrals), other_core(amplitudes)
+    integral_refs = [ab_row, cd_row, cd_there, integrals, v_there]
 
     kept = [None] * row_n
     gone = scalars
@@ -263,89 +269,94 @@
             "mask_integrals",
             functools.partial(mask_body, by, row_n, sub),
             scalars,
-            [ab_row, cd_row, integrals],
+            integral_refs,
             [((rows, k_here), bf16)],
         )
         kept[by] = shift(gone, "row", -by)
 
-    amplitudes, _ = lax.optimization_barrier((amplitudes, gone))
+    wide = -(-columns // LANES) * LANES
     flat, *sent = call(
         "send_columns",
         functools.partial(send_body, soon + late, n, col_n),
         scalars,
-        [amplitudes],
-        [((k_here, -(-columns // LANES) * LANES), bf16)] + [((chunk, k_here), bf16)] * (col_n - 1),
+        [after(amplitudes, gone)],
+        [((k_here, wide), bf16)] + [((chunk, k_here), bf16)] * (col_n - 1),
     )
-    away = {r: shift(value, "col", -r) for r, value in zip(soon, sent)}
-
-    first, later, kept[0] = call(
+    sent = dict(zip(soon + late, sent))
+    away = {r: shift(sent[r], "col", -r) for r in soon}
+
+    own_here, own_there, kept[0] = call(
         "keep_columns",
-        functools.partial(keep_body, soon, late, n, col_n, row_n, sub),
+        functools.partial(keep_body, soon + late, n, col_n, row_n, sub),
         scalars,
-        [flat, ab_row, cd_row, integrals],
-        [
-            (((len(soon) + 2) * chunk + 2 * tall, k_here), bf16),
-            ((len(late) * chunk, k_here), bf16),
-            ((2 * tall, k_here), bf16),
-        ],
+        [flat, t_there] + integral_refs,
+        [(((col_n + 1) * chunk, k_here), bf16)] * 2 + [((rows, k_here), bf16)],
+        scratch=[pltpu.VMEM((k_here, wide), bf16)],
     )
-    away, kept[1:], first, *sent = lax.optimization_barrier((away, kept[1:], first, *sent[len(soon) :]))
-    first_there = other_core(first)
-    passed = [other_core(a) for a in kept[1:]]
-    away_there = {r: other_core(away[r]) for r in soon}
-    for r, value in zip(late, sent):
-        away[r] = shift(value, "col", -r)
-
-    rounded = {}
-    before, later_there = [], None
-    for place, (r, y_first) in enumerate(chunks):
-        if r in late and later_there is None:
-            _, later, *arrived = lax.optimization_barrier((before, later, *[away[q] for q in late]))
-            for q, value in zip(late, arrived):
-                away[q] = value
-                away_there[q] = other_core(value)
-            later_there = other_core(later)
-        if r in late:
-            own, at, turned = (later, later_there), late.index(r), 0
-        else:
-            own, at, turned = (first, first_there), place, len(soon) + 1 if r == 0 else 0
-        others = (first, first_there) if r == 0 else (away[r], away_there[r])
-        if y_first:
+
+    first_y = {r: r not in soon for r in range(col_n)}
+    away_there, crossed, added, rounded = {}, {}, {}, {}
+
+    def sum_pairs(r):
+        others = (own_here, own_there) if r == 0 else (away[r], away_there[r])
+        place, turned = ([0] + soon + late).index(r), col_n if r == 0 else 0
+        if first_y[r]:
             shapes = [((row_n, chunk, tall), i16), ((row_n, chunk, tall), f32)]
         else:
             shapes = [((chunk, 2 * tall), i16)] * (row_n - 1) + [((chunk, 2 * tall), f32)]
         sums = call(
             "sum_pairs",
-            functools.partial(sum_body, at, turned, row_n, y_first),
+            functools.partial(sum_body, place, turned, row_n, first_y[r]),
             scalars,
-            [*own, *others, first_there, *kept, *passed],
+            [own_here, own_there, *others, *kept],
             shapes,
         )
-        if y_first:
-            crossed = [other_y(sums[0])]
-        else:
-            crossed = [shift(value, "row", by + 1) for by, value in enumerate(sums[:-1])]
-        before += crossed if place < 2 else sums[:1]
-        if y_first:
+        if first_y[r]:
+            crossed[r] = [sums[1], other_y(sums[0])]
+        else:
+            crossed[r] = [sums[-1]] + [shift(value, "row", by + 1) for by, value in enumerate(sums[:-1])]
+        return sums
+
+    def add_pairs(r):
+        if first_y[r]:
             own_sum, *coded = call(
                 "add_other_y",
                 add_y_body,
                 scalars,
-                [sums[1]] + crossed,
+                crossed[r],
                 [((chunk, tall), f32)] + [((chunk, tall), i16)] * (row_n - 1),
             )
-            last = [shift(value, "row", by + 1) for by, value in enumerate(coded)]
+            added[r] = [own_sum] + [shift(value, "row", by + 1) for by, value in enumerate(coded)]
         else:
             coded, own_sum = call(
-                "add_other_x",
-                add_x_body,
-                scalars,
-                [sums[-1]] + crossed,
-                [((chunk, tall), i16), ((chunk, tall), f32)],
+                "add_other_x", add_x_body, scalars, crossed[r], [((chunk, tall), i16), ((chunk, tall), f32)]
             )
-            last = [other_y(coded)]
-        (mine,) = call("round_pairs", round_body, scalars, [own_sum] + last, [((chunk, tall), bf16)])
+            added[r] = [own_sum, other_y(coded)]
+        return own_sum
+
+    def round_pairs(r):
+        (mine,) = call("round_pairs", round_body, scalars, added[r], [((chunk, tall), bf16)])
         rounded[r] = [mine] if r == 0 else [mine, shift(mine, "col", r)]
+        return mine
+
+    inside = sum_pairs(0)
+    arrived = after([away[r] for r in soon], inside)
+    for r in late:
+        away[r] = shift(after(sent[r], arrived), "col", -r)
+    for r, value in zip(soon, arrived):
+        away_there[r] = other_core(value)
+    sums = [sum_pairs(r) for r in soon]
+    early = [add_pairs(soon[0]), add_pairs(0)]
+    for r in late:
+        away_there[r] = other_core(after(away[r], early, sums))
+    sums = [sum_pairs(r) for r in late]
+    early = [round_pairs(soon[0]), round_pairs(0)]
+    for r in soon[1:] + late:
+        crossed[r] = after(crossed[r], early)
+        add_pairs(r)
+    for r in soon[1:] + late:
+        added[r] = after(added[r], rounded[soon[0]])
+        round_pairs(r)
 
     done = None
     for group in ([0] + soon, late):

time: 107 us -> 114 us (1.065)
  Pallas kernels: 40 us -> 48.5 us
  waiting for transfers between devices: 39.8 us -> 34 us
  starting transfers between devices: 24 us -> 27.4 us
    ppermute x11, waiting for transfers between devices: 28.8 us -> 17.5 us  [shift(): lax.ppermute(array, axis, [(i, (i + by) % count) for i in range(count)])]
    pallas_call x17, Pallas kernels: 40 us -> 48.5 us  [call(): pl.pallas_call(body, name=name, out_shape=shapes, compiler_params=pltpu.C...]
    ppermute x11, starting transfers between devices: 17.1 us -> 21.1 us  [shift(): lax.ppermute(array, axis, [(i, (i + by) % count) for i in range(count)])]
    ppermute x6, waiting for transfers between devices: 5.38 us -> 8.49 us  [other_core(): return lax.ppermute(array, 'depth', [(i, i ^ 1) for i in range(depth_n)])]
    ppermute x4, waiting for transfers between devices: 5.63 us -> 8.02 us  [other_y(): return lax.ppermute(array, 'depth', [(i, i ^ 2) for i in range(depth_n)])]
    unnamed x12 -> x10, local copies, waits for them, and re-layouts: 3.14 us -> 3.13 us
  transfers between devices with their start and end apart: 21 -> 21, of which waited for: 10 -> 10; matrix products, arithmetic and copies ran while one was open for 0% -> 0% of each run, Pallas kernels for 32% -> 40%
where the time goes in v7:
time: 114 us; the launch traced here: 113 us
  Pallas kernels  48.5 us (43%)
  waiting for transfers between devices  34 us (30%)
  starting transfers between devices  27.4 us (24%)
  local copies, waits for them, and re-layouts  3.13 us (3%)
    pallas_call x17, Pallas kernels, call(): pl.pallas_call(body, name=name, out_shape=shapes, compiler_params=pltpu.C...  48.5 us
    ppermute x11, starting transfers between devices, shift(): lax.ppermute(array, axis, [(i, (i + by) % count) for i in range(count)])  21.1 us
    ppermute x11, waiting for transfers between devices, shift(): lax.ppermute(array, axis, [(i, (i + by) % count) for i in range(count)])  17.5 us
    ppermute x6, waiting for transfers between devices, other_core(): return lax.ppermute(array, 'depth', [(i, i ^ 1) for i in range(depth_n)])  8.49 us
    ppermute x4, waiting for transfers between devices, other_y(): return lax.ppermute(array, 'depth', [(i, i ^ 2) for i in range(depth_n)])  8.02 us
    ppermute x4, starting transfers between devices, other_y(): return lax.ppermute(array, 'depth', [(i, i ^ 2) for i in range(depth_n)])  4.65 us
    unnamed x10, local copies, waits for them, and re-layouts  3.13 us
  transfers between devices with their start and end apart: 21, of which 10 were waited for; matrix products, arithmetic and copies ran while one was open for 0% of the time, Pallas kernels for 40%

profile of v7, /device:TPU:0, one launch (start us, length us, event | category | flops | bytes accessed | tf_op | source)
XLA Modules:
  0.0 113.3 jit_solution(6156333035540482559)
XLA Ops:
  0.0 0.5 collective-permute-start.1
  0.5 0.5 collective-permute-start
  1.0 0.1 pad_add_fusion.s_ref
  1.0 7.4 %collective-permute-done.cd_there = s32[10,128]{1,0:T(8,128)S(1)} collective-permute-done((s32[10,128]{1,0:T(8,128)}, s32[10,128]{1,0:T(8,128)S(1)}, u32[]{:S(2)}, u32[]{:S(2)}) %collective-permute-start) | collective-permute-done | bytes 5152 | tf_op jit(solution)/shard_map/ppermute | solution.py:251
  8.4 1.7 %copy-done = bf16[1024,1280]{1,0:T(8,128)(2,1)S(1)} copy-done((bf16[1024,1280]{1,0:T(8,128)(2,1)S(1)}, bf16[1024,1280]{1,0:T(8,128)(2,1)}, u32[]{:S(2)}) %copy-start) | copy-done | bytes 2621464
  10.1 0.7 copy-done.3
  10.8 0.7 copy-done.4
  11.5 2.9 %mask_integrals.1 = bf16[1024,640]{1,0:T(8,128)(2,1)S(1)} custom-call(s32[4]{0:T(128)S(1)} %pad_add_fusion.s_ref, s32[8,128]{1,0:T(8,128)S(1)} %bitcast.10, s32[10,128]{1,0:T(8,128)S(1)} %bitcast.8, s32[10,128]{1,0:T(8,128)S(1)} %collective-permute-done.cd_there, bf16[1024,1280]{1,0:T(8,128)(2,1)S(1)} %copy-done, ...), custom_call_target="tpu_custom_call" | custom-call | flops 1 | bytes 1 | tf_op jit(solution)/shard_map/mask_integrals/pallas_call | solution.py:87
  14.4 3.5 %collective-permute-start.5 = (bf16[1024,640]{1,0:T(8,128)(2,1)S(1)}, bf16[1024,640]{1,0:T(8,128)(2,1)S(1)}, u32[]{:S(2)}, u32[]{:S(2)}) collective-permute-start(bf16[1024,640]{1,0:T(8,128)(2,1)S(1)} %mask_integrals.1), channel_id=1, source_target_pairs={{0,16},{16,0},{1,17},{17,1},{2,18},{18,2},{3,19},{19,3},{4,20},{20... | collective-permute-start | bytes 3932168 | tf_op jit(solution)/shard_map/ppermute | solution.py:248
  17.9 5.1 %send_columns.1 = (bf16[640,2560]{1,0:T(8,128)(2,1)S(1)}, bf16[320,640]{1,0:T(8,128)(2,1)S(1)}, bf16[320,640]{1,0:T(8,128)(2,1)S(1)}, bf16[320,640]{1,0:T(8,128)(2,1)S(1)}) custom-call(s32[4]{0:T(128)S(1)} %pad_add_fusion.s_ref, bf16[320,2,2500]{2,1,0:T(2,128)(2,1)S(1)} %copy-done.2), custom_call_target="tpu_custom_call" | custom-call | flops 1 | bytes 1 | tf_op jit(solution)/shard_map/send_columns/pallas_call | solution.py:87
  23.0 2.7 %collective-permute-start.3 = (bf16[320,640]{1,0:T(8,128)(2,1)S(1)}, bf16[320,640]{1,0:T(8,128)(2,1)S(1)}, u32[]{:S(2)}, u32[]{:S(2)}) collective-permute-start(bf16[320,640]{1,0:T(8,128)(2,1)S(1)} %get-tuple-element.46), channel_id=1, source_target_pairs={{0,8},{4,12},{8,0},{12,4},{1,9},{5,13},{9,1},{13,5},{2,10},{6,14},... | collective-permute-start | bytes 1228808 | tf_op jit(solution)/shard_map/ppermute | solution.py:248
  25.7 1.3 %collective-permute-start.4 = (bf16[320,640]{1,0:T(8,128)(2,1)S(1)}, bf16[320,640]{1,0:T(8,128)(2,1)S(1)}, u32[]{:S(2)}, u32[]{:S(2)}) collective-permute-start(bf16[320,640]{1,0:T(8,128)(2,1)S(1)} %get-tuple-element.47), channel_id=1, source_target_pairs={{0,12},{4,0},{8,4},{12,8},{1,13},{5,1},{9,5},{13,9},{2,14},{6,2},{... | collective-permute-start | bytes 1228808 | tf_op jit(solution)/shard_map/ppermute | solution.py:248
  27.1 18.0 %keep_columns.1 = (bf16[1600,640]{1,0:T(8,128)(2,1)S(1)}, bf16[1600,640]{1,0:T(8,128)(2,1)S(1)}, bf16[1024,640]{1,0:T(8,128)(2,1)S(1)}) custom-call(s32[4]{0:T(128)S(1)} %pad_add_fusion.s_ref, bf16[640,2560]{1,0:T(8,128)(2,1)S(1)} %get-tuple-element.42.flat_ref, bf16[320,2,2500]{2,1,0:T(2,128)(2,1)} %collective-permute-done.2.t_there, ...), custom_call_target="tpu_custom_call" | custom-call | flops 1 | bytes 1 | tf_op jit(solution)/shard_map/keep_columns/pallas_call | solution.py:87
  45.1 1.9 %collective-permute-done.5.refs_1_ = bf16[1024,640]{1,0:T(8,128)(2,1)S(1)} collective-permute-done((bf16[1024,640]{1,0:T(8,128)(2,1)S(1)}, bf16[1024,640]{1,0:T(8,128)(2,1)S(1)}, u32[]{:S(2)}, u32[]{:S(2)}) %collective-permute-start.5) | collective-permute-done | bytes 1310752 | tf_op jit(solution)/shard_map/ppermute | solution.py:248
  47.0 2.5 %sum_pairs.4 = (s16[2,320,256]{2,1,0:T(8,128)(2,1)S(1)}, f32[2,320,256]{2,1,0:T(8,128)S(1)}) custom-call(s32[4]{0:T(128)S(1)} %pad_add_fusion.s_ref, bf16[1600,640]{1,0:T(8,128)(2,1)S(1)} %get-tuple-element.43.own_here.away_here, bf16[1600,640]{1,0:T(8,128)(2,1)S(1)} %get-tuple-element.44.own_there.away_there, ...), custom_call_target="tpu_custom_call" | custom-call | flops 1 | bytes 1 | tf_op jit(solution)/shard_map/sum_pairs/pallas_call | solution.py:87
  49.6 0.5 collective-permute-start.10
  50.1 3.9 %collective-permute-start.6 = (bf16[320,640]{1,0:T(8,128)(2,1)S(1)}, bf16[320,640]{1,0:T(8,128)(2,1)S(1)}, u32[]{:S(2)}, u32[]{:S(2)}) collective-permute-start(bf16[320,640]{1,0:T(8,128)(2,1)S(1)} %get-tuple-element.53), channel_id=1, source_target_pairs={{0,4},{4,8},{8,12},{12,0},{1,5},{5,9},{9,13},{13,1},{2,6},{6,10},{... | collective-permute-start | bytes 1228808 | tf_op jit(solution)/shard_map/ppermute | solution.py:248
  54.0 1.5 %collective-permute-start.9 = (s16[2,320,256]{2,1,0:T(8,128)(2,1)S(1)}, s16[2,320,256]{2,1,0:T(8,128)(2,1)S(1)}, u32[]{:S(2)}, u32[]{:S(2)}) collective-permute-start(s16[2,320,256]{2,1,0:T(8,128)(2,1)S(1)} %get-tuple-element.49), channel_id=1, source_target_pairs={{0,2},{1,3},{2,0},{3,1},{4,6},{5,7},{6,4},{7,5},{8,10},{9,11},{10,... | collective-permute-start | bytes 983048 | tf_op jit(solution)/shard_map/ppermute | solution.py:254
  55.5 2.5 %sum_pairs.5 = (s16[320,512]{1,0:T(8,128)(2,1)S(1)}, f32[320,512]{1,0:T(8,128)S(1)}) custom-call(s32[4]{0:T(128)S(1)} %pad_add_fusion.s_ref, bf16[1600,640]{1,0:T(8,128)(2,1)S(1)} %get-tuple-element.43.own_here.away_here, bf16[1600,640]{1,0:T(8,128)(2,1)S(1)} %get-tuple-element.44.own_there.away_there, ...), custom_call_target="tpu_custom_call" | custom-call | flops 1 | bytes 1 | tf_op jit(solution)/shard_map/sum_pairs/pallas_call | solution.py:87
  58.1 0.6 collective-permute-start.8
  58.7 4.7 %collective-permute-done.9.coded_ref = s16[2,320,256]{2,1,0:T(8,128)(2,1)S(1)} collective-permute-done((s16[2,320,256]{2,1,0:T(8,128)(2,1)S(1)}, s16[2,320,256]{2,1,0:T(8,128)(2,1)S(1)}, u32[]{:S(2)}, u32[]{:S(2)}) %collective-permute-start.9) | collective-permute-done | bytes 327712 | tf_op jit(solution)/shard_map/ppermute | solution.py:254
  63.3 0.7 add_other_y.2
  64.1 2.5 %sum_pairs.6 = (s16[320,512]{1,0:T(8,128)(2,1)S(1)}, f32[320,512]{1,0:T(8,128)S(1)}) custom-call(s32[4]{0:T(128)S(1)} %pad_add_fusion.s_ref, bf16[1600,640]{1,0:T(8,128)(2,1)S(1)} %get-tuple-element.43.own_here.away_here, bf16[1600,640]{1,0:T(8,128)(2,1)S(1)} %get-tuple-element.44.own_there.away_there, ...), custom_call_target="tpu_custom_call" | custom-call | flops 1 | bytes 1 | tf_op jit(solution)/shard_map/sum_pairs/pallas_call | solution.py:87
  66.6 0.6 collective-permute-done.8.refs_0_
  67.2 0.7 add_other_x.2
  68.0 0.6 collective-permute-start.18
  68.6 1.1 collective-permute-done.11.away_there
  69.8 2.5 %sum_pairs.7 = (s16[2,320,256]{2,1,0:T(8,128)(2,1)S(1)}, f32[2,320,256]{2,1,0:T(8,128)S(1)}) custom-call(s32[4]{0:T(128)S(1)} %pad_add_fusion.s_ref, bf16[1600,640]{1,0:T(8,128)(2,1)S(1)} %get-tuple-element.43.own_here.away_here, bf16[1600,640]{1,0:T(8,128)(2,1)S(1)} %get-tuple-element.44.own_there.away_there, ...), custom_call_target="tpu_custom_call" | custom-call | flops 1 | bytes 1 | tf_op jit(solution)/shard_map/sum_pairs/pallas_call | solution.py:87
  72.3 1.0 collective-permute-start.12
  73.3 0.5 collective-permute-start.14
  73.9 1.1 collective-permute-start.13
  74.9 6.8 %collective-permute-done.14.refs_0_ = s16[320,256]{1,0:T(8,128)(2,1)S(1)} collective-permute-done((s16[320,256]{1,0:T(8,128)(2,1)S(1)}, s16[320,256]{1,0:T(8,128)(2,1)S(1)}, u32[]{:S(2)}, u32[]{:S(2)}) %collective-permute-start.14) | collective-permute-done | bytes 163872 | tf_op jit(solution)/shard_map/ppermute | solution.py:248
  81.7 0.6 round_pairs.5.refs_0_
  82.3 3.3 %collective-permute-done.13.refs_0_ = s16[320,256]{1,0:T(8,128)(2,1)S(1)} collective-permute-done((s16[320,256]{1,0:T(8,128)(2,1)S(1)}, s16[320,256]{1,0:T(8,128)(2,1)S(1)}, u32[]{:S(2)}, u32[]{:S(2)}) %collective-permute-start.13) | collective-permute-done | bytes 163872 | tf_op jit(solution)/shard_map/ppermute | solution.py:254
  85.6 0.6 round_pairs.4.refs_1_
  86.2 3.4 %collective-permute-start.16 = (bf16[320,256]{1,0:T(8,128)(2,1)S(1)}, bf16[320,256]{1,0:T(8,128)(2,1)S(1)}, u32[]{:S(2)}, u32[]{:S(2)}) collective-permute-start(bf16[320,256]{1,0:T(8,128)(2,1)S(1)} %round_pairs.4.refs_1_), channel_id=1, source_target_pairs={{0,8},{4,12},{8,0},{12,4},{1,9},{5,13},{9,1},{13,5},{2,10},{6,14},... | collective-permute-start | bytes 491528 | tf_op jit(solution)/shard_map/ppermute | solution.py:248
  89.7 0.7 add_other_x.3
  90.4 1.0 collective-permute-start.19
  91.5 0.7 add_other_y.3
  92.2 0.6 collective-permute-start.15
  92.8 3.9 %collective-permute-done.16.refs_2_ = bf16[320,256]{1,0:T(8,128)(2,1)S(1)} collective-permute-done((bf16[320,256]{1,0:T(8,128)(2,1)S(1)}, bf16[320,256]{1,0:T(8,128)(2,1)S(1)}, u32[]{:S(2)}, u32[]{:S(2)}) %collective-permute-start.16) | collective-permute-done | bytes 163872 | tf_op jit(solution)/shard_map/ppermute | solution.py:248
  96.7 0.6 round_pairs.7.refs_3_
  97.3 0.2 collective-permute-done.15.refs_0_
  97.6 0.6 round_pairs.6.refs_0_
  98.2 3.9 %collective-permute-start.17 = (bf16[320,256]{1,0:T(8,128)(2,1)S(1)}, bf16[320,256]{1,0:T(8,128)(2,1)S(1)}, u32[]{:S(2)}, u32[]{:S(2)}) collective-permute-start(bf16[320,256]{1,0:T(8,128)(2,1)S(1)} %round_pairs.6.refs_0_), channel_id=1, source_target_pairs={{0,12},{4,0},{8,4},{12,8},{1,13},{5,1},{9,5},{13,9},{2,14},{6,2},{... | collective-permute-start | bytes 491528 | tf_op jit(solution)/shard_map/ppermute | solution.py:248
  102.1 4.2 %collective-permute-done.20.refs_4_ = bf16[320,256]{1,0:T(8,128)(2,1)S(1)} collective-permute-done((bf16[320,256]{1,0:T(8,128)(2,1)S(1)}, bf16[320,256]{1,0:T(8,128)(2,1)S(1)}, u32[]{:S(2)}, u32[]{:S(2)}) %collective-permute-start.20) | collective-permute-done | bytes 163872 | tf_op jit(solution)/shard_map/ppermute | solution.py:248
  106.2 4.1 %place_pairs.2.refs_2_ = bf16[2500,256]{1,0:T(8,128)(2,1)S(1)} custom-call(s32[4]{0:T(128)S(1)} %pad_add_fusion.s_ref, bf16[320,256]{1,0:T(8,128)(2,1)S(1)} %round_pairs.5.refs_0_, bf16[320,256]{1,0:T(8,128)(2,1)S(1)} %round_pairs.4.refs_1_, bf16[320,256]{1,0:T(8,128)(2,1)S(1)} %collective-permute-done.16.refs_2_, bf16[320,256]{1,0:T(8,128)(2,1)S(1)} %round_pairs.7.refs_3_, ...), custom_call_target="tpu_custom_call" | custom-call | flops 1 | bytes 1 | tf_op jit(solution)/shard_map/place_pairs/pallas_call | solution.py:87
  110.4 2.9 %place_pairs.3 = bf16[2500,256]{1,0:T(8,128)(2,1)} custom-call(s32[4]{0:T(128)S(1)} %pad_add_fusion.s_ref, bf16[320,256]{1,0:T(8,128)(2,1)S(1)} %round_pairs.6.refs_0_, bf16[320,256]{1,0:T(8,128)(2,1)S(1)} %collective-permute-done.17.refs_1_, bf16[2500,256]{1,0:T(8,128)(2,1)S(1)} %place_pairs.2.refs_2_), custom_call_target="tpu_custom_call" | custom-call | flops 1 | bytes 1 | tf_op jit(solution)/shard_map/place_pairs/pallas_call | solution.py:87
  (22 shorter events, 0.3 us)
Async XLA Ops:
  0.0 8.4 %collective-permute-start.1 = (bf16[1024,1280]{1,0:T(8,128)(2,1)}, bf16[1024,1280]{1,0:T(8,128)(2,1)S(1)}, u32[]{:S(2)}, u32[]{:S(2)}) collective-permute-start(bf16[1024,1280]{1,0:T(8,128)(2,1)} %v_here.3), channel_id=1, source_target_pairs={{0,1},{1,0},{2,3},{3,2},{4,5},{5,4},{6,7},{7,6},{8,9},{9,8},{10,11... | collective-permute-start | bytes 7864328 | tf_op jit(solution)/shard_map/ppermute | solution.py:251
  0.5 26.6 %collective-permute-start.2 = (bf16[320,2,2500]{2,1,0:T(2,128)(2,1)}, bf16[320,2,2500]{2,1,0:T(2,128)(2,1)}, u32[]{:S(2)}, u32[]{:S(2)}) collective-permute-start(bf16[320,2,2500]{2,1,0:T(2,128)(2,1)} %t_ref), channel_id=1, source_target_pairs={{0,1},{1,0},{2,3},{3,2},{4,5},{5,4},{6,7},{7,6},{8,9},{9,8},{10,11... | collective-permute-start | bytes 9600008 | tf_op jit(solution)/shard_map/ppermute | solution.py:251
  0.5 7.9 %collective-permute-start = (s32[10,128]{1,0:T(8,128)}, s32[10,128]{1,0:T(8,128)S(1)}, u32[]{:S(2)}, u32[]{:S(2)}) collective-permute-start(s32[10,128]{1,0:T(8,128)} %bitcast.7), channel_id=1, source_target_pairs={{0,1},{1,0},{2,3},{3,2},{4,5},{5,4},{6,7},{7,6},{8,9},{9,8},{10,11... | collective-permute-start | bytes 15368 | tf_op jit(solution)/shard_map/ppermute | solution.py:251
  8.4 1.7 %copy-start = (bf16[1024,1280]{1,0:T(8,128)(2,1)S(1)}, bf16[1024,1280]{1,0:T(8,128)(2,1)}, u32[]{:S(2)}) copy-start(bf16[1024,1280]{1,0:T(8,128)(2,1)} %v_here.3) | copy-start | bytes 7864324
  10.1 0.7 copy-start.3
  10.8 0.7 copy-start.4
  11.5 6.4 %copy-start.2 = (bf16[320,2,2500]{2,1,0:T(2,128)(2,1)S(1)}, bf16[320,2,2500]{2,1,0:T(2,128)(2,1)}, u32[]{:S(2)}) copy-start(bf16[320,2,2500]{2,1,0:T(2,128)(2,1)} %t_ref) | copy-start | bytes 9600004
  14.4 12.6 %copy-start.1 = (bf16[1024,1280]{1,0:T(8,128)(2,1)S(1)}, bf16[1024,1280]{1,0:T(8,128)(2,1)}, u32[]{:S(2)}) copy-start(bf16[1024,1280]{1,0:T(8,128)(2,1)} %v_here.3) | copy-start | bytes 7864324
  14.4 32.5 %collective-permute-start.5 = (bf16[1024,640]{1,0:T(8,128)(2,1)S(1)}, bf16[1024,640]{1,0:T(8,128)(2,1)S(1)}, u32[]{:S(2)}, u32[]{:S(2)}) collective-permute-start(bf16[1024,640]{1,0:T(8,128)(2,1)S(1)} %mask_integrals.1), channel_id=1, source_target_pairs={{0,16},{16,0},{1,17},{17,1},{2,18},{18,2},{3,19},{19,3},{4,20},{20... | collective-permute-start | bytes 3932168 | tf_op jit(solution)/shard_map/ppermute | solution.py:248
  23.0 26.4 %collective-permute-start.3 = (bf16[320,640]{1,0:T(8,128)(2,1)S(1)}, bf16[320,640]{1,0:T(8,128)(2,1)S(1)}, u32[]{:S(2)}, u32[]{:S(2)}) collective-permute-start(bf16[320,640]{1,0:T(8,128)(2,1)S(1)} %get-tuple-element.46), channel_id=1, source_target_pairs={{0,8},{4,12},{8,0},{12,4},{1,9},{5,13},{9,1},{13,5},{2,10},{6,14},... | collective-permute-start | bytes 1228808 | tf_op jit(solution)/shard_map/ppermute | solution.py:248
  25.7 23.8 %collective-permute-start.4 = (bf16[320,640]{1,0:T(8,128)(2,1)S(1)}, bf16[320,640]{1,0:T(8,128)(2,1)S(1)}, u32[]{:S(2)}, u32[]{:S(2)}) collective-permute-start(bf16[320,640]{1,0:T(8,128)(2,1)S(1)} %get-tuple-element.47), channel_id=1, source_target_pairs={{0,12},{4,0},{8,4},{12,8},{1,13},{5,1},{9,5},{13,9},{2,14},{6,2},{... | collective-permute-start | bytes 1228808 | tf_op jit(solution)/shard_map/ppermute | solution.py:248
  49.5 6.0 %collective-permute-start.7 = (bf16[320,640]{1,0:T(8,128)(2,1)S(1)}, bf16[320,640]{1,0:T(8,128)(2,1)S(1)}, u32[]{:S(2)}, u32[]{:S(2)}) collective-permute-start(bf16[320,640]{1,0:T(8,128)(2,1)S(1)} %collective-permute-done.3.away_here), channel_id=1, source_target_pairs={{0,1},{1,0},{2,3},{3,2},{4,5},{5,4},{6,7},{7,6},{8,9},{9,8},{10,11... | collective-permute-start | bytes 1228808 | tf_op jit(solution)/shard_map/ppermute | solution.py:251
  49.6 14.5 %collective-permute-start.10 = (bf16[320,640]{1,0:T(8,128)(2,1)S(1)}, bf16[320,640]{1,0:T(8,128)(2,1)S(1)}, u32[]{:S(2)}, u32[]{:S(2)}) collective-permute-start(bf16[320,640]{1,0:T(8,128)(2,1)S(1)} %collective-permute-done.4.away_here), channel_id=1, source_target_pairs={{0,1},{1,0},{2,3},{3,2},{4,5},{5,4},{6,7},{7,6},{8,9},{9,8},{10,11... | collective-permute-start | bytes 1228808 | tf_op jit(solution)/shard_map/ppermute | solution.py:251
  50.1 17.9 %collective-permute-start.6 = (bf16[320,640]{1,0:T(8,128)(2,1)S(1)}, bf16[320,640]{1,0:T(8,128)(2,1)S(1)}, u32[]{:S(2)}, u32[]{:S(2)}) collective-permute-start(bf16[320,640]{1,0:T(8,128)(2,1)S(1)} %get-tuple-element.53), channel_id=1, source_target_pairs={{0,4},{4,8},{8,12},{12,0},{1,5},{5,9},{9,13},{13,1},{2,6},{6,10},{... | collective-permute-start | bytes 1228808 | tf_op jit(solution)/shard_map/ppermute | solution.py:248
  54.0 9.4 %collective-permute-start.9 = (s16[2,320,256]{2,1,0:T(8,128)(2,1)S(1)}, s16[2,320,256]{2,1,0:T(8,128)(2,1)S(1)}, u32[]{:S(2)}, u32[]{:S(2)}) collective-permute-start(s16[2,320,256]{2,1,0:T(8,128)(2,1)S(1)} %get-tuple-element.49), channel_id=1, source_target_pairs={{0,2},{1,3},{2,0},{3,1},{4,6},{5,7},{6,4},{7,5},{8,10},{9,11},{10,... | collective-permute-start | bytes 983048 | tf_op jit(solution)/shard_map/ppermute | solution.py:254
  58.1 9.1 %collective-permute-start.8 = (s16[320,512]{1,0:T(8,128)(2,1)S(1)}, s16[320,512]{1,0:T(8,128)(2,1)S(1)}, u32[]{:S(2)}, u32[]{:S(2)}) collective-permute-start(s16[320,512]{1,0:T(8,128)(2,1)S(1)} %get-tuple-element.55), channel_id=1, source_target_pairs={{0,16},{16,0},{1,17},{17,1},{2,18},{18,2},{3,19},{19,3},{4,20},{20... | collective-permute-start | bytes 983048 | tf_op jit(solution)/shard_map/ppermute | solution.py:248
  68.0 1.8 %collective-permute-start.11 = (bf16[320,640]{1,0:T(8,128)(2,1)S(1)}, bf16[320,640]{1,0:T(8,128)(2,1)S(1)}, u32[]{:S(2)}, u32[]{:S(2)}) collective-permute-start(bf16[320,640]{1,0:T(8,128)(2,1)S(1)} %collective-permute-done.6.away_here), channel_id=1, source_target_pairs={{0,1},{1,0},{2,3},{3,2},{4,5},{5,4},{6,7},{7,6},{8,9},{9,8},{10,11... | collective-permute-start | bytes 1228808 | tf_op jit(solution)/shard_map/ppermute | solution.py:251
  68.0 21.6 %collective-permute-start.18 = (s16[320,512]{1,0:T(8,128)(2,1)S(1)}, s16[320,512]{1,0:T(8,128)(2,1)S(1)}, u32[]{:S(2)}, u32[]{:S(2)}) collective-permute-start(s16[320,512]{1,0:T(8,128)(2,1)S(1)} %get-tuple-element.58), channel_id=1, source_target_pairs={{0,16},{16,0},{1,17},{17,1},{2,18},{18,2},{3,19},{19,3},{4,20},{20... | collective-permute-start | bytes 983048 | tf_op jit(solution)/shard_map/ppermute | solution.py:248
  72.3 19.2 %collective-permute-start.12 = (s16[2,320,256]{2,1,0:T(8,128)(2,1)S(1)}, s16[2,320,256]{2,1,0:T(8,128)(2,1)S(1)}, u32[]{:S(2)}, u32[]{:S(2)}) collective-permute-start(s16[2,320,256]{2,1,0:T(8,128)(2,1)S(1)} %get-tuple-element.62), channel_id=1, source_target_pairs={{0,2},{1,3},{2,0},{3,1},{4,6},{5,7},{6,4},{7,5},{8,10},{9,11},{10,... | collective-permute-start | bytes 983048 | tf_op jit(solution)/shard_map/ppermute | solution.py:254
  73.3 8.3 %collective-permute-start.14 = (s16[320,256]{1,0:T(8,128)(2,1)S(1)}, s16[320,256]{1,0:T(8,128)(2,1)S(1)}, u32[]{:S(2)}, u32[]{:S(2)}) collective-permute-start(s16[320,256]{1,0:T(8,128)(2,1)S(1)} %get-tuple-element.64), channel_id=1, source_target_pairs={{0,16},{16,0},{1,17},{17,1},{2,18},{18,2},{3,19},{19,3},{4,20},{20... | collective-permute-start | bytes 491528 | tf_op jit(solution)/shard_map/ppermute | solution.py:248
  73.9 11.8 %collective-permute-start.13 = (s16[320,256]{1,0:T(8,128)(2,1)S(1)}, s16[320,256]{1,0:T(8,128)(2,1)S(1)}, u32[]{:S(2)}, u32[]{:S(2)}) collective-permute-start(s16[320,256]{1,0:T(8,128)(2,1)S(1)} %get-tuple-element.63), channel_id=1, source_target_pairs={{0,2},{1,3},{2,0},{3,1},{4,6},{5,7},{6,4},{7,5},{8,10},{9,11},{10,... | collective-permute-start | bytes 491528 | tf_op jit(solution)/shard_map/ppermute | solution.py:254
  86.2 10.4 %collective-permute-start.16 = (bf16[320,256]{1,0:T(8,128)(2,1)S(1)}, bf16[320,256]{1,0:T(8,128)(2,1)S(1)}, u32[]{:S(2)}, u32[]{:S(2)}) collective-permute-start(bf16[320,256]{1,0:T(8,128)(2,1)S(1)} %round_pairs.4.refs_1_), channel_id=1, source_target_pairs={{0,8},{4,12},{8,0},{12,4},{1,9},{5,13},{9,1},{13,5},{2,10},{6,14},... | collective-permute-start | bytes 491528 | tf_op jit(solution)/shard_map/ppermute | solution.py:248
  90.4 6.3 %collective-permute-start.19 = (s16[320,256]{1,0:T(8,128)(2,1)S(1)}, s16[320,256]{1,0:T(8,128)(2,1)S(1)}, u32[]{:S(2)}, u32[]{:S(2)}) collective-permute-start(s16[320,256]{1,0:T(8,128)(2,1)S(1)} %get-tuple-element.74), channel_id=1, source_target_pairs={{0,2},{1,3},{2,0},{3,1},{4,6},{5,7},{6,4},{7,5},{8,10},{9,11},{10,... | collective-permute-start | bytes 491528 | tf_op jit(solution)/shard_map/ppermute | solution.py:254
  92.2 5.4 %collective-permute-start.15 = (s16[320,256]{1,0:T(8,128)(2,1)S(1)}, s16[320,256]{1,0:T(8,128)(2,1)S(1)}, u32[]{:S(2)}, u32[]{:S(2)}) collective-permute-start(s16[320,256]{1,0:T(8,128)(2,1)S(1)} %get-tuple-element.68), channel_id=1, source_target_pairs={{0,16},{16,0},{1,17},{17,1},{2,18},{18,2},{3,19},{19,3},{4,20},{20... | collective-permute-start | bytes 491528 | tf_op jit(solution)/shard_map/ppermute | solution.py:248
  97.3 9.0 %collective-permute-start.20 = (bf16[320,256]{1,0:T(8,128)(2,1)S(1)}, bf16[320,256]{1,0:T(8,128)(2,1)S(1)}, u32[]{:S(2)}, u32[]{:S(2)}) collective-permute-start(bf16[320,256]{1,0:T(8,128)(2,1)S(1)} %round_pairs.7.refs_3_), channel_id=1, source_target_pairs={{0,4},{4,8},{8,12},{12,0},{1,5},{5,9},{9,13},{13,1},{2,6},{6,10},{... | collective-permute-start | bytes 491528 | tf_op jit(solution)/shard_map/ppermute | solution.py:248
  98.2 12.2 %collective-permute-start.17 = (bf16[320,256]{1,0:T(8,128)(2,1)S(1)}, bf16[320,256]{1,0:T(8,128)(2,1)S(1)}, u32[]{:S(2)}, u32[]{:S(2)}) collective-permute-start(bf16[320,256]{1,0:T(8,128)(2,1)S(1)} %round_pairs.6.refs_0_), channel_id=1, source_target_pairs={{0,12},{4,0},{8,4},{12,8},{1,13},{5,1},{9,5},{13,9},{2,14},{6,2},{... | collective-permute-start | bytes 491528 | tf_op jit(solution)/shard_map/ppermute | solution.py:248

commit v8 on v5

--- a/solution.py
+++ b/solution.py
@@ -12,7 +12,7 @@
 TOP = 32000.0
 STEPS = 256.0
 CORES = 2
-TILE = 512
+TILE = 1264
 LANES = 128
 VMEM_BYTES = 32 * 2**20
 
@@ -154,11 +154,11 @@
     kept_ref[...] = masked[half:]
 
 
-def sum_body(first, count, groups, y_first, s_ref, own_here, own_there, *refs):
+def sum_body(first, count, groups, way, s_ref, own_here, own_there, *refs):
     away, refs = refs[: 2 * count], refs[2 * count :]
     keeps, passes, outs = refs[:groups], refs[groups : 2 * groups - 1], refs[2 * groups - 1 :]
     high, tall = outs[-1].shape[-2:]
-    tall = tall if y_first else tall // 2
+    tall = tall // 2 if way == "x" else tall
     chunk = high // count
     pairs = own_here.shape[0] - 2 * tall
 
@@ -169,18 +169,22 @@
     tr = jnp.concatenate([rows(ref) for ref in away[:count]], axis=0)
     tro = jnp.concatenate([rows(ref) for ref in away[count:]], axis=0)
     left = jnp.concatenate([own_here[mine], own_there[mine], tr, tro], axis=1)
-    for g in range(groups):
+    for g in reversed(range(groups)):
         start = keeps[g].shape[0] - 2 * tall
         a = keeps[g][start:]
         b = own_there[pairs:] if g == 0 else passes[g - 1][: 2 * tall]
         total = dot_nt(left, jnp.concatenate([a, b, -a, -b], axis=1))
-        if y_first:
+        if way == "y":
             outs[0][g] = encode(total[:, :tall])
             outs[1][g] = total[:, tall:]
-        elif g == 0:
-            outs[-1][...] = total
-        else:
-            outs[g - 1][...] = encode(total)
+        elif way == "x":
+            if g == 0:
+                outs[-1][...] = total
+            else:
+                outs[g - 1][...] = encode(total)
+        else:
+            outs[2 * g][...] = encode(total[:, :tall])
+            outs[2 * g + 1][...] = total[:, tall:] if g == 0 else encode(total[:, tall:])
 
 
 def add_y_body(s_ref, kept_ref, coded_ref, own_ref, *out_refs):
@@ -212,25 +216,24 @@
         out_ref[...] = rounded[k * chunk : (k + 1) * chunk]
 
 
-def place_body(order, n, col_n, before, s_ref, *refs):
+def place_body(items, n, col_n, before, s_ref, *refs):
     out_ref = refs[-1]
     z = s_ref[1]
     chunk = refs[0].shape[0]
     place = lax.broadcasted_iota(jnp.int32, (1, chunk), 1)
     at = lax.broadcasted_iota(jnp.int32, (out_ref.shape[0], chunk), 0) + pl.program_id(0) * out_ref.shape[0]
     signs = []
-    for r in order:
+    for r, mine in items:
         if r == 0:
             inside, turned = inside_columns(place, n, z)
-            signs.append(jnp.where(at == inside, 1.0, jnp.where(at == turned, -1.0, 0.0)))
-        else:
-            plus = pair_columns(place, n, z, lax.rem(z + r, col_n), True)
-            minus = pair_columns(place, n, z, lax.rem(z - r + col_n, col_n), False)
-            signs.append(jnp.where(at == plus, 1.0, 0.0))
-            signs.append(jnp.where(at == minus, -1.0, 0.0))
-    signs = jnp.concatenate([sign.astype(jnp.bfloat16) for sign in signs], axis=1)
-    values = jnp.concatenate([ref[...] for ref in refs[: 2 * len(order) - order.count(0)]], axis=0)
-    total = dot_nn(signs, values)
+            sign = jnp.where(at == inside, 1.0, jnp.where(at == turned, -1.0, 0.0))
+        elif mine:
+            sign = jnp.where(at == pair_columns(place, n, z, lax.rem(z + r, col_n), True), 1.0, 0.0)
+        else:
+            sign = jnp.where(at == pair_columns(place, n, z, lax.rem(z - r + col_n, col_n), False), -1.0, 0.0)
+        signs.append(sign.astype(jnp.bfloat16))
+    values = jnp.concatenate([ref[...] for ref in refs[: len(items)]], axis=0)
+    total = dot_nn(jnp.concatenate(signs, axis=1), values)
     if before:
         total = total + refs[-2][...].astype(jnp.float32)
     out_ref[...] = total.astype(jnp.bfloat16)
@@ -248,9 +251,6 @@
     chunk = -(-((n * n + 1) // 2 + 1) // 16) * 16
     far = col_n // 2
     near = [r for r in range(1, col_n) if r != far]
-    half = (len(near) + 1) // 2
-    groups = [([0] + near[:half], True), (near[half:], False), ([far], False)]
-    groups = [(group, y_first) for group, y_first in groups if group]
     order = [0] + near + [far]
     bf16, i16, f32 = jnp.bfloat16, jnp.int16, jnp.float32
 
@@ -263,6 +263,13 @@
 
     def other_y(array):
         return lax.ppermute(array, "depth", [(i, i ^ 2) for i in range(depth_n)])
+
+    def across(array, by):
+        pairs = [(i * depth_n + j, (i + by) % row_n * depth_n + (j ^ 2)) for i in range(row_n) for j in range(depth_n)]
+        return lax.ppermute(array, ("row", "depth"), pairs)
+
+    def after(values, *earlier):
+        return lax.optimization_barrier((values, earlier))[0]
 
     scalars = jnp.stack([x, z, y, core]).astype(jnp.int32)
     ab_row, cd_row = ab_irrep.reshape(-1, LANES), cd_irrep.reshape(-1, LANES)
@@ -304,65 +311,89 @@
     away[far] = shift(far_sent, "col", -far)
     passed = [other_core(a) for a in kept[1:]]
 
-    rounded, arrived = {}, []
-    for group, y_first in groups:
+    crossed, added, rounded = {}, {}, {}
+
+    def sum_pairs(group, way):
         first, count = order.index(group[0]), len(group)
         high = count * chunk
-        if far in group:
-            _, away[far] = lax.optimization_barrier((arrived, away[far]))
-            away_there[far] = other_core(away[far])
+        if way == "y":
+            shapes = [((row_n, high, tall), i16), ((row_n, high, tall), f32)]
+        elif way == "x":
+            shapes = [((high, 2 * tall), i16)] * (row_n - 1) + [((high, 2 * tall), f32)]
+        else:
+            shapes = [((high, tall), i16), ((high, tall), f32)] + [((high, tall), i16)] * (2 * row_n - 2)
         here = [both if r == 0 else away[r] for r in group]
         there = [both_there if r == 0 else away_there[r] for r in group]
-        if group == groups[1][0]:
-            _, here[0] = lax.optimization_barrier((sums[0], here[0]))
-        if y_first:
-            shapes = [((row_n, high, tall), i16), ((row_n, high, tall), f32)]
-        else:
-            shapes = [((high, 2 * tall), i16)] * (row_n - 1) + [((high, 2 * tall), f32)]
         sums = call(
             "sum_pairs",
-            functools.partial(sum_body, first, count, row_n, y_first),
+            functools.partial(sum_body, first, count, row_n, way),
             scalars,
             [both, both_there] + here + there + kept + passed,
             shapes,
         )
-        if y_first:
-            own_sum, *others = call(
+        if way == "y":
+            crossed[group] = [sums[1], other_y(sums[0])]
+        elif way == "x":
+            crossed[group] = [sums[-1]] + [shift(value, "row", by + 1) for by, value in enumerate(sums[:-1])]
+        else:
+            crossed[group] = [sums[1], other_y(sums[0])]
+            for by in range(1, row_n):
+                crossed[group] += [across(sums[2 * by], by), shift(sums[2 * by + 1], "row", by)]
+        return sums
+
+    def add_pairs(group, way):
+        high = len(group) * chunk
+        if way == "y":
+            own_sum, *coded = call(
                 "add_other_y",
                 add_y_body,
                 scalars,
-                [sums[1], other_y(sums[0])],
+                crossed[group],
                 [((high, tall), f32)] + [((high, tall), i16)] * (row_n - 1),
             )
-            last = [shift(other, "row", by + 1) for by, other in enumerate(others)]
-        else:
-            arrived = [shift(coded, "row", by + 1) for by, coded in enumerate(sums[:-1])]
+            added[group] = [own_sum] + [shift(value, "row", by + 1) for by, value in enumerate(coded)]
+        else:
             coded, own_sum = call(
-                "add_other_x",
-                add_x_body,
-                scalars,
-                [sums[-1]] + arrived,
-                [((high, tall), i16), ((high, tall), f32)],
+                "add_other_x", add_x_body, scalars, crossed[group], [((high, tall), i16), ((high, tall), f32)]
             )
-            last = [other_y(coded)]
+            added[group] = [own_sum, other_y(coded)]
+        return own_sum
+
+    def round_pairs(group, sums):
         mine = call(
             "round_pairs",
-            functools.partial(round_body, count),
+            functools.partial(round_body, len(group)),
             scalars,
-            [own_sum] + last,
-            [((chunk, tall), bf16)] * count,
+            sums,
+            [((chunk, tall), bf16)] * len(group),
         )
         for r, value in zip(group, mine):
-            rounded[r] = [value] if r == 0 else [value, shift(value, "col", r)]
+            rounded[r, True] = value
+            if r:
+                rounded[r, False] = shift(value, "col", r)
+        return mine
+
+    y_group, x_group, last = (0, *near[:1]), tuple(near[1:]), (far,)
+    sum_pairs(x_group, "x")
+    sums = sum_pairs(y_group, "y")
+    early = add_pairs(x_group, "x")
+    away[far] = after(away[far], early, sums)
+    away_there[far] = other_core(away[far])
+    sums = sum_pairs(last, "direct")
+    round_pairs(x_group, after(added[x_group], sums))
+    early = add_pairs(y_group, "y")
+    round_pairs(last, after(crossed[last], early, [rounded[r, False] for r in x_group]))
+    round_pairs(y_group, added[y_group])
 
     done = None
-    for group in ([0] + near, [far]):
-        sources = [value for r in group for value in rounded[r]]
+    ends = [(r, False) for r in near[:1] + [far]]
+    for items in ([item for item in rounded if item not in ends], ends):
+        sources = [rounded[item] for item in items]
         tile = (TILE, tall), lambda g, s: (g, 0)
         sources += [] if done is None else [(done, *tile)]
         (done,) = call(
             "place_pairs",
-            functools.partial(place_body, group, n, col_n, done is not None),
+            functools.partial(place_body, items, n, col_n, done is not None),
             scalars,
             sources,
             [((columns, tall), bf16, *tile)],

time: 103 us -> 101 us (0.981)
  waiting for transfers between devices: 31.8 us -> 34.4 us
  Pallas kernels: 40.1 us -> 37.7 us
  starting transfers between devices: 27.2 us -> 25.6 us
    ppermute x3, waiting for transfers between devices: 2.4 us -> 5.99 us  [other_y(): return lax.ppermute(array, 'depth', [(i, i ^ 2) for i in range(depth_n)])]
    pallas_call x14 -> x13, Pallas kernels: 40.1 us -> 37.7 us  [call(): pl.pallas_call(body, name=name, out_shape=shapes, compiler_params=pltpu.C...]
    ppermute x5, waiting for transfers between devices: 5.38 us -> 3.64 us  [other_core(): return lax.ppermute(array, 'depth', [(i, i ^ 1) for i in range(depth_n)])]
    ppermute x3, starting transfers between devices: 5.12 us -> 3.72 us  [other_y(): return lax.ppermute(array, 'depth', [(i, i ^ 2) for i in range(depth_n)])]
    ppermute x10, starting transfers between devices: 21.1 us -> 19.9 us  [shift(): lax.ppermute(array, axis, [(i, (i + by) % count) for i in range(count)])]
  transfers between devices with their start and end apart: 18 -> 19, of which waited for: 11 -> 10; matrix products, arithmetic and copies ran while one was open for 0% -> 0% of each run, Pallas kernels for 33% -> 32%
where the time goes in v8:
time: 101 us
  Pallas kernels  37.7 us (37%)
  waiting for transfers between devices  34.4 us (34%)
  starting transfers between devices  25.6 us (25%)
  local copies, waits for them, and re-layouts  3.14 us (3%)
    pallas_call x13, Pallas kernels, call(): pl.pallas_call(body, name=name, out_shape=shapes, compiler_params=pltpu.C...  37.7 us
    ppermute x10, waiting for transfers between devices, shift(): lax.ppermute(array, axis, [(i, (i + by) % count) for i in range(count)])  23.9 us
    ppermute x10, starting transfers between devices, shift(): lax.ppermute(array, axis, [(i, (i + by) % count) for i in range(count)])  19.9 us
    ppermute x3, waiting for transfers between devices, other_y(): return lax.ppermute(array, 'depth', [(i, i ^ 2) for i in range(depth_n)])  5.99 us
    ppermute x3, starting transfers between devices, other_y(): return lax.ppermute(array, 'depth', [(i, i ^ 2) for i in range(depth_n)])  3.72 us
    ppermute x5, waiting for transfers between devices, other_core(): return lax.ppermute(array, 'depth', [(i, i ^ 1) for i in range(depth_n)])  3.64 us
    unnamed x12, local copies, waits for them, and re-layouts  3.14 us
  transfers between devices with their start and end apart: 19, of which 10 were waited for; matrix products, arithmetic and copies ran while one was open for 0% of the time, Pallas kernels for 32%

profile of v8, /device:TPU:0, one launch (start us, length us, event | category | flops | bytes accessed | tf_op | source)
XLA Modules:
  0.0 101.0 jit_solution(4456043519723919259)
XLA Ops:
  0.0 0.1 pad_add_fusion.s_ref
  0.1 1.7 %copy-done = bf16[1024,1280]{1,0:T(8,128)(2,1)S(1)} copy-done((bf16[1024,1280]{1,0:T(8,128)(2,1)S(1)}, bf16[1024,1280]{1,0:T(8,128)(2,1)}, u32[]{:S(2)}) %copy-start) | copy-done | bytes 2621464
  1.8 0.7 copy-done.3
  2.5 0.7 copy-done.5
  3.2 2.9 %mask_integrals.1 = bf16[1024,640]{1,0:T(8,128)(2,1)S(1)} custom-call(s32[4]{0:T(128)S(1)} %pad_add_fusion.s_ref, s32[8,128]{1,0:T(8,128)S(1)} %bitcast.9, s32[10,128]{1,0:T(8,128)S(1)} %bitcast.7, bf16[1024,1280]{1,0:T(8,128)(2,1)S(1)} %copy-done), custom_call_target="tpu_custom_call" | custom-call | flops 1 | bytes 1 | tf_op jit(solution)/shard_map/mask_integrals/pallas_call | solution.py:86
  6.1 0.0 copy-start.1
  6.1 0.0 copy-start.4
  6.1 3.0 %collective-permute-start = (bf16[1024,640]{1,0:T(8,128)(2,1)S(1)}, bf16[1024,640]{1,0:T(8,128)(2,1)S(1)}, u32[]{:S(2)}, u32[]{:S(2)}) collective-permute-start(bf16[1024,640]{1,0:T(8,128)(2,1)S(1)} %mask_integrals.1), channel_id=1, source_target_pairs={{0,16},{16,0},{1,17},{17,1},{2,18},{18,2},{3,19},{19,3},{4,20},{20... | collective-permute-start | bytes 3932168 | tf_op jit(solution)/shard_map/ppermute | solution.py:259
  9.1 5.1 %send_columns.1 = (bf16[640,2560]{1,0:T(8,128)(2,1)S(1)}, bf16[320,640]{1,0:T(8,128)(2,1)S(1)}, bf16[320,640]{1,0:T(8,128)(2,1)S(1)}, bf16[320,640]{1,0:T(8,128)(2,1)S(1)}) custom-call(s32[4]{0:T(128)S(1)} %pad_add_fusion.s_ref, bf16[320,2,2500]{2,1,0:T(2,128)(2,1)S(1)} %copy-done.2), custom_call_target="tpu_custom_call" | custom-call | flops 1 | bytes 1 | tf_op jit(solution)/shard_map/send_columns/pallas_call | solution.py:86
  14.3 3.7 %collective-permute-start.1 = (bf16[320,640]{1,0:T(8,128)(2,1)S(1)}, bf16[320,640]{1,0:T(8,128)(2,1)S(1)}, u32[]{:S(2)}, u32[]{:S(2)}) collective-permute-start(bf16[320,640]{1,0:T(8,128)(2,1)S(1)} %get-tuple-element.44), channel_id=1, source_target_pairs={{0,12},{4,0},{8,4},{12,8},{1,13},{5,1},{9,5},{13,9},{2,14},{6,2},{... | collective-permute-start | bytes 1228808 | tf_op jit(solution)/shard_map/ppermute | solution.py:259
  17.9 0.0 collective-permute-start.2
  17.9 9.6 %keep_columns.1 = (bf16[2112,640]{1,0:T(8,128)(2,1)S(1)}, bf16[512,640]{1,0:T(8,128)(2,1)S(1)}) custom-call(s32[4]{0:T(128)S(1)} %pad_add_fusion.s_ref, bf16[640,2560]{1,0:T(8,128)(2,1)S(1)} %get-tuple-element.41.flat_ref, s32[8,128]{1,0:T(8,128)S(1)} %bitcast.10, s32[10,128]{1,0:T(8,128)S(1)} %bitcast.8, bf16[1024,1280]{1,0:T(8,128)(2,1)S(1)} %copy-done.1), custom_call_target="tpu_custom_call" | custom-call | flops 1 | bytes 1 | tf_op jit(solution)/shard_map/keep_columns/pallas_call | solution.py:86
  27.5 0.3 collective-permute-done.1.refs_1_
  27.8 8.2 %collective-permute-done.2.refs_0_ = bf16[320,640]{1,0:T(8,128)(2,1)S(1)} collective-permute-done((bf16[320,640]{1,0:T(8,128)(2,1)S(1)}, bf16[320,640]{1,0:T(8,128)(2,1)S(1)}, u32[]{:S(2)}, u32[]{:S(2)}) %collective-permute-start.2) | collective-permute-done | bytes 409632 | tf_op jit(solution)/shard_map/ppermute | solution.py:259
  36.0 1.8 %collective-permute-done.refs_5_.refs_3_ = bf16[1024,640]{1,0:T(8,128)(2,1)S(1)} collective-permute-done((bf16[1024,640]{1,0:T(8,128)(2,1)S(1)}, bf16[1024,640]{1,0:T(8,128)(2,1)S(1)}, u32[]{:S(2)}, u32[]{:S(2)}) %collective-permute-start) | collective-permute-done | bytes 1310752 | tf_op jit(solution)/shard_map/ppermute | solution.py:259
  37.9 0.0 collective-permute-start.3
  37.9 0.5 collective-permute-start.5
  38.4 0.0 collective-permute-start.4
  38.4 0.5 collective-permute-start.10
  38.9 2.8 %collective-permute-start.9 = (bf16[320,640]{1,0:T(8,128)(2,1)S(1)}, bf16[320,640]{1,0:T(8,128)(2,1)S(1)}, u32[]{:S(2)}, u32[]{:S(2)}) collective-permute-start(bf16[320,640]{1,0:T(8,128)(2,1)S(1)} %get-tuple-element.57), channel_id=1, source_target_pairs={{0,8},{4,12},{8,0},{12,4},{1,9},{5,13},{9,1},{13,5},{2,10},{6,14},... | collective-permute-start | bytes 1228808 | tf_op jit(solution)/shard_map/ppermute | solution.py:259
  41.7 3.6 %collective-permute-done.4.refs_3_ = bf16[320,640]{1,0:T(8,128)(2,1)S(1)} collective-permute-done((bf16[320,640]{1,0:T(8,128)(2,1)S(1)}, bf16[320,640]{1,0:T(8,128)(2,1)S(1)}, u32[]{:S(2)}, u32[]{:S(2)}) %collective-permute-start.4) | collective-permute-done | bytes 409632 | tf_op jit(solution)/shard_map/ppermute | solution.py:262
  45.4 4.3 %sum_pairs.3 = (s16[2,640,256]{2,1,0:T(8,128)(2,1)S(1)}, f32[2,640,256]{2,1,0:T(8,128)S(1)}) custom-call(s32[4]{0:T(128)S(1)} %pad_add_fusion.s_ref, bf16[2112,640]{1,0:T(8,128)(2,1)S(1)} %get-tuple-element.48.own_here.refs_0_, bf16[2112,640]{1,0:T(8,128)(2,1)S(1)} %collective-permute-done.3.own_there.refs_2_, ...), custom_call_target="tpu_custom_call" | custom-call | flops 1 | bytes 1 | tf_op jit(solution)/shard_map/sum_pairs/pallas_call | solution.py:86
  49.7 1.8 %collective-permute-start.6 = (s16[2,640,256]{2,1,0:T(8,128)(2,1)S(1)}, s16[2,640,256]{2,1,0:T(8,128)(2,1)S(1)}, u32[]{:S(2)}, u32[]{:S(2)}) collective-permute-start(s16[2,640,256]{2,1,0:T(8,128)(2,1)S(1)} %get-tuple-element.53), channel_id=1, source_target_pairs={{0,2},{1,3},{2,0},{3,1},{4,6},{5,7},{6,4},{7,5},{8,10},{9,11},{10,... | collective-permute-start | bytes 1966088 | tf_op jit(solution)/shard_map/ppermute | solution.py:265
  51.5 2.7 %sum_pairs.4 = (s16[320,512]{1,0:T(8,128)(2,1)S(1)}, f32[320,512]{1,0:T(8,128)S(1)}) custom-call(s32[4]{0:T(128)S(1)} %pad_add_fusion.s_ref, bf16[2112,640]{1,0:T(8,128)(2,1)S(1)} %get-tuple-element.48.own_here.refs_0_, bf16[2112,640]{1,0:T(8,128)(2,1)S(1)} %collective-permute-done.3.own_there.refs_2_, bf16[320,640]{1,0:T(8,128)(2,1)S(1)} %collective-permute-done.2.refs_0_, ...), custom_call_target="tpu_custom_call" | custom-call | flops 1 | bytes 1 | tf_op jit(solution)/shard_map/sum_pairs/pallas_call | solution.py:86
  54.2 1.6 %collective-permute-start.11 = (s16[320,512]{1,0:T(8,128)(2,1)S(1)}, s16[320,512]{1,0:T(8,128)(2,1)S(1)}, u32[]{:S(2)}, u32[]{:S(2)}) collective-permute-start(s16[320,512]{1,0:T(8,128)(2,1)S(1)} %get-tuple-element.60), channel_id=1, source_target_pairs={{0,16},{16,0},{1,17},{17,1},{2,18},{18,2},{3,19},{19,3},{4,20},{20... | collective-permute-start | bytes 983048 | tf_op jit(solution)/shard_map/ppermute | solution.py:259
  55.8 8.0 %collective-permute-done.11.refs_0_ = s16[320,512]{1,0:T(8,128)(2,1)S(1)} collective-permute-done((s16[320,512]{1,0:T(8,128)(2,1)S(1)}, s16[320,512]{1,0:T(8,128)(2,1)S(1)}, u32[]{:S(2)}, u32[]{:S(2)}) %collective-permute-start.11) | collective-permute-done | bytes 327712 | tf_op jit(solution)/shard_map/ppermute | solution.py:259
  63.8 0.7 add_other_x.1
  64.5 0.1 collective-permute-start.12
  64.6 0.4 collective-permute-start.16
  65.0 1.6 %collective-permute-done.6.coded_ref = s16[2,640,256]{2,1,0:T(8,128)(2,1)S(1)} collective-permute-done((s16[2,640,256]{2,1,0:T(8,128)(2,1)S(1)}, s16[2,640,256]{2,1,0:T(8,128)(2,1)S(1)}, u32[]{:S(2)}, u32[]{:S(2)}) %collective-permute-start.6) | collective-permute-done | bytes 655392 | tf_op jit(solution)/shard_map/ppermute | solution.py:265
  66.5 0.9 add_other_y.1
  67.5 1.8 %collective-permute-start.7 = (s16[640,256]{1,0:T(8,128)(2,1)S(1)}, s16[640,256]{1,0:T(8,128)(2,1)S(1)}, u32[]{:S(2)}, u32[]{:S(2)}) collective-permute-start(s16[640,256]{1,0:T(8,128)(2,1)S(1)} %get-tuple-element.55), channel_id=1, source_target_pairs={{0,16},{16,0},{1,17},{17,1},{2,18},{18,2},{3,19},{19,3},{4,20},{20... | collective-permute-start | bytes 983048 | tf_op jit(solution)/shard_map/ppermute | solution.py:259
  69.3 2.5 %sum_pairs.5 = (s16[320,256]{1,0:T(8,128)(2,1)S(1)}, f32[320,256]{1,0:T(8,128)S(1)}, s16[320,256]{1,0:T(8,128)(2,1)S(1)}, s16[320,256]{1,0:T(8,128)(2,1)S(1)}) custom-call(s32[4]{0:T(128)S(1)} %pad_add_fusion.s_ref, bf16[2112,640]{1,0:T(8,128)(2,1)S(1)} %get-tuple-element.48.own_here.refs_0_, bf16[2112,640]{1,0:T(8,128)(2,1)S(1)} %collective-permute-done.3.own_there.refs_2_, ...), custom_call_target="tpu_custom_call" | custom-call | flops 1 | bytes 1 | tf_op jit(solution)/shard_map/sum_pairs/pallas_call | solution.py:86
  71.8 0.6 round_pairs.4.refs_0_
  72.4 3.7 %collective-permute-start.17 = (bf16[320,256]{1,0:T(8,128)(2,1)S(1)}, bf16[320,256]{1,0:T(8,128)(2,1)S(1)}, u32[]{:S(2)}, u32[]{:S(2)}) collective-permute-start(bf16[320,256]{1,0:T(8,128)(2,1)S(1)} %round_pairs.4.refs_0_), channel_id=1, source_target_pairs={{0,12},{4,0},{8,4},{12,8},{1,13},{5,1},{9,5},{13,9},{2,14},{6,2},{... | collective-permute-start | bytes 491528 | tf_op jit(solution)/shard_map/ppermute | solution.py:259
  76.1 1.5 %collective-permute-start.13 = (s16[320,256]{1,0:T(8,128)(2,1)S(1)}, s16[320,256]{1,0:T(8,128)(2,1)S(1)}, u32[]{:S(2)}, u32[]{:S(2)}) collective-permute-start(s16[320,256]{1,0:T(8,128)(2,1)S(1)} %get-tuple-element.64), channel_id=1, source_target_pairs={{0,2},{1,3},{2,0},{3,1},{4,6},{5,7},{6,4},{7,5},{8,10},{9,11},{10,... | collective-permute-start | bytes 491528 | tf_op jit(solution)/shard_map/ppermute | solution.py:265
  77.6 0.9 collective-permute-start.14
  78.4 1.1 %collective-permute-start.15 = (s16[320,256]{1,0:T(8,128)(2,1)S(1)}, s16[320,256]{1,0:T(8,128)(2,1)S(1)}, u32[]{:S(2)}, u32[]{:S(2)}) collective-permute-start(s16[320,256]{1,0:T(8,128)(2,1)S(1)} %get-tuple-element.66), channel_id=1, source_target_pairs={{0,16},{16,0},{1,17},{17,1},{2,18},{18,2},{3,19},{19,3},{4,20},{20... | collective-permute-start | bytes 491528 | tf_op jit(solution)/shard_map/ppermute | solution.py:259
  79.6 4.4 %collective-permute-done.13.refs_0_ = s16[320,256]{1,0:T(8,128)(2,1)S(1)} collective-permute-done((s16[320,256]{1,0:T(8,128)(2,1)S(1)}, s16[320,256]{1,0:T(8,128)(2,1)S(1)}, u32[]{:S(2)}, u32[]{:S(2)}) %collective-permute-start.13) | collective-permute-done | bytes 163872 | tf_op jit(solution)/shard_map/ppermute | solution.py:265
  84.0 0.8 collective-permute-done.14.refs_1_
  84.8 0.9 collective-permute-done.15.refs_2_
  85.7 0.7 round_pairs.5.refs_2_
  86.4 0.7 collective-permute-start.18
  87.1 0.6 round_pairs.3
  87.7 1.6 %collective-permute-start.8 = (bf16[320,256]{1,0:T(8,128)(2,1)S(1)}, bf16[320,256]{1,0:T(8,128)(2,1)S(1)}, u32[]{:S(2)}, u32[]{:S(2)}) collective-permute-start(bf16[320,256]{1,0:T(8,128)(2,1)S(1)} %get-tuple-element.56.refs_4_), channel_id=1, source_target_pairs={{0,4},{4,8},{8,12},{12,0},{1,5},{5,9},{9,13},{13,1},{2,6},{6,10},{... | collective-permute-start | bytes 491528 | tf_op jit(solution)/shard_map/ppermute | solution.py:259
  89.4 4.1 %place_pairs.2.refs_2_ = bf16[2500,256]{1,0:T(8,128)(2,1)S(1)} custom-call(s32[4]{0:T(128)S(1)} %pad_add_fusion.s_ref, bf16[320,256]{1,0:T(8,128)(2,1)S(1)} %round_pairs.4.refs_0_, bf16[320,256]{1,0:T(8,128)(2,1)S(1)} %collective-permute-done.17.refs_1_, bf16[320,256]{1,0:T(8,128)(2,1)S(1)} %round_pairs.5.refs_2_, ...), custom_call_target="tpu_custom_call" | custom-call | flops 1 | bytes 1 | tf_op jit(solution)/shard_map/place_pairs/pallas_call | solution.py:86
  93.4 4.7 %collective-permute-done.18.refs_1_ = bf16[320,256]{1,0:T(8,128)(2,1)S(1)} collective-permute-done((bf16[320,256]{1,0:T(8,128)(2,1)S(1)}, bf16[320,256]{1,0:T(8,128)(2,1)S(1)}, u32[]{:S(2)}, u32[]{:S(2)}) %collective-permute-start.18) | collective-permute-done | bytes 163872 | tf_op jit(solution)/shard_map/ppermute | solution.py:259
  98.1 2.9 %place_pairs.3 = bf16[2500,256]{1,0:T(8,128)(2,1)} custom-call(s32[4]{0:T(128)S(1)} %pad_add_fusion.s_ref, bf16[320,256]{1,0:T(8,128)(2,1)S(1)} %collective-permute-done.8.refs_0_, bf16[320,256]{1,0:T(8,128)(2,1)S(1)} %collective-permute-done.18.refs_1_, bf16[2500,256]{1,0:T(8,128)(2,1)S(1)} %place_pairs.2.refs_2_), custom_call_target="tpu_custom_call" | custom-call | flops 1 | bytes 1 | tf_op jit(solution)/shard_map/place_pairs/pallas_call | solution.py:86
  (16 shorter events, 0.0 us)
Async XLA Ops:
  0.1 1.7 %copy-start = (bf16[1024,1280]{1,0:T(8,128)(2,1)S(1)}, bf16[1024,1280]{1,0:T(8,128)(2,1)}, u32[]{:S(2)}) copy-start(bf16[1024,1280]{1,0:T(8,128)(2,1)} %v_ref.3) | copy-start | bytes 7864324
  1.8 0.7 copy-start.3
  2.5 0.7 copy-start.5
  3.2 5.9 %copy-start.2 = (bf16[320,2,2500]{2,1,0:T(2,128)(2,1)S(1)}, bf16[320,2,2500]{2,1,0:T(2,128)(2,1)}, u32[]{:S(2)}) copy-start(bf16[320,2,2500]{2,1,0:T(2,128)(2,1)} %t_ref) | copy-start | bytes 9600004
  6.1 11.8 %copy-start.1 = (bf16[1024,1280]{1,0:T(8,128)(2,1)S(1)}, bf16[1024,1280]{1,0:T(8,128)(2,1)}, u32[]{:S(2)}) copy-start(bf16[1024,1280]{1,0:T(8,128)(2,1)} %v_ref.3) | copy-start | bytes 7864324
  6.1 11.8 %copy-start.4 = (s32[1280]{0:T(1024)S(1)}, s32[1280]{0:T(1024)}, u32[]{:S(2)}) copy-start(s32[1280]{0:T(1024)} %param.7) | copy-start | bytes 15364
  6.1 31.8 %collective-permute-start = (bf16[1024,640]{1,0:T(8,128)(2,1)S(1)}, bf16[1024,640]{1,0:T(8,128)(2,1)S(1)}, u32[]{:S(2)}, u32[]{:S(2)}) collective-permute-start(bf16[1024,640]{1,0:T(8,128)(2,1)S(1)} %mask_integrals.1), channel_id=1, source_target_pairs={{0,16},{16,0},{1,17},{17,1},{2,18},{18,2},{3,19},{19,3},{4,20},{20... | collective-permute-start | bytes 3932168 | tf_op jit(solution)/shard_map/ppermute | solution.py:259
  14.3 13.6 %collective-permute-start.1 = (bf16[320,640]{1,0:T(8,128)(2,1)S(1)}, bf16[320,640]{1,0:T(8,128)(2,1)S(1)}, u32[]{:S(2)}, u32[]{:S(2)}) collective-permute-start(bf16[320,640]{1,0:T(8,128)(2,1)S(1)} %get-tuple-element.44), channel_id=1, source_target_pairs={{0,12},{4,0},{8,4},{12,8},{1,13},{5,1},{9,5},{13,9},{2,14},{6,2},{... | collective-permute-start | bytes 1228808 | tf_op jit(solution)/shard_map/ppermute | solution.py:259
  17.9 18.1 %collective-permute-start.2 = (bf16[320,640]{1,0:T(8,128)(2,1)S(1)}, bf16[320,640]{1,0:T(8,128)(2,1)S(1)}, u32[]{:S(2)}, u32[]{:S(2)}) collective-permute-start(bf16[320,640]{1,0:T(8,128)(2,1)S(1)} %get-tuple-element.45), channel_id=1, source_target_pairs={{0,4},{4,8},{8,12},{12,0},{1,5},{5,9},{9,13},{13,1},{2,6},{6,10},{... | collective-permute-start | bytes 1228808 | tf_op jit(solution)/shard_map/ppermute | solution.py:259
  37.9 7.5 %collective-permute-start.3 = (bf16[2112,640]{1,0:T(8,128)(2,1)S(1)}, bf16[2112,640]{1,0:T(8,128)(2,1)S(1)}, u32[]{:S(2)}, u32[]{:S(2)}) collective-permute-start(bf16[2112,640]{1,0:T(8,128)(2,1)S(1)} %get-tuple-element.48.own_here.refs_0_), channel_id=1, source_target_pairs={{0,1},{1,0},{2,3},{3,2},{4,5},{5,4},{6,7},{7,6},{8,9},{9,8},{10,11... | collective-permute-start | bytes 8110088 | tf_op jit(solution)/shard_map/ppermute | solution.py:262
  37.9 7.5 %collective-permute-start.5 = (bf16[1024,640]{1,0:T(8,128)(2,1)S(1)}, bf16[1024,640]{1,0:T(8,128)(2,1)S(1)}, u32[]{:S(2)}, u32[]{:S(2)}) collective-permute-start(bf16[1024,640]{1,0:T(8,128)(2,1)S(1)} %collective-permute-done.refs_5_.refs_3_), channel_id=1, source_target_pairs={{0,1},{1,0},{2,3},{3,2},{4,5},{5,4},{6,7},{7,6},{8,9},{9,8},{10,11... | collective-permute-start | bytes 3932168 | tf_op jit(solution)/shard_map/ppermute | solution.py:262
  38.4 7.0 %collective-permute-start.4 = (bf16[320,640]{1,0:T(8,128)(2,1)S(1)}, bf16[320,640]{1,0:T(8,128)(2,1)S(1)}, u32[]{:S(2)}, u32[]{:S(2)}) collective-permute-start(bf16[320,640]{1,0:T(8,128)(2,1)S(1)} %collective-permute-done.1.refs_1_), channel_id=1, source_target_pairs={{0,1},{1,0},{2,3},{3,2},{4,5},{5,4},{6,7},{7,6},{8,9},{9,8},{10,11... | collective-permute-start | bytes 1228808 | tf_op jit(solution)/shard_map/ppermute | solution.py:262
  38.4 13.1 %collective-permute-start.10 = (bf16[320,640]{1,0:T(8,128)(2,1)S(1)}, bf16[320,640]{1,0:T(8,128)(2,1)S(1)}, u32[]{:S(2)}, u32[]{:S(2)}) collective-permute-start(bf16[320,640]{1,0:T(8,128)(2,1)S(1)} %collective-permute-done.2.refs_0_), channel_id=1, source_target_pairs={{0,1},{1,0},{2,3},{3,2},{4,5},{5,4},{6,7},{7,6},{8,9},{9,8},{10,11... | collective-permute-start | bytes 1228808 | tf_op jit(solution)/shard_map/ppermute | solution.py:262
  38.9 25.6 %collective-permute-start.9 = (bf16[320,640]{1,0:T(8,128)(2,1)S(1)}, bf16[320,640]{1,0:T(8,128)(2,1)S(1)}, u32[]{:S(2)}, u32[]{:S(2)}) collective-permute-start(bf16[320,640]{1,0:T(8,128)(2,1)S(1)} %get-tuple-element.57), channel_id=1, source_target_pairs={{0,8},{4,12},{8,0},{12,4},{1,9},{5,13},{9,1},{13,5},{2,10},{6,14},... | collective-permute-start | bytes 1228808 | tf_op jit(solution)/shard_map/ppermute | solution.py:259
  49.7 16.9 %collective-permute-start.6 = (s16[2,640,256]{2,1,0:T(8,128)(2,1)S(1)}, s16[2,640,256]{2,1,0:T(8,128)(2,1)S(1)}, u32[]{:S(2)}, u32[]{:S(2)}) collective-permute-start(s16[2,640,256]{2,1,0:T(8,128)(2,1)S(1)} %get-tuple-element.53), channel_id=1, source_target_pairs={{0,2},{1,3},{2,0},{3,1},{4,6},{5,7},{6,4},{7,5},{8,10},{9,11},{10,... | collective-permute-start | bytes 1966088 | tf_op jit(solution)/shard_map/ppermute | solution.py:265
  54.2 9.5 %collective-permute-start.11 = (s16[320,512]{1,0:T(8,128)(2,1)S(1)}, s16[320,512]{1,0:T(8,128)(2,1)S(1)}, u32[]{:S(2)}, u32[]{:S(2)}) collective-permute-start(s16[320,512]{1,0:T(8,128)(2,1)S(1)} %get-tuple-element.60), channel_id=1, source_target_pairs={{0,16},{16,0},{1,17},{17,1},{2,18},{18,2},{3,19},{19,3},{4,20},{20... | collective-permute-start | bytes 983048 | tf_op jit(solution)/shard_map/ppermute | solution.py:259
  64.5 4.7 %collective-permute-start.12 = (bf16[320,640]{1,0:T(8,128)(2,1)S(1)}, bf16[320,640]{1,0:T(8,128)(2,1)S(1)}, u32[]{:S(2)}, u32[]{:S(2)}) collective-permute-start(bf16[320,640]{1,0:T(8,128)(2,1)S(1)} %collective-permute-done.9.refs_0_), channel_id=1, source_target_pairs={{0,1},{1,0},{2,3},{3,2},{4,5},{5,4},{6,7},{7,6},{8,9},{9,8},{10,11... | collective-permute-start | bytes 1228808 | tf_op jit(solution)/shard_map/ppermute | solution.py:262
  64.6 7.2 %collective-permute-start.16 = (s16[320,256]{1,0:T(8,128)(2,1)S(1)}, s16[320,256]{1,0:T(8,128)(2,1)S(1)}, u32[]{:S(2)}, u32[]{:S(2)}) collective-permute-start(s16[320,256]{1,0:T(8,128)(2,1)S(1)} %get-tuple-element.67), channel_id=1, source_target_pairs={{0,2},{1,3},{2,0},{3,1},{4,6},{5,7},{6,4},{7,5},{8,10},{9,11},{10,... | collective-permute-start | bytes 491528 | tf_op jit(solution)/shard_map/ppermute | solution.py:265
  67.5 19.6 %collective-permute-start.7 = (s16[640,256]{1,0:T(8,128)(2,1)S(1)}, s16[640,256]{1,0:T(8,128)(2,1)S(1)}, u32[]{:S(2)}, u32[]{:S(2)}) collective-permute-start(s16[640,256]{1,0:T(8,128)(2,1)S(1)} %get-tuple-element.55), channel_id=1, source_target_pairs={{0,16},{16,0},{1,17},{17,1},{2,18},{18,2},{3,19},{19,3},{4,20},{20... | collective-permute-start | bytes 983048 | tf_op jit(solution)/shard_map/ppermute | solution.py:259
  72.4 7.1 %collective-permute-start.17 = (bf16[320,256]{1,0:T(8,128)(2,1)S(1)}, bf16[320,256]{1,0:T(8,128)(2,1)S(1)}, u32[]{:S(2)}, u32[]{:S(2)}) collective-permute-start(bf16[320,256]{1,0:T(8,128)(2,1)S(1)} %round_pairs.4.refs_0_), channel_id=1, source_target_pairs={{0,12},{4,0},{8,4},{12,8},{1,13},{5,1},{9,5},{13,9},{2,14},{6,2},{... | collective-permute-start | bytes 491528 | tf_op jit(solution)/shard_map/ppermute | solution.py:259
  76.1 7.9 %collective-permute-start.13 = (s16[320,256]{1,0:T(8,128)(2,1)S(1)}, s16[320,256]{1,0:T(8,128)(2,1)S(1)}, u32[]{:S(2)}, u32[]{:S(2)}) collective-permute-start(s16[320,256]{1,0:T(8,128)(2,1)S(1)} %get-tuple-element.64), channel_id=1, source_target_pairs={{0,2},{1,3},{2,0},{3,1},{4,6},{5,7},{6,4},{7,5},{8,10},{9,11},{10,... | collective-permute-start | bytes 491528 | tf_op jit(solution)/shard_map/ppermute | solution.py:265
  77.6 7.2 %collective-permute-start.14 = (s16[320,256]{1,0:T(8,128)(2,1)S(1)}, s16[320,256]{1,0:T(8,128)(2,1)S(1)}, u32[]{:S(2)}, u32[]{:S(2)}) collective-permute-start(s16[320,256]{1,0:T(8,128)(2,1)S(1)} %get-tuple-element.65), channel_id=1, source_target_pairs={{0,18},{1,19},{2,16},{3,17},{16,2},{17,3},{18,0},{19,1},{4,22},{5,... | collective-permute-start | bytes 491528 | tf_op jit(solution)/shard_map/ppermute | solution.py:269
  78.4 7.3 %collective-permute-start.15 = (s16[320,256]{1,0:T(8,128)(2,1)S(1)}, s16[320,256]{1,0:T(8,128)(2,1)S(1)}, u32[]{:S(2)}, u32[]{:S(2)}) collective-permute-start(s16[320,256]{1,0:T(8,128)(2,1)S(1)} %get-tuple-element.66), channel_id=1, source_target_pairs={{0,16},{16,0},{1,17},{17,1},{2,18},{18,2},{3,19},{19,3},{4,20},{20... | collective-permute-start | bytes 491528 | tf_op jit(solution)/shard_map/ppermute | solution.py:259
  86.4 11.7 %collective-permute-start.18 = (bf16[320,256]{1,0:T(8,128)(2,1)S(1)}, bf16[320,256]{1,0:T(8,128)(2,1)S(1)}, u32[]{:S(2)}, u32[]{:S(2)}) collective-permute-start(bf16[320,256]{1,0:T(8,128)(2,1)S(1)} %round_pairs.5.refs_2_), channel_id=1, source_target_pairs={{0,8},{4,12},{8,0},{12,4},{1,9},{5,13},{9,1},{13,5},{2,10},{6,14},... | collective-permute-start | bytes 491528 | tf_op jit(solution)/shard_map/ppermute | solution.py:259
  87.7 10.4 %collective-permute-start.8 = (bf16[320,256]{1,0:T(8,128)(2,1)S(1)}, bf16[320,256]{1,0:T(8,128)(2,1)S(1)}, u32[]{:S(2)}, u32[]{:S(2)}) collective-permute-start(bf16[320,256]{1,0:T(8,128)(2,1)S(1)} %get-tuple-element.56.refs_4_), channel_id=1, source_target_pairs={{0,4},{4,8},{8,12},{12,0},{1,5},{5,9},{9,13},{13,1},{2,6},{6,10},{... | collective-permute-start | bytes 491528 | tf_op jit(solution)/shard_map/ppermute | solution.py:259

commit v9 on v8

--- a/solution.py
+++ b/solution.py
@@ -374,19 +374,21 @@
         return mine
 
     y_group, x_group, last = (0, *near[:1]), tuple(near[1:]), (far,)
-    sum_pairs(x_group, "x")
+    sums = sum_pairs(x_group, "x")
+    kept[0] = after(kept[0], sums)
     sums = sum_pairs(y_group, "y")
     early = add_pairs(x_group, "x")
     away[far] = after(away[far], early, sums)
     away_there[far] = other_core(away[far])
     sums = sum_pairs(last, "direct")
     round_pairs(x_group, after(added[x_group], sums))
-    early = add_pairs(y_group, "y")
-    round_pairs(last, after(crossed[last], early, [rounded[r, False] for r in x_group]))
+    early = round_pairs(last, after(crossed[last], [rounded[r, False] for r in x_group]))
+    crossed[y_group] = after(crossed[y_group], early)
+    add_pairs(y_group, "y")
     round_pairs(y_group, added[y_group])
 
     done = None
-    ends = [(r, False) for r in near[:1] + [far]]
+    ends = [(r, False) for r in near[:1]]
     for items in ([item for item in rounded if item not in ends], ends):
         sources = [rounded[item] for item in items]
         tile = (TILE, tall), lambda g, s: (g, 0)

time: 101 us -> 107 us (1.059)
  waiting for transfers between devices: 34.4 us -> 42.9 us
  starting transfers between devices: 25.6 us -> 23.3 us
    ppermute x3, waiting for transfers between devices: 5.99 us -> 14.2 us  [other_y(): return lax.ppermute(array, 'depth', [(i, i ^ 2) for i in range(depth_n)])]
    ppermute x10, starting transfers between devices: 19.9 us -> 17.1 us  [shift(): lax.ppermute(array, axis, [(i, (i + by) % count) for i in range(count)])]
  transfers between devices with their start and end apart: 19 -> 19, of which waited for: 10 -> 13; matrix products, arithmetic and copies ran while one was open for 0% -> 0% of each run, Pallas kernels for 32% -> 29%
where the time goes in v9:
time: 107 us
  waiting for transfers between devices  42.9 us (40%)
  Pallas kernels  37.6 us (35%)
  starting transfers between devices  23.3 us (22%)
  local copies, waits for them, and re-layouts  3.14 us (3%)
    pallas_call x13, Pallas kernels, call(): pl.pallas_call(body, name=name, out_shape=shapes, compiler_params=pltpu.C...  37.6 us
    ppermute x10, waiting for transfers between devices, shift(): lax.ppermute(array, axis, [(i, (i + by) % count) for i in range(count)])  24.1 us
    ppermute x10, starting transfers between devices, shift(): lax.ppermute(array, axis, [(i, (i + by) % count) for i in range(count)])  17.1 us
    ppermute x3, waiting for transfers between devices, other_y(): return lax.ppermute(array, 'depth', [(i, i ^ 2) for i in range(depth_n)])  14.2 us
    ppermute x3, starting transfers between devices, other_y(): return lax.ppermute(array, 'depth', [(i, i ^ 2) for i in range(depth_n)])  4.68 us
    ppermute x5, waiting for transfers between devices, other_core(): return lax.ppermute(array, 'depth', [(i, i ^ 1) for i in range(depth_n)])  3.8 us
    unnamed x12, local copies, waits for them, and re-layouts  3.14 us
  transfers between devices with their start and end apart: 19, of which 13 were waited for; matrix products, arithmetic and copies ran while one was open for 0% of the time, Pallas kernels for 29%

profile of v9, /device:TPU:0, one launch (start us, length us, event | category | flops | bytes accessed | tf_op | source)
XLA Modules:
  0.0 107.2 jit_solution(9812152536858901503)
XLA Ops:
  0.0 0.1 pad_add_fusion.s_ref
  0.1 1.7 %copy-done = bf16[1024,1280]{1,0:T(8,128)(2,1)S(1)} copy-done((bf16[1024,1280]{1,0:T(8,128)(2,1)S(1)}, bf16[1024,1280]{1,0:T(8,128)(2,1)}, u32[]{:S(2)}) %copy-start) | copy-done | bytes 2621464
  1.8 0.7 copy-done.3
  2.5 0.7 copy-done.5
  3.2 2.9 %mask_integrals.1 = bf16[1024,640]{1,0:T(8,128)(2,1)S(1)} custom-call(s32[4]{0:T(128)S(1)} %pad_add_fusion.s_ref, s32[8,128]{1,0:T(8,128)S(1)} %bitcast.9, s32[10,128]{1,0:T(8,128)S(1)} %bitcast.7, bf16[1024,1280]{1,0:T(8,128)(2,1)S(1)} %copy-done), custom_call_target="tpu_custom_call" | custom-call | flops 1 | bytes 1 | tf_op jit(solution)/shard_map/mask_integrals/pallas_call | solution.py:86
  6.1 0.0 copy-start.1
  6.1 0.0 copy-start.4
  6.1 3.0 %collective-permute-start = (bf16[1024,640]{1,0:T(8,128)(2,1)S(1)}, bf16[1024,640]{1,0:T(8,128)(2,1)S(1)}, u32[]{:S(2)}, u32[]{:S(2)}) collective-permute-start(bf16[1024,640]{1,0:T(8,128)(2,1)S(1)} %mask_integrals.1), channel_id=1, source_target_pairs={{0,16},{16,0},{1,17},{17,1},{2,18},{18,2},{3,19},{19,3},{4,20},{20... | collective-permute-start | bytes 3932168 | tf_op jit(solution)/shard_map/ppermute | solution.py:259
  9.1 5.1 %send_columns.1 = (bf16[640,2560]{1,0:T(8,128)(2,1)S(1)}, bf16[320,640]{1,0:T(8,128)(2,1)S(1)}, bf16[320,640]{1,0:T(8,128)(2,1)S(1)}, bf16[320,640]{1,0:T(8,128)(2,1)S(1)}) custom-call(s32[4]{0:T(128)S(1)} %pad_add_fusion.s_ref, bf16[320,2,2500]{2,1,0:T(2,128)(2,1)S(1)} %copy-done.2), custom_call_target="tpu_custom_call" | custom-call | flops 1 | bytes 1 | tf_op jit(solution)/shard_map/send_columns/pallas_call | solution.py:86
  14.3 3.7 %collective-permute-start.1 = (bf16[320,640]{1,0:T(8,128)(2,1)S(1)}, bf16[320,640]{1,0:T(8,128)(2,1)S(1)}, u32[]{:S(2)}, u32[]{:S(2)}) collective-permute-start(bf16[320,640]{1,0:T(8,128)(2,1)S(1)} %get-tuple-element.47), channel_id=1, source_target_pairs={{0,12},{4,0},{8,4},{12,8},{1,13},{5,1},{9,5},{13,9},{2,14},{6,2},{... | collective-permute-start | bytes 1228808 | tf_op jit(solution)/shard_map/ppermute | solution.py:259
  17.9 0.0 collective-permute-start.2
  17.9 9.6 %keep_columns.1 = (bf16[2112,640]{1,0:T(8,128)(2,1)S(1)}, bf16[512,640]{1,0:T(8,128)(2,1)S(1)}) custom-call(s32[4]{0:T(128)S(1)} %pad_add_fusion.s_ref, bf16[640,2560]{1,0:T(8,128)(2,1)S(1)} %get-tuple-element.44.flat_ref, s32[8,128]{1,0:T(8,128)S(1)} %bitcast.10, s32[10,128]{1,0:T(8,128)S(1)} %bitcast.8, bf16[1024,1280]{1,0:T(8,128)(2,1)S(1)} %copy-done.1), custom_call_target="tpu_custom_call" | custom-call | flops 1 | bytes 1 | tf_op jit(solution)/shard_map/keep_columns/pallas_call | solution.py:86
  27.5 0.3 collective-permute-done.1.refs_1_
  27.8 8.2 %collective-permute-done.2.refs_0_ = bf16[320,640]{1,0:T(8,128)(2,1)S(1)} collective-permute-done((bf16[320,640]{1,0:T(8,128)(2,1)S(1)}, bf16[320,640]{1,0:T(8,128)(2,1)S(1)}, u32[]{:S(2)}, u32[]{:S(2)}) %collective-permute-start.2) | collective-permute-done | bytes 409632 | tf_op jit(solution)/shard_map/ppermute | solution.py:259
  36.0 1.8 %collective-permute-done.refs_3_.refs_5_ = bf16[1024,640]{1,0:T(8,128)(2,1)S(1)} collective-permute-done((bf16[1024,640]{1,0:T(8,128)(2,1)S(1)}, bf16[1024,640]{1,0:T(8,128)(2,1)S(1)}, u32[]{:S(2)}, u32[]{:S(2)}) %collective-permute-start) | collective-permute-done | bytes 1310752 | tf_op jit(solution)/shard_map/ppermute | solution.py:259
  37.9 0.5 collective-permute-start.6
  38.4 0.0 collective-permute-start.5
  38.4 0.5 collective-permute-start.4
  38.9 2.8 %collective-permute-start.8 = (bf16[320,640]{1,0:T(8,128)(2,1)S(1)}, bf16[320,640]{1,0:T(8,128)(2,1)S(1)}, u32[]{:S(2)}, u32[]{:S(2)}) collective-permute-start(bf16[320,640]{1,0:T(8,128)(2,1)S(1)} %get-tuple-element.61), channel_id=1, source_target_pairs={{0,8},{4,12},{8,0},{12,4},{1,9},{5,13},{9,1},{13,5},{2,10},{6,14},... | collective-permute-start | bytes 1228808 | tf_op jit(solution)/shard_map/ppermute | solution.py:259
  41.7 3.6 %collective-permute-done.5.refs_1_ = bf16[320,640]{1,0:T(8,128)(2,1)S(1)} collective-permute-done((bf16[320,640]{1,0:T(8,128)(2,1)S(1)}, bf16[320,640]{1,0:T(8,128)(2,1)S(1)}, u32[]{:S(2)}, u32[]{:S(2)}) %collective-permute-start.5) | collective-permute-done | bytes 409632 | tf_op jit(solution)/shard_map/ppermute | solution.py:262
  45.4 2.5 %sum_pairs.3 = (s16[320,512]{1,0:T(8,128)(2,1)S(1)}, f32[320,512]{1,0:T(8,128)S(1)}) custom-call(s32[4]{0:T(128)S(1)} %pad_add_fusion.s_ref, bf16[2112,640]{1,0:T(8,128)(2,1)S(1)} %get-tuple-element.51.own_here.refs_0_, bf16[2112,640]{1,0:T(8,128)(2,1)S(1)} %collective-permute-done.3.own_there.refs_2_, bf16[320,640]{1,0:T(8,128)(2,1)S(1)} %collective-permute-done.2.refs_0_, ...), custom_call_target="tpu_custom_call" | custom-call | flops 1 | bytes 1 | tf_op jit(solution)/shard_map/sum_pairs/pallas_call | solution.py:86
  47.9 1.8 %collective-permute-start.9 = (s16[320,512]{1,0:T(8,128)(2,1)S(1)}, s16[320,512]{1,0:T(8,128)(2,1)S(1)}, u32[]{:S(2)}, u32[]{:S(2)}) collective-permute-start(s16[320,512]{1,0:T(8,128)(2,1)S(1)} %get-tuple-element.56), channel_id=1, source_target_pairs={{0,16},{16,0},{1,17},{17,1},{2,18},{18,2},{3,19},{19,3},{4,20},{20... | collective-permute-start | bytes 983048 | tf_op jit(solution)/shard_map/ppermute | solution.py:259
  49.7 4.5 %sum_pairs.4 = (s16[2,640,256]{2,1,0:T(8,128)(2,1)S(1)}, f32[2,640,256]{2,1,0:T(8,128)S(1)}) custom-call(s32[4]{0:T(128)S(1)} %pad_add_fusion.s_ref, bf16[2112,640]{1,0:T(8,128)(2,1)S(1)} %get-tuple-element.51.own_here.refs_0_, bf16[2112,640]{1,0:T(8,128)(2,1)S(1)} %collective-permute-done.3.own_there.refs_2_, ...), custom_call_target="tpu_custom_call" | custom-call | flops 1 | bytes 1 | tf_op jit(solution)/shard_map/sum_pairs/pallas_call | solution.py:86
  54.2 1.6 %collective-permute-start.7 = (s16[2,640,256]{2,1,0:T(8,128)(2,1)S(1)}, s16[2,640,256]{2,1,0:T(8,128)(2,1)S(1)}, u32[]{:S(2)}, u32[]{:S(2)}) collective-permute-start(s16[2,640,256]{2,1,0:T(8,128)(2,1)S(1)} %get-tuple-element.60), channel_id=1, source_target_pairs={{0,2},{1,3},{2,0},{3,1},{4,6},{5,7},{6,4},{7,5},{8,10},{9,11},{10,... | collective-permute-start | bytes 1966088 | tf_op jit(solution)/shard_map/ppermute | solution.py:265
  55.8 1.9 %collective-permute-done.9.refs_0_ = s16[320,512]{1,0:T(8,128)(2,1)S(1)} collective-permute-done((s16[320,512]{1,0:T(8,128)(2,1)S(1)}, s16[320,512]{1,0:T(8,128)(2,1)S(1)}, u32[]{:S(2)}, u32[]{:S(2)}) %collective-permute-start.9) | collective-permute-done | bytes 327712 | tf_op jit(solution)/shard_map/ppermute | solution.py:259
  57.7 0.7 add_other_x.1
  58.4 1.7 %collective-permute-done.8.refs_0_ = bf16[320,640]{1,0:T(8,128)(2,1)S(1)} collective-permute-done((bf16[320,640]{1,0:T(8,128)(2,1)S(1)}, bf16[320,640]{1,0:T(8,128)(2,1)S(1)}, u32[]{:S(2)}, u32[]{:S(2)}) %collective-permute-start.8) | collective-permute-done | bytes 409632 | tf_op jit(solution)/shard_map/ppermute | solution.py:259
  60.2 1.6 %collective-permute-start.14 = (s16[320,256]{1,0:T(8,128)(2,1)S(1)}, s16[320,256]{1,0:T(8,128)(2,1)S(1)}, u32[]{:S(2)}, u32[]{:S(2)}) collective-permute-start(s16[320,256]{1,0:T(8,128)(2,1)S(1)} %get-tuple-element.68), channel_id=1, source_target_pairs={{0,2},{1,3},{2,0},{3,1},{4,6},{5,7},{6,4},{7,5},{8,10},{9,11},{10,... | collective-permute-start | bytes 491528 | tf_op jit(solution)/shard_map/ppermute | solution.py:265
  61.7 0.2 collective-permute-done.10.refs_1_
  61.9 2.5 %sum_pairs.5 = (s16[320,256]{1,0:T(8,128)(2,1)S(1)}, f32[320,256]{1,0:T(8,128)S(1)}, s16[320,256]{1,0:T(8,128)(2,1)S(1)}, s16[320,256]{1,0:T(8,128)(2,1)S(1)}) custom-call(s32[4]{0:T(128)S(1)} %pad_add_fusion.s_ref, bf16[2112,640]{1,0:T(8,128)(2,1)S(1)} %get-tuple-element.51.own_here.refs_0_, bf16[2112,640]{1,0:T(8,128)(2,1)S(1)} %collective-permute-done.3.own_there.refs_2_, ...), custom_call_target="tpu_custom_call" | custom-call | flops 1 | bytes 1 | tf_op jit(solution)/shard_map/sum_pairs/pallas_call | solution.py:86
  64.4 9.8 %collective-permute-done.14.refs_0_ = s16[320,256]{1,0:T(8,128)(2,1)S(1)} collective-permute-done((s16[320,256]{1,0:T(8,128)(2,1)S(1)}, s16[320,256]{1,0:T(8,128)(2,1)S(1)}, u32[]{:S(2)}, u32[]{:S(2)}) %collective-permute-start.14) | collective-permute-done | bytes 163872 | tf_op jit(solution)/shard_map/ppermute | solution.py:265
  74.2 0.6 round_pairs.3.refs_0_
  74.9 3.7 %collective-permute-start.15 = (bf16[320,256]{1,0:T(8,128)(2,1)S(1)}, bf16[320,256]{1,0:T(8,128)(2,1)S(1)}, u32[]{:S(2)}, u32[]{:S(2)}) collective-permute-start(bf16[320,256]{1,0:T(8,128)(2,1)S(1)} %round_pairs.3.refs_0_), channel_id=1, source_target_pairs={{0,12},{4,0},{8,4},{12,8},{1,13},{5,1},{9,5},{13,9},{2,14},{6,2},{... | collective-permute-start | bytes 491528 | tf_op jit(solution)/shard_map/ppermute | solution.py:259
  78.5 1.5 %collective-permute-start.11 = (s16[320,256]{1,0:T(8,128)(2,1)S(1)}, s16[320,256]{1,0:T(8,128)(2,1)S(1)}, u32[]{:S(2)}, u32[]{:S(2)}) collective-permute-start(s16[320,256]{1,0:T(8,128)(2,1)S(1)} %get-tuple-element.65), channel_id=1, source_target_pairs={{0,2},{1,3},{2,0},{3,1},{4,6},{5,7},{6,4},{7,5},{8,10},{9,11},{10,... | collective-permute-start | bytes 491528 | tf_op jit(solution)/shard_map/ppermute | solution.py:265
  80.0 0.5 collective-permute-start.12
  80.5 1.5 %collective-permute-start.13 = (s16[320,256]{1,0:T(8,128)(2,1)S(1)}, s16[320,256]{1,0:T(8,128)(2,1)S(1)}, u32[]{:S(2)}, u32[]{:S(2)}) collective-permute-start(s16[320,256]{1,0:T(8,128)(2,1)S(1)} %get-tuple-element.67), channel_id=1, source_target_pairs={{0,16},{16,0},{1,17},{17,1},{2,18},{18,2},{3,19},{19,3},{4,20},{20... | collective-permute-start | bytes 491528 | tf_op jit(solution)/shard_map/ppermute | solution.py:259
  82.0 4.4 %collective-permute-done.11.refs_0_ = s16[320,256]{1,0:T(8,128)(2,1)S(1)} collective-permute-done((s16[320,256]{1,0:T(8,128)(2,1)S(1)}, s16[320,256]{1,0:T(8,128)(2,1)S(1)}, u32[]{:S(2)}, u32[]{:S(2)}) %collective-permute-start.11) | collective-permute-done | bytes 163872 | tf_op jit(solution)/shard_map/ppermute | solution.py:265
  86.4 0.9 collective-permute-done.12.refs_1_
  87.2 0.8 collective-permute-done.13.refs_2_
  88.1 0.7 round_pairs.4.refs_2_
  88.8 0.9 add_other_y.1
  89.7 0.6 collective-permute-start.16
  90.3 6.6 %collective-permute-done.16.refs_0_ = s16[640,256]{1,0:T(8,128)(2,1)S(1)} collective-permute-done((s16[640,256]{1,0:T(8,128)(2,1)S(1)}, s16[640,256]{1,0:T(8,128)(2,1)S(1)}, u32[]{:S(2)}, u32[]{:S(2)}) %collective-permute-start.16) | collective-permute-done | bytes 327712 | tf_op jit(solution)/shard_map/ppermute | solution.py:259
  96.9 0.6 round_pairs.5
  97.6 0.1 collective-permute-start.17
  97.7 4.4 %place_pairs.2.refs_1_ = bf16[2500,256]{1,0:T(8,128)(2,1)S(1)} custom-call(s32[4]{0:T(128)S(1)} %pad_add_fusion.s_ref, bf16[320,256]{1,0:T(8,128)(2,1)S(1)} %round_pairs.3.refs_0_, bf16[320,256]{1,0:T(8,128)(2,1)S(1)} %collective-permute-done.15.refs_1_, bf16[320,256]{1,0:T(8,128)(2,1)S(1)} %round_pairs.4.refs_2_, ...), custom_call_target="tpu_custom_call" | custom-call | flops 1 | bytes 1 | tf_op jit(solution)/shard_map/place_pairs/pallas_call | solution.py:86
  102.1 2.6 %collective-permute-done.17.refs_0_ = bf16[320,256]{1,0:T(8,128)(2,1)S(1)} collective-permute-done((bf16[320,256]{1,0:T(8,128)(2,1)S(1)}, bf16[320,256]{1,0:T(8,128)(2,1)S(1)}, u32[]{:S(2)}, u32[]{:S(2)}) %collective-permute-start.17) | collective-permute-done | bytes 163872 | tf_op jit(solution)/shard_map/ppermute | solution.py:259
  104.8 2.4 %place_pairs.3 = bf16[2500,256]{1,0:T(8,128)(2,1)} custom-call(s32[4]{0:T(128)S(1)} %pad_add_fusion.s_ref, bf16[320,256]{1,0:T(8,128)(2,1)S(1)} %collective-permute-done.17.refs_0_, bf16[2500,256]{1,0:T(8,128)(2,1)S(1)} %place_pairs.2.refs_1_), custom_call_target="tpu_custom_call" | custom-call | flops 1 | bytes 1 | tf_op jit(solution)/shard_map/place_pairs/pallas_call | solution.py:86
  (16 shorter events, 0.0 us)
Async XLA Ops:
  0.1 1.7 %copy-start = (bf16[1024,1280]{1,0:T(8,128)(2,1)S(1)}, bf16[1024,1280]{1,0:T(8,128)(2,1)}, u32[]{:S(2)}) copy-start(bf16[1024,1280]{1,0:T(8,128)(2,1)} %v_ref.3) | copy-start | bytes 7864324
  1.8 0.7 copy-start.3
  2.5 0.7 copy-start.5
  3.2 5.9 %copy-start.2 = (bf16[320,2,2500]{2,1,0:T(2,128)(2,1)S(1)}, bf16[320,2,2500]{2,1,0:T(2,128)(2,1)}, u32[]{:S(2)}) copy-start(bf16[320,2,2500]{2,1,0:T(2,128)(2,1)} %t_ref) | copy-start | bytes 9600004
  6.1 11.8 %copy-start.1 = (bf16[1024,1280]{1,0:T(8,128)(2,1)S(1)}, bf16[1024,1280]{1,0:T(8,128)(2,1)}, u32[]{:S(2)}) copy-start(bf16[1024,1280]{1,0:T(8,128)(2,1)} %v_ref.3) | copy-start | bytes 7864324
  6.1 11.8 %copy-start.4 = (s32[1280]{0:T(1024)S(1)}, s32[1280]{0:T(1024)}, u32[]{:S(2)}) copy-start(s32[1280]{0:T(1024)} %param.7) | copy-start | bytes 15364
  6.1 31.8 %collective-permute-start = (bf16[1024,640]{1,0:T(8,128)(2,1)S(1)}, bf16[1024,640]{1,0:T(8,128)(2,1)S(1)}, u32[]{:S(2)}, u32[]{:S(2)}) collective-permute-start(bf16[1024,640]{1,0:T(8,128)(2,1)S(1)} %mask_integrals.1), channel_id=1, source_target_pairs={{0,16},{16,0},{1,17},{17,1},{2,18},{18,2},{3,19},{19,3},{4,20},{20... | collective-permute-start | bytes 3932168 | tf_op jit(solution)/shard_map/ppermute | solution.py:259
  14.3 13.6 %collective-permute-start.1 = (bf16[320,640]{1,0:T(8,128)(2,1)S(1)}, bf16[320,640]{1,0:T(8,128)(2,1)S(1)}, u32[]{:S(2)}, u32[]{:S(2)}) collective-permute-start(bf16[320,640]{1,0:T(8,128)(2,1)S(1)} %get-tuple-element.47), channel_id=1, source_target_pairs={{0,12},{4,0},{8,4},{12,8},{1,13},{5,1},{9,5},{13,9},{2,14},{6,2},{... | collective-permute-start | bytes 1228808 | tf_op jit(solution)/shard_map/ppermute | solution.py:259
  17.9 18.1 %collective-permute-start.2 = (bf16[320,640]{1,0:T(8,128)(2,1)S(1)}, bf16[320,640]{1,0:T(8,128)(2,1)S(1)}, u32[]{:S(2)}, u32[]{:S(2)}) collective-permute-start(bf16[320,640]{1,0:T(8,128)(2,1)S(1)} %get-tuple-element.48), channel_id=1, source_target_pairs={{0,4},{4,8},{8,12},{12,0},{1,5},{5,9},{9,13},{13,1},{2,6},{6,10},{... | collective-permute-start | bytes 1228808 | tf_op jit(solution)/shard_map/ppermute | solution.py:259
  37.9 7.5 %collective-permute-start.3 = (bf16[2112,640]{1,0:T(8,128)(2,1)S(1)}, bf16[2112,640]{1,0:T(8,128)(2,1)S(1)}, u32[]{:S(2)}, u32[]{:S(2)}) collective-permute-start(bf16[2112,640]{1,0:T(8,128)(2,1)S(1)} %get-tuple-element.51.own_here.refs_0_), channel_id=1, source_target_pairs={{0,1},{1,0},{2,3},{3,2},{4,5},{5,4},{6,7},{7,6},{8,9},{9,8},{10,11... | collective-permute-start | bytes 8110088 | tf_op jit(solution)/shard_map/ppermute | solution.py:262
  37.9 7.5 %collective-permute-start.6 = (bf16[1024,640]{1,0:T(8,128)(2,1)S(1)}, bf16[1024,640]{1,0:T(8,128)(2,1)S(1)}, u32[]{:S(2)}, u32[]{:S(2)}) collective-permute-start(bf16[1024,640]{1,0:T(8,128)(2,1)S(1)} %collective-permute-done.refs_3_.refs_5_), channel_id=1, source_target_pairs={{0,1},{1,0},{2,3},{3,2},{4,5},{5,4},{6,7},{7,6},{8,9},{9,8},{10,11... | collective-permute-start | bytes 3932168 | tf_op jit(solution)/shard_map/ppermute | solution.py:262
  38.4 7.0 %collective-permute-start.5 = (bf16[320,640]{1,0:T(8,128)(2,1)S(1)}, bf16[320,640]{1,0:T(8,128)(2,1)S(1)}, u32[]{:S(2)}, u32[]{:S(2)}) collective-permute-start(bf16[320,640]{1,0:T(8,128)(2,1)S(1)} %collective-permute-done.2.refs_0_), channel_id=1, source_target_pairs={{0,1},{1,0},{2,3},{3,2},{4,5},{5,4},{6,7},{7,6},{8,9},{9,8},{10,11... | collective-permute-start | bytes 1228808 | tf_op jit(solution)/shard_map/ppermute | solution.py:262
  38.4 11.3 %collective-permute-start.4 = (bf16[320,640]{1,0:T(8,128)(2,1)S(1)}, bf16[320,640]{1,0:T(8,128)(2,1)S(1)}, u32[]{:S(2)}, u32[]{:S(2)}) collective-permute-start(bf16[320,640]{1,0:T(8,128)(2,1)S(1)} %collective-permute-done.1.refs_1_), channel_id=1, source_target_pairs={{0,1},{1,0},{2,3},{3,2},{4,5},{5,4},{6,7},{7,6},{8,9},{9,8},{10,11... | collective-permute-start | bytes 1228808 | tf_op jit(solution)/shard_map/ppermute | solution.py:262
  38.9 21.2 %collective-permute-start.8 = (bf16[320,640]{1,0:T(8,128)(2,1)S(1)}, bf16[320,640]{1,0:T(8,128)(2,1)S(1)}, u32[]{:S(2)}, u32[]{:S(2)}) collective-permute-start(bf16[320,640]{1,0:T(8,128)(2,1)S(1)} %get-tuple-element.61), channel_id=1, source_target_pairs={{0,8},{4,12},{8,0},{12,4},{1,9},{5,13},{9,1},{13,5},{2,10},{6,14},... | collective-permute-start | bytes 1228808 | tf_op jit(solution)/shard_map/ppermute | solution.py:259
  47.9 9.8 %collective-permute-start.9 = (s16[320,512]{1,0:T(8,128)(2,1)S(1)}, s16[320,512]{1,0:T(8,128)(2,1)S(1)}, u32[]{:S(2)}, u32[]{:S(2)}) collective-permute-start(s16[320,512]{1,0:T(8,128)(2,1)S(1)} %get-tuple-element.56), channel_id=1, source_target_pairs={{0,16},{16,0},{1,17},{17,1},{2,18},{18,2},{3,19},{19,3},{4,20},{20... | collective-permute-start | bytes 983048 | tf_op jit(solution)/shard_map/ppermute | solution.py:259
  54.2 34.6 %collective-permute-start.7 = (s16[2,640,256]{2,1,0:T(8,128)(2,1)S(1)}, s16[2,640,256]{2,1,0:T(8,128)(2,1)S(1)}, u32[]{:S(2)}, u32[]{:S(2)}) collective-permute-start(s16[2,640,256]{2,1,0:T(8,128)(2,1)S(1)} %get-tuple-element.60), channel_id=1, source_target_pairs={{0,2},{1,3},{2,0},{3,1},{4,6},{5,7},{6,4},{7,5},{8,10},{9,11},{10,... | collective-permute-start | bytes 1966088 | tf_op jit(solution)/shard_map/ppermute | solution.py:265
  60.2 1.7 %collective-permute-start.10 = (bf16[320,640]{1,0:T(8,128)(2,1)S(1)}, bf16[320,640]{1,0:T(8,128)(2,1)S(1)}, u32[]{:S(2)}, u32[]{:S(2)}) collective-permute-start(bf16[320,640]{1,0:T(8,128)(2,1)S(1)} %collective-permute-done.8.refs_0_), channel_id=1, source_target_pairs={{0,1},{1,0},{2,3},{3,2},{4,5},{5,4},{6,7},{7,6},{8,9},{9,8},{10,11... | collective-permute-start | bytes 1228808 | tf_op jit(solution)/shard_map/ppermute | solution.py:262
  60.2 14.1 %collective-permute-start.14 = (s16[320,256]{1,0:T(8,128)(2,1)S(1)}, s16[320,256]{1,0:T(8,128)(2,1)S(1)}, u32[]{:S(2)}, u32[]{:S(2)}) collective-permute-start(s16[320,256]{1,0:T(8,128)(2,1)S(1)} %get-tuple-element.68), channel_id=1, source_target_pairs={{0,2},{1,3},{2,0},{3,1},{4,6},{5,7},{6,4},{7,5},{8,10},{9,11},{10,... | collective-permute-start | bytes 491528 | tf_op jit(solution)/shard_map/ppermute | solution.py:265
  74.9 7.2 %collective-permute-start.15 = (bf16[320,256]{1,0:T(8,128)(2,1)S(1)}, bf16[320,256]{1,0:T(8,128)(2,1)S(1)}, u32[]{:S(2)}, u32[]{:S(2)}) collective-permute-start(bf16[320,256]{1,0:T(8,128)(2,1)S(1)} %round_pairs.3.refs_0_), channel_id=1, source_target_pairs={{0,12},{4,0},{8,4},{12,8},{1,13},{5,1},{9,5},{13,9},{2,14},{6,2},{... | collective-permute-start | bytes 491528 | tf_op jit(solution)/shard_map/ppermute | solution.py:259
  78.5 7.9 %collective-permute-start.11 = (s16[320,256]{1,0:T(8,128)(2,1)S(1)}, s16[320,256]{1,0:T(8,128)(2,1)S(1)}, u32[]{:S(2)}, u32[]{:S(2)}) collective-permute-start(s16[320,256]{1,0:T(8,128)(2,1)S(1)} %get-tuple-element.65), channel_id=1, source_target_pairs={{0,2},{1,3},{2,0},{3,1},{4,6},{5,7},{6,4},{7,5},{8,10},{9,11},{10,... | collective-permute-start | bytes 491528 | tf_op jit(solution)/shard_map/ppermute | solution.py:265
  80.0 7.2 %collective-permute-start.12 = (s16[320,256]{1,0:T(8,128)(2,1)S(1)}, s16[320,256]{1,0:T(8,128)(2,1)S(1)}, u32[]{:S(2)}, u32[]{:S(2)}) collective-permute-start(s16[320,256]{1,0:T(8,128)(2,1)S(1)} %get-tuple-element.66), channel_id=1, source_target_pairs={{0,18},{1,19},{2,16},{3,17},{16,2},{17,3},{18,0},{19,1},{4,22},{5,... | collective-permute-start | bytes 491528 | tf_op jit(solution)/shard_map/ppermute | solution.py:269
  80.5 7.6 %collective-permute-start.13 = (s16[320,256]{1,0:T(8,128)(2,1)S(1)}, s16[320,256]{1,0:T(8,128)(2,1)S(1)}, u32[]{:S(2)}, u32[]{:S(2)}) collective-permute-start(s16[320,256]{1,0:T(8,128)(2,1)S(1)} %get-tuple-element.67), channel_id=1, source_target_pairs={{0,16},{16,0},{1,17},{17,1},{2,18},{18,2},{3,19},{19,3},{4,20},{20... | collective-permute-start | bytes 491528 | tf_op jit(solution)/shard_map/ppermute | solution.py:259
  89.7 7.2 %collective-permute-start.16 = (s16[640,256]{1,0:T(8,128)(2,1)S(1)}, s16[640,256]{1,0:T(8,128)(2,1)S(1)}, u32[]{:S(2)}, u32[]{:S(2)}) collective-permute-start(s16[640,256]{1,0:T(8,128)(2,1)S(1)} %get-tuple-element.78), channel_id=1, source_target_pairs={{0,16},{16,0},{1,17},{17,1},{2,18},{18,2},{3,19},{19,3},{4,20},{20... | collective-permute-start | bytes 983048 | tf_op jit(solution)/shard_map/ppermute | solution.py:259
  90.3 7.4 %collective-permute-start.18 = (bf16[320,256]{1,0:T(8,128)(2,1)S(1)}, bf16[320,256]{1,0:T(8,128)(2,1)S(1)}, u32[]{:S(2)}, u32[]{:S(2)}) collective-permute-start(bf16[320,256]{1,0:T(8,128)(2,1)S(1)} %round_pairs.4.refs_2_), channel_id=1, source_target_pairs={{0,8},{4,12},{8,0},{12,4},{1,9},{5,13},{9,1},{13,5},{2,10},{6,14},... | collective-permute-start | bytes 491528 | tf_op jit(solution)/shard_map/ppermute | solution.py:259
  97.6 7.2 %collective-permute-start.17 = (bf16[320,256]{1,0:T(8,128)(2,1)S(1)}, bf16[320,256]{1,0:T(8,128)(2,1)S(1)}, u32[]{:S(2)}, u32[]{:S(2)}) collective-permute-start(bf16[320,256]{1,0:T(8,128)(2,1)S(1)} %get-tuple-element.79.refs_5_), channel_id=1, source_target_pairs={{0,4},{4,8},{8,12},{12,0},{1,5},{5,9},{9,13},{13,1},{2,6},{6,10},{... | collective-permute-start | bytes 491528 | tf_op jit(solution)/shard_map/ppermute | solution.py:259

commit v10 on v8

--- a/solution.py
+++ b/solution.py
@@ -381,12 +381,12 @@
     away_there[far] = other_core(away[far])
     sums = sum_pairs(last, "direct")
     round_pairs(x_group, after(added[x_group], sums))
-    early = add_pairs(y_group, "y")
+    add_pairs(y_group, "y")
+    early = round_pairs(y_group, added[y_group])
     round_pairs(last, after(crossed[last], early, [rounded[r, False] for r in x_group]))
-    round_pairs(y_group, added[y_group])
 
     done = None
-    ends = [(r, False) for r in near[:1] + [far]]
+    ends = [(far, False)]
     for items in ([item for item in rounded if item not in ends], ends):
         sources = [rounded[item] for item in items]
         tile = (TILE, tall), lambda g, s: (g, 0)

time: 101 us -> 97.2 us (0.962)
  waiting for transfers between devices: 34.4 us -> 32.3 us
  starting transfers between devices: 25.6 us -> 24 us
    ppermute x10, starting transfers between devices: 19.9 us -> 18.4 us  [shift(): lax.ppermute(array, axis, [(i, (i + by) % count) for i in range(count)])]
    ppermute x10, waiting for transfers between devices: 23.9 us -> 22.6 us  [shift(): lax.ppermute(array, axis, [(i, (i + by) % count) for i in range(count)])]
  transfers between devices with their start and end apart: 19 -> 19, of which waited for: 10 -> 11; matrix products, arithmetic and copies ran while one was open for 0% -> 0% of each run, Pallas kernels for 32% -> 33%
where the time goes in v10:
time: 97.2 us; the launch traced here: 97 us
  Pallas kernels  37.3 us (38%)
  waiting for transfers between devices  32.3 us (33%)
  starting transfers between devices  24 us (25%)
  local copies, waits for them, and re-layouts  3.14 us (3%)
    pallas_call x13, Pallas kernels, call(): pl.pallas_call(body, name=name, out_shape=shapes, compiler_params=pltpu.C...  37.3 us
    ppermute x10, waiting for transfers between devices, shift(): lax.ppermute(array, axis, [(i, (i + by) % count) for i in range(count)])  22.6 us
    ppermute x10, starting transfers between devices, shift(): lax.ppermute(array, axis, [(i, (i + by) % count) for i in range(count)])  18.4 us
    ppermute x3, waiting for transfers between devices, other_y(): return lax.ppermute(array, 'depth', [(i, i ^ 2) for i in range(depth_n)])  5.26 us
    ppermute x3, starting transfers between devices, other_y(): return lax.ppermute(array, 'depth', [(i, i ^ 2) for i in range(depth_n)])  3.72 us
    ppermute x5, waiting for transfers between devices, other_core(): return lax.ppermute(array, 'depth', [(i, i ^ 1) for i in range(depth_n)])  3.64 us
    unnamed x12, local copies, waits for them, and re-layouts  3.14 us
  transfers between devices with their start and end apart: 19, of which 11 were waited for; matrix products, arithmetic and copies ran while one was open for 0% of the time, Pallas kernels for 33%

profile of v10, /device:TPU:0, one launch (start us, length us, event | category | flops | bytes accessed | tf_op | source)
XLA Modules:
  0.0 97.0 jit_solution(7809033119903487711)
XLA Ops:
  0.0 0.1 pad_add_fusion.s_ref
  0.1 1.7 %copy-done = bf16[1024,1280]{1,0:T(8,128)(2,1)S(1)} copy-done((bf16[1024,1280]{1,0:T(8,128)(2,1)S(1)}, bf16[1024,1280]{1,0:T(8,128)(2,1)}, u32[]{:S(2)}) %copy-start) | copy-done | bytes 2621464
  1.8 0.7 copy-done.3
  2.5 0.7 copy-done.5
  3.2 2.9 %mask_integrals.1 = bf16[1024,640]{1,0:T(8,128)(2,1)S(1)} custom-call(s32[4]{0:T(128)S(1)} %pad_add_fusion.s_ref, s32[8,128]{1,0:T(8,128)S(1)} %bitcast.9, s32[10,128]{1,0:T(8,128)S(1)} %bitcast.7, bf16[1024,1280]{1,0:T(8,128)(2,1)S(1)} %copy-done), custom_call_target="tpu_custom_call" | custom-call | flops 1 | bytes 1 | tf_op jit(solution)/shard_map/mask_integrals/pallas_call | solution.py:86
  6.1 0.0 copy-start.1
  6.1 0.0 copy-start.4
  6.1 3.0 %collective-permute-start = (bf16[1024,640]{1,0:T(8,128)(2,1)S(1)}, bf16[1024,640]{1,0:T(8,128)(2,1)S(1)}, u32[]{:S(2)}, u32[]{:S(2)}) collective-permute-start(bf16[1024,640]{1,0:T(8,128)(2,1)S(1)} %mask_integrals.1), channel_id=1, source_target_pairs={{0,16},{16,0},{1,17},{17,1},{2,18},{18,2},{3,19},{19,3},{4,20},{20... | collective-permute-start | bytes 3932168 | tf_op jit(solution)/shard_map/ppermute | solution.py:259
  9.1 5.1 %send_columns.1 = (bf16[640,2560]{1,0:T(8,128)(2,1)S(1)}, bf16[320,640]{1,0:T(8,128)(2,1)S(1)}, bf16[320,640]{1,0:T(8,128)(2,1)S(1)}, bf16[320,640]{1,0:T(8,128)(2,1)S(1)}) custom-call(s32[4]{0:T(128)S(1)} %pad_add_fusion.s_ref, bf16[320,2,2500]{2,1,0:T(2,128)(2,1)S(1)} %copy-done.2), custom_call_target="tpu_custom_call" | custom-call | flops 1 | bytes 1 | tf_op jit(solution)/shard_map/send_columns/pallas_call | solution.py:86
  14.3 3.7 %collective-permute-start.1 = (bf16[320,640]{1,0:T(8,128)(2,1)S(1)}, bf16[320,640]{1,0:T(8,128)(2,1)S(1)}, u32[]{:S(2)}, u32[]{:S(2)}) collective-permute-start(bf16[320,640]{1,0:T(8,128)(2,1)S(1)} %get-tuple-element.44), channel_id=1, source_target_pairs={{0,12},{4,0},{8,4},{12,8},{1,13},{5,1},{9,5},{13,9},{2,14},{6,2},{... | collective-permute-start | bytes 1228808 | tf_op jit(solution)/shard_map/ppermute | solution.py:259
  17.9 0.0 collective-permute-start.2
  17.9 9.6 %keep_columns.1 = (bf16[2112,640]{1,0:T(8,128)(2,1)S(1)}, bf16[512,640]{1,0:T(8,128)(2,1)S(1)}) custom-call(s32[4]{0:T(128)S(1)} %pad_add_fusion.s_ref, bf16[640,2560]{1,0:T(8,128)(2,1)S(1)} %get-tuple-element.41.flat_ref, s32[8,128]{1,0:T(8,128)S(1)} %bitcast.10, s32[10,128]{1,0:T(8,128)S(1)} %bitcast.8, bf16[1024,1280]{1,0:T(8,128)(2,1)S(1)} %copy-done.1), custom_call_target="tpu_custom_call" | custom-call | flops 1 | bytes 1 | tf_op jit(solution)/shard_map/keep_columns/pallas_call | solution.py:86
  27.5 0.3 collective-permute-done.1.refs_1_
  27.8 8.2 %collective-permute-done.2.refs_0_ = bf16[320,640]{1,0:T(8,128)(2,1)S(1)} collective-permute-done((bf16[320,640]{1,0:T(8,128)(2,1)S(1)}, bf16[320,640]{1,0:T(8,128)(2,1)S(1)}, u32[]{:S(2)}, u32[]{:S(2)}) %collective-permute-start.2) | collective-permute-done | bytes 409632 | tf_op jit(solution)/shard_map/ppermute | solution.py:259
  36.0 1.8 %collective-permute-done.refs_3_.refs_5_ = bf16[1024,640]{1,0:T(8,128)(2,1)S(1)} collective-permute-done((bf16[1024,640]{1,0:T(8,128)(2,1)S(1)}, bf16[1024,640]{1,0:T(8,128)(2,1)S(1)}, u32[]{:S(2)}, u32[]{:S(2)}) %collective-permute-start) | collective-permute-done | bytes 1310752 | tf_op jit(solution)/shard_map/ppermute | solution.py:259
  37.9 0.5 collective-permute-start.6
  38.4 0.0 collective-permute-start.8
  38.4 0.5 collective-permute-start.5
  38.9 2.8 %collective-permute-start.4 = (bf16[320,640]{1,0:T(8,128)(2,1)S(1)}, bf16[320,640]{1,0:T(8,128)(2,1)S(1)}, u32[]{:S(2)}, u32[]{:S(2)}) collective-permute-start(bf16[320,640]{1,0:T(8,128)(2,1)S(1)} %get-tuple-element.49), channel_id=1, source_target_pairs={{0,8},{4,12},{8,0},{12,4},{1,9},{5,13},{9,1},{13,5},{2,10},{6,14},... | collective-permute-start | bytes 1228808 | tf_op jit(solution)/shard_map/ppermute | solution.py:259
  41.7 3.6 %collective-permute-done.8.refs_3_ = bf16[320,640]{1,0:T(8,128)(2,1)S(1)} collective-permute-done((bf16[320,640]{1,0:T(8,128)(2,1)S(1)}, bf16[320,640]{1,0:T(8,128)(2,1)S(1)}, u32[]{:S(2)}, u32[]{:S(2)}) %collective-permute-start.8) | collective-permute-done | bytes 409632 | tf_op jit(solution)/shard_map/ppermute | solution.py:262
  45.4 4.3 %sum_pairs.4 = (s16[2,640,256]{2,1,0:T(8,128)(2,1)S(1)}, f32[2,640,256]{2,1,0:T(8,128)S(1)}) custom-call(s32[4]{0:T(128)S(1)} %pad_add_fusion.s_ref, bf16[2112,640]{1,0:T(8,128)(2,1)S(1)} %get-tuple-element.48.own_here.refs_0_, bf16[2112,640]{1,0:T(8,128)(2,1)S(1)} %collective-permute-done.3.own_there.refs_2_, ...), custom_call_target="tpu_custom_call" | custom-call | flops 1 | bytes 1 | tf_op jit(solution)/shard_map/sum_pairs/pallas_call | solution.py:86
  49.7 1.8 %collective-permute-start.13 = (s16[2,640,256]{2,1,0:T(8,128)(2,1)S(1)}, s16[2,640,256]{2,1,0:T(8,128)(2,1)S(1)}, u32[]{:S(2)}, u32[]{:S(2)}) collective-permute-start(s16[2,640,256]{2,1,0:T(8,128)(2,1)S(1)} %get-tuple-element.57), channel_id=1, source_target_pairs={{0,2},{1,3},{2,0},{3,1},{4,6},{5,7},{6,4},{7,5},{8,10},{9,11},{10,... | collective-permute-start | bytes 1966088 | tf_op jit(solution)/shard_map/ppermute | solution.py:265
  51.5 2.7 %sum_pairs.3 = (s16[320,512]{1,0:T(8,128)(2,1)S(1)}, f32[320,512]{1,0:T(8,128)S(1)}) custom-call(s32[4]{0:T(128)S(1)} %pad_add_fusion.s_ref, bf16[2112,640]{1,0:T(8,128)(2,1)S(1)} %get-tuple-element.48.own_here.refs_0_, bf16[2112,640]{1,0:T(8,128)(2,1)S(1)} %collective-permute-done.3.own_there.refs_2_, bf16[320,640]{1,0:T(8,128)(2,1)S(1)} %collective-permute-done.2.refs_0_, ...), custom_call_target="tpu_custom_call" | custom-call | flops 1 | bytes 1 | tf_op jit(solution)/shard_map/sum_pairs/pallas_call | solution.py:86
  54.2 1.6 %collective-permute-start.7 = (s16[320,512]{1,0:T(8,128)(2,1)S(1)}, s16[320,512]{1,0:T(8,128)(2,1)S(1)}, u32[]{:S(2)}, u32[]{:S(2)}) collective-permute-start(s16[320,512]{1,0:T(8,128)(2,1)S(1)} %get-tuple-element.54), channel_id=1, source_target_pairs={{0,16},{16,0},{1,17},{17,1},{2,18},{18,2},{3,19},{19,3},{4,20},{20... | collective-permute-start | bytes 983048 | tf_op jit(solution)/shard_map/ppermute | solution.py:259
  55.8 8.0 %collective-permute-done.7.refs_0_ = s16[320,512]{1,0:T(8,128)(2,1)S(1)} collective-permute-done((s16[320,512]{1,0:T(8,128)(2,1)S(1)}, s16[320,512]{1,0:T(8,128)(2,1)S(1)}, u32[]{:S(2)}, u32[]{:S(2)}) %collective-permute-start.7) | collective-permute-done | bytes 327712 | tf_op jit(solution)/shard_map/ppermute | solution.py:259
  63.8 0.7 add_other_x.1
  64.5 0.1 collective-permute-start.9
  64.6 0.4 collective-permute-start.15
  65.0 1.6 %collective-permute-done.13.coded_ref = s16[2,640,256]{2,1,0:T(8,128)(2,1)S(1)} collective-permute-done((s16[2,640,256]{2,1,0:T(8,128)(2,1)S(1)}, s16[2,640,256]{2,1,0:T(8,128)(2,1)S(1)}, u32[]{:S(2)}, u32[]{:S(2)}) %collective-permute-start.13) | collective-permute-done | bytes 655392 | tf_op jit(solution)/shard_map/ppermute | solution.py:265
  66.5 0.9 add_other_y.1
  67.5 1.8 %collective-permute-start.14 = (s16[640,256]{1,0:T(8,128)(2,1)S(1)}, s16[640,256]{1,0:T(8,128)(2,1)S(1)}, u32[]{:S(2)}, u32[]{:S(2)}) collective-permute-start(s16[640,256]{1,0:T(8,128)(2,1)S(1)} %get-tuple-element.65), channel_id=1, source_target_pairs={{0,16},{16,0},{1,17},{17,1},{2,18},{18,2},{3,19},{19,3},{4,20},{20... | collective-permute-start | bytes 983048 | tf_op jit(solution)/shard_map/ppermute | solution.py:259
  69.3 2.5 %sum_pairs.5 = (s16[320,256]{1,0:T(8,128)(2,1)S(1)}, f32[320,256]{1,0:T(8,128)S(1)}, s16[320,256]{1,0:T(8,128)(2,1)S(1)}, s16[320,256]{1,0:T(8,128)(2,1)S(1)}) custom-call(s32[4]{0:T(128)S(1)} %pad_add_fusion.s_ref, bf16[2112,640]{1,0:T(8,128)(2,1)S(1)} %get-tuple-element.48.own_here.refs_0_, bf16[2112,640]{1,0:T(8,128)(2,1)S(1)} %collective-permute-done.3.own_there.refs_2_, ...), custom_call_target="tpu_custom_call" | custom-call | flops 1 | bytes 1 | tf_op jit(solution)/shard_map/sum_pairs/pallas_call | solution.py:86
  71.8 0.6 round_pairs.4.refs_0_
  72.4 3.7 %collective-permute-start.16 = (bf16[320,256]{1,0:T(8,128)(2,1)S(1)}, bf16[320,256]{1,0:T(8,128)(2,1)S(1)}, u32[]{:S(2)}, u32[]{:S(2)}) collective-permute-start(bf16[320,256]{1,0:T(8,128)(2,1)S(1)} %round_pairs.4.refs_0_), channel_id=1, source_target_pairs={{0,12},{4,0},{8,4},{12,8},{1,13},{5,1},{9,5},{13,9},{2,14},{6,2},{... | collective-permute-start | bytes 491528 | tf_op jit(solution)/shard_map/ppermute | solution.py:259
  76.1 1.5 %collective-permute-start.10 = (s16[320,256]{1,0:T(8,128)(2,1)S(1)}, s16[320,256]{1,0:T(8,128)(2,1)S(1)}, u32[]{:S(2)}, u32[]{:S(2)}) collective-permute-start(s16[320,256]{1,0:T(8,128)(2,1)S(1)} %get-tuple-element.61), channel_id=1, source_target_pairs={{0,2},{1,3},{2,0},{3,1},{4,6},{5,7},{6,4},{7,5},{8,10},{9,11},{10,... | collective-permute-start | bytes 491528 | tf_op jit(solution)/shard_map/ppermute | solution.py:265
  77.6 0.9 collective-permute-start.11
  78.4 1.1 %collective-permute-start.12 = (s16[320,256]{1,0:T(8,128)(2,1)S(1)}, s16[320,256]{1,0:T(8,128)(2,1)S(1)}, u32[]{:S(2)}, u32[]{:S(2)}) collective-permute-start(s16[320,256]{1,0:T(8,128)(2,1)S(1)} %get-tuple-element.63), channel_id=1, source_target_pairs={{0,16},{16,0},{1,17},{17,1},{2,18},{18,2},{3,19},{19,3},{4,20},{20... | collective-permute-start | bytes 491528 | tf_op jit(solution)/shard_map/ppermute | solution.py:259
  79.6 0.6 round_pairs.3
  80.2 0.1 collective-permute-start.18
  80.3 3.7 %collective-permute-done.10.refs_0_ = s16[320,256]{1,0:T(8,128)(2,1)S(1)} collective-permute-done((s16[320,256]{1,0:T(8,128)(2,1)S(1)}, s16[320,256]{1,0:T(8,128)(2,1)S(1)}, u32[]{:S(2)}, u32[]{:S(2)}) %collective-permute-start.10) | collective-permute-done | bytes 163872 | tf_op jit(solution)/shard_map/ppermute | solution.py:265
  84.0 0.8 collective-permute-done.11.refs_1_
  84.8 0.9 collective-permute-done.12.refs_2_
  85.7 0.7 round_pairs.5.refs_5_
  86.4 0.7 collective-permute-start.17
  87.1 0.3 collective-permute-done.18.refs_4_
  87.4 4.1 %place_pairs.2.refs_1_ = bf16[2500,256]{1,0:T(8,128)(2,1)S(1)} custom-call(s32[4]{0:T(128)S(1)} %pad_add_fusion.s_ref, bf16[320,256]{1,0:T(8,128)(2,1)S(1)} %round_pairs.4.refs_0_, bf16[320,256]{1,0:T(8,128)(2,1)S(1)} %collective-permute-done.16.refs_1_, bf16[320,256]{1,0:T(8,128)(2,1)S(1)} %get-tuple-element.66.refs_2_, ...), custom_call_target="tpu_custom_call" | custom-call | flops 1 | bytes 1 | tf_op jit(solution)/shard_map/place_pairs/pallas_call | solution.py:86
  91.5 3.1 %collective-permute-done.17.refs_0_ = bf16[320,256]{1,0:T(8,128)(2,1)S(1)} collective-permute-done((bf16[320,256]{1,0:T(8,128)(2,1)S(1)}, bf16[320,256]{1,0:T(8,128)(2,1)S(1)}, u32[]{:S(2)}, u32[]{:S(2)}) %collective-permute-start.17) | collective-permute-done | bytes 163872 | tf_op jit(solution)/shard_map/ppermute | solution.py:259
  94.6 2.4 %place_pairs.3 = bf16[2500,256]{1,0:T(8,128)(2,1)} custom-call(s32[4]{0:T(128)S(1)} %pad_add_fusion.s_ref, bf16[320,256]{1,0:T(8,128)(2,1)S(1)} %collective-permute-done.17.refs_0_, bf16[2500,256]{1,0:T(8,128)(2,1)S(1)} %place_pairs.2.refs_1_), custom_call_target="tpu_custom_call" | custom-call | flops 1 | bytes 1 | tf_op jit(solution)/shard_map/place_pairs/pallas_call | solution.py:86
  (16 shorter events, 0.0 us)
Async XLA Ops:
  0.1 1.7 %copy-start = (bf16[1024,1280]{1,0:T(8,128)(2,1)S(1)}, bf16[1024,1280]{1,0:T(8,128)(2,1)}, u32[]{:S(2)}) copy-start(bf16[1024,1280]{1,0:T(8,128)(2,1)} %v_ref.3) | copy-start | bytes 7864324
  1.8 0.7 copy-start.3
  2.5 0.7 copy-start.5
  3.2 5.9 %copy-start.2 = (bf16[320,2,2500]{2,1,0:T(2,128)(2,1)S(1)}, bf16[320,2,2500]{2,1,0:T(2,128)(2,1)}, u32[]{:S(2)}) copy-start(bf16[320,2,2500]{2,1,0:T(2,128)(2,1)} %t_ref) | copy-start | bytes 9600004
  6.1 11.8 %copy-start.1 = (bf16[1024,1280]{1,0:T(8,128)(2,1)S(1)}, bf16[1024,1280]{1,0:T(8,128)(2,1)}, u32[]{:S(2)}) copy-start(bf16[1024,1280]{1,0:T(8,128)(2,1)} %v_ref.3) | copy-start | bytes 7864324
  6.1 11.8 %copy-start.4 = (s32[1280]{0:T(1024)S(1)}, s32[1280]{0:T(1024)}, u32[]{:S(2)}) copy-start(s32[1280]{0:T(1024)} %param.7) | copy-start | bytes 15364
  6.1 31.8 %collective-permute-start = (bf16[1024,640]{1,0:T(8,128)(2,1)S(1)}, bf16[1024,640]{1,0:T(8,128)(2,1)S(1)}, u32[]{:S(2)}, u32[]{:S(2)}) collective-permute-start(bf16[1024,640]{1,0:T(8,128)(2,1)S(1)} %mask_integrals.1), channel_id=1, source_target_pairs={{0,16},{16,0},{1,17},{17,1},{2,18},{18,2},{3,19},{19,3},{4,20},{20... | collective-permute-start | bytes 3932168 | tf_op jit(solution)/shard_map/ppermute | solution.py:259
  14.3 13.6 %collective-permute-start.1 = (bf16[320,640]{1,0:T(8,128)(2,1)S(1)}, bf16[320,640]{1,0:T(8,128)(2,1)S(1)}, u32[]{:S(2)}, u32[]{:S(2)}) collective-permute-start(bf16[320,640]{1,0:T(8,128)(2,1)S(1)} %get-tuple-element.44), channel_id=1, source_target_pairs={{0,12},{4,0},{8,4},{12,8},{1,13},{5,1},{9,5},{13,9},{2,14},{6,2},{... | collective-permute-start | bytes 1228808 | tf_op jit(solution)/shard_map/ppermute | solution.py:259
  17.9 18.1 %collective-permute-start.2 = (bf16[320,640]{1,0:T(8,128)(2,1)S(1)}, bf16[320,640]{1,0:T(8,128)(2,1)S(1)}, u32[]{:S(2)}, u32[]{:S(2)}) collective-permute-start(bf16[320,640]{1,0:T(8,128)(2,1)S(1)} %get-tuple-element.45), channel_id=1, source_target_pairs={{0,4},{4,8},{8,12},{12,0},{1,5},{5,9},{9,13},{13,1},{2,6},{6,10},{... | collective-permute-start | bytes 1228808 | tf_op jit(solution)/shard_map/ppermute | solution.py:259
  37.9 7.5 %collective-permute-start.3 = (bf16[2112,640]{1,0:T(8,128)(2,1)S(1)}, bf16[2112,640]{1,0:T(8,128)(2,1)S(1)}, u32[]{:S(2)}, u32[]{:S(2)}) collective-permute-start(bf16[2112,640]{1,0:T(8,128)(2,1)S(1)} %get-tuple-element.48.own_here.refs_0_), channel_id=1, source_target_pairs={{0,1},{1,0},{2,3},{3,2},{4,5},{5,4},{6,7},{7,6},{8,9},{9,8},{10,11... | collective-permute-start | bytes 8110088 | tf_op jit(solution)/shard_map/ppermute | solution.py:262
  37.9 7.5 %collective-permute-start.6 = (bf16[1024,640]{1,0:T(8,128)(2,1)S(1)}, bf16[1024,640]{1,0:T(8,128)(2,1)S(1)}, u32[]{:S(2)}, u32[]{:S(2)}) collective-permute-start(bf16[1024,640]{1,0:T(8,128)(2,1)S(1)} %collective-permute-done.refs_3_.refs_5_), channel_id=1, source_target_pairs={{0,1},{1,0},{2,3},{3,2},{4,5},{5,4},{6,7},{7,6},{8,9},{9,8},{10,11... | collective-permute-start | bytes 3932168 | tf_op jit(solution)/shard_map/ppermute | solution.py:262
  38.4 7.0 %collective-permute-start.8 = (bf16[320,640]{1,0:T(8,128)(2,1)S(1)}, bf16[320,640]{1,0:T(8,128)(2,1)S(1)}, u32[]{:S(2)}, u32[]{:S(2)}) collective-permute-start(bf16[320,640]{1,0:T(8,128)(2,1)S(1)} %collective-permute-done.1.refs_1_), channel_id=1, source_target_pairs={{0,1},{1,0},{2,3},{3,2},{4,5},{5,4},{6,7},{7,6},{8,9},{9,8},{10,11... | collective-permute-start | bytes 1228808 | tf_op jit(solution)/shard_map/ppermute | solution.py:262
  38.4 13.1 %collective-permute-start.5 = (bf16[320,640]{1,0:T(8,128)(2,1)S(1)}, bf16[320,640]{1,0:T(8,128)(2,1)S(1)}, u32[]{:S(2)}, u32[]{:S(2)}) collective-permute-start(bf16[320,640]{1,0:T(8,128)(2,1)S(1)} %collective-permute-done.2.refs_0_), channel_id=1, source_target_pairs={{0,1},{1,0},{2,3},{3,2},{4,5},{5,4},{6,7},{7,6},{8,9},{9,8},{10,11... | collective-permute-start | bytes 1228808 | tf_op jit(solution)/shard_map/ppermute | solution.py:262
  38.9 25.6 %collective-permute-start.4 = (bf16[320,640]{1,0:T(8,128)(2,1)S(1)}, bf16[320,640]{1,0:T(8,128)(2,1)S(1)}, u32[]{:S(2)}, u32[]{:S(2)}) collective-permute-start(bf16[320,640]{1,0:T(8,128)(2,1)S(1)} %get-tuple-element.49), channel_id=1, source_target_pairs={{0,8},{4,12},{8,0},{12,4},{1,9},{5,13},{9,1},{13,5},{2,10},{6,14},... | collective-permute-start | bytes 1228808 | tf_op jit(solution)/shard_map/ppermute | solution.py:259
  49.7 16.9 %collective-permute-start.13 = (s16[2,640,256]{2,1,0:T(8,128)(2,1)S(1)}, s16[2,640,256]{2,1,0:T(8,128)(2,1)S(1)}, u32[]{:S(2)}, u32[]{:S(2)}) collective-permute-start(s16[2,640,256]{2,1,0:T(8,128)(2,1)S(1)} %get-tuple-element.57), channel_id=1, source_target_pairs={{0,2},{1,3},{2,0},{3,1},{4,6},{5,7},{6,4},{7,5},{8,10},{9,11},{10,... | collective-permute-start | bytes 1966088 | tf_op jit(solution)/shard_map/ppermute | solution.py:265
  54.2 9.5 %collective-permute-start.7 = (s16[320,512]{1,0:T(8,128)(2,1)S(1)}, s16[320,512]{1,0:T(8,128)(2,1)S(1)}, u32[]{:S(2)}, u32[]{:S(2)}) collective-permute-start(s16[320,512]{1,0:T(8,128)(2,1)S(1)} %get-tuple-element.54), channel_id=1, source_target_pairs={{0,16},{16,0},{1,17},{17,1},{2,18},{18,2},{3,19},{19,3},{4,20},{20... | collective-permute-start | bytes 983048 | tf_op jit(solution)/shard_map/ppermute | solution.py:259
  64.5 4.7 %collective-permute-start.9 = (bf16[320,640]{1,0:T(8,128)(2,1)S(1)}, bf16[320,640]{1,0:T(8,128)(2,1)S(1)}, u32[]{:S(2)}, u32[]{:S(2)}) collective-permute-start(bf16[320,640]{1,0:T(8,128)(2,1)S(1)} %collective-permute-done.4.refs_0_), channel_id=1, source_target_pairs={{0,1},{1,0},{2,3},{3,2},{4,5},{5,4},{6,7},{7,6},{8,9},{9,8},{10,11... | collective-permute-start | bytes 1228808 | tf_op jit(solution)/shard_map/ppermute | solution.py:262
  64.6 7.2 %collective-permute-start.15 = (s16[320,256]{1,0:T(8,128)(2,1)S(1)}, s16[320,256]{1,0:T(8,128)(2,1)S(1)}, u32[]{:S(2)}, u32[]{:S(2)}) collective-permute-start(s16[320,256]{1,0:T(8,128)(2,1)S(1)} %get-tuple-element.68), channel_id=1, source_target_pairs={{0,2},{1,3},{2,0},{3,1},{4,6},{5,7},{6,4},{7,5},{8,10},{9,11},{10,... | collective-permute-start | bytes 491528 | tf_op jit(solution)/shard_map/ppermute | solution.py:265
  67.5 12.1 %collective-permute-start.14 = (s16[640,256]{1,0:T(8,128)(2,1)S(1)}, s16[640,256]{1,0:T(8,128)(2,1)S(1)}, u32[]{:S(2)}, u32[]{:S(2)}) collective-permute-start(s16[640,256]{1,0:T(8,128)(2,1)S(1)} %get-tuple-element.65), channel_id=1, source_target_pairs={{0,16},{16,0},{1,17},{17,1},{2,18},{18,2},{3,19},{19,3},{4,20},{20... | collective-permute-start | bytes 983048 | tf_op jit(solution)/shard_map/ppermute | solution.py:259
  72.4 7.9 %collective-permute-start.16 = (bf16[320,256]{1,0:T(8,128)(2,1)S(1)}, bf16[320,256]{1,0:T(8,128)(2,1)S(1)}, u32[]{:S(2)}, u32[]{:S(2)}) collective-permute-start(bf16[320,256]{1,0:T(8,128)(2,1)S(1)} %round_pairs.4.refs_0_), channel_id=1, source_target_pairs={{0,12},{4,0},{8,4},{12,8},{1,13},{5,1},{9,5},{13,9},{2,14},{6,2},{... | collective-permute-start | bytes 491528 | tf_op jit(solution)/shard_map/ppermute | solution.py:259
  76.1 7.9 %collective-permute-start.10 = (s16[320,256]{1,0:T(8,128)(2,1)S(1)}, s16[320,256]{1,0:T(8,128)(2,1)S(1)}, u32[]{:S(2)}, u32[]{:S(2)}) collective-permute-start(s16[320,256]{1,0:T(8,128)(2,1)S(1)} %get-tuple-element.61), channel_id=1, source_target_pairs={{0,2},{1,3},{2,0},{3,1},{4,6},{5,7},{6,4},{7,5},{8,10},{9,11},{10,... | collective-permute-start | bytes 491528 | tf_op jit(solution)/shard_map/ppermute | solution.py:265
  77.6 7.2 %collective-permute-start.11 = (s16[320,256]{1,0:T(8,128)(2,1)S(1)}, s16[320,256]{1,0:T(8,128)(2,1)S(1)}, u32[]{:S(2)}, u32[]{:S(2)}) collective-permute-start(s16[320,256]{1,0:T(8,128)(2,1)S(1)} %get-tuple-element.62), channel_id=1, source_target_pairs={{0,18},{1,19},{2,16},{3,17},{16,2},{17,3},{18,0},{19,1},{4,22},{5,... | collective-permute-start | bytes 491528 | tf_op jit(solution)/shard_map/ppermute | solution.py:269
  78.4 7.3 %collective-permute-start.12 = (s16[320,256]{1,0:T(8,128)(2,1)S(1)}, s16[320,256]{1,0:T(8,128)(2,1)S(1)}, u32[]{:S(2)}, u32[]{:S(2)}) collective-permute-start(s16[320,256]{1,0:T(8,128)(2,1)S(1)} %get-tuple-element.63), channel_id=1, source_target_pairs={{0,16},{16,0},{1,17},{17,1},{2,18},{18,2},{3,19},{19,3},{4,20},{20... | collective-permute-start | bytes 491528 | tf_op jit(solution)/shard_map/ppermute | solution.py:259
  80.2 7.2 %collective-permute-start.18 = (bf16[320,256]{1,0:T(8,128)(2,1)S(1)}, bf16[320,256]{1,0:T(8,128)(2,1)S(1)}, u32[]{:S(2)}, u32[]{:S(2)}) collective-permute-start(bf16[320,256]{1,0:T(8,128)(2,1)S(1)} %get-tuple-element.67.refs_3_), channel_id=1, source_target_pairs={{0,4},{4,8},{8,12},{12,0},{1,5},{5,9},{9,13},{13,1},{2,6},{6,10},{... | collective-permute-start | bytes 491528 | tf_op jit(solution)/shard_map/ppermute | solution.py:259
  86.4 8.2 %collective-permute-start.17 = (bf16[320,256]{1,0:T(8,128)(2,1)S(1)}, bf16[320,256]{1,0:T(8,128)(2,1)S(1)}, u32[]{:S(2)}, u32[]{:S(2)}) collective-permute-start(bf16[320,256]{1,0:T(8,128)(2,1)S(1)} %round_pairs.5.refs_5_), channel_id=1, source_target_pairs={{0,8},{4,12},{8,0},{12,4},{1,9},{5,13},{9,1},{13,5},{2,10},{6,14},... | collective-permute-start | bytes 491528 | tf_op jit(solution)/shard_map/ppermute | solution.py:259

commit v11 on v10

--- a/solution.py
+++ b/solution.py
@@ -356,7 +356,7 @@
             coded, own_sum = call(
                 "add_other_x", add_x_body, scalars, crossed[group], [((high, tall), i16), ((high, tall), f32)]
             )
-            added[group] = [own_sum, other_y(coded)]
+            added[group] = [own_sum, coded]
         return own_sum
 
     def round_pairs(group, sums):
@@ -380,10 +380,12 @@
     away[far] = after(away[far], early, sums)
     away_there[far] = other_core(away[far])
     sums = sum_pairs(last, "direct")
-    round_pairs(x_group, after(added[x_group], sums))
+    own_sum, coded = after(added[x_group], sums)
+    added[x_group] = [own_sum, other_y(coded)]
     add_pairs(y_group, "y")
     early = round_pairs(y_group, added[y_group])
-    round_pairs(last, after(crossed[last], early, [rounded[r, False] for r in x_group]))
+    round_pairs(x_group, added[x_group])
+    round_pairs(last, after(crossed[last], early, rounded[x_group[0], True]))
 
     done = None
     ends = [(far, False)]

time: 97.2 us -> 101 us (1.039)
  waiting for transfers between devices: 32.3 us -> 34.1 us
  starting transfers between devices: 24 us -> 25.6 us
    ppermute x3, waiting for transfers between devices: 5.26 us -> 6.7 us  [other_y(): return lax.ppermute(array, 'depth', [(i, i ^ 2) for i in range(depth_n)])]
    ppermute x10, waiting for transfers between devices: 22.6 us -> 23.8 us  [shift(): lax.ppermute(array, axis, [(i, (i + by) % count) for i in range(count)])]
  transfers between devices with their start and end apart: 19 -> 19, of which waited for: 11 -> 9; matrix products, arithmetic and copies ran while one was open for 0% -> 0% of each run, Pallas kernels for 33% -> 32%
where the time goes in v11:
time: 101 us
  Pallas kernels  37.7 us (37%)
  waiting for transfers between devices  34.1 us (34%)
  starting transfers between devices  25.6 us (25%)
  local copies, waits for them, and re-layouts  3.14 us (3%)
    pallas_call x13, Pallas kernels, call(): pl.pallas_call(body, name=name, out_shape=shapes, compiler_params=pltpu.C...  37.7 us
    ppermute x10, waiting for transfers between devices, shift(): lax.ppermute(array, axis, [(i, (i + by) % count) for i in range(count)])  23.8 us
    ppermute x10, starting transfers between devices, shift(): lax.ppermute(array, axis, [(i, (i + by) % count) for i in range(count)])  19.1 us
    ppermute x3, waiting for transfers between devices, other_y(): return lax.ppermute(array, 'depth', [(i, i ^ 2) for i in range(depth_n)])  6.7 us
    ppermute x3, starting transfers between devices, other_y(): return lax.ppermute(array, 'depth', [(i, i ^ 2) for i in range(depth_n)])  3.93 us
    ppermute x5, waiting for transfers between devices, other_core(): return lax.ppermute(array, 'depth', [(i, i ^ 1) for i in range(depth_n)])  3.64 us
    unnamed x12, local copies, waits for them, and re-layouts  3.14 us
  transfers between devices with their start and end apart: 19, of which 9 were waited for; matrix products, arithmetic and copies ran while one was open for 0% of the time, Pallas kernels for 32%

profile of v11, /device:TPU:0, one launch (start us, length us, event | category | flops | bytes accessed | tf_op | source)
XLA Modules:
  0.0 100.8 jit_solution(5959754223846064660)
XLA Ops:
  0.0 0.1 pad_add_fusion.s_ref
  0.1 1.7 %copy-done = bf16[1024,1280]{1,0:T(8,128)(2,1)S(1)} copy-done((bf16[1024,1280]{1,0:T(8,128)(2,1)S(1)}, bf16[1024,1280]{1,0:T(8,128)(2,1)}, u32[]{:S(2)}) %copy-start) | copy-done | bytes 2621464
  1.8 0.7 copy-done.3
  2.5 0.7 copy-done.5
  3.2 2.9 %mask_integrals.1 = bf16[1024,640]{1,0:T(8,128)(2,1)S(1)} custom-call(s32[4]{0:T(128)S(1)} %pad_add_fusion.s_ref, s32[8,128]{1,0:T(8,128)S(1)} %bitcast.9, s32[10,128]{1,0:T(8,128)S(1)} %bitcast.7, bf16[1024,1280]{1,0:T(8,128)(2,1)S(1)} %copy-done), custom_call_target="tpu_custom_call" | custom-call | flops 1 | bytes 1 | tf_op jit(solution)/shard_map/mask_integrals/pallas_call | solution.py:86
  6.1 0.0 copy-start.1
  6.1 0.0 copy-start.4
  6.1 3.0 %collective-permute-start = (bf16[1024,640]{1,0:T(8,128)(2,1)S(1)}, bf16[1024,640]{1,0:T(8,128)(2,1)S(1)}, u32[]{:S(2)}, u32[]{:S(2)}) collective-permute-start(bf16[1024,640]{1,0:T(8,128)(2,1)S(1)} %mask_integrals.1), channel_id=1, source_target_pairs={{0,16},{16,0},{1,17},{17,1},{2,18},{18,2},{3,19},{19,3},{4,20},{20... | collective-permute-start | bytes 3932168 | tf_op jit(solution)/shard_map/ppermute | solution.py:259
  9.1 5.1 %send_columns.1 = (bf16[640,2560]{1,0:T(8,128)(2,1)S(1)}, bf16[320,640]{1,0:T(8,128)(2,1)S(1)}, bf16[320,640]{1,0:T(8,128)(2,1)S(1)}, bf16[320,640]{1,0:T(8,128)(2,1)S(1)}) custom-call(s32[4]{0:T(128)S(1)} %pad_add_fusion.s_ref, bf16[320,2,2500]{2,1,0:T(2,128)(2,1)S(1)} %copy-done.2), custom_call_target="tpu_custom_call" | custom-call | flops 1 | bytes 1 | tf_op jit(solution)/shard_map/send_columns/pallas_call | solution.py:86
  14.3 3.7 %collective-permute-start.1 = (bf16[320,640]{1,0:T(8,128)(2,1)S(1)}, bf16[320,640]{1,0:T(8,128)(2,1)S(1)}, u32[]{:S(2)}, u32[]{:S(2)}) collective-permute-start(bf16[320,640]{1,0:T(8,128)(2,1)S(1)} %get-tuple-element.44), channel_id=1, source_target_pairs={{0,12},{4,0},{8,4},{12,8},{1,13},{5,1},{9,5},{13,9},{2,14},{6,2},{... | collective-permute-start | bytes 1228808 | tf_op jit(solution)/shard_map/ppermute | solution.py:259
  17.9 0.0 collective-permute-start.2
  17.9 9.6 %keep_columns.1 = (bf16[2112,640]{1,0:T(8,128)(2,1)S(1)}, bf16[512,640]{1,0:T(8,128)(2,1)S(1)}) custom-call(s32[4]{0:T(128)S(1)} %pad_add_fusion.s_ref, bf16[640,2560]{1,0:T(8,128)(2,1)S(1)} %get-tuple-element.41.flat_ref, s32[8,128]{1,0:T(8,128)S(1)} %bitcast.10, s32[10,128]{1,0:T(8,128)S(1)} %bitcast.8, bf16[1024,1280]{1,0:T(8,128)(2,1)S(1)} %copy-done.1), custom_call_target="tpu_custom_call" | custom-call | flops 1 | bytes 1 | tf_op jit(solution)/shard_map/keep_columns/pallas_call | solution.py:86
  27.5 0.3 collective-permute-done.1.refs_1_
  27.8 8.2 %collective-permute-done.2.refs_0_ = bf16[320,640]{1,0:T(8,128)(2,1)S(1)} collective-permute-done((bf16[320,640]{1,0:T(8,128)(2,1)S(1)}, bf16[320,640]{1,0:T(8,128)(2,1)S(1)}, u32[]{:S(2)}, u32[]{:S(2)}) %collective-permute-start.2) | collective-permute-done | bytes 409632 | tf_op jit(solution)/shard_map/ppermute | solution.py:259
  36.0 1.8 %collective-permute-done.refs_3_.refs_5_ = bf16[1024,640]{1,0:T(8,128)(2,1)S(1)} collective-permute-done((bf16[1024,640]{1,0:T(8,128)(2,1)S(1)}, bf16[1024,640]{1,0:T(8,128)(2,1)S(1)}, u32[]{:S(2)}, u32[]{:S(2)}) %collective-permute-start) | collective-permute-done | bytes 1310752 | tf_op jit(solution)/shard_map/ppermute | solution.py:259
  37.9 0.5 collective-permute-start.6
  38.4 0.0 collective-permute-start.8
  38.4 0.5 collective-permute-start.5
  38.9 2.8 %collective-permute-start.4 = (bf16[320,640]{1,0:T(8,128)(2,1)S(1)}, bf16[320,640]{1,0:T(8,128)(2,1)S(1)}, u32[]{:S(2)}, u32[]{:S(2)}) collective-permute-start(bf16[320,640]{1,0:T(8,128)(2,1)S(1)} %get-tuple-element.49), channel_id=1, source_target_pairs={{0,8},{4,12},{8,0},{12,4},{1,9},{5,13},{9,1},{13,5},{2,10},{6,14},... | collective-permute-start | bytes 1228808 | tf_op jit(solution)/shard_map/ppermute | solution.py:259
  41.7 3.6 %collective-permute-done.8.refs_3_ = bf16[320,640]{1,0:T(8,128)(2,1)S(1)} collective-permute-done((bf16[320,640]{1,0:T(8,128)(2,1)S(1)}, bf16[320,640]{1,0:T(8,128)(2,1)S(1)}, u32[]{:S(2)}, u32[]{:S(2)}) %collective-permute-start.8) | collective-permute-done | bytes 409632 | tf_op jit(solution)/shard_map/ppermute | solution.py:262
  45.4 0.0 collective-permute-done.6.refs_4_.refs_6_
  45.4 0.0 collective-permute-done.3.own_there.refs_2_
  45.4 4.3 %sum_pairs.4 = (s16[2,640,256]{2,1,0:T(8,128)(2,1)S(1)}, f32[2,640,256]{2,1,0:T(8,128)S(1)}) custom-call(s32[4]{0:T(128)S(1)} %pad_add_fusion.s_ref, bf16[2112,640]{1,0:T(8,128)(2,1)S(1)} %get-tuple-element.48.own_here.refs_0_, bf16[2112,640]{1,0:T(8,128)(2,1)S(1)} %collective-permute-done.3.own_there.refs_2_, ...), custom_call_target="tpu_custom_call" | custom-call | flops 1 | bytes 1 | tf_op jit(solution)/shard_map/sum_pairs/pallas_call | solution.py:86
  49.7 1.8 %collective-permute-start.13 = (s16[2,640,256]{2,1,0:T(8,128)(2,1)S(1)}, s16[2,640,256]{2,1,0:T(8,128)(2,1)S(1)}, u32[]{:S(2)}, u32[]{:S(2)}) collective-permute-start(s16[2,640,256]{2,1,0:T(8,128)(2,1)S(1)} %get-tuple-element.57), channel_id=1, source_target_pairs={{0,2},{1,3},{2,0},{3,1},{4,6},{5,7},{6,4},{7,5},{8,10},{9,11},{10,... | collective-permute-start | bytes 1966088 | tf_op jit(solution)/shard_map/ppermute | solution.py:265
  51.5 2.7 %sum_pairs.3 = (s16[320,512]{1,0:T(8,128)(2,1)S(1)}, f32[320,512]{1,0:T(8,128)S(1)}) custom-call(s32[4]{0:T(128)S(1)} %pad_add_fusion.s_ref, bf16[2112,640]{1,0:T(8,128)(2,1)S(1)} %get-tuple-element.48.own_here.refs_0_, bf16[2112,640]{1,0:T(8,128)(2,1)S(1)} %collective-permute-done.3.own_there.refs_2_, bf16[320,640]{1,0:T(8,128)(2,1)S(1)} %collective-permute-done.2.refs_0_, ...), custom_call_target="tpu_custom_call" | custom-call | flops 1 | bytes 1 | tf_op jit(solution)/shard_map/sum_pairs/pallas_call | solution.py:86
  54.2 1.6 %collective-permute-start.7 = (s16[320,512]{1,0:T(8,128)(2,1)S(1)}, s16[320,512]{1,0:T(8,128)(2,1)S(1)}, u32[]{:S(2)}, u32[]{:S(2)}) collective-permute-start(s16[320,512]{1,0:T(8,128)(2,1)S(1)} %get-tuple-element.54), channel_id=1, source_target_pairs={{0,16},{16,0},{1,17},{17,1},{2,18},{18,2},{3,19},{19,3},{4,20},{20... | collective-permute-start | bytes 983048 | tf_op jit(solution)/shard_map/ppermute | solution.py:259
  55.8 8.0 %collective-permute-done.7.refs_0_ = s16[320,512]{1,0:T(8,128)(2,1)S(1)} collective-permute-done((s16[320,512]{1,0:T(8,128)(2,1)S(1)}, s16[320,512]{1,0:T(8,128)(2,1)S(1)}, u32[]{:S(2)}, u32[]{:S(2)}) %collective-permute-start.7) | collective-permute-done | bytes 327712 | tf_op jit(solution)/shard_map/ppermute | solution.py:259
  63.8 0.7 add_other_x.1
  64.5 0.1 collective-permute-start.9
  64.6 1.9 %collective-permute-done.13.coded_ref = s16[2,640,256]{2,1,0:T(8,128)(2,1)S(1)} collective-permute-done((s16[2,640,256]{2,1,0:T(8,128)(2,1)S(1)}, s16[2,640,256]{2,1,0:T(8,128)(2,1)S(1)}, u32[]{:S(2)}, u32[]{:S(2)}) %collective-permute-start.13) | collective-permute-done | bytes 655392 | tf_op jit(solution)/shard_map/ppermute | solution.py:265
  66.5 0.9 add_other_y.1
  67.5 1.8 %collective-permute-start.14 = (s16[640,256]{1,0:T(8,128)(2,1)S(1)}, s16[640,256]{1,0:T(8,128)(2,1)S(1)}, u32[]{:S(2)}, u32[]{:S(2)}) collective-permute-start(s16[640,256]{1,0:T(8,128)(2,1)S(1)} %get-tuple-element.65), channel_id=1, source_target_pairs={{0,16},{16,0},{1,17},{17,1},{2,18},{18,2},{3,19},{19,3},{4,20},{20... | collective-permute-start | bytes 983048 | tf_op jit(solution)/shard_map/ppermute | solution.py:259
  69.3 2.5 %sum_pairs.5 = (s16[320,256]{1,0:T(8,128)(2,1)S(1)}, f32[320,256]{1,0:T(8,128)S(1)}, s16[320,256]{1,0:T(8,128)(2,1)S(1)}, s16[320,256]{1,0:T(8,128)(2,1)S(1)}) custom-call(s32[4]{0:T(128)S(1)} %pad_add_fusion.s_ref, bf16[2112,640]{1,0:T(8,128)(2,1)S(1)} %get-tuple-element.48.own_here.refs_0_, bf16[2112,640]{1,0:T(8,128)(2,1)S(1)} %collective-permute-done.3.own_there.refs_2_, ...), custom_call_target="tpu_custom_call" | custom-call | flops 1 | bytes 1 | tf_op jit(solution)/shard_map/sum_pairs/pallas_call | solution.py:86
  71.8 1.6 %collective-permute-start.15 = (s16[320,256]{1,0:T(8,128)(2,1)S(1)}, s16[320,256]{1,0:T(8,128)(2,1)S(1)}, u32[]{:S(2)}, u32[]{:S(2)}) collective-permute-start(s16[320,256]{1,0:T(8,128)(2,1)S(1)} %get-tuple-element.70), channel_id=1, source_target_pairs={{0,2},{1,3},{2,0},{3,1},{4,6},{5,7},{6,4},{7,5},{8,10},{9,11},{10,... | collective-permute-start | bytes 491528 | tf_op jit(solution)/shard_map/ppermute | solution.py:265
  73.4 0.5 collective-permute-start.10
  73.9 1.5 %collective-permute-start.11 = (s16[320,256]{1,0:T(8,128)(2,1)S(1)}, s16[320,256]{1,0:T(8,128)(2,1)S(1)}, u32[]{:S(2)}, u32[]{:S(2)}) collective-permute-start(s16[320,256]{1,0:T(8,128)(2,1)S(1)} %get-tuple-element.62), channel_id=1, source_target_pairs={{0,18},{1,19},{2,16},{3,17},{16,2},{17,3},{18,0},{19,1},{4,22},{5,... | collective-permute-start | bytes 491528 | tf_op jit(solution)/shard_map/ppermute | solution.py:269
  75.4 1.5 %collective-permute-start.12 = (s16[320,256]{1,0:T(8,128)(2,1)S(1)}, s16[320,256]{1,0:T(8,128)(2,1)S(1)}, u32[]{:S(2)}, u32[]{:S(2)}) collective-permute-start(s16[320,256]{1,0:T(8,128)(2,1)S(1)} %get-tuple-element.63), channel_id=1, source_target_pairs={{0,16},{16,0},{1,17},{17,1},{2,18},{18,2},{3,19},{19,3},{4,20},{20... | collective-permute-start | bytes 491528 | tf_op jit(solution)/shard_map/ppermute | solution.py:259
  76.9 4.8 %collective-permute-done.15.refs_0_ = s16[320,256]{1,0:T(8,128)(2,1)S(1)} collective-permute-done((s16[320,256]{1,0:T(8,128)(2,1)S(1)}, s16[320,256]{1,0:T(8,128)(2,1)S(1)}, u32[]{:S(2)}, u32[]{:S(2)}) %collective-permute-start.15) | collective-permute-done | bytes 163872 | tf_op jit(solution)/shard_map/ppermute | solution.py:265
  81.7 0.6 round_pairs.4.refs_3_
  82.3 3.6 %collective-permute-start.18 = (bf16[320,256]{1,0:T(8,128)(2,1)S(1)}, bf16[320,256]{1,0:T(8,128)(2,1)S(1)}, u32[]{:S(2)}, u32[]{:S(2)}) collective-permute-start(bf16[320,256]{1,0:T(8,128)(2,1)S(1)} %round_pairs.4.refs_3_), channel_id=1, source_target_pairs={{0,12},{4,0},{8,4},{12,8},{1,13},{5,1},{9,5},{13,9},{2,14},{6,2},{... | collective-permute-start | bytes 491528 | tf_op jit(solution)/shard_map/ppermute | solution.py:259
  85.9 0.6 round_pairs.3
  86.5 0.1 collective-permute-start.17
  86.6 0.7 round_pairs.5.refs_5_
  87.3 1.1 %collective-permute-start.16 = (bf16[320,256]{1,0:T(8,128)(2,1)S(1)}, bf16[320,256]{1,0:T(8,128)(2,1)S(1)}, u32[]{:S(2)}, u32[]{:S(2)}) collective-permute-start(bf16[320,256]{1,0:T(8,128)(2,1)S(1)} %round_pairs.5.refs_5_), channel_id=1, source_target_pairs={{0,8},{4,12},{8,0},{12,4},{1,9},{5,13},{9,1},{13,5},{2,10},{6,14},... | collective-permute-start | bytes 491528 | tf_op jit(solution)/shard_map/ppermute | solution.py:259
  88.4 0.7 collective-permute-done.18.refs_4_
  89.1 4.7 %collective-permute-done.17.refs_2_ = bf16[320,256]{1,0:T(8,128)(2,1)S(1)} collective-permute-done((bf16[320,256]{1,0:T(8,128)(2,1)S(1)}, bf16[320,256]{1,0:T(8,128)(2,1)S(1)}, u32[]{:S(2)}, u32[]{:S(2)}) %collective-permute-start.17) | collective-permute-done | bytes 163872 | tf_op jit(solution)/shard_map/ppermute | solution.py:259
  93.8 4.5 %place_pairs.2.refs_1_ = bf16[2500,256]{1,0:T(8,128)(2,1)S(1)} custom-call(s32[4]{0:T(128)S(1)} %pad_add_fusion.s_ref, bf16[320,256]{1,0:T(8,128)(2,1)S(1)} %get-tuple-element.66.refs_0_, bf16[320,256]{1,0:T(8,128)(2,1)S(1)} %get-tuple-element.67.refs_1_, bf16[320,256]{1,0:T(8,128)(2,1)S(1)} %collective-permute-done.17.refs_2_, ...), custom_call_target="tpu_custom_call" | custom-call | flops 1 | bytes 1 | tf_op jit(solution)/shard_map/place_pairs/pallas_call | solution.py:86
  98.4 2.4 %place_pairs.3 = bf16[2500,256]{1,0:T(8,128)(2,1)} custom-call(s32[4]{0:T(128)S(1)} %pad_add_fusion.s_ref, bf16[320,256]{1,0:T(8,128)(2,1)S(1)} %collective-permute-done.16.refs_0_, bf16[2500,256]{1,0:T(8,128)(2,1)S(1)} %place_pairs.2.refs_1_), custom_call_target="tpu_custom_call" | custom-call | flops 1 | bytes 1 | tf_op jit(solution)/shard_map/place_pairs/pallas_call | solution.py:86
  (16 shorter events, 0.0 us)
Async XLA Ops:
  0.1 1.7 %copy-start = (bf16[1024,1280]{1,0:T(8,128)(2,1)S(1)}, bf16[1024,1280]{1,0:T(8,128)(2,1)}, u32[]{:S(2)}) copy-start(bf16[1024,1280]{1,0:T(8,128)(2,1)} %v_ref.3) | copy-start | bytes 7864324
  1.8 0.7 copy-start.3
  2.5 0.7 copy-start.5
  3.2 5.9 %copy-start.2 = (bf16[320,2,2500]{2,1,0:T(2,128)(2,1)S(1)}, bf16[320,2,2500]{2,1,0:T(2,128)(2,1)}, u32[]{:S(2)}) copy-start(bf16[320,2,2500]{2,1,0:T(2,128)(2,1)} %t_ref) | copy-start | bytes 9600004
  6.1 11.8 %copy-start.1 = (bf16[1024,1280]{1,0:T(8,128)(2,1)S(1)}, bf16[1024,1280]{1,0:T(8,128)(2,1)}, u32[]{:S(2)}) copy-start(bf16[1024,1280]{1,0:T(8,128)(2,1)} %v_ref.3) | copy-start | bytes 7864324
  6.1 11.8 %copy-start.4 = (s32[1280]{0:T(1024)S(1)}, s32[1280]{0:T(1024)}, u32[]{:S(2)}) copy-start(s32[1280]{0:T(1024)} %param.7) | copy-start | bytes 15364
  6.1 31.8 %collective-permute-start = (bf16[1024,640]{1,0:T(8,128)(2,1)S(1)}, bf16[1024,640]{1,0:T(8,128)(2,1)S(1)}, u32[]{:S(2)}, u32[]{:S(2)}) collective-permute-start(bf16[1024,640]{1,0:T(8,128)(2,1)S(1)} %mask_integrals.1), channel_id=1, source_target_pairs={{0,16},{16,0},{1,17},{17,1},{2,18},{18,2},{3,19},{19,3},{4,20},{20... | collective-permute-start | bytes 3932168 | tf_op jit(solution)/shard_map/ppermute | solution.py:259
  14.3 13.6 %collective-permute-start.1 = (bf16[320,640]{1,0:T(8,128)(2,1)S(1)}, bf16[320,640]{1,0:T(8,128)(2,1)S(1)}, u32[]{:S(2)}, u32[]{:S(2)}) collective-permute-start(bf16[320,640]{1,0:T(8,128)(2,1)S(1)} %get-tuple-element.44), channel_id=1, source_target_pairs={{0,12},{4,0},{8,4},{12,8},{1,13},{5,1},{9,5},{13,9},{2,14},{6,2},{... | collective-permute-start | bytes 1228808 | tf_op jit(solution)/shard_map/ppermute | solution.py:259
  17.9 18.1 %collective-permute-start.2 = (bf16[320,640]{1,0:T(8,128)(2,1)S(1)}, bf16[320,640]{1,0:T(8,128)(2,1)S(1)}, u32[]{:S(2)}, u32[]{:S(2)}) collective-permute-start(bf16[320,640]{1,0:T(8,128)(2,1)S(1)} %get-tuple-element.45), channel_id=1, source_target_pairs={{0,4},{4,8},{8,12},{12,0},{1,5},{5,9},{9,13},{13,1},{2,6},{6,10},{... | collective-permute-start | bytes 1228808 | tf_op jit(solution)/shard_map/ppermute | solution.py:259
  37.9 7.5 %collective-permute-start.3 = (bf16[2112,640]{1,0:T(8,128)(2,1)S(1)}, bf16[2112,640]{1,0:T(8,128)(2,1)S(1)}, u32[]{:S(2)}, u32[]{:S(2)}) collective-permute-start(bf16[2112,640]{1,0:T(8,128)(2,1)S(1)} %get-tuple-element.48.own_here.refs_0_), channel_id=1, source_target_pairs={{0,1},{1,0},{2,3},{3,2},{4,5},{5,4},{6,7},{7,6},{8,9},{9,8},{10,11... | collective-permute-start | bytes 8110088 | tf_op jit(solution)/shard_map/ppermute | solution.py:262
  37.9 7.5 %collective-permute-start.6 = (bf16[1024,640]{1,0:T(8,128)(2,1)S(1)}, bf16[1024,640]{1,0:T(8,128)(2,1)S(1)}, u32[]{:S(2)}, u32[]{:S(2)}) collective-permute-start(bf16[1024,640]{1,0:T(8,128)(2,1)S(1)} %collective-permute-done.refs_3_.refs_5_), channel_id=1, source_target_pairs={{0,1},{1,0},{2,3},{3,2},{4,5},{5,4},{6,7},{7,6},{8,9},{9,8},{10,11... | collective-permute-start | bytes 3932168 | tf_op jit(solution)/shard_map/ppermute | solution.py:262
  38.4 7.0 %collective-permute-start.8 = (bf16[320,640]{1,0:T(8,128)(2,1)S(1)}, bf16[320,640]{1,0:T(8,128)(2,1)S(1)}, u32[]{:S(2)}, u32[]{:S(2)}) collective-permute-start(bf16[320,640]{1,0:T(8,128)(2,1)S(1)} %collective-permute-done.1.refs_1_), channel_id=1, source_target_pairs={{0,1},{1,0},{2,3},{3,2},{4,5},{5,4},{6,7},{7,6},{8,9},{9,8},{10,11... | collective-permute-start | bytes 1228808 | tf_op jit(solution)/shard_map/ppermute | solution.py:262
  38.4 13.1 %collective-permute-start.5 = (bf16[320,640]{1,0:T(8,128)(2,1)S(1)}, bf16[320,640]{1,0:T(8,128)(2,1)S(1)}, u32[]{:S(2)}, u32[]{:S(2)}) collective-permute-start(bf16[320,640]{1,0:T(8,128)(2,1)S(1)} %collective-permute-done.2.refs_0_), channel_id=1, source_target_pairs={{0,1},{1,0},{2,3},{3,2},{4,5},{5,4},{6,7},{7,6},{8,9},{9,8},{10,11... | collective-permute-start | bytes 1228808 | tf_op jit(solution)/shard_map/ppermute | solution.py:262
  38.9 25.6 %collective-permute-start.4 = (bf16[320,640]{1,0:T(8,128)(2,1)S(1)}, bf16[320,640]{1,0:T(8,128)(2,1)S(1)}, u32[]{:S(2)}, u32[]{:S(2)}) collective-permute-start(bf16[320,640]{1,0:T(8,128)(2,1)S(1)} %get-tuple-element.49), channel_id=1, source_target_pairs={{0,8},{4,12},{8,0},{12,4},{1,9},{5,13},{9,1},{13,5},{2,10},{6,14},... | collective-permute-start | bytes 1228808 | tf_op jit(solution)/shard_map/ppermute | solution.py:259
  49.7 16.9 %collective-permute-start.13 = (s16[2,640,256]{2,1,0:T(8,128)(2,1)S(1)}, s16[2,640,256]{2,1,0:T(8,128)(2,1)S(1)}, u32[]{:S(2)}, u32[]{:S(2)}) collective-permute-start(s16[2,640,256]{2,1,0:T(8,128)(2,1)S(1)} %get-tuple-element.57), channel_id=1, source_target_pairs={{0,2},{1,3},{2,0},{3,1},{4,6},{5,7},{6,4},{7,5},{8,10},{9,11},{10,... | collective-permute-start | bytes 1966088 | tf_op jit(solution)/shard_map/ppermute | solution.py:265
  54.2 9.5 %collective-permute-start.7 = (s16[320,512]{1,0:T(8,128)(2,1)S(1)}, s16[320,512]{1,0:T(8,128)(2,1)S(1)}, u32[]{:S(2)}, u32[]{:S(2)}) collective-permute-start(s16[320,512]{1,0:T(8,128)(2,1)S(1)} %get-tuple-element.54), channel_id=1, source_target_pairs={{0,16},{16,0},{1,17},{17,1},{2,18},{18,2},{3,19},{19,3},{4,20},{20... | collective-permute-start | bytes 983048 | tf_op jit(solution)/shard_map/ppermute | solution.py:259
  64.5 4.7 %collective-permute-start.9 = (bf16[320,640]{1,0:T(8,128)(2,1)S(1)}, bf16[320,640]{1,0:T(8,128)(2,1)S(1)}, u32[]{:S(2)}, u32[]{:S(2)}) collective-permute-start(bf16[320,640]{1,0:T(8,128)(2,1)S(1)} %collective-permute-done.4.refs_0_), channel_id=1, source_target_pairs={{0,1},{1,0},{2,3},{3,2},{4,5},{5,4},{6,7},{7,6},{8,9},{9,8},{10,11... | collective-permute-start | bytes 1228808 | tf_op jit(solution)/shard_map/ppermute | solution.py:262
  67.5 18.4 %collective-permute-start.14 = (s16[640,256]{1,0:T(8,128)(2,1)S(1)}, s16[640,256]{1,0:T(8,128)(2,1)S(1)}, u32[]{:S(2)}, u32[]{:S(2)}) collective-permute-start(s16[640,256]{1,0:T(8,128)(2,1)S(1)} %get-tuple-element.65), channel_id=1, source_target_pairs={{0,16},{16,0},{1,17},{17,1},{2,18},{18,2},{3,19},{19,3},{4,20},{20... | collective-permute-start | bytes 983048 | tf_op jit(solution)/shard_map/ppermute | solution.py:259
  71.8 9.9 %collective-permute-start.15 = (s16[320,256]{1,0:T(8,128)(2,1)S(1)}, s16[320,256]{1,0:T(8,128)(2,1)S(1)}, u32[]{:S(2)}, u32[]{:S(2)}) collective-permute-start(s16[320,256]{1,0:T(8,128)(2,1)S(1)} %get-tuple-element.70), channel_id=1, source_target_pairs={{0,2},{1,3},{2,0},{3,1},{4,6},{5,7},{6,4},{7,5},{8,10},{9,11},{10,... | collective-permute-start | bytes 491528 | tf_op jit(solution)/shard_map/ppermute | solution.py:265
  73.4 13.2 %collective-permute-start.10 = (s16[320,256]{1,0:T(8,128)(2,1)S(1)}, s16[320,256]{1,0:T(8,128)(2,1)S(1)}, u32[]{:S(2)}, u32[]{:S(2)}) collective-permute-start(s16[320,256]{1,0:T(8,128)(2,1)S(1)} %get-tuple-element.61), channel_id=1, source_target_pairs={{0,2},{1,3},{2,0},{3,1},{4,6},{5,7},{6,4},{7,5},{8,10},{9,11},{10,... | collective-permute-start | bytes 491528 | tf_op jit(solution)/shard_map/ppermute | solution.py:265
  73.9 12.7 %collective-permute-start.11 = (s16[320,256]{1,0:T(8,128)(2,1)S(1)}, s16[320,256]{1,0:T(8,128)(2,1)S(1)}, u32[]{:S(2)}, u32[]{:S(2)}) collective-permute-start(s16[320,256]{1,0:T(8,128)(2,1)S(1)} %get-tuple-element.62), channel_id=1, source_target_pairs={{0,18},{1,19},{2,16},{3,17},{16,2},{17,3},{18,0},{19,1},{4,22},{5,... | collective-permute-start | bytes 491528 | tf_op jit(solution)/shard_map/ppermute | solution.py:269
  75.4 11.2 %collective-permute-start.12 = (s16[320,256]{1,0:T(8,128)(2,1)S(1)}, s16[320,256]{1,0:T(8,128)(2,1)S(1)}, u32[]{:S(2)}, u32[]{:S(2)}) collective-permute-start(s16[320,256]{1,0:T(8,128)(2,1)S(1)} %get-tuple-element.63), channel_id=1, source_target_pairs={{0,16},{16,0},{1,17},{17,1},{2,18},{18,2},{3,19},{19,3},{4,20},{20... | collective-permute-start | bytes 491528 | tf_op jit(solution)/shard_map/ppermute | solution.py:259
  82.3 6.9 %collective-permute-start.18 = (bf16[320,256]{1,0:T(8,128)(2,1)S(1)}, bf16[320,256]{1,0:T(8,128)(2,1)S(1)}, u32[]{:S(2)}, u32[]{:S(2)}) collective-permute-start(bf16[320,256]{1,0:T(8,128)(2,1)S(1)} %round_pairs.4.refs_3_), channel_id=1, source_target_pairs={{0,12},{4,0},{8,4},{12,8},{1,13},{5,1},{9,5},{13,9},{2,14},{6,2},{... | collective-permute-start | bytes 491528 | tf_op jit(solution)/shard_map/ppermute | solution.py:259
  86.5 7.3 %collective-permute-start.17 = (bf16[320,256]{1,0:T(8,128)(2,1)S(1)}, bf16[320,256]{1,0:T(8,128)(2,1)S(1)}, u32[]{:S(2)}, u32[]{:S(2)}) collective-permute-start(bf16[320,256]{1,0:T(8,128)(2,1)S(1)} %get-tuple-element.67.refs_1_), channel_id=1, source_target_pairs={{0,4},{4,8},{8,12},{12,0},{1,5},{5,9},{9,13},{13,1},{2,6},{6,10},{... | collective-permute-start | bytes 491528 | tf_op jit(solution)/shard_map/ppermute | solution.py:259
  87.3 11.0 %collective-permute-start.16 = (bf16[320,256]{1,0:T(8,128)(2,1)S(1)}, bf16[320,256]{1,0:T(8,128)(2,1)S(1)}, u32[]{:S(2)}, u32[]{:S(2)}) collective-permute-start(bf16[320,256]{1,0:T(8,128)(2,1)S(1)} %round_pairs.5.refs_5_), channel_id=1, source_target_pairs={{0,8},{4,12},{8,0},{12,4},{1,9},{5,13},{9,1},{13,5},{2,10},{6,14},... | collective-permute-start | bytes 491528 | tf_op jit(solution)/shard_map/ppermute | solution.py:259

commit v12 on v10

--- a/solution.py
+++ b/solution.py
@@ -117,8 +117,10 @@
     return dot_nt(jnp.concatenate(blocks, axis=0), one_hot_rows(wanted, cd_here)).astype(jnp.bfloat16)
 
 
-def mask_body(by, row_n, sub, s_ref, ab_ref, cd_ref, v_ref, out_ref):
-    out_ref[...] = masked_rows(by, row_n, sub, out_ref.shape[1], s_ref, ab_ref, cd_ref, v_ref)
+def mask_body(by, row_n, sub, s_ref, ab_ref, cd_ref, v_ref, pass_ref, keep_ref):
+    masked = masked_rows(by, row_n, sub, keep_ref.shape[1], s_ref, ab_ref, cd_ref, v_ref)
+    pass_ref[...] = masked[: pass_ref.shape[0]]
+    keep_ref[...] = masked[pass_ref.shape[0] :]
 
 
 def one_hot_rows(columns, width):
@@ -274,19 +276,19 @@
     scalars = jnp.stack([x, z, y, core]).astype(jnp.int32)
     ab_row, cd_row = ab_irrep.reshape(-1, LANES), cd_irrep.reshape(-1, LANES)
 
-    kept = [None] * row_n
-    gone = scalars
+    kept, passed = [None] * row_n, [None] * row_n
+    stay = scalars
     for by in range(1, row_n):
-        (gone,) = call(
+        gone, stay = call(
             "mask_integrals",
             functools.partial(mask_body, by, row_n, sub),
             scalars,
             [ab_row, cd_row, integrals],
-            [((rows, k_here), bf16)],
+            [((2 * tall, k_here), bf16)] * 2,
         )
-        kept[by] = shift(gone, "row", -by)
-
-    amplitudes, _ = lax.optimization_barrier((amplitudes, gone))
+        passed[by], kept[by] = shift(gone, "row", -by), shift(stay, "row", -by)
+
+    amplitudes, _ = lax.optimization_barrier((amplitudes, stay))
     sent_order = near + [far]
     flat, *sent = call(
         "send_columns",
@@ -305,11 +307,12 @@
         [(((col_n + 1) * chunk + 2 * tall, k_here), bf16), ((2 * tall, k_here), bf16)],
     )
     far_sent, away = lax.optimization_barrier((sent[-1], away))
-    behind, kept[1:], *arrived = lax.optimization_barrier((both, kept[1:], *[away[r] for r in near]))
+    arrived = lax.optimization_barrier((both, kept[1:], passed[1:], *[away[r] for r in near]))
+    behind, kept[1:], passed, *arrived = arrived
     away_there = {r: other_core(a) for r, a in zip(near, arrived)}
     both_there = other_core(behind)
     away[far] = shift(far_sent, "col", -far)
-    passed = [other_core(a) for a in kept[1:]]
+    passed = [other_core(a) for a in passed]
 
     crossed, added, rounded = {}, {}, {}
 

time: 97.2 us -> 96.3 us (level)
  waiting for transfers between devices: 32.3 us -> 29.6 us
  local copies, waits for them, and re-layouts: 3.14 us -> 5.06 us
    ppermute x10 -> x11, waiting for transfers between devices: 22.6 us -> 20.4 us  [shift(): lax.ppermute(array, axis, [(i, (i + by) % count) for i in range(count)])]
    unnamed x12, local copies, waits for them, and re-layouts: 3.14 us -> 5.06 us
    ppermute x10 -> x11, starting transfers between devices: 18.4 us -> 18.3 us  [shift(): lax.ppermute(array, axis, [(i, (i + by) % count) for i in range(count)])]
  transfers between devices with their start and end apart: 19 -> 20, of which waited for: 11 -> 10; matrix products, arithmetic and copies ran while one was open for 0% -> 0% of each run, Pallas kernels for 33% -> 33%
where the time goes in v12:
time: 96.3 us; the launch traced here: 96.1 us
  Pallas kernels  37.3 us (39%)
  waiting for transfers between devices  29.6 us (31%)
  starting transfers between devices  23.9 us (25%)
  local copies, waits for them, and re-layouts  5.06 us (5%)
    pallas_call x13, Pallas kernels, call(): pl.pallas_call(body, name=name, out_shape=shapes, compiler_params=pltpu.C...  37.3 us
    ppermute x11, waiting for transfers between devices, shift(): lax.ppermute(array, axis, [(i, (i + by) % count) for i in range(count)])  20.4 us
    ppermute x11, starting transfers between devices, shift(): lax.ppermute(array, axis, [(i, (i + by) % count) for i in range(count)])  18.3 us
    ppermute x3, waiting for transfers between devices, other_y(): return lax.ppermute(array, 'depth', [(i, i ^ 2) for i in range(depth_n)])  5.29 us
    unnamed x12, local copies, waits for them, and re-layouts  5.06 us
    ppermute x3, starting transfers between devices, other_y(): return lax.ppermute(array, 'depth', [(i, i ^ 2) for i in range(depth_n)])  3.68 us
    ppermute x5, waiting for transfers between devices, other_core(): return lax.ppermute(array, 'depth', [(i, i ^ 1) for i in range(depth_n)])  3.03 us
  transfers between devices with their start and end apart: 20, of which 10 were waited for; matrix products, arithmetic and copies ran while one was open for 0% of the time, Pallas kernels for 33%

profile of v12, /device:TPU:0, one launch (start us, length us, event | category | flops | bytes accessed | tf_op | source)
XLA Modules:
  0.0 96.1 jit_solution(16224285678575558288)
XLA Ops:
  0.0 0.1 pad_add_fusion.s_ref
  0.1 1.7 %copy-done = bf16[1024,1280]{1,0:T(8,128)(2,1)S(1)} copy-done((bf16[1024,1280]{1,0:T(8,128)(2,1)S(1)}, bf16[1024,1280]{1,0:T(8,128)(2,1)}, u32[]{:S(2)}) %copy-start) | copy-done | bytes 2621464
  1.8 0.7 copy-done.3
  2.5 0.7 copy-done.5
  3.2 2.9 %mask_integrals.1 = (bf16[512,640]{1,0:T(8,128)(2,1)S(1)}, bf16[512,640]{1,0:T(8,128)(2,1)S(1)}) custom-call(s32[4]{0:T(128)S(1)} %pad_add_fusion.s_ref, s32[8,128]{1,0:T(8,128)S(1)} %bitcast.9, s32[10,128]{1,0:T(8,128)S(1)} %bitcast.7, bf16[1024,1280]{1,0:T(8,128)(2,1)S(1)} %copy-done), custom_call_target="tpu_custom_call" | custom-call | flops 1 | bytes 1 | tf_op jit(solution)/shard_map/mask_integrals/pallas_call | solution.py:86
  6.1 3.0 %collective-permute-start.1 = (bf16[512,640]{1,0:T(8,128)(2,1)S(1)}, bf16[512,640]{1,0:T(8,128)(2,1)S(1)}, u32[]{:S(2)}, u32[]{:S(2)}) collective-permute-start(bf16[512,640]{1,0:T(8,128)(2,1)S(1)} %get-tuple-element.47), channel_id=1, source_target_pairs={{0,16},{16,0},{1,17},{17,1},{2,18},{18,2},{3,19},{19,3},{4,20},{20... | collective-permute-start | bytes 1966088 | tf_op jit(solution)/shard_map/ppermute | solution.py:261
  9.1 0.1 collective-permute-start
  9.2 1.9 %copy-done.2 = bf16[320,2,2500]{2,1,0:T(2,128)(2,1)S(1)} copy-done((bf16[320,2,2500]{2,1,0:T(2,128)(2,1)S(1)}, bf16[320,2,2500]{2,1,0:T(2,128)(2,1)}, u32[]{:S(2)}) %copy-start.2) | copy-done | bytes 3200024
  11.1 5.1 %send_columns.1 = (bf16[640,2560]{1,0:T(8,128)(2,1)S(1)}, bf16[320,640]{1,0:T(8,128)(2,1)S(1)}, bf16[320,640]{1,0:T(8,128)(2,1)S(1)}, bf16[320,640]{1,0:T(8,128)(2,1)S(1)}) custom-call(s32[4]{0:T(128)S(1)} %pad_add_fusion.s_ref, bf16[320,2,2500]{2,1,0:T(2,128)(2,1)S(1)} %copy-done.2), custom_call_target="tpu_custom_call" | custom-call | flops 1 | bytes 1 | tf_op jit(solution)/shard_map/send_columns/pallas_call | solution.py:86
  16.2 4.1 %collective-permute-start.2 = (bf16[320,640]{1,0:T(8,128)(2,1)S(1)}, bf16[320,640]{1,0:T(8,128)(2,1)S(1)}, u32[]{:S(2)}, u32[]{:S(2)}) collective-permute-start(bf16[320,640]{1,0:T(8,128)(2,1)S(1)} %get-tuple-element.49), channel_id=1, source_target_pairs={{0,12},{4,0},{8,4},{12,8},{1,13},{5,1},{9,5},{13,9},{2,14},{6,2},{... | collective-permute-start | bytes 1228808 | tf_op jit(solution)/shard_map/ppermute | solution.py:261
  20.3 0.0 collective-permute-start.3
  20.4 9.6 %keep_columns.1 = (bf16[2112,640]{1,0:T(8,128)(2,1)S(1)}, bf16[512,640]{1,0:T(8,128)(2,1)S(1)}) custom-call(s32[4]{0:T(128)S(1)} %pad_add_fusion.s_ref, bf16[640,2560]{1,0:T(8,128)(2,1)S(1)} %get-tuple-element.45.flat_ref, s32[8,128]{1,0:T(8,128)S(1)} %bitcast.10, s32[10,128]{1,0:T(8,128)S(1)} %bitcast.8, bf16[1024,1280]{1,0:T(8,128)(2,1)S(1)} %copy-done.1), custom_call_target="tpu_custom_call" | custom-call | flops 1 | bytes 1 | tf_op jit(solution)/shard_map/keep_columns/pallas_call | solution.py:86
  30.0 0.3 collective-permute-done.2.refs_1_
  30.3 7.9 %collective-permute-done.3.refs_0_ = bf16[320,640]{1,0:T(8,128)(2,1)S(1)} collective-permute-done((bf16[320,640]{1,0:T(8,128)(2,1)S(1)}, bf16[320,640]{1,0:T(8,128)(2,1)S(1)}, u32[]{:S(2)}, u32[]{:S(2)}) %collective-permute-start.3) | collective-permute-done | bytes 409632 | tf_op jit(solution)/shard_map/ppermute | solution.py:261
  38.2 0.0 collective-permute-done.1
  38.2 0.5 collective-permute-start.7
  38.7 0.1 collective-permute-start.9
  38.8 0.4 collective-permute-start.6
  39.2 2.5 %collective-permute-start.5 = (bf16[320,640]{1,0:T(8,128)(2,1)S(1)}, bf16[320,640]{1,0:T(8,128)(2,1)S(1)}, u32[]{:S(2)}, u32[]{:S(2)}) collective-permute-start(bf16[320,640]{1,0:T(8,128)(2,1)S(1)} %get-tuple-element.54), channel_id=1, source_target_pairs={{0,8},{4,12},{8,0},{12,4},{1,9},{5,13},{9,1},{13,5},{2,10},{6,14},... | collective-permute-start | bytes 1228808 | tf_op jit(solution)/shard_map/ppermute | solution.py:261
  41.7 3.0 %collective-permute-done.9.refs_3_ = bf16[320,640]{1,0:T(8,128)(2,1)S(1)} collective-permute-done((bf16[320,640]{1,0:T(8,128)(2,1)S(1)}, bf16[320,640]{1,0:T(8,128)(2,1)S(1)}, u32[]{:S(2)}, u32[]{:S(2)}) %collective-permute-start.9) | collective-permute-done | bytes 409632 | tf_op jit(solution)/shard_map/ppermute | solution.py:264
  44.8 4.3 %sum_pairs.4 = (s16[2,640,256]{2,1,0:T(8,128)(2,1)S(1)}, f32[2,640,256]{2,1,0:T(8,128)S(1)}) custom-call(s32[4]{0:T(128)S(1)} %pad_add_fusion.s_ref, bf16[2112,640]{1,0:T(8,128)(2,1)S(1)} %get-tuple-element.53.own_here.refs_0_, bf16[2112,640]{1,0:T(8,128)(2,1)S(1)} %collective-permute-done.4.own_there.refs_2_, ...), custom_call_target="tpu_custom_call" | custom-call | flops 1 | bytes 1 | tf_op jit(solution)/shard_map/sum_pairs/pallas_call | solution.py:86
  49.0 1.6 %collective-permute-start.14 = (s16[2,640,256]{2,1,0:T(8,128)(2,1)S(1)}, s16[2,640,256]{2,1,0:T(8,128)(2,1)S(1)}, u32[]{:S(2)}, u32[]{:S(2)}) collective-permute-start(s16[2,640,256]{2,1,0:T(8,128)(2,1)S(1)} %get-tuple-element.63), channel_id=1, source_target_pairs={{0,2},{1,3},{2,0},{3,1},{4,6},{5,7},{6,4},{7,5},{8,10},{9,11},{10,... | collective-permute-start | bytes 1966088 | tf_op jit(solution)/shard_map/ppermute | solution.py:267
  50.6 2.7 %sum_pairs.3 = (s16[320,512]{1,0:T(8,128)(2,1)S(1)}, f32[320,512]{1,0:T(8,128)S(1)}) custom-call(s32[4]{0:T(128)S(1)} %pad_add_fusion.s_ref, bf16[2112,640]{1,0:T(8,128)(2,1)S(1)} %get-tuple-element.53.own_here.refs_0_, bf16[2112,640]{1,0:T(8,128)(2,1)S(1)} %collective-permute-done.4.own_there.refs_2_, bf16[320,640]{1,0:T(8,128)(2,1)S(1)} %collective-permute-done.3.refs_0_, ...), custom_call_target="tpu_custom_call" | custom-call | flops 1 | bytes 1 | tf_op jit(solution)/shard_map/sum_pairs/pallas_call | solution.py:86
  53.4 1.6 %collective-permute-start.8 = (s16[320,512]{1,0:T(8,128)(2,1)S(1)}, s16[320,512]{1,0:T(8,128)(2,1)S(1)}, u32[]{:S(2)}, u32[]{:S(2)}) collective-permute-start(s16[320,512]{1,0:T(8,128)(2,1)S(1)} %get-tuple-element.60), channel_id=1, source_target_pairs={{0,16},{16,0},{1,17},{17,1},{2,18},{18,2},{3,19},{19,3},{4,20},{20... | collective-permute-start | bytes 983048 | tf_op jit(solution)/shard_map/ppermute | solution.py:261
  54.9 8.0 %collective-permute-done.8.refs_0_ = s16[320,512]{1,0:T(8,128)(2,1)S(1)} collective-permute-done((s16[320,512]{1,0:T(8,128)(2,1)S(1)}, s16[320,512]{1,0:T(8,128)(2,1)S(1)}, u32[]{:S(2)}, u32[]{:S(2)}) %collective-permute-start.8) | collective-permute-done | bytes 327712 | tf_op jit(solution)/shard_map/ppermute | solution.py:261
  62.9 0.7 add_other_x.1
  63.6 0.1 collective-permute-start.10
  63.7 0.6 collective-permute-start.16
  64.3 1.6 %collective-permute-done.14.coded_ref = s16[2,640,256]{2,1,0:T(8,128)(2,1)S(1)} collective-permute-done((s16[2,640,256]{2,1,0:T(8,128)(2,1)S(1)}, s16[2,640,256]{2,1,0:T(8,128)(2,1)S(1)}, u32[]{:S(2)}, u32[]{:S(2)}) %collective-permute-start.14) | collective-permute-done | bytes 655392 | tf_op jit(solution)/shard_map/ppermute | solution.py:267
  65.9 0.9 add_other_y.1
  66.8 1.6 %collective-permute-start.15 = (s16[640,256]{1,0:T(8,128)(2,1)S(1)}, s16[640,256]{1,0:T(8,128)(2,1)S(1)}, u32[]{:S(2)}, u32[]{:S(2)}) collective-permute-start(s16[640,256]{1,0:T(8,128)(2,1)S(1)} %get-tuple-element.71), channel_id=1, source_target_pairs={{0,16},{16,0},{1,17},{17,1},{2,18},{18,2},{3,19},{19,3},{4,20},{20... | collective-permute-start | bytes 983048 | tf_op jit(solution)/shard_map/ppermute | solution.py:261
  68.4 2.5 %sum_pairs.5 = (s16[320,256]{1,0:T(8,128)(2,1)S(1)}, f32[320,256]{1,0:T(8,128)S(1)}, s16[320,256]{1,0:T(8,128)(2,1)S(1)}, s16[320,256]{1,0:T(8,128)(2,1)S(1)}) custom-call(s32[4]{0:T(128)S(1)} %pad_add_fusion.s_ref, bf16[2112,640]{1,0:T(8,128)(2,1)S(1)} %get-tuple-element.53.own_here.refs_0_, bf16[2112,640]{1,0:T(8,128)(2,1)S(1)} %collective-permute-done.4.own_there.refs_2_, ...), custom_call_target="tpu_custom_call" | custom-call | flops 1 | bytes 1 | tf_op jit(solution)/shard_map/sum_pairs/pallas_call | solution.py:86
  70.9 0.6 round_pairs.4.refs_0_
  71.5 3.6 %collective-permute-start.17 = (bf16[320,256]{1,0:T(8,128)(2,1)S(1)}, bf16[320,256]{1,0:T(8,128)(2,1)S(1)}, u32[]{:S(2)}, u32[]{:S(2)}) collective-permute-start(bf16[320,256]{1,0:T(8,128)(2,1)S(1)} %round_pairs.4.refs_0_), channel_id=1, source_target_pairs={{0,12},{4,0},{8,4},{12,8},{1,13},{5,1},{9,5},{13,9},{2,14},{6,2},{... | collective-permute-start | bytes 491528 | tf_op jit(solution)/shard_map/ppermute | solution.py:261
  75.1 1.5 %collective-permute-start.11 = (s16[320,256]{1,0:T(8,128)(2,1)S(1)}, s16[320,256]{1,0:T(8,128)(2,1)S(1)}, u32[]{:S(2)}, u32[]{:S(2)}) collective-permute-start(s16[320,256]{1,0:T(8,128)(2,1)S(1)} %get-tuple-element.67), channel_id=1, source_target_pairs={{0,2},{1,3},{2,0},{3,1},{4,6},{5,7},{6,4},{7,5},{8,10},{9,11},{10,... | collective-permute-start | bytes 491528 | tf_op jit(solution)/shard_map/ppermute | solution.py:267
  76.6 0.8 collective-permute-start.12
  77.5 1.1 %collective-permute-start.13 = (s16[320,256]{1,0:T(8,128)(2,1)S(1)}, s16[320,256]{1,0:T(8,128)(2,1)S(1)}, u32[]{:S(2)}, u32[]{:S(2)}) collective-permute-start(s16[320,256]{1,0:T(8,128)(2,1)S(1)} %get-tuple-element.69), channel_id=1, source_target_pairs={{0,16},{16,0},{1,17},{17,1},{2,18},{18,2},{3,19},{19,3},{4,20},{20... | collective-permute-start | bytes 491528 | tf_op jit(solution)/shard_map/ppermute | solution.py:261
  78.6 0.6 round_pairs.3
  79.3 0.1 collective-permute-start.19
  79.3 3.7 %collective-permute-done.11.refs_0_ = s16[320,256]{1,0:T(8,128)(2,1)S(1)} collective-permute-done((s16[320,256]{1,0:T(8,128)(2,1)S(1)}, s16[320,256]{1,0:T(8,128)(2,1)S(1)}, u32[]{:S(2)}, u32[]{:S(2)}) %collective-permute-start.11) | collective-permute-done | bytes 163872 | tf_op jit(solution)/shard_map/ppermute | solution.py:267
  83.0 0.8 collective-permute-done.12.refs_1_
  83.9 0.9 collective-permute-done.13.refs_2_
  84.7 0.7 round_pairs.5.refs_5_
  85.4 0.7 collective-permute-start.18
  86.1 0.3 collective-permute-done.19.refs_4_
  86.4 4.1 %place_pairs.2.refs_1_ = bf16[2500,256]{1,0:T(8,128)(2,1)S(1)} custom-call(s32[4]{0:T(128)S(1)} %pad_add_fusion.s_ref, bf16[320,256]{1,0:T(8,128)(2,1)S(1)} %round_pairs.4.refs_0_, bf16[320,256]{1,0:T(8,128)(2,1)S(1)} %collective-permute-done.17.refs_1_, bf16[320,256]{1,0:T(8,128)(2,1)S(1)} %get-tuple-element.72.refs_2_, ...), custom_call_target="tpu_custom_call" | custom-call | flops 1 | bytes 1 | tf_op jit(solution)/shard_map/place_pairs/pallas_call | solution.py:86
  90.6 3.1 %collective-permute-done.18.refs_0_ = bf16[320,256]{1,0:T(8,128)(2,1)S(1)} collective-permute-done((bf16[320,256]{1,0:T(8,128)(2,1)S(1)}, bf16[320,256]{1,0:T(8,128)(2,1)S(1)}, u32[]{:S(2)}, u32[]{:S(2)}) %collective-permute-start.18) | collective-permute-done | bytes 163872 | tf_op jit(solution)/shard_map/ppermute | solution.py:261
  93.6 2.4 %place_pairs.3 = bf16[2500,256]{1,0:T(8,128)(2,1)} custom-call(s32[4]{0:T(128)S(1)} %pad_add_fusion.s_ref, bf16[320,256]{1,0:T(8,128)(2,1)S(1)} %collective-permute-done.18.refs_0_, bf16[2500,256]{1,0:T(8,128)(2,1)S(1)} %place_pairs.2.refs_1_), custom_call_target="tpu_custom_call" | custom-call | flops 1 | bytes 1 | tf_op jit(solution)/shard_map/place_pairs/pallas_call | solution.py:86
  (18 shorter events, 0.0 us)
Async XLA Ops:
  0.1 1.7 %copy-start = (bf16[1024,1280]{1,0:T(8,128)(2,1)S(1)}, bf16[1024,1280]{1,0:T(8,128)(2,1)}, u32[]{:S(2)}) copy-start(bf16[1024,1280]{1,0:T(8,128)(2,1)} %v_ref.3) | copy-start | bytes 7864324
  1.8 0.7 copy-start.3
  2.5 0.7 copy-start.5
  3.2 17.1 %copy-start.1 = (bf16[1024,1280]{1,0:T(8,128)(2,1)S(1)}, bf16[1024,1280]{1,0:T(8,128)(2,1)}, u32[]{:S(2)}) copy-start(bf16[1024,1280]{1,0:T(8,128)(2,1)} %v_ref.3) | copy-start | bytes 7864324
  3.2 17.1 %copy-start.4 = (s32[1280]{0:T(1024)S(1)}, s32[1280]{0:T(1024)}, u32[]{:S(2)}) copy-start(s32[1280]{0:T(1024)} %param.7) | copy-start | bytes 15364
  6.1 32.1 %collective-permute-start.1 = (bf16[512,640]{1,0:T(8,128)(2,1)S(1)}, bf16[512,640]{1,0:T(8,128)(2,1)S(1)}, u32[]{:S(2)}, u32[]{:S(2)}) collective-permute-start(bf16[512,640]{1,0:T(8,128)(2,1)S(1)} %get-tuple-element.47), channel_id=1, source_target_pairs={{0,16},{16,0},{1,17},{17,1},{2,18},{18,2},{3,19},{19,3},{4,20},{20... | collective-permute-start | bytes 1966088 | tf_op jit(solution)/shard_map/ppermute | solution.py:261
  9.1 29.1 %collective-permute-start = (bf16[512,640]{1,0:T(8,128)(2,1)S(1)}, bf16[512,640]{1,0:T(8,128)(2,1)S(1)}, u32[]{:S(2)}, u32[]{:S(2)}) collective-permute-start(bf16[512,640]{1,0:T(8,128)(2,1)S(1)} %get-tuple-element.43), channel_id=1, source_target_pairs={{0,16},{16,0},{1,17},{17,1},{2,18},{18,2},{3,19},{19,3},{4,20},{20... | collective-permute-start | bytes 1966088 | tf_op jit(solution)/shard_map/ppermute | solution.py:261
  9.2 1.9 %copy-start.2 = (bf16[320,2,2500]{2,1,0:T(2,128)(2,1)S(1)}, bf16[320,2,2500]{2,1,0:T(2,128)(2,1)}, u32[]{:S(2)}) copy-start(bf16[320,2,2500]{2,1,0:T(2,128)(2,1)} %t_ref) | copy-start | bytes 9600004
  16.2 14.0 %collective-permute-start.2 = (bf16[320,640]{1,0:T(8,128)(2,1)S(1)}, bf16[320,640]{1,0:T(8,128)(2,1)S(1)}, u32[]{:S(2)}, u32[]{:S(2)}) collective-permute-start(bf16[320,640]{1,0:T(8,128)(2,1)S(1)} %get-tuple-element.49), channel_id=1, source_target_pairs={{0,12},{4,0},{8,4},{12,8},{1,13},{5,1},{9,5},{13,9},{2,14},{6,2},{... | collective-permute-start | bytes 1228808 | tf_op jit(solution)/shard_map/ppermute | solution.py:261
  20.3 17.8 %collective-permute-start.3 = (bf16[320,640]{1,0:T(8,128)(2,1)S(1)}, bf16[320,640]{1,0:T(8,128)(2,1)S(1)}, u32[]{:S(2)}, u32[]{:S(2)}) collective-permute-start(bf16[320,640]{1,0:T(8,128)(2,1)S(1)} %get-tuple-element.50), channel_id=1, source_target_pairs={{0,4},{4,8},{8,12},{12,0},{1,5},{5,9},{9,13},{13,1},{2,6},{6,10},{... | collective-permute-start | bytes 1228808 | tf_op jit(solution)/shard_map/ppermute | solution.py:261
  38.2 6.6 %collective-permute-start.4 = (bf16[2112,640]{1,0:T(8,128)(2,1)S(1)}, bf16[2112,640]{1,0:T(8,128)(2,1)S(1)}, u32[]{:S(2)}, u32[]{:S(2)}) collective-permute-start(bf16[2112,640]{1,0:T(8,128)(2,1)S(1)} %get-tuple-element.53.own_here.refs_0_), channel_id=1, source_target_pairs={{0,1},{1,0},{2,3},{3,2},{4,5},{5,4},{6,7},{7,6},{8,9},{9,8},{10,11... | collective-permute-start | bytes 8110088 | tf_op jit(solution)/shard_map/ppermute | solution.py:264
  38.2 6.5 %collective-permute-start.7 = (bf16[512,640]{1,0:T(8,128)(2,1)S(1)}, bf16[512,640]{1,0:T(8,128)(2,1)S(1)}, u32[]{:S(2)}, u32[]{:S(2)}) collective-permute-start(bf16[512,640]{1,0:T(8,128)(2,1)S(1)} %collective-permute-done.1), channel_id=1, source_target_pairs={{0,1},{1,0},{2,3},{3,2},{4,5},{5,4},{6,7},{7,6},{8,9},{9,8},{10,11... | collective-permute-start | bytes 1966088 | tf_op jit(solution)/shard_map/ppermute | solution.py:264
  38.7 6.0 %collective-permute-start.9 = (bf16[320,640]{1,0:T(8,128)(2,1)S(1)}, bf16[320,640]{1,0:T(8,128)(2,1)S(1)}, u32[]{:S(2)}, u32[]{:S(2)}) collective-permute-start(bf16[320,640]{1,0:T(8,128)(2,1)S(1)} %collective-permute-done.2.refs_1_), channel_id=1, source_target_pairs={{0,1},{1,0},{2,3},{3,2},{4,5},{5,4},{6,7},{7,6},{8,9},{9,8},{10,11... | collective-permute-start | bytes 1228808 | tf_op jit(solution)/shard_map/ppermute | solution.py:264
  38.8 11.8 %collective-permute-start.6 = (bf16[320,640]{1,0:T(8,128)(2,1)S(1)}, bf16[320,640]{1,0:T(8,128)(2,1)S(1)}, u32[]{:S(2)}, u32[]{:S(2)}) collective-permute-start(bf16[320,640]{1,0:T(8,128)(2,1)S(1)} %collective-permute-done.3.refs_0_), channel_id=1, source_target_pairs={{0,1},{1,0},{2,3},{3,2},{4,5},{5,4},{6,7},{7,6},{8,9},{9,8},{10,11... | collective-permute-start | bytes 1228808 | tf_op jit(solution)/shard_map/ppermute | solution.py:264
  39.2 24.4 %collective-permute-start.5 = (bf16[320,640]{1,0:T(8,128)(2,1)S(1)}, bf16[320,640]{1,0:T(8,128)(2,1)S(1)}, u32[]{:S(2)}, u32[]{:S(2)}) collective-permute-start(bf16[320,640]{1,0:T(8,128)(2,1)S(1)} %get-tuple-element.54), channel_id=1, source_target_pairs={{0,8},{4,12},{8,0},{12,4},{1,9},{5,13},{9,1},{13,5},{2,10},{6,14},... | collective-permute-start | bytes 1228808 | tf_op jit(solution)/shard_map/ppermute | solution.py:261
  49.0 16.8 %collective-permute-start.14 = (s16[2,640,256]{2,1,0:T(8,128)(2,1)S(1)}, s16[2,640,256]{2,1,0:T(8,128)(2,1)S(1)}, u32[]{:S(2)}, u32[]{:S(2)}) collective-permute-start(s16[2,640,256]{2,1,0:T(8,128)(2,1)S(1)} %get-tuple-element.63), channel_id=1, source_target_pairs={{0,2},{1,3},{2,0},{3,1},{4,6},{5,7},{6,4},{7,5},{8,10},{9,11},{10,... | collective-permute-start | bytes 1966088 | tf_op jit(solution)/shard_map/ppermute | solution.py:267
  53.4 9.5 %collective-permute-start.8 = (s16[320,512]{1,0:T(8,128)(2,1)S(1)}, s16[320,512]{1,0:T(8,128)(2,1)S(1)}, u32[]{:S(2)}, u32[]{:S(2)}) collective-permute-start(s16[320,512]{1,0:T(8,128)(2,1)S(1)} %get-tuple-element.60), channel_id=1, source_target_pairs={{0,16},{16,0},{1,17},{17,1},{2,18},{18,2},{3,19},{19,3},{4,20},{20... | collective-permute-start | bytes 983048 | tf_op jit(solution)/shard_map/ppermute | solution.py:261
  63.6 4.7 %collective-permute-start.10 = (bf16[320,640]{1,0:T(8,128)(2,1)S(1)}, bf16[320,640]{1,0:T(8,128)(2,1)S(1)}, u32[]{:S(2)}, u32[]{:S(2)}) collective-permute-start(bf16[320,640]{1,0:T(8,128)(2,1)S(1)} %collective-permute-done.5.refs_0_), channel_id=1, source_target_pairs={{0,1},{1,0},{2,3},{3,2},{4,5},{5,4},{6,7},{7,6},{8,9},{9,8},{10,11... | collective-permute-start | bytes 1228808 | tf_op jit(solution)/shard_map/ppermute | solution.py:264
  63.7 7.2 %collective-permute-start.16 = (s16[320,256]{1,0:T(8,128)(2,1)S(1)}, s16[320,256]{1,0:T(8,128)(2,1)S(1)}, u32[]{:S(2)}, u32[]{:S(2)}) collective-permute-start(s16[320,256]{1,0:T(8,128)(2,1)S(1)} %get-tuple-element.74), channel_id=1, source_target_pairs={{0,2},{1,3},{2,0},{3,1},{4,6},{5,7},{6,4},{7,5},{8,10},{9,11},{10,... | collective-permute-start | bytes 491528 | tf_op jit(solution)/shard_map/ppermute | solution.py:267
  66.8 11.8 %collective-permute-start.15 = (s16[640,256]{1,0:T(8,128)(2,1)S(1)}, s16[640,256]{1,0:T(8,128)(2,1)S(1)}, u32[]{:S(2)}, u32[]{:S(2)}) collective-permute-start(s16[640,256]{1,0:T(8,128)(2,1)S(1)} %get-tuple-element.71), channel_id=1, source_target_pairs={{0,16},{16,0},{1,17},{17,1},{2,18},{18,2},{3,19},{19,3},{4,20},{20... | collective-permute-start | bytes 983048 | tf_op jit(solution)/shard_map/ppermute | solution.py:261
  71.5 7.8 %collective-permute-start.17 = (bf16[320,256]{1,0:T(8,128)(2,1)S(1)}, bf16[320,256]{1,0:T(8,128)(2,1)S(1)}, u32[]{:S(2)}, u32[]{:S(2)}) collective-permute-start(bf16[320,256]{1,0:T(8,128)(2,1)S(1)} %round_pairs.4.refs_0_), channel_id=1, source_target_pairs={{0,12},{4,0},{8,4},{12,8},{1,13},{5,1},{9,5},{13,9},{2,14},{6,2},{... | collective-permute-start | bytes 491528 | tf_op jit(solution)/shard_map/ppermute | solution.py:261
  75.1 7.9 %collective-permute-start.11 = (s16[320,256]{1,0:T(8,128)(2,1)S(1)}, s16[320,256]{1,0:T(8,128)(2,1)S(1)}, u32[]{:S(2)}, u32[]{:S(2)}) collective-permute-start(s16[320,256]{1,0:T(8,128)(2,1)S(1)} %get-tuple-element.67), channel_id=1, source_target_pairs={{0,2},{1,3},{2,0},{3,1},{4,6},{5,7},{6,4},{7,5},{8,10},{9,11},{10,... | collective-permute-start | bytes 491528 | tf_op jit(solution)/shard_map/ppermute | solution.py:267
  76.6 7.2 %collective-permute-start.12 = (s16[320,256]{1,0:T(8,128)(2,1)S(1)}, s16[320,256]{1,0:T(8,128)(2,1)S(1)}, u32[]{:S(2)}, u32[]{:S(2)}) collective-permute-start(s16[320,256]{1,0:T(8,128)(2,1)S(1)} %get-tuple-element.68), channel_id=1, source_target_pairs={{0,18},{1,19},{2,16},{3,17},{16,2},{17,3},{18,0},{19,1},{4,22},{5,... | collective-permute-start | bytes 491528 | tf_op jit(solution)/shard_map/ppermute | solution.py:271
  77.5 7.3 %collective-permute-start.13 = (s16[320,256]{1,0:T(8,128)(2,1)S(1)}, s16[320,256]{1,0:T(8,128)(2,1)S(1)}, u32[]{:S(2)}, u32[]{:S(2)}) collective-permute-start(s16[320,256]{1,0:T(8,128)(2,1)S(1)} %get-tuple-element.69), channel_id=1, source_target_pairs={{0,16},{16,0},{1,17},{17,1},{2,18},{18,2},{3,19},{19,3},{4,20},{20... | collective-permute-start | bytes 491528 | tf_op jit(solution)/shard_map/ppermute | solution.py:261
  79.3 7.2 %collective-permute-start.19 = (bf16[320,256]{1,0:T(8,128)(2,1)S(1)}, bf16[320,256]{1,0:T(8,128)(2,1)S(1)}, u32[]{:S(2)}, u32[]{:S(2)}) collective-permute-start(bf16[320,256]{1,0:T(8,128)(2,1)S(1)} %get-tuple-element.73.refs_3_), channel_id=1, source_target_pairs={{0,4},{4,8},{8,12},{12,0},{1,5},{5,9},{9,13},{13,1},{2,6},{6,10},{... | collective-permute-start | bytes 491528 | tf_op jit(solution)/shard_map/ppermute | solution.py:261
  85.4 8.2 %collective-permute-start.18 = (bf16[320,256]{1,0:T(8,128)(2,1)S(1)}, bf16[320,256]{1,0:T(8,128)(2,1)S(1)}, u32[]{:S(2)}, u32[]{:S(2)}) collective-permute-start(bf16[320,256]{1,0:T(8,128)(2,1)S(1)} %round_pairs.5.refs_5_), channel_id=1, source_target_pairs={{0,8},{4,12},{8,0},{12,4},{1,9},{5,13},{9,1},{13,5},{2,10},{6,14},... | collective-permute-start | bytes 491528 | tf_op jit(solution)/shard_map/ppermute | solution.py:261

commit v13 on v12

--- a/solution.py
+++ b/solution.py
@@ -142,15 +142,17 @@
         out_ref[...] = picked[k * chunk : (k + 1) * chunk]
 
 
-def keep_body(order, n, col_n, row_n, sub, s_ref, flat_ref, ab_ref, cd_ref, v_ref, both_ref, kept_ref):
+def keep_body(order, n, col_n, row_n, sub, s_ref, flat_ref, ab_ref, cd_ref, v_ref, both_ref, kept_ref, far_ref):
     z = s_ref[1]
     half, k_here = kept_ref.shape
     pairs = both_ref.shape[0] - half
     place = lax.broadcasted_iota(jnp.int32, (pairs // (len(order) + 1), 1), 0)
     inside, turned = inside_columns(place, n, z)
     picks = [inside if r == 0 else pair_columns(place, n, z, lax.rem(z + r, col_n), True) for r in order] + [turned]
+    picks.append(pair_columns(place, n, z, lax.rem(z - order[-1] + col_n, col_n), False))
     picked = dot_nt(one_hot_rows(jnp.concatenate(picks, axis=0), flat_ref.shape[1]), flat_ref[...])
-    both_ref[:pairs] = picked.astype(jnp.bfloat16)
+    both_ref[:pairs] = picked[:pairs].astype(jnp.bfloat16)
+    far_ref[...] = picked[pairs:].astype(jnp.bfloat16)
     masked = masked_rows(0, row_n, sub, k_here, s_ref, ab_ref, cd_ref, v_ref)
     both_ref[pairs:] = masked[:half]
     kept_ref[...] = masked[half:]
@@ -289,24 +291,24 @@
         passed[by], kept[by] = shift(gone, "row", -by), shift(stay, "row", -by)
 
     amplitudes, _ = lax.optimization_barrier((amplitudes, stay))
-    sent_order = near + [far]
+    sent_order = near
     flat, *sent = call(
         "send_columns",
         functools.partial(send_body, sent_order, n, col_n),
         scalars,
         [amplitudes],
-        [((k_here, -(-columns // LANES) * LANES), bf16)] + [((chunk, k_here), bf16)] * len(sent_order),
+        [((k_here, -(-columns // LANES) * LANES), bf16)] + [((chunk, k_here), bf16)] * len(near),
     )
     away = {r: shift(s, "col", -r) for r, s in zip(near, sent)}
 
-    both, kept[0] = call(
+    both, kept[0], far_sent = call(
         "keep_columns",
         functools.partial(keep_body, order, n, col_n, row_n, sub),
         scalars,
         [flat, ab_row, cd_row, integrals],
-        [(((col_n + 1) * chunk + 2 * tall, k_here), bf16), ((2 * tall, k_here), bf16)],
+        [(((col_n + 1) * chunk + 2 * tall, k_here), bf16), ((2 * tall, k_here), bf16), ((chunk, k_here), bf16)],
     )
-    far_sent, away = lax.optimization_barrier((sent[-1], away))
+    far_sent, away = lax.optimization_barrier((far_sent, away))
     arrived = lax.optimization_barrier((both, kept[1:], passed[1:], *[away[r] for r in near]))
     behind, kept[1:], passed, *arrived = arrived
     away_there = {r: other_core(a) for r, a in zip(near, arrived)}

time: 96.3 us -> 96.4 us (level)
  no operation moved by 1% of the time
where the time goes in v13:
time: 96.4 us; the launch traced here: 96.2 us
  Pallas kernels  37.4 us (39%)
  waiting for transfers between devices  28.9 us (30%)
  starting transfers between devices  24.6 us (26%)
  local copies, waits for them, and re-layouts  5.06 us (5%)
    pallas_call x13, Pallas kernels, call(): pl.pallas_call(body, name=name, out_shape=shapes, compiler_params=pltpu.C...  37.4 us
    ppermute x11, waiting for transfers between devices, shift(): lax.ppermute(array, axis, [(i, (i + by) % count) for i in range(count)])  19.9 us
    ppermute x11, starting transfers between devices, shift(): lax.ppermute(array, axis, [(i, (i + by) % count) for i in range(count)])  19.2 us
    ppermute x3, waiting for transfers between devices, other_y(): return lax.ppermute(array, 'depth', [(i, i ^ 2) for i in range(depth_n)])  5.28 us
    unnamed x12, local copies, waits for them, and re-layouts  5.06 us
    ppermute x3, starting transfers between devices, other_y(): return lax.ppermute(array, 'depth', [(i, i ^ 2) for i in range(depth_n)])  3.94 us
    ppermute x5, waiting for transfers between devices, other_core(): return lax.ppermute(array, 'depth', [(i, i ^ 1) for i in range(depth_n)])  2.7 us
  transfers between devices with their start and end apart: 20, of which 10 were waited for; matrix products, arithmetic and copies ran while one was open for 0% of the time, Pallas kernels for 33%

profile of v13, /device:TPU:0, one launch (start us, length us, event | category | flops | bytes accessed | tf_op | source)
XLA Modules:
  0.0 96.2 jit_solution(6595523243470045122)
XLA Ops:
  0.0 0.1 pad_add_fusion.s_ref
  0.1 1.7 %copy-done = bf16[1024,1280]{1,0:T(8,128)(2,1)S(1)} copy-done((bf16[1024,1280]{1,0:T(8,128)(2,1)S(1)}, bf16[1024,1280]{1,0:T(8,128)(2,1)}, u32[]{:S(2)}) %copy-start) | copy-done | bytes 2621464
  1.8 0.7 copy-done.3
  2.5 0.7 copy-done.5
  3.2 2.9 %mask_integrals.1 = (bf16[512,640]{1,0:T(8,128)(2,1)S(1)}, bf16[512,640]{1,0:T(8,128)(2,1)S(1)}) custom-call(s32[4]{0:T(128)S(1)} %pad_add_fusion.s_ref, s32[8,128]{1,0:T(8,128)S(1)} %bitcast.9, s32[10,128]{1,0:T(8,128)S(1)} %bitcast.7, bf16[1024,1280]{1,0:T(8,128)(2,1)S(1)} %copy-done), custom_call_target="tpu_custom_call" | custom-call | flops 1 | bytes 1 | tf_op jit(solution)/shard_map/mask_integrals/pallas_call | solution.py:86
  6.1 3.0 %collective-permute-start.1 = (bf16[512,640]{1,0:T(8,128)(2,1)S(1)}, bf16[512,640]{1,0:T(8,128)(2,1)S(1)}, u32[]{:S(2)}, u32[]{:S(2)}) collective-permute-start(bf16[512,640]{1,0:T(8,128)(2,1)S(1)} %get-tuple-element.47), channel_id=1, source_target_pairs={{0,16},{16,0},{1,17},{17,1},{2,18},{18,2},{3,19},{19,3},{4,20},{20... | collective-permute-start | bytes 1966088 | tf_op jit(solution)/shard_map/ppermute | solution.py:263
  9.1 0.1 collective-permute-start
  9.2 1.9 %copy-done.2 = bf16[320,2,2500]{2,1,0:T(2,128)(2,1)S(1)} copy-done((bf16[320,2,2500]{2,1,0:T(2,128)(2,1)S(1)}, bf16[320,2,2500]{2,1,0:T(2,128)(2,1)}, u32[]{:S(2)}) %copy-start.2) | copy-done | bytes 3200024
  11.1 3.7 %send_columns.1 = (bf16[640,2560]{1,0:T(8,128)(2,1)S(1)}, bf16[320,640]{1,0:T(8,128)(2,1)S(1)}, bf16[320,640]{1,0:T(8,128)(2,1)S(1)}) custom-call(s32[4]{0:T(128)S(1)} %pad_add_fusion.s_ref, bf16[320,2,2500]{2,1,0:T(2,128)(2,1)S(1)} %copy-done.2), custom_call_target="tpu_custom_call" | custom-call | flops 1 | bytes 1 | tf_op jit(solution)/shard_map/send_columns/pallas_call | solution.py:86
  14.8 4.1 %collective-permute-start.2 = (bf16[320,640]{1,0:T(8,128)(2,1)S(1)}, bf16[320,640]{1,0:T(8,128)(2,1)S(1)}, u32[]{:S(2)}, u32[]{:S(2)}) collective-permute-start(bf16[320,640]{1,0:T(8,128)(2,1)S(1)} %get-tuple-element.49), channel_id=1, source_target_pairs={{0,12},{4,0},{8,4},{12,8},{1,13},{5,1},{9,5},{13,9},{2,14},{6,2},{... | collective-permute-start | bytes 1228808 | tf_op jit(solution)/shard_map/ppermute | solution.py:263
  18.9 0.0 collective-permute-start.3
  18.9 11.1 %keep_columns.1 = (bf16[2112,640]{1,0:T(8,128)(2,1)S(1)}, bf16[512,640]{1,0:T(8,128)(2,1)S(1)}, bf16[320,640]{1,0:T(8,128)(2,1)S(1)}) custom-call(s32[4]{0:T(128)S(1)} %pad_add_fusion.s_ref, bf16[640,2560]{1,0:T(8,128)(2,1)S(1)} %get-tuple-element.45.flat_ref, s32[8,128]{1,0:T(8,128)S(1)} %bitcast.10, s32[10,128]{1,0:T(8,128)S(1)} %bitcast.8, ...), custom_call_target="tpu_custom_call" | custom-call | flops 1 | bytes 1 | tf_op jit(solution)/shard_map/keep_columns/pallas_call | solution.py:86
  30.1 6.7 %collective-permute-done.3.refs_0_ = bf16[320,640]{1,0:T(8,128)(2,1)S(1)} collective-permute-done((bf16[320,640]{1,0:T(8,128)(2,1)S(1)}, bf16[320,640]{1,0:T(8,128)(2,1)S(1)}, u32[]{:S(2)}, u32[]{:S(2)}) %collective-permute-start.3) | collective-permute-done | bytes 409632 | tf_op jit(solution)/shard_map/ppermute | solution.py:263
  36.8 1.1 %collective-permute-done.refs_3_.refs_5_ = bf16[512,640]{1,0:T(8,128)(2,1)S(1)} collective-permute-done((bf16[512,640]{1,0:T(8,128)(2,1)S(1)}, bf16[512,640]{1,0:T(8,128)(2,1)S(1)}, u32[]{:S(2)}, u32[]{:S(2)}) %collective-permute-start) | collective-permute-done | bytes 655392 | tf_op jit(solution)/shard_map/ppermute | solution.py:263
  37.9 0.5 collective-permute-start.7
  38.4 0.0 collective-permute-start.9
  38.4 0.5 collective-permute-start.6
  38.9 2.8 %collective-permute-start.5 = (bf16[320,640]{1,0:T(8,128)(2,1)S(1)}, bf16[320,640]{1,0:T(8,128)(2,1)S(1)}, u32[]{:S(2)}, u32[]{:S(2)}) collective-permute-start(bf16[320,640]{1,0:T(8,128)(2,1)S(1)} %get-tuple-element.54), channel_id=1, source_target_pairs={{0,8},{4,12},{8,0},{12,4},{1,9},{5,13},{9,1},{13,5},{2,10},{6,14},... | collective-permute-start | bytes 1228808 | tf_op jit(solution)/shard_map/ppermute | solution.py:263
  41.7 2.7 %collective-permute-done.9.refs_3_ = bf16[320,640]{1,0:T(8,128)(2,1)S(1)} collective-permute-done((bf16[320,640]{1,0:T(8,128)(2,1)S(1)}, bf16[320,640]{1,0:T(8,128)(2,1)S(1)}, u32[]{:S(2)}, u32[]{:S(2)}) %collective-permute-start.9) | collective-permute-done | bytes 409632 | tf_op jit(solution)/shard_map/ppermute | solution.py:266
  44.4 0.0 collective-permute-done.7.refs_4_.refs_6_
  44.4 4.5 %sum_pairs.4 = (s16[2,640,256]{2,1,0:T(8,128)(2,1)S(1)}, f32[2,640,256]{2,1,0:T(8,128)S(1)}) custom-call(s32[4]{0:T(128)S(1)} %pad_add_fusion.s_ref, bf16[2112,640]{1,0:T(8,128)(2,1)S(1)} %get-tuple-element.53.own_here.refs_0_, bf16[2112,640]{1,0:T(8,128)(2,1)S(1)} %collective-permute-done.4.own_there.refs_2_, ...), custom_call_target="tpu_custom_call" | custom-call | flops 1 | bytes 1 | tf_op jit(solution)/shard_map/sum_pairs/pallas_call | solution.py:86
  48.9 1.8 %collective-permute-start.14 = (s16[2,640,256]{2,1,0:T(8,128)(2,1)S(1)}, s16[2,640,256]{2,1,0:T(8,128)(2,1)S(1)}, u32[]{:S(2)}, u32[]{:S(2)}) collective-permute-start(s16[2,640,256]{2,1,0:T(8,128)(2,1)S(1)} %get-tuple-element.63), channel_id=1, source_target_pairs={{0,2},{1,3},{2,0},{3,1},{4,6},{5,7},{6,4},{7,5},{8,10},{9,11},{10,... | collective-permute-start | bytes 1966088 | tf_op jit(solution)/shard_map/ppermute | solution.py:269
  50.8 2.5 %sum_pairs.3 = (s16[320,512]{1,0:T(8,128)(2,1)S(1)}, f32[320,512]{1,0:T(8,128)S(1)}) custom-call(s32[4]{0:T(128)S(1)} %pad_add_fusion.s_ref, bf16[2112,640]{1,0:T(8,128)(2,1)S(1)} %get-tuple-element.53.own_here.refs_0_, bf16[2112,640]{1,0:T(8,128)(2,1)S(1)} %collective-permute-done.4.own_there.refs_2_, bf16[320,640]{1,0:T(8,128)(2,1)S(1)} %collective-permute-done.3.refs_0_, ...), custom_call_target="tpu_custom_call" | custom-call | flops 1 | bytes 1 | tf_op jit(solution)/shard_map/sum_pairs/pallas_call | solution.py:86
  53.3 1.6 %collective-permute-start.8 = (s16[320,512]{1,0:T(8,128)(2,1)S(1)}, s16[320,512]{1,0:T(8,128)(2,1)S(1)}, u32[]{:S(2)}, u32[]{:S(2)}) collective-permute-start(s16[320,512]{1,0:T(8,128)(2,1)S(1)} %get-tuple-element.60), channel_id=1, source_target_pairs={{0,16},{16,0},{1,17},{17,1},{2,18},{18,2},{3,19},{19,3},{4,20},{20... | collective-permute-start | bytes 983048 | tf_op jit(solution)/shard_map/ppermute | solution.py:263
  54.8 8.0 %collective-permute-done.8.refs_0_ = s16[320,512]{1,0:T(8,128)(2,1)S(1)} collective-permute-done((s16[320,512]{1,0:T(8,128)(2,1)S(1)}, s16[320,512]{1,0:T(8,128)(2,1)S(1)}, u32[]{:S(2)}, u32[]{:S(2)}) %collective-permute-start.8) | collective-permute-done | bytes 327712 | tf_op jit(solution)/shard_map/ppermute | solution.py:263
  62.8 0.7 add_other_x.1
  63.6 0.1 collective-permute-start.10
  63.6 0.4 collective-permute-start.16
  64.0 1.8 %collective-permute-done.14.coded_ref = s16[2,640,256]{2,1,0:T(8,128)(2,1)S(1)} collective-permute-done((s16[2,640,256]{2,1,0:T(8,128)(2,1)S(1)}, s16[2,640,256]{2,1,0:T(8,128)(2,1)S(1)}, u32[]{:S(2)}, u32[]{:S(2)}) %collective-permute-start.14) | collective-permute-done | bytes 655392 | tf_op jit(solution)/shard_map/ppermute | solution.py:269
  65.8 0.9 add_other_y.1
  66.7 1.8 %collective-permute-start.15 = (s16[640,256]{1,0:T(8,128)(2,1)S(1)}, s16[640,256]{1,0:T(8,128)(2,1)S(1)}, u32[]{:S(2)}, u32[]{:S(2)}) collective-permute-start(s16[640,256]{1,0:T(8,128)(2,1)S(1)} %get-tuple-element.71), channel_id=1, source_target_pairs={{0,16},{16,0},{1,17},{17,1},{2,18},{18,2},{3,19},{19,3},{4,20},{20... | collective-permute-start | bytes 983048 | tf_op jit(solution)/shard_map/ppermute | solution.py:263
  68.5 2.5 %sum_pairs.5 = (s16[320,256]{1,0:T(8,128)(2,1)S(1)}, f32[320,256]{1,0:T(8,128)S(1)}, s16[320,256]{1,0:T(8,128)(2,1)S(1)}, s16[320,256]{1,0:T(8,128)(2,1)S(1)}) custom-call(s32[4]{0:T(128)S(1)} %pad_add_fusion.s_ref, bf16[2112,640]{1,0:T(8,128)(2,1)S(1)} %get-tuple-element.53.own_here.refs_0_, bf16[2112,640]{1,0:T(8,128)(2,1)S(1)} %collective-permute-done.4.own_there.refs_2_, ...), custom_call_target="tpu_custom_call" | custom-call | flops 1 | bytes 1 | tf_op jit(solution)/shard_map/sum_pairs/pallas_call | solution.py:86
  71.1 0.6 round_pairs.4.refs_0_
  71.7 3.6 %collective-permute-start.17 = (bf16[320,256]{1,0:T(8,128)(2,1)S(1)}, bf16[320,256]{1,0:T(8,128)(2,1)S(1)}, u32[]{:S(2)}, u32[]{:S(2)}) collective-permute-start(bf16[320,256]{1,0:T(8,128)(2,1)S(1)} %round_pairs.4.refs_0_), channel_id=1, source_target_pairs={{0,12},{4,0},{8,4},{12,8},{1,13},{5,1},{9,5},{13,9},{2,14},{6,2},{... | collective-permute-start | bytes 491528 | tf_op jit(solution)/shard_map/ppermute | solution.py:263
  75.3 1.7 %collective-permute-start.11 = (s16[320,256]{1,0:T(8,128)(2,1)S(1)}, s16[320,256]{1,0:T(8,128)(2,1)S(1)}, u32[]{:S(2)}, u32[]{:S(2)}) collective-permute-start(s16[320,256]{1,0:T(8,128)(2,1)S(1)} %get-tuple-element.67), channel_id=1, source_target_pairs={{0,2},{1,3},{2,0},{3,1},{4,6},{5,7},{6,4},{7,5},{8,10},{9,11},{10,... | collective-permute-start | bytes 491528 | tf_op jit(solution)/shard_map/ppermute | solution.py:269
  77.1 0.4 collective-permute-start.12
  77.5 1.4 %collective-permute-start.13 = (s16[320,256]{1,0:T(8,128)(2,1)S(1)}, s16[320,256]{1,0:T(8,128)(2,1)S(1)}, u32[]{:S(2)}, u32[]{:S(2)}) collective-permute-start(s16[320,256]{1,0:T(8,128)(2,1)S(1)} %get-tuple-element.69), channel_id=1, source_target_pairs={{0,16},{16,0},{1,17},{17,1},{2,18},{18,2},{3,19},{19,3},{4,20},{20... | collective-permute-start | bytes 491528 | tf_op jit(solution)/shard_map/ppermute | solution.py:263
  78.8 0.6 round_pairs.3
  79.5 0.1 collective-permute-start.19
  79.5 3.5 %collective-permute-done.11.refs_0_ = s16[320,256]{1,0:T(8,128)(2,1)S(1)} collective-permute-done((s16[320,256]{1,0:T(8,128)(2,1)S(1)}, s16[320,256]{1,0:T(8,128)(2,1)S(1)}, u32[]{:S(2)}, u32[]{:S(2)}) %collective-permute-start.11) | collective-permute-done | bytes 163872 | tf_op jit(solution)/shard_map/ppermute | solution.py:269
  83.0 1.1 %collective-permute-done.12.refs_1_ = s16[320,256]{1,0:T(8,128)(2,1)S(1)} collective-permute-done((s16[320,256]{1,0:T(8,128)(2,1)S(1)}, s16[320,256]{1,0:T(8,128)(2,1)S(1)}, u32[]{:S(2)}, u32[]{:S(2)}) %collective-permute-start.12) | collective-permute-done | bytes 163872 | tf_op jit(solution)/shard_map/ppermute | solution.py:273
  84.1 0.8 collective-permute-done.13.refs_2_
  84.9 0.7 round_pairs.5.refs_5_
  85.6 0.7 collective-permute-start.18
  86.4 0.3 collective-permute-done.19.refs_4_
  86.6 4.1 %place_pairs.2.refs_1_ = bf16[2500,256]{1,0:T(8,128)(2,1)S(1)} custom-call(s32[4]{0:T(128)S(1)} %pad_add_fusion.s_ref, bf16[320,256]{1,0:T(8,128)(2,1)S(1)} %round_pairs.4.refs_0_, bf16[320,256]{1,0:T(8,128)(2,1)S(1)} %collective-permute-done.17.refs_1_, bf16[320,256]{1,0:T(8,128)(2,1)S(1)} %get-tuple-element.72.refs_2_, ...), custom_call_target="tpu_custom_call" | custom-call | flops 1 | bytes 1 | tf_op jit(solution)/shard_map/place_pairs/pallas_call | solution.py:86
  90.8 3.0 %collective-permute-done.18.refs_0_ = bf16[320,256]{1,0:T(8,128)(2,1)S(1)} collective-permute-done((bf16[320,256]{1,0:T(8,128)(2,1)S(1)}, bf16[320,256]{1,0:T(8,128)(2,1)S(1)}, u32[]{:S(2)}, u32[]{:S(2)}) %collective-permute-start.18) | collective-permute-done | bytes 163872 | tf_op jit(solution)/shard_map/ppermute | solution.py:263
  93.8 2.4 %place_pairs.3 = bf16[2500,256]{1,0:T(8,128)(2,1)} custom-call(s32[4]{0:T(128)S(1)} %pad_add_fusion.s_ref, bf16[320,256]{1,0:T(8,128)(2,1)S(1)} %collective-permute-done.18.refs_0_, bf16[2500,256]{1,0:T(8,128)(2,1)S(1)} %place_pairs.2.refs_1_), custom_call_target="tpu_custom_call" | custom-call | flops 1 | bytes 1 | tf_op jit(solution)/shard_map/place_pairs/pallas_call | solution.py:86
  (18 shorter events, 0.0 us)
Async XLA Ops:
  0.1 1.7 %copy-start = (bf16[1024,1280]{1,0:T(8,128)(2,1)S(1)}, bf16[1024,1280]{1,0:T(8,128)(2,1)}, u32[]{:S(2)}) copy-start(bf16[1024,1280]{1,0:T(8,128)(2,1)} %v_ref.3) | copy-start | bytes 7864324
  1.8 0.7 copy-start.3
  2.5 0.7 copy-start.5
  3.2 15.7 %copy-start.1 = (bf16[1024,1280]{1,0:T(8,128)(2,1)S(1)}, bf16[1024,1280]{1,0:T(8,128)(2,1)}, u32[]{:S(2)}) copy-start(bf16[1024,1280]{1,0:T(8,128)(2,1)} %v_ref.3) | copy-start | bytes 7864324
  3.2 15.7 %copy-start.4 = (s32[1280]{0:T(1024)S(1)}, s32[1280]{0:T(1024)}, u32[]{:S(2)}) copy-start(s32[1280]{0:T(1024)} %param.7) | copy-start | bytes 15364
  6.1 30.7 %collective-permute-start.1 = (bf16[512,640]{1,0:T(8,128)(2,1)S(1)}, bf16[512,640]{1,0:T(8,128)(2,1)S(1)}, u32[]{:S(2)}, u32[]{:S(2)}) collective-permute-start(bf16[512,640]{1,0:T(8,128)(2,1)S(1)} %get-tuple-element.47), channel_id=1, source_target_pairs={{0,16},{16,0},{1,17},{17,1},{2,18},{18,2},{3,19},{19,3},{4,20},{20... | collective-permute-start | bytes 1966088 | tf_op jit(solution)/shard_map/ppermute | solution.py:263
  9.1 28.8 %collective-permute-start = (bf16[512,640]{1,0:T(8,128)(2,1)S(1)}, bf16[512,640]{1,0:T(8,128)(2,1)S(1)}, u32[]{:S(2)}, u32[]{:S(2)}) collective-permute-start(bf16[512,640]{1,0:T(8,128)(2,1)S(1)} %get-tuple-element.43), channel_id=1, source_target_pairs={{0,16},{16,0},{1,17},{17,1},{2,18},{18,2},{3,19},{19,3},{4,20},{20... | collective-permute-start | bytes 1966088 | tf_op jit(solution)/shard_map/ppermute | solution.py:263
  9.2 1.9 %copy-start.2 = (bf16[320,2,2500]{2,1,0:T(2,128)(2,1)S(1)}, bf16[320,2,2500]{2,1,0:T(2,128)(2,1)}, u32[]{:S(2)}) copy-start(bf16[320,2,2500]{2,1,0:T(2,128)(2,1)} %t_ref) | copy-start | bytes 9600004
  14.8 15.2 %collective-permute-start.2 = (bf16[320,640]{1,0:T(8,128)(2,1)S(1)}, bf16[320,640]{1,0:T(8,128)(2,1)S(1)}, u32[]{:S(2)}, u32[]{:S(2)}) collective-permute-start(bf16[320,640]{1,0:T(8,128)(2,1)S(1)} %get-tuple-element.49), channel_id=1, source_target_pairs={{0,12},{4,0},{8,4},{12,8},{1,13},{5,1},{9,5},{13,9},{2,14},{6,2},{... | collective-permute-start | bytes 1228808 | tf_op jit(solution)/shard_map/ppermute | solution.py:263
  18.9 17.8 %collective-permute-start.3 = (bf16[320,640]{1,0:T(8,128)(2,1)S(1)}, bf16[320,640]{1,0:T(8,128)(2,1)S(1)}, u32[]{:S(2)}, u32[]{:S(2)}) collective-permute-start(bf16[320,640]{1,0:T(8,128)(2,1)S(1)} %get-tuple-element.50), channel_id=1, source_target_pairs={{0,4},{4,8},{8,12},{12,0},{1,5},{5,9},{9,13},{13,1},{2,6},{6,10},{... | collective-permute-start | bytes 1228808 | tf_op jit(solution)/shard_map/ppermute | solution.py:263
  37.9 6.6 %collective-permute-start.4 = (bf16[2112,640]{1,0:T(8,128)(2,1)S(1)}, bf16[2112,640]{1,0:T(8,128)(2,1)S(1)}, u32[]{:S(2)}, u32[]{:S(2)}) collective-permute-start(bf16[2112,640]{1,0:T(8,128)(2,1)S(1)} %get-tuple-element.53.own_here.refs_0_), channel_id=1, source_target_pairs={{0,1},{1,0},{2,3},{3,2},{4,5},{5,4},{6,7},{7,6},{8,9},{9,8},{10,11... | collective-permute-start | bytes 8110088 | tf_op jit(solution)/shard_map/ppermute | solution.py:266
  37.9 6.5 %collective-permute-start.7 = (bf16[512,640]{1,0:T(8,128)(2,1)S(1)}, bf16[512,640]{1,0:T(8,128)(2,1)S(1)}, u32[]{:S(2)}, u32[]{:S(2)}) collective-permute-start(bf16[512,640]{1,0:T(8,128)(2,1)S(1)} %collective-permute-done.1), channel_id=1, source_target_pairs={{0,1},{1,0},{2,3},{3,2},{4,5},{5,4},{6,7},{7,6},{8,9},{9,8},{10,11... | collective-permute-start | bytes 1966088 | tf_op jit(solution)/shard_map/ppermute | solution.py:266
  38.4 6.0 %collective-permute-start.9 = (bf16[320,640]{1,0:T(8,128)(2,1)S(1)}, bf16[320,640]{1,0:T(8,128)(2,1)S(1)}, u32[]{:S(2)}, u32[]{:S(2)}) collective-permute-start(bf16[320,640]{1,0:T(8,128)(2,1)S(1)} %collective-permute-done.2.refs_1_), channel_id=1, source_target_pairs={{0,1},{1,0},{2,3},{3,2},{4,5},{5,4},{6,7},{7,6},{8,9},{9,8},{10,11... | collective-permute-start | bytes 1228808 | tf_op jit(solution)/shard_map/ppermute | solution.py:266
  38.4 12.4 %collective-permute-start.6 = (bf16[320,640]{1,0:T(8,128)(2,1)S(1)}, bf16[320,640]{1,0:T(8,128)(2,1)S(1)}, u32[]{:S(2)}, u32[]{:S(2)}) collective-permute-start(bf16[320,640]{1,0:T(8,128)(2,1)S(1)} %collective-permute-done.3.refs_0_), channel_id=1, source_target_pairs={{0,1},{1,0},{2,3},{3,2},{4,5},{5,4},{6,7},{7,6},{8,9},{9,8},{10,11... | collective-permute-start | bytes 1228808 | tf_op jit(solution)/shard_map/ppermute | solution.py:266
  38.9 24.7 %collective-permute-start.5 = (bf16[320,640]{1,0:T(8,128)(2,1)S(1)}, bf16[320,640]{1,0:T(8,128)(2,1)S(1)}, u32[]{:S(2)}, u32[]{:S(2)}) collective-permute-start(bf16[320,640]{1,0:T(8,128)(2,1)S(1)} %get-tuple-element.54), channel_id=1, source_target_pairs={{0,8},{4,12},{8,0},{12,4},{1,9},{5,13},{9,1},{13,5},{2,10},{6,14},... | collective-permute-start | bytes 1228808 | tf_op jit(solution)/shard_map/ppermute | solution.py:263
  48.9 16.9 %collective-permute-start.14 = (s16[2,640,256]{2,1,0:T(8,128)(2,1)S(1)}, s16[2,640,256]{2,1,0:T(8,128)(2,1)S(1)}, u32[]{:S(2)}, u32[]{:S(2)}) collective-permute-start(s16[2,640,256]{2,1,0:T(8,128)(2,1)S(1)} %get-tuple-element.63), channel_id=1, source_target_pairs={{0,2},{1,3},{2,0},{3,1},{4,6},{5,7},{6,4},{7,5},{8,10},{9,11},{10,... | collective-permute-start | bytes 1966088 | tf_op jit(solution)/shard_map/ppermute | solution.py:269
  53.3 9.5 %collective-permute-start.8 = (s16[320,512]{1,0:T(8,128)(2,1)S(1)}, s16[320,512]{1,0:T(8,128)(2,1)S(1)}, u32[]{:S(2)}, u32[]{:S(2)}) collective-permute-start(s16[320,512]{1,0:T(8,128)(2,1)S(1)} %get-tuple-element.60), channel_id=1, source_target_pairs={{0,16},{16,0},{1,17},{17,1},{2,18},{18,2},{3,19},{19,3},{4,20},{20... | collective-permute-start | bytes 983048 | tf_op jit(solution)/shard_map/ppermute | solution.py:263
  63.6 5.0 %collective-permute-start.10 = (bf16[320,640]{1,0:T(8,128)(2,1)S(1)}, bf16[320,640]{1,0:T(8,128)(2,1)S(1)}, u32[]{:S(2)}, u32[]{:S(2)}) collective-permute-start(bf16[320,640]{1,0:T(8,128)(2,1)S(1)} %collective-permute-done.5.refs_0_), channel_id=1, source_target_pairs={{0,1},{1,0},{2,3},{3,2},{4,5},{5,4},{6,7},{7,6},{8,9},{9,8},{10,11... | collective-permute-start | bytes 1228808 | tf_op jit(solution)/shard_map/ppermute | solution.py:266
  63.6 7.4 %collective-permute-start.16 = (s16[320,256]{1,0:T(8,128)(2,1)S(1)}, s16[320,256]{1,0:T(8,128)(2,1)S(1)}, u32[]{:S(2)}, u32[]{:S(2)}) collective-permute-start(s16[320,256]{1,0:T(8,128)(2,1)S(1)} %get-tuple-element.74), channel_id=1, source_target_pairs={{0,2},{1,3},{2,0},{3,1},{4,6},{5,7},{6,4},{7,5},{8,10},{9,11},{10,... | collective-permute-start | bytes 491528 | tf_op jit(solution)/shard_map/ppermute | solution.py:269
  66.7 12.1 %collective-permute-start.15 = (s16[640,256]{1,0:T(8,128)(2,1)S(1)}, s16[640,256]{1,0:T(8,128)(2,1)S(1)}, u32[]{:S(2)}, u32[]{:S(2)}) collective-permute-start(s16[640,256]{1,0:T(8,128)(2,1)S(1)} %get-tuple-element.71), channel_id=1, source_target_pairs={{0,16},{16,0},{1,17},{17,1},{2,18},{18,2},{3,19},{19,3},{4,20},{20... | collective-permute-start | bytes 983048 | tf_op jit(solution)/shard_map/ppermute | solution.py:263
  71.7 7.9 %collective-permute-start.17 = (bf16[320,256]{1,0:T(8,128)(2,1)S(1)}, bf16[320,256]{1,0:T(8,128)(2,1)S(1)}, u32[]{:S(2)}, u32[]{:S(2)}) collective-permute-start(bf16[320,256]{1,0:T(8,128)(2,1)S(1)} %round_pairs.4.refs_0_), channel_id=1, source_target_pairs={{0,12},{4,0},{8,4},{12,8},{1,13},{5,1},{9,5},{13,9},{2,14},{6,2},{... | collective-permute-start | bytes 491528 | tf_op jit(solution)/shard_map/ppermute | solution.py:263
  75.3 7.7 %collective-permute-start.11 = (s16[320,256]{1,0:T(8,128)(2,1)S(1)}, s16[320,256]{1,0:T(8,128)(2,1)S(1)}, u32[]{:S(2)}, u32[]{:S(2)}) collective-permute-start(s16[320,256]{1,0:T(8,128)(2,1)S(1)} %get-tuple-element.67), channel_id=1, source_target_pairs={{0,2},{1,3},{2,0},{3,1},{4,6},{5,7},{6,4},{7,5},{8,10},{9,11},{10,... | collective-permute-start | bytes 491528 | tf_op jit(solution)/shard_map/ppermute | solution.py:269
  77.1 7.0 %collective-permute-start.12 = (s16[320,256]{1,0:T(8,128)(2,1)S(1)}, s16[320,256]{1,0:T(8,128)(2,1)S(1)}, u32[]{:S(2)}, u32[]{:S(2)}) collective-permute-start(s16[320,256]{1,0:T(8,128)(2,1)S(1)} %get-tuple-element.68), channel_id=1, source_target_pairs={{0,18},{1,19},{2,16},{3,17},{16,2},{17,3},{18,0},{19,1},{4,22},{5,... | collective-permute-start | bytes 491528 | tf_op jit(solution)/shard_map/ppermute | solution.py:273
  77.5 7.5 %collective-permute-start.13 = (s16[320,256]{1,0:T(8,128)(2,1)S(1)}, s16[320,256]{1,0:T(8,128)(2,1)S(1)}, u32[]{:S(2)}, u32[]{:S(2)}) collective-permute-start(s16[320,256]{1,0:T(8,128)(2,1)S(1)} %get-tuple-element.69), channel_id=1, source_target_pairs={{0,16},{16,0},{1,17},{17,1},{2,18},{18,2},{3,19},{19,3},{4,20},{20... | collective-permute-start | bytes 491528 | tf_op jit(solution)/shard_map/ppermute | solution.py:263
  79.5 7.2 %collective-permute-start.19 = (bf16[320,256]{1,0:T(8,128)(2,1)S(1)}, bf16[320,256]{1,0:T(8,128)(2,1)S(1)}, u32[]{:S(2)}, u32[]{:S(2)}) collective-permute-start(bf16[320,256]{1,0:T(8,128)(2,1)S(1)} %get-tuple-element.73.refs_3_), channel_id=1, source_target_pairs={{0,4},{4,8},{8,12},{12,0},{1,5},{5,9},{9,13},{13,1},{2,6},{6,10},{... | collective-permute-start | bytes 491528 | tf_op jit(solution)/shard_map/ppermute | solution.py:263
  85.6 8.2 %collective-permute-start.18 = (bf16[320,256]{1,0:T(8,128)(2,1)S(1)}, bf16[320,256]{1,0:T(8,128)(2,1)S(1)}, u32[]{:S(2)}, u32[]{:S(2)}) collective-permute-start(bf16[320,256]{1,0:T(8,128)(2,1)S(1)} %round_pairs.5.refs_5_), channel_id=1, source_target_pairs={{0,8},{4,12},{8,0},{12,4},{1,9},{5,13},{9,1},{13,5},{2,10},{6,14},... | collective-permute-start | bytes 491528 | tf_op jit(solution)/shard_map/ppermute | solution.py:263
